TPU v7x, 32 devices: a whole 2x2x4 slice. The times are simulated.
32 devices in a mesh: wide: 8 (over z, x), narrow: 4 (over y, core).
Axes of the slice: x: 2, y: 2, z: 4, core: 2. Of those that a mesh axis runs over, the one named last changes fastest.
Arguments:
- features: bfloat16 [32, 20, 24, 2048], P(('wide', 'narrow')), may hold values from -40 to 40
- low_level: bfloat16 [32, 80, 96, 256], P(('wide', 'narrow')), may hold values from -40 to 40
- widths: int32 [32, 4], P(('wide', 'narrow')), may hold values from 1 to 20, 24 in all within a row
- w_point: bfloat16 [2, 2048, 256], P(None, 'wide', 'narrow'), may hold values from -0.125 to 0.125
- w_atrous: bfloat16 [3, 9, 2048, 256], P(None, None, 'wide', 'narrow'), may hold values from -0.046875 to 0.046875
- w_proj: bfloat16 [1280, 256], P('wide', 'narrow'), may hold values from -0.15625 to 0.15625
- w_low: bfloat16 [256, 48], P('wide', 'narrow'), may hold values from -0.375 to 0.375
- w_dec1: bfloat16 [9, 304, 256], P(None, 'narrow', 'wide'), may hold values from -0.109375 to 0.109375
- w_dec2: bfloat16 [9, 256, 256], P(None, 'wide', 'narrow'), may hold values from -0.125 to 0.125
- w_cls: bfloat16 [256, 21], replicated, may hold values from -0.375 to 0.375
- b_cls: float32 [21], replicated, may hold values from -3 to 3
- gains: float32 [8, 256], replicated, may hold values from 0.5 to 1.5
- biases: float32 [8, 256], replicated, may hold values from -3 to 3
- low_gain: float32 [48], replicated, may hold values from 0.5 to 1.5
- low_bias: float32 [48], replicated, may hold values from -3 to 3
- logit_grad: bfloat16 [32, 80, 96, 21], P(('wide', 'narrow')), may hold values from -6 to 6
Outputs:
- logits: bfloat16 [32, 80, 96, 21], P(('wide', 'narrow'))
- grad_features: bfloat16 [32, 20, 24, 2048], P(('wide', 'narrow'))
- grad_low_level: bfloat16 [32, 80, 96, 256], P(('wide', 'narrow'))
- grad_w_point: float32 [2, 2048, 256], P(None, 'wide', 'narrow')
- grad_w_atrous: float32 [3, 9, 2048, 256], P(None, None, 'wide', 'narrow')
- grad_w_proj: float32 [1280, 256], P('wide', 'narrow')
- grad_w_low: float32 [256, 48], P('wide', 'narrow')
- grad_w_dec1: float32 [9, 304, 256], P(None, 'narrow', 'wide')
- grad_w_dec2: float32 [9, 256, 256], P(None, 'wide', 'narrow')
- grad_w_cls: float32 [256, 21], replicated
- grad_b_cls: float32 [21], replicated
- grad_gains: float32 [8, 256], replicated
- grad_biases: float32 [8, 256], replicated
- grad_low_gain: float32 [48], replicated
- grad_low_bias: float32 [48], replicated
All inputs are finite; a program needn't handle non-finite values.
Results may differ from a plain program's by a relative error of at most 0.04.
Values may be sent and summed in bfloat16 or wider, within the bound.
No kernel may reach another device: no remote copies, remote signals or barrier semaphores. Data moves between devices by JAX's collectives and lax.ppermute only.
A program may use at most 512 MiB of HBM per device.

v0:
```python
import jax
import jax.numpy as jnp
from jax import lax
from jax.sharding import PartitionSpec as P

epsilon = 1e-05
highest = lax.Precision.HIGHEST
dilations = (6, 12, 18)


def band_ids(widths, columns):
    ends_all = jnp.cumsum(widths, axis=1)
    position = jnp.arange(columns, dtype=jnp.int32)
    band_index = jnp.sum(
        (position[None, :, None] >= ends_all[:, None, :]).astype(jnp.int32), axis=2
    )
    return jnp.where(band_index < widths.shape[1] - 1, band_index, -1)


def shifted(values, row_shift, col_shift):
    height = values.shape[1]
    columns = values.shape[2]
    padded = jnp.pad(
        values, ((0, 0), (abs(row_shift), abs(row_shift)), (abs(col_shift), abs(col_shift)), (0, 0))
    )
    row_start = abs(row_shift) + row_shift
    col_start = abs(col_shift) + col_shift
    return padded[:, row_start : row_start + height, col_start : col_start + columns, :]


def tap_mask(image_ids, height, row_shift, col_shift):
    columns = image_ids.shape[1]
    padded = jnp.pad(image_ids, ((0, 0), (abs(col_shift), abs(col_shift))), constant_values=-2)
    col_start = abs(col_shift) + col_shift
    other_ids = padded[:, col_start : col_start + columns]
    same_image = (other_ids == image_ids).astype(jnp.float32)
    row_place = jnp.arange(height) + row_shift
    inside = ((row_place >= 0) & (row_place < height)).astype(jnp.float32)
    return (inside[None, :, None] * same_image[:, None, :])[..., None]


def tap_offsets(dilation):
    return [
        ((tap_index // 3 - 1) * dilation, (tap_index % 3 - 1) * dilation) for tap_index in range(9)
    ]


def conv_forward(values, kernel, image_ids, dilation):
    products = jnp.einsum("nhwc,tcd->tnhwd", values, kernel, preferred_element_type=jnp.float32)
    running = jnp.zeros(products.shape[1:], jnp.float32)
    for tap_index, offset_pair in enumerate(tap_offsets(dilation)):
        row_shift, col_shift = offset_pair
        running = running + tap_mask(image_ids, values.shape[1], row_shift, col_shift) * shifted(
            products[tap_index], row_shift, col_shift
        )
    return running


def conv_backward(values, kernel, grad_low, image_ids, dilation):
    sources = []
    for row_shift, col_shift in tap_offsets(dilation):
        masked = (
            tap_mask(image_ids, grad_low.shape[1], row_shift, col_shift).astype(jnp.bfloat16)
            * grad_low
        )
        sources.append(shifted(masked, -row_shift, -col_shift))
    stacked = jnp.stack(sources)
    input_grad = jnp.einsum("tnhwd,tcd->nhwc", stacked, kernel, preferred_element_type=jnp.float32)
    kernel_grad = jnp.einsum("nhwc,tnhwd->tcd", values, stacked, preferred_element_type=jnp.float32)
    return (input_grad, kernel_grad)


def linear_weights(out_count, in_count):
    position = jnp.arange(out_count, dtype=jnp.int32)
    scaled = 2 * position - 3
    left_index = jnp.floor_divide(scaled, 8)
    fraction = (scaled - 8 * left_index).astype(jnp.float32) / 8.0
    lower_index = jnp.clip(left_index, 0, in_count - 1)
    upper_index = jnp.clip(left_index + 1, 0, in_count - 1)
    return (position, lower_index, upper_index, fraction)


def row_table(out_count, in_count):
    position, lower_index, upper_index, fraction = linear_weights(out_count, in_count)
    source = jnp.arange(in_count, dtype=jnp.int32)[None, :]
    lower_part = (1.0 - fraction)[:, None] * (source == lower_index[:, None]).astype(jnp.float32)
    upper_part = fraction[:, None] * (source == upper_index[:, None]).astype(jnp.float32)
    return lower_part + upper_part


def column_table(image_ids):
    columns = image_ids.shape[1]
    position, lower_index, upper_index, fraction = linear_weights(4 * columns, columns)
    source = jnp.arange(columns, dtype=jnp.int32)[None, :]

    def picker(index_row):
        return (source == index_row[:, None]).astype(jnp.int32)

    def lookup(index_row):
        return jnp.sum(image_ids[:, None, :] * picker(index_row)[None], axis=2)

    own_index = position // 4
    own_id = lookup(own_index)
    weight_lower = (1.0 - fraction)[None, :] * (lookup(lower_index) == own_id).astype(jnp.float32)
    weight_upper = fraction[None, :] * (lookup(upper_index) == own_id).astype(jnp.float32)
    weight_own = 1.0 - weight_lower - weight_upper
    table = weight_lower[:, :, None] * picker(lower_index)[None].astype(jnp.float32)
    table = table + weight_upper[:, :, None] * picker(upper_index)[None].astype(jnp.float32)
    table = table + weight_own[:, :, None] * picker(own_index)[None].astype(jnp.float32)
    return table


def normalize(values, valid_map, mean_row, variance, gain_row, bias_row):
    norm_scale = lax.rsqrt(variance + epsilon)
    centered = (values - mean_row) * norm_scale
    shaped = centered * gain_row + bias_row
    return (valid_map * jax.nn.silu(shaped), centered, shaped, norm_scale)


def norm_grad_terms(upstream, valid_map, centered, shaped):
    sigmoid_value = jax.nn.sigmoid(shaped)
    local_term = valid_map * upstream * sigmoid_value * (1.0 + shaped * (1.0 - sigmoid_value))
    axes = tuple(range(local_term.ndim - 1))
    return (local_term, jnp.sum(local_term * centered, axis=axes), jnp.sum(local_term, axis=axes))


def norm_grad_finish(
    local_term, valid_map, centered, norm_scale, gain_row, gain_sum, bias_sum, count_all
):
    inner = local_term - bias_sum / count_all - centered * gain_sum / count_all
    return (valid_map * gain_row * norm_scale * inner).astype(jnp.bfloat16)


def first_sums(blocks):
    return jnp.concatenate(
        [
            jnp.sum(values * valid_map, axis=tuple(range(values.ndim - 1)))
            for values, valid_map in blocks
        ]
    )


def square_sums(blocks, means_all):
    pieces = []
    for block_pair, mean_row in zip(blocks, means_all):
        values, valid_map = block_pair
        centered = values - mean_row
        pieces.append(jnp.sum(centered * centered * valid_map, axis=tuple(range(values.ndim - 1))))
    return jnp.concatenate(pieces)


def split_channels(flat, blocks):
    pieces = []
    offset = 0
    for values, valid_map in blocks:
        pieces.append(flat[offset : offset + values.shape[-1]])
        offset = offset + values.shape[-1]
    return pieces


def first_counts(pixel_total, images_total):
    pixel_count = pixel_total[0]
    return [pixel_count, pixel_count, pixel_count, pixel_count, images_total, 16.0 * pixel_count]


def first_moments(blocks, local_count, images_total):
    firsts, pixel_total = lax.psum((first_sums(blocks), local_count), ("wide", "narrow"))
    counts = first_counts(pixel_total, images_total)
    means_all = [
        piece / count_all for piece, count_all in zip(split_channels(firsts, blocks), counts)
    ]
    seconds = lax.psum(square_sums(blocks, means_all), ("wide", "narrow"))
    variances = [
        piece / count_all for piece, count_all in zip(split_channels(seconds, blocks), counts)
    ]
    return (means_all, variances, pixel_total)


def moments(values, valid_map, count_all):
    blocks = [(values, valid_map)]
    firsts = lax.psum(first_sums(blocks), ("wide", "narrow"))
    mean_row = firsts / count_all
    seconds = lax.psum(square_sums(blocks, [mean_row]), ("wide", "narrow"))
    variance = seconds / count_all
    return (mean_row, variance)


def pack_pairs(pairs):
    return jnp.concatenate(
        [pair_item[0] for pair_item in pairs] + [pair_item[1] for pair_item in pairs]
    )


def unpack_pairs(flat, pairs):
    lengths = [pair_item[0].shape[0] for pair_item in pairs]
    half_point = sum(lengths)
    result_pairs = []
    offset = 0
    for length_now in lengths:
        result_pairs.append(
            (
                flat[offset : offset + length_now],
                flat[half_point + offset : half_point + offset + length_now],
            )
        )
        offset = offset + length_now
    return result_pairs


def gradient_sums(pairs):
    return unpack_pairs(lax.psum(pack_pairs(pairs), ("wide", "narrow")), pairs)


def per_device(
    features,
    low_level,
    widths,
    w_point,
    w_atrous,
    w_proj,
    w_low,
    w_dec1,
    w_dec2,
    w_cls,
    b_cls,
    gains,
    biases,
    low_gain,
    low_bias,
    logit_grad,
):
    canvases = features.shape[0]
    height = features.shape[1]
    columns = features.shape[2]
    fine_columns = low_level.shape[2]
    images = widths.shape[1] - 1
    channels = gains.shape[1]
    images_total = float(canvases * lax.axis_size("wide") * lax.axis_size("narrow") * images)
    point_part, atrous_part, proj_part, reduce_part, decode_part, refine_part = (
        lax.all_gather(w_point, "narrow", axis=2, tiled=True),
        lax.all_gather(w_atrous, "narrow", axis=3, tiled=True),
        lax.all_gather(w_proj, "narrow", axis=1, tiled=True),
        lax.all_gather(w_low, "narrow", axis=1, tiled=True),
        lax.all_gather(w_dec1, "narrow", axis=1, tiled=True),
        lax.all_gather(w_dec2, "narrow", axis=2, tiled=True),
    )
    point_full, atrous_full, proj_full, reduce_full, decode_full, refine_full = (
        lax.all_gather(point_part, "wide", axis=1, tiled=True),
        lax.all_gather(atrous_part, "wide", axis=2, tiled=True),
        lax.all_gather(proj_part, "wide", axis=0, tiled=True),
        lax.all_gather(reduce_part, "wide", axis=0, tiled=True),
        lax.all_gather(decode_part, "wide", axis=2, tiled=True),
        lax.all_gather(refine_part, "wide", axis=1, tiled=True),
    )
    ids_coarse = band_ids(widths, columns)
    ids_fine = band_ids(4 * widths, fine_columns)
    valid_coarse = (ids_coarse >= 0).astype(jnp.float32)[:, None, :, None]
    valid_fine = (ids_fine >= 0).astype(jnp.float32)[:, None, :, None]
    all_ones = jnp.ones((1, 1, 1), jnp.float32)
    local_count = (height * jnp.sum(widths[:, :images])).astype(jnp.float32).reshape(1)
    member = (ids_coarse[:, :, None] == jnp.arange(images, dtype=jnp.int32)[None, None, :]).astype(
        jnp.float32
    )
    member_low = member.astype(jnp.bfloat16)
    image_sizes = (height * widths[:, :images]).astype(jnp.float32)
    coarse_z = [
        jnp.einsum("nhwc,cd->nhwd", features, point_full[0], preferred_element_type=jnp.float32)
    ]
    for branch in range(3):
        coarse_z.append(conv_forward(features, atrous_full[branch], ids_coarse, dilations[branch]))
    pooled = (
        jnp.einsum("nhwc,nwk->nkc", features, member_low, preferred_element_type=jnp.float32)
        / image_sizes[:, :, None]
    ).astype(jnp.bfloat16)
    pool_z = jnp.einsum("nkc,cd->nkd", pooled, point_full[1], preferred_element_type=jnp.float32)
    reduce_z = jnp.einsum(
        "nhwc,cd->nhwd", low_level, reduce_full, preferred_element_type=jnp.float32
    )
    blocks = [(item_z, valid_coarse) for item_z in coarse_z] + [
        (pool_z, all_ones),
        (reduce_z, valid_fine),
    ]
    section_means, section_vars, pixel_total = first_moments(blocks, local_count, images_total)
    pixel_count = pixel_total[0]
    fine_count = 16.0 * pixel_count
    gain_rows = [gains[0], gains[1], gains[2], gains[3], gains[4], low_gain]
    bias_rows = [biases[0], biases[1], biases[2], biases[3], biases[4], low_bias]
    kept = []
    activations = []
    for index in range(6):
        block_values, block_valid = blocks[index]
        result = normalize(
            block_values,
            block_valid,
            section_means[index],
            section_vars[index],
            gain_rows[index],
            bias_rows[index],
        )
        kept.append(result[1:])
        activations.append(result[0].astype(jnp.bfloat16))
    spread = jnp.einsum(
        "nwk,nkd->nwd", member_low, activations[4], preferred_element_type=jnp.float32
    ).astype(jnp.bfloat16)
    spread = jnp.broadcast_to(spread[:, None], (canvases, height, columns, channels))
    joined_coarse = jnp.concatenate(activations[:4] + [spread], axis=-1)
    proj_z = jnp.einsum(
        "nhwc,cd->nhwd", joined_coarse, proj_full, preferred_element_type=jnp.float32
    )
    proj_mean, proj_var = moments(proj_z, valid_coarse, pixel_count)
    proj_act, proj_centered, proj_shaped, proj_scale = normalize(
        proj_z, valid_coarse, proj_mean, proj_var, gains[5], biases[5]
    )
    proj_act = proj_act.astype(jnp.bfloat16)
    rows_table = row_table(4 * height, height)
    cols_table = column_table(ids_coarse)
    rows_up = jnp.einsum(
        "Yy,nyxc->nYxc",
        rows_table.astype(jnp.bfloat16),
        proj_act,
        preferred_element_type=jnp.float32,
    )
    upsampled = jnp.einsum("nXx,nYxc->nYXc", cols_table, rows_up, precision=highest).astype(
        jnp.bfloat16
    )
    joined_fine = jnp.concatenate([upsampled, activations[5]], axis=-1)
    decode_z = conv_forward(joined_fine, decode_full, ids_fine, 1)
    decode_mean, decode_var = moments(decode_z, valid_fine, fine_count)
    decode_act, decode_centered, decode_shaped, decode_scale = normalize(
        decode_z, valid_fine, decode_mean, decode_var, gains[6], biases[6]
    )
    decode_act = decode_act.astype(jnp.bfloat16)
    refine_z = conv_forward(decode_act, refine_full, ids_fine, 1)
    refine_mean, refine_var = moments(refine_z, valid_fine, fine_count)
    refine_act, refine_centered, refine_shaped, refine_scale = normalize(
        refine_z, valid_fine, refine_mean, refine_var, gains[7], biases[7]
    )
    refine_act = refine_act.astype(jnp.bfloat16)
    logits = (
        valid_fine
        * (
            jnp.einsum("nhwc,ck->nhwk", refine_act, w_cls, preferred_element_type=jnp.float32)
            + b_cls
        )
    ).astype(jnp.bfloat16)
    point_again, atrous_again, proj_again, reduce_again, decode_again, refine_again = (
        lax.all_gather(w_point, "narrow", axis=2, tiled=True),
        lax.all_gather(w_atrous, "narrow", axis=3, tiled=True),
        lax.all_gather(w_proj, "narrow", axis=1, tiled=True),
        lax.all_gather(w_low, "narrow", axis=1, tiled=True),
        lax.all_gather(w_dec1, "narrow", axis=1, tiled=True),
        lax.all_gather(w_dec2, "narrow", axis=2, tiled=True),
    )
    point_back, atrous_back, proj_back, reduce_back, decode_back, refine_back = (
        lax.all_gather(point_again, "wide", axis=1, tiled=True),
        lax.all_gather(atrous_again, "wide", axis=2, tiled=True),
        lax.all_gather(proj_again, "wide", axis=0, tiled=True),
        lax.all_gather(reduce_again, "wide", axis=0, tiled=True),
        lax.all_gather(decode_again, "wide", axis=2, tiled=True),
        lax.all_gather(refine_again, "wide", axis=1, tiled=True),
    )
    masked_grad = valid_fine.astype(jnp.bfloat16) * logit_grad
    cls_weight_grad = jnp.einsum(
        "nhwc,nhwk->ck", refine_act, masked_grad, preferred_element_type=jnp.float32
    )
    cls_bias_grad = jnp.sum(masked_grad.astype(jnp.float32), axis=(0, 1, 2))
    refine_up = jnp.einsum("nhwk,ck->nhwc", masked_grad, w_cls, preferred_element_type=jnp.float32)
    refine_local, refine_gain, refine_bias = norm_grad_terms(
        refine_up, valid_fine, refine_centered, refine_shaped
    )
    refine_gain, refine_bias = gradient_sums([(refine_gain, refine_bias)])[0]
    refine_dz = norm_grad_finish(
        refine_local,
        valid_fine,
        refine_centered,
        refine_scale,
        gains[7],
        refine_gain,
        refine_bias,
        fine_count,
    )
    decode_up, refine_kernel_grad = conv_backward(decode_act, refine_back, refine_dz, ids_fine, 1)
    decode_local, decode_gain, decode_bias = norm_grad_terms(
        decode_up, valid_fine, decode_centered, decode_shaped
    )
    decode_gain, decode_bias = gradient_sums([(decode_gain, decode_bias)])[0]
    decode_dz = norm_grad_finish(
        decode_local,
        valid_fine,
        decode_centered,
        decode_scale,
        gains[6],
        decode_gain,
        decode_bias,
        fine_count,
    )
    joined_grad, decode_kernel_grad = conv_backward(
        joined_fine, decode_back, decode_dz, ids_fine, 1
    )
    up_grad = joined_grad[..., :channels].astype(jnp.bfloat16)
    reduce_up = joined_grad[..., channels:]
    rows_grad = jnp.einsum(
        "nXx,nYXc->nYxc",
        cols_table.astype(jnp.bfloat16),
        up_grad,
        preferred_element_type=jnp.float32,
    )
    proj_up = jnp.einsum("Yy,nYxc->nyxc", rows_table, rows_grad, precision=highest)
    proj_local, proj_gain, proj_bias = norm_grad_terms(
        proj_up, valid_coarse, proj_centered, proj_shaped
    )
    reduce_local, reduce_gain, reduce_bias = norm_grad_terms(
        reduce_up, valid_fine, kept[5][0], kept[5][1]
    )
    summed_pairs = gradient_sums([(proj_gain, proj_bias), (reduce_gain, reduce_bias)])
    proj_gain, proj_bias = summed_pairs[0]
    reduce_gain, reduce_bias = summed_pairs[1]
    proj_dz = norm_grad_finish(
        proj_local,
        valid_coarse,
        proj_centered,
        proj_scale,
        gains[5],
        proj_gain,
        proj_bias,
        pixel_count,
    )
    reduce_dz = norm_grad_finish(
        reduce_local,
        valid_fine,
        kept[5][0],
        kept[5][2],
        low_gain,
        reduce_gain,
        reduce_bias,
        fine_count,
    )
    reduce_kernel_grad = jnp.einsum(
        "nhwc,nhwd->cd", low_level, reduce_dz, preferred_element_type=jnp.float32
    )
    low_level_grad = jnp.einsum(
        "nhwd,cd->nhwc", reduce_dz, reduce_back, preferred_element_type=jnp.float32
    ).astype(jnp.bfloat16)
    proj_kernel_grad = jnp.einsum(
        "nhwc,nhwd->cd", joined_coarse, proj_dz, preferred_element_type=jnp.float32
    )
    concat_grad = jnp.einsum(
        "nhwd,cd->nhwc", proj_dz, proj_back, preferred_element_type=jnp.float32
    )
    branch_terms = []
    for index in range(4):
        upstream = concat_grad[..., index * channels : (index + 1) * channels]
        branch_terms.append(norm_grad_terms(upstream, valid_coarse, kept[index][0], kept[index][1]))
    pool_up = jnp.einsum(
        "nhwd,nwk->nkd", concat_grad[..., 4 * channels :], member, precision=highest
    )
    branch_terms.append(norm_grad_terms(pool_up, all_ones, kept[4][0], kept[4][1]))
    local_pairs = [(term_item[1], term_item[2]) for term_item in branch_terms]
    flat_sums, cls_weight_grad, cls_bias_grad = lax.psum(
        (pack_pairs(local_pairs), cls_weight_grad, cls_bias_grad), ("wide", "narrow")
    )
    last_pairs = unpack_pairs(flat_sums, local_pairs)
    valid_list = [valid_coarse, valid_coarse, valid_coarse, valid_coarse, all_ones]
    count_list = [pixel_count, pixel_count, pixel_count, pixel_count, images_total]
    branch_dz = [
        norm_grad_finish(
            branch_terms[index][0],
            valid_list[index],
            kept[index][0],
            kept[index][2],
            gains[index],
            last_pairs[index][0],
            last_pairs[index][1],
            count_list[index],
        )
        for index in range(5)
    ]
    point_grad = jnp.stack(
        [
            jnp.einsum("nhwc,nhwd->cd", features, branch_dz[0], preferred_element_type=jnp.float32),
            jnp.einsum("nkc,nkd->cd", pooled, branch_dz[4], preferred_element_type=jnp.float32),
        ]
    )
    features_grad = jnp.einsum(
        "nhwd,cd->nhwc", branch_dz[0], point_back[0], preferred_element_type=jnp.float32
    )
    atrous_list = []
    for branch in range(3):
        input_part, kernel_part = conv_backward(
            features, atrous_back[branch], branch_dz[branch + 1], ids_coarse, dilations[branch]
        )
        features_grad = features_grad + input_part
        atrous_list.append(kernel_part)
    pooled_grad = (
        jnp.einsum("nkd,cd->nkc", branch_dz[4], point_back[1], preferred_element_type=jnp.float32)
        / image_sizes[:, :, None]
    )
    features_grad = (
        features_grad + jnp.einsum("nwk,nkc->nwc", member, pooled_grad, precision=highest)[:, None]
    )
    atrous_grad = jnp.stack(atrous_list)
    all_grads = (
        point_grad,
        atrous_grad,
        proj_kernel_grad,
        reduce_kernel_grad,
        decode_kernel_grad,
        refine_kernel_grad,
    )
    point_wide, atrous_wide, proj_wide, reduce_wide, decode_wide, refine_wide = (
        lax.psum_scatter(all_grads[0], "wide", scatter_dimension=1, tiled=True),
        lax.psum_scatter(all_grads[1], "wide", scatter_dimension=2, tiled=True),
        lax.psum_scatter(all_grads[2], "wide", scatter_dimension=0, tiled=True),
        lax.psum_scatter(all_grads[3], "wide", scatter_dimension=0, tiled=True),
        lax.psum_scatter(all_grads[4], "wide", scatter_dimension=2, tiled=True),
        lax.psum_scatter(all_grads[5], "wide", scatter_dimension=1, tiled=True),
    )
    point_owned, atrous_owned, proj_owned, reduce_owned, decode_owned, refine_owned = (
        lax.psum_scatter(
            point_wide.astype(jnp.bfloat16), "narrow", scatter_dimension=2, tiled=True
        ).astype(jnp.float32),
        lax.psum_scatter(
            atrous_wide.astype(jnp.bfloat16), "narrow", scatter_dimension=3, tiled=True
        ).astype(jnp.float32),
        lax.psum_scatter(
            proj_wide.astype(jnp.bfloat16), "narrow", scatter_dimension=1, tiled=True
        ).astype(jnp.float32),
        lax.psum_scatter(
            reduce_wide.astype(jnp.bfloat16), "narrow", scatter_dimension=1, tiled=True
        ).astype(jnp.float32),
        lax.psum_scatter(
            decode_wide.astype(jnp.bfloat16), "narrow", scatter_dimension=1, tiled=True
        ).astype(jnp.float32),
        lax.psum_scatter(
            refine_wide.astype(jnp.bfloat16), "narrow", scatter_dimension=2, tiled=True
        ).astype(jnp.float32),
    )
    gains_grad = jnp.stack(
        [
            last_pairs[0][0],
            last_pairs[1][0],
            last_pairs[2][0],
            last_pairs[3][0],
            last_pairs[4][0],
            proj_gain,
            decode_gain,
            refine_gain,
        ]
    )
    biases_grad = jnp.stack(
        [
            last_pairs[0][1],
            last_pairs[1][1],
            last_pairs[2][1],
            last_pairs[3][1],
            last_pairs[4][1],
            proj_bias,
            decode_bias,
            refine_bias,
        ]
    )
    return (
        logits,
        features_grad.astype(jnp.bfloat16),
        low_level_grad,
        point_owned,
        atrous_owned,
        proj_owned,
        reduce_owned,
        decode_owned,
        refine_owned,
        cls_weight_grad,
        cls_bias_grad,
        gains_grad,
        biases_grad,
        reduce_gain,
        reduce_bias,
    )


def solution(mesh):
    in_specs = (
        P(("wide", "narrow"), None, None, None),
        P(("wide", "narrow"), None, None, None),
        P(("wide", "narrow"), None),
        P(None, "wide", "narrow"),
        P(None, None, "wide", "narrow"),
        P("wide", "narrow"),
        P("wide", "narrow"),
        P(None, "narrow", "wide"),
        P(None, "wide", "narrow"),
        P(),
        P(),
        P(),
        P(),
        P(),
        P(),
        P(("wide", "narrow"), None, None, None),
    )
    out_specs = (
        P(("wide", "narrow"), None, None, None),
        P(("wide", "narrow"), None, None, None),
        P(("wide", "narrow"), None, None, None),
        P(None, "wide", "narrow"),
        P(None, None, "wide", "narrow"),
        P("wide", "narrow"),
        P("wide", "narrow"),
        P(None, "narrow", "wide"),
        P(None, "wide", "narrow"),
        P(),
        P(),
        P(),
        P(),
        P(),
        P(),
    )
    return jax.shard_map(
        per_device, mesh=mesh, in_specs=in_specs, out_specs=out_specs, check_vma=False
    )
```

profile of v0, /device:TPU:1, one launch (start us, length us, event | category | flops | bytes accessed | tf_op | source)
XLA Modules:
  0.0 3053.9 jit_solution(9606740323095055837)
XLA Ops:
  17.0 25.9 all-gather.9.cloned.1.call-done
  49.1 11.3 all_gather.56
  63.1 10.1 all_gather.58
  94.7 59.7 %all_gather.53 = bf16[256,48]{1,0:T(8,128)(2,1)S(1)} all-gather(bf16[32,48]{1,0:T(8,128)(2,1)S(1)} %bitcast.817), channel_id=1, replica_groups=mesh['wide'=8,'narrow'=4] {'wide'}, dimensions={0}, use_global_device_ids=true | all-gather | bytes 27648 | tf_op jit(solution)/shard_map/all_gather | solution.py:251
  154.6 18.2 all_gather.54
  173.0 44.5 %all_gather.55 = bf16[1280,256]{1,0:T(8,128)(2,1)} all-gather(bf16[160,256]{1,0:T(8,128)(2,1)S(1)} %copy.201), channel_id=1, replica_groups=mesh['wide'=8,'narrow'=4] {'wide'}, dimensions={0}, use_global_device_ids=true | all-gather | bytes 737280 | tf_op jit(solution)/shard_map/all_gather | solution.py:250
  231.1 416.8 %all-gather.11.cloned.1.call-done = bf16[3,9,2048,256]{3,2,1,0:T(8,128)(2,1)} async-done(((bf16[3,9,256,256]{3,2,1,0:T(8,128)(2,1)}), bf16[3,9,2048,256]{3,2,1,0:T(8,128)(2,1)}) %all-gather.11.cloned.1.call-update) | async-done | bytes 28311568 | tf_op jit(solution)/shard_map/all_gather | solution.py:249
  683.0 39.3 %all-reduce.88 = (f32[1328]{0:T(1024)S(1)}, f32[]{:T(128)}) all-reduce(f32[1328]{0:T(1024)} %constant_dynamic-update-slice_fusion.15, f32[]{:T(128)S(6)} %convert_element_type.1203), channel_id=1, replica_groups=mesh['wide'=8,'narrow'=4] {'wide','narrow'}, use_global_device_ids=true, to_apply=%region_11.12 | all-reduce | flops 1329 | bytes 10632 | tf_op jit(solution)/shard_map/psum | solution.py:167
  734.1 41.3 %psum.107 = f32[1328]{0:T(1024)S(1)} all-reduce(f32[1328]{0:T(1024)} %constant_dynamic-update-slice_fusion.16), channel_id=1, replica_groups=mesh['wide'=8,'narrow'=4] {'wide','narrow'}, use_global_device_ids=true, to_apply=%region_20.21 | all-reduce | flops 1328 | bytes 10624 | tf_op jit(solution)/shard_map/psum | solution.py:172
  789.3 39.3 %psum.108 = f32[256]{0:T(256)S(1)} all-reduce(f32[256]{0:T(256)S(1)} %get-tuple-element.421), channel_id=1, replica_groups=mesh['wide'=8,'narrow'=4] {'wide','narrow'}, use_global_device_ids=true, to_apply=%region_22.23 | all-reduce | flops 256 | bytes 2048 | tf_op jit(solution)/shard_map/psum | solution.py:181
  829.4 40.7 %psum.109 = f32[256]{0:T(256)S(1)} all-reduce(f32[256]{0:T(256)S(1)} %multiply_reduce_fusion.11), channel_id=1, replica_groups=mesh['wide'=8,'narrow'=4] {'wide','narrow'}, use_global_device_ids=true, to_apply=%region_24.25 | all-reduce | flops 256 | bytes 2048 | tf_op jit(solution)/shard_map/psum | solution.py:183
  880.3 30.6 %convolution_bitcast_fusion.1 = f32[9,1,80,96,256]{4,3,0,2,1:T(8,128)} fusion(bf16[1,80,96,48]{3,2,1,0:T(8,128)(2,1)S(1)} %copy-done.30, bf16[1,80,96,256]{3,2,1,0:T(8,128)(2,1)} %convert_bitcast_fusion.1, bf16[9,304,256]{1,2,0:T(8,128)(2,1)} %all-gather.13.cloned.1.call-done), kind=kOutput, calls=%fused_computation.10 | convolution fusion | flops 10767728640 | bytes 76849152 | tf_op jit(solution)/shard_map/nhwc,tcd->tnhwd/dot_general | solution.py:49
  911.0 41.2 %slice_bitcast_fusion.26 = (f32[1,80,96,256]{3,2,1,0:T(8,128)}, f32[1,80,96,256]{3,2,1,0:T(8,128)}, f32[1,80,96,256]{3,2,1,0:T(8,128)}, f32[1,80,96,256]{3,2,1,0...) fusion(f32[9,1,80,96,256]{4,3,0,2,1:T(8,128)} %convolution_bitc, ...), kind=kLoop, calls=%fused_computation.88 | loop fusion | bytes 125829120 | tf_op jit(solution)/shard_map/squeeze | solution.py:54
  952.2 25.3 multiply_reduce_fusion.5
  977.6 39.3 %psum.110 = f32[256]{0:T(256)S(1)} all-reduce(f32[256]{0:T(256)S(1)} %get-tuple-element.156), channel_id=1, replica_groups=mesh['wide'=8,'narrow'=4] {'wide','narrow'}, use_global_device_ids=true, to_apply=%region_29.30 | all-reduce | flops 256 | bytes 2048 | tf_op jit(solution)/shard_map/psum | solution.py:181
  1021.6 40.8 %psum.111 = f32[256]{0:T(256)S(1)} all-reduce(f32[256]{0:T(256)S(1)} %multiply_reduce_fusion.4), channel_id=1, replica_groups=mesh['wide'=8,'narrow'=4] {'wide','narrow'}, use_global_device_ids=true, to_apply=%region_31.32 | all-reduce | flops 256 | bytes 2048 | tf_op jit(solution)/shard_map/psum | solution.py:183
  1063.1 28.8 convolution_bitcast_fusion
  1092.0 41.1 %slice_bitcast_fusion.17 = (f32[1,80,96,256]{3,2,1,0:T(8,128)}, f32[1,80,96,256]{3,2,1,0:T(8,128)}, f32[1,80,96,256]{3,2,1,0:T(8,128)}, f32[1,80,96,256]{3,2,1,0...) fusion(f32[9,1,80,96,256]{4,3,2,1,0:T(8,128)} %convolution_bitc, ...), kind=kLoop, calls=%fused_computation.78 | loop fusion | bytes 125829120 | tf_op jit(solution)/shard_map/squeeze | solution.py:54
  1133.1 25.2 multiply_reduce_fusion.3
  1158.4 39.5 %psum.112 = f32[256]{0:T(256)S(1)} all-reduce(f32[256]{0:T(256)S(1)} %get-tuple-element.154), channel_id=1, replica_groups=mesh['wide'=8,'narrow'=4] {'wide','narrow'}, use_global_device_ids=true, to_apply=%region_33.34 | all-reduce | flops 256 | bytes 2048 | tf_op jit(solution)/shard_map/psum | solution.py:181
  1202.6 40.8 %psum.113 = f32[256]{0:T(256)S(1)} all-reduce(f32[256]{0:T(256)S(1)} %multiply_reduce_fusion.2), channel_id=1, replica_groups=mesh['wide'=8,'narrow'=4] {'wide','narrow'}, use_global_device_ids=true, to_apply=%region_35.36 | all-reduce | flops 256 | bytes 2048 | tf_op jit(solution)/shard_map/psum | solution.py:183
  1243.5 10.2 multiply_reduce_fusion.1
  1253.7 39.3 %psum.114 = f32[512]{0:T(512)S(1)} all-reduce(f32[512]{0:T(512)S(1)} %pad_maximum_fusion.6), channel_id=1, replica_groups=mesh['wide'=8,'narrow'=4] {'wide','narrow'}, use_global_device_ids=true, to_apply=%region_38.39 | all-reduce | flops 512 | bytes 4096 | tf_op jit(solution)/shard_map/psum | solution.py:211
  1300.6 8.2 broadcast_multiply_fusion.3
  1343.7 19.8 fusion.140
  1363.5 22.5 multiply_reduce_fusion
  1385.9 40.8 %psum.115 = f32[512]{0:T(512)S(1)} all-reduce(f32[512]{0:T(512)S(1)} %pad_maximum_fusion.7), channel_id=1, replica_groups=mesh['wide'=8,'narrow'=4] {'wide','narrow'}, use_global_device_ids=true, to_apply=%region_41.42 | all-reduce | flops 512 | bytes 4096 | tf_op jit(solution)/shard_map/psum | solution.py:211
  1434.2 8.2 broadcast_multiply_fusion.2
  1477.3 18.4 fusion.133
  1495.7 19.4 fusion.56
  1523.0 39.2 %psum.116 = f32[608]{0:T(1024)S(1)} all-reduce(f32[608]{0:T(1024)S(1)} %pad_maximum_fusion.5), channel_id=1, replica_groups=mesh['wide'=8,'narrow'=4] {'wide','narrow'}, use_global_device_ids=true, to_apply=%region_46.47 | all-reduce | flops 608 | bytes 4864 | tf_op jit(solution)/shard_map/psum | solution.py:211
  1578.5 43.3 %all-reduce.87 = (f32[2560]{0:T(1024)S(1)}, f32[256,21]{0,1:T(8,128)}, f32[21]{0:T(128)}) all-reduce(f32[2560]{0:T(1024)S(1)} %constant_dynamic-update-slice_fusion.18, f32[256,21]{0,1:T(8,128)S(1)} %fusion.168, f32[21]{0:T(128)S(1)} %copy-done.230), channel_id=1, replica_groups=mesh['wide'=8,'narrow'=4] {'wide','narrow'}, use_global_device_ids=true, to_apply=%region_58.59 | all-reduce | flops 7957 | bytes 63656 | tf_op jit(solution)/shard_map/psum | solution.py:459
  1675.4 10.8 convolution_bitcast_fusion.2
  1686.3 10.9 convolution_bitcast_fusion.3
  1701.1 10.9 convolution_bitcast_fusion.4
  1712.0 39.0 %pad_maximum_fusion = f32[3,9,2048,256]{2,3,1,0:T(8,128)} fusion(f32[1,9,2048,256]{2,3,1,0:T(8,128)} %convolution_bitcast_fusion.2, f32[1,9,2048,256]{2,3,1,0:T(8,128)} %convolution_bitcast_fusion.3, f32[1,9,2048,256]{2,3,1,0:T(8,128)} %convolution_bitcast_fusion.4), kind=kLoop, calls=%fused_computation | loop fusion | flops 28311552 | bytes 113246208 | tf_op jit(solution)/shard_map/stack | solution.py:501
  1768.9 86.8 %reduce-scatter.30.cloned.1.call-done = f32[9,304,32]{1,0,2:T(8,128)} async-done(((f32[9,304,256]{1,0,2:T(8,128)}), f32[9,304,32]{1,0,2:T(8,128)}) %reduce-scatter.30.cloned.1.call-update) | async-done | bytes 350224 | tf_op jit(solution)/shard_map/reduce_scatter | solution.py:515
  1858.2 90.0 %reduce-scatter.20.cloned.1.call-done = f32[2,256,256]{1,2,0:T(8,128)} async-done(((f32[2,2048,256]{1,2,0:T(8,128)}), f32[2,256,256]{1,2,0:T(8,128)}) %reduce-scatter.20.cloned.1.call-update) | async-done | bytes 524304 | tf_op jit(solution)/shard_map/reduce_scatter | solution.py:511
  1950.3 883.7 %reduce-scatter.24.cloned.1.call-done = f32[3,9,256,256]{2,3,1,0:T(8,128)} async-done(((f32[3,9,2048,256]{2,3,1,0:T(8,128)}), f32[3,9,256,256]{2,3,1,0:T(8,128)}) %reduce-scatter.24.cloned.1.call-update) | async-done | bytes 7077904 | tf_op jit(solution)/shard_map/reduce_scatter | solution.py:512
  2850.5 10.6 fusion.9
  2861.1 10.6 fusion.11
  2871.9 11.8 fusion.105
  2883.7 12.6 reduce-scatter.36.cloned.1.call-done
  2911.2 8.2 reduce-scatter.34.cloned.1.call-done
  2921.0 21.0 reduce-scatter.38.cloned.1.call-done
  2945.3 32.3 %all-reduce.91.cloned.1.call-done = bf16[9,304,32]{2,1,0:T(8,128)(2,1)} async-done(((bf16[9,304,32]{2,1,0:T(8,128)(2,1)}), bf16[9,304,32]{2,1,0:T(8,128)(2,1)}) %all-reduce.91.cloned.1.call-update) | async-done | bytes 175120
  2979.4 22.0 reduce-scatter.22.cloned.1.call-done
  3002.9 41.6 %reduce-scatter.26.cloned.1.call-done = bf16[3,9,256,64]{2,3,1,0:T(8,128)(2,1)} async-done(((bf16[3,9,256,256]{2,3,1,0:T(8,128)(2,1)}), bf16[3,9,256,64]{2,3,1,0:T(8,128)(2,1)}) %reduce-scatter.26.cloned.1.call-update) | async-done | bytes 884752 | tf_op jit(solution)/shard_map/reduce_scatter | solution.py:522
  (794 shorter events, 361.6 us)
Async XLA Ops:
  7.2 1236.3 %copy-start = (bf16[256,21]{0,1:T(8,128)(2,1)S(1)}, bf16[256,21]{0,1:T(8,128)(2,1)}, u32[]{:S(2)}) copy-start(bf16[256,21]{0,1:T(8,128)(2,1)} %param.25) | copy-start | bytes 32260
  7.2 35.7 %all-gather.9.cloned.1.call-start = ((), (), s32[]{:S(2)}) async-start(), calls=%async_computation.11 | async-start | bytes 4423680 | tf_op jit(solution)/shard_map/all_gather | solution.py:241
  7.9 217.0 %all-gather.7.cloned.1.call-start = ((), (), s32[]{:S(2)}) async-start(), calls=%async_computation.10 | async-start | bytes 2359296 | tf_op jit(solution)/shard_map/all_gather | solution.py:248
  16.9 631.0 %all-gather.11.cloned.1.call-start = ((), (), s32[]{:S(2)}) async-start(), calls=%async_computation.12 | async-start | bytes 31850496 | tf_op jit(solution)/shard_map/all_gather | solution.py:249
  48.7 105.7 %copy-start.13 = (bf16[1,20,24,2048]{3,2,1,0:T(8,128)(2,1)S(1)}, bf16[1,20,24,2048]{3,2,1,0:T(8,128)(2,1)}, u32[]{:S(2)}) copy-start(bf16[1,20,24,2048]{3,2,1,0:T(8,128)(2,1)} %param.16) | copy-start | bytes 5898244
  48.7 831.6 %all-gather.13.cloned.1.call-start = ((), (), s32[]{:S(2)}) async-start(), calls=%async_computation.13 | async-start | bytes 1990656 | tf_op jit(solution)/shard_map/all_gather | solution.py:252
  60.4 94.2 %copy-start.85 = (bf16[160,64]{0,1:T(8,128)(2,1)S(1)}, bf16[160,64]{0,1:T(8,128)(2,1)}, u32[]{:S(2)}) copy-start(bf16[160,64]{0,1:T(8,128)(2,1)} %param.21) | copy-start | bytes 61444
  61.9 1001.2 %all-gather.15.cloned.1.call-start = ((), (), s32[]{:S(2)}) async-start(), calls=%async_computation.14 | async-start | bytes 1327104 | tf_op jit(solution)/shard_map/all_gather | solution.py:253
  74.6 1682.2 %reduce-scatter.28.cloned.1.call-start = ((), (), s32[]{:S(2)}) async-start(), calls=%async_computation.19 | async-start | bytes 1474560 | tf_op jit(solution)/shard_map/reduce_scatter | solution.py:513
  74.6 148.1 %copy-start.178 = (s32[96]{0:T(128)}, s32[96]{0:T(128)S(1)}, u32[]{:S(2)}) copy-start(s32[96]{0:T(128)S(1)} %broadcast_clamp_fusion) | copy-start | bytes 1156
  74.7 148.1 %copy-start.181 = (s32[96]{0:T(128)}, s32[96]{0:T(128)S(1)}, u32[]{:S(2)}) copy-start(s32[96]{0:T(128)S(1)} %add_clamp_fusion) | copy-start | bytes 1156
  74.7 148.1 %copy-start.195 = (f32[80]{0:T(128)}, f32[80]{0:T(128)S(1)}, u32[]{:S(2)}) copy-start(f32[80]{0:T(128)S(1)} %and_convert_fusion.7) | copy-start | bytes 964
  74.7 148.1 %copy-start.184 = (s32[96]{0:T(128)}, s32[96]{0:T(128)S(1)}, u32[]{:S(2)}) copy-start(s32[96]{0:T(128)S(1)} %and_select_fusion) | copy-start | bytes 1156
  74.7 148.1 %copy-start.197 = (f32[80]{0:T(128)}, f32[80]{0:T(128)S(1)}, u32[]{:S(2)}) copy-start(f32[80]{0:T(128)S(1)} %compare_convert_fusion) | copy-start | bytes 964
  74.8 148.1 %copy-start.199 = (f32[80]{0:T(128)}, f32[80]{0:T(128)S(1)}, u32[]{:S(2)}) copy-start(f32[80]{0:T(128)S(1)} %and_convert_fusion) | copy-start | bytes 964
  78.6 145.3 %copy-start.216 = (f32[20]{0:T(128)}, f32[20]{0:T(128)S(1)}, u32[]{:S(2)}) copy-start(f32[20]{0:T(128)S(1)} %and_convert_fusion.6) | copy-start | bytes 244
  78.6 145.3 %copy-start.218 = (f32[20]{0:T(128)}, f32[20]{0:T(128)S(1)}, u32[]{:S(2)}) copy-start(f32[20]{0:T(128)S(1)} %compare_convert_fusion.6) | copy-start | bytes 244
  78.6 145.3 %copy-start.220 = (f32[20]{0:T(128)}, f32[20]{0:T(128)S(1)}, u32[]{:S(2)}) copy-start(f32[20]{0:T(128)S(1)} %and_convert_fusion.5) | copy-start | bytes 244
  78.6 145.2 %copy-start.222 = (f32[20]{0:T(128)}, f32[20]{0:T(128)S(1)}, u32[]{:S(2)}) copy-start(f32[20]{0:T(128)S(1)} %and_convert_fusion.4) | copy-start | bytes 244
  78.6 145.2 %copy-start.224 = (f32[20]{0:T(128)}, f32[20]{0:T(128)S(1)}, u32[]{:S(2)}) copy-start(f32[20]{0:T(128)S(1)} %and_convert_fusion.3) | copy-start | bytes 244
  78.7 145.2 %copy-start.226 = (f32[20]{0:T(128)}, f32[20]{0:T(128)S(1)}, u32[]{:S(2)}) copy-start(f32[20]{0:T(128)S(1)} %and_convert_fusion.2) | copy-start | bytes 244
  78.7 145.2 %copy-start.228 = (f32[20]{0:T(128)}, f32[20]{0:T(128)S(1)}, u32[]{:S(2)}) copy-start(f32[20]{0:T(128)S(1)} %and_convert_fusion.1) | copy-start | bytes 244
  79.0 983.3 %copy-start.53 = (f32[24]{0:T(128)}, f32[24]{0:T(128)S(1)}, u32[]{:S(2)}) copy-start(f32[24]{0:T(128)S(1)} %compare_convert_fusion.9) | copy-start | bytes 292
  79.0 143.8 %copy-start.238 = (s32[24]{0:T(128)}, s32[24]{0:T(128)S(1)}, u32[]{:S(2)}) copy-start(s32[24]{0:T(128)S(1)} %compare_select_fusion.1) | copy-start | bytes 292
  79.9 1438.1 %copy-start.61 = (f32[96]{0:T(128)}, f32[96]{0:T(128)S(1)}, u32[]{:S(2)}) copy-start(f32[96]{0:T(128)S(1)} %get-tuple-element.404) | copy-start | bytes 1156
  81.2 141.6 %copy-start.257 = (f32[3]{0:T(128)}, f32[3]{0:T(128)S(1)}, u32[]{:S(2)}) copy-start(f32[3]{0:T(128)S(1)} %get-tuple-element.408) | copy-start | bytes 40
  222.8 555.3 %copy-start.1 = (f32[80,96,48]{1,2,0:T(8,128)}, f32[80,96,48]{1,2,0:T(8,128)S(1)}, u32[]{:S(2)}) copy-start(f32[80,96,48]{1,2,0:T(8,128)S(1)} %get-tuple-element.420) | copy-start | bytes 4423684
  676.4 109.0 %copy-start.10 = (f32[1,20,24,256]{3,2,1,0:T(8,128)}, f32[1,20,24,256]{3,2,1,0:T(8,128)S(1)}, u32[]{:S(2)}) copy-start(f32[1,20,24,256]{3,2,1,0:T(8,128)S(1)} %get-tuple-element.161) | copy-start | bytes 1474564
  676.4 110.0 %copy-start.6 = (f32[1,20,24,256]{3,2,1,0:T(8,128)}, f32[1,20,24,256]{3,2,1,0:T(8,128)S(1)}, u32[]{:S(2)}) copy-start(f32[1,20,24,256]{3,2,1,0:T(8,128)S(1)} %get-tuple-element.162) | copy-start | bytes 1474564
  676.4 110.8 %copy-start.8 = (f32[1,20,24,256]{3,2,1,0:T(8,128)}, f32[1,20,24,256]{3,2,1,0:T(8,128)S(1)}, u32[]{:S(2)}) copy-start(f32[1,20,24,256]{3,2,1,0:T(8,128)S(1)} %get-tuple-element.163) | copy-start | bytes 1474564
  778.1 284.2 %copy-start.89 = (f32[256]{0:T(256)}, f32[256]{0:T(256)S(1)}, u32[]{:S(2)}) copy-start(f32[256]{0:T(256)S(1)} %get-tuple-element.267) | copy-start | bytes 3076
  778.2 284.2 %copy-start.91 = (f32[256]{0:T(256)}, f32[256]{0:T(256)S(1)}, u32[]{:S(2)}) copy-start(f32[256]{0:T(256)S(1)} %get-tuple-element.264) | copy-start | bytes 3076
  780.6 90.2 %copy-start.108 = (f32[1,256]{1,0:T(1,128)S(1)}, f32[1,256]{1,0:T(1,128)}, u32[]{:S(2)}) copy-start(f32[1,256]{1,0:T(1,128)} %get-tuple-element.269) | copy-start | bytes 3076
  789.2 91.0 %copy-start.17 = (f32[20,24,256]{2,1,0:T(8,128)}, f32[20,24,256]{2,1,0:T(8,128)S(1)}, u32[]{:S(2)}) copy-start(f32[20,24,256]{2,1,0:T(8,128)S(1)} %get-tuple-element.422) | copy-start | bytes 1474564
  870.8 191.6 %copy-start.113 = (f32[256]{0:T(256)}, f32[256]{0:T(256)S(1)}, u32[]{:S(2)}) copy-start(f32[256]{0:T(256)S(1)} %add_rsqrt_fusion.2) | copy-start | bytes 3076
  1578.0 180.6 %reduce-scatter.32.cloned.1.call-start = ((), (), s32[]{:S(2)}) async-start(), calls=%async_computation.21 | async-start | bytes 4718592 | tf_op jit(solution)/shard_map/reduce_scatter | solution.py:516
  1646.3 209.5 %reduce-scatter.30.cloned.1.call-start = ((), (), s32[]{:S(2)}) async-start(), calls=%async_computation.20 | async-start | bytes 7077888 | tf_op jit(solution)/shard_map/reduce_scatter | solution.py:515
  1686.2 262.1 %reduce-scatter.20.cloned.1.call-start = ((), (), s32[]{:S(2)}) async-start(), calls=%async_computation.15 | async-start | bytes 4718592 | tf_op jit(solution)/shard_map/reduce_scatter | solution.py:511
  1697.2 1136.9 %reduce-scatter.24.cloned.1.call-start = ((), (), s32[]{:S(2)}) async-start(), calls=%async_computation.17 | async-start | bytes 63700992 | tf_op jit(solution)/shard_map/reduce_scatter | solution.py:512
  1751.1 1145.2 %reduce-scatter.36.cloned.1.call-start = ((), (), s32[]{:S(2)}) async-start(), calls=%async_computation.23 | async-start | bytes 147456
  1756.7 1162.7 %reduce-scatter.34.cloned.1.call-start = ((), (), s32[]{:S(2)}) async-start(), calls=%async_computation.22 | async-start | bytes 163840
  1758.5 1183.5 %reduce-scatter.38.cloned.1.call-start = ((), (), s32[]{:S(2)}) async-start(), calls=%async_computation.24 | async-start | bytes 245760
  1768.9 1208.7 %all-reduce.91.cloned.1.call-start = ((), (), s32[]{:S(2)}) async-start(), calls=%async_computation.25 | async-start | bytes 1400832
  1858.2 1143.2 %reduce-scatter.22.cloned.1.call-start = ((), (), s32[]{:S(2)}) async-start(), calls=%async_computation.16 | async-start | bytes 327680 | tf_op jit(solution)/shard_map/reduce_scatter | solution.py:519
  1950.1 889.3 %copy-start.242 = (u32[32]{0:T(128)S(1)}, u32[32]{0:T(128)}, u32[]{:S(2)}) copy-start(u32[32]{0:T(128)} %constant.318) | copy-start | bytes 388
  1950.1 891.2 %copy-start.246 = (f32[21]{0:T(128)S(1)}, f32[21]{0:T(128)}, u32[]{:S(2)}) copy-start(f32[21]{0:T(128)} %param.26) | copy-start | bytes 256
  1950.1 1094.4 %reduce-scatter.26.cloned.1.call-start = ((), (), s32[]{:S(2)}) async-start(), calls=%async_computation.18 | async-start | bytes 4423680 | tf_op jit(solution)/shard_map/reduce_scatter | solution.py:522
  2904.9 5.6 collective-permute-start
  (228 other events, 3995.9 us)
Sparse Core Ops, SparseCore 0:
  9.6 33.2 all-gather.8
  45.6 47.7 all-gather.6
  95.5 552.3 all-gather.10
  649.9 44.8 all-gather.12
  697.4 40.0 all-gather.14
  1578.1 64.3 reduce-scatter.27
  1646.4 88.3 reduce-scatter.31
  1738.9 116.8 reduce-scatter.29
  1859.8 88.3 reduce-scatter.19
  1952.1 881.9 reduce-scatter.23
  2838.3 57.9 reduce-scatter.35
  2899.3 20.0 reduce-scatter.33
  2921.8 20.0 reduce-scatter.37
  2944.8 32.7 all-reduce.90
  2979.9 21.4 reduce-scatter.21
  3004.0 40.4 reduce-scatter.25
where the time goes:
time: 3060 us; the launch traced here: 3050 us
  waiting for transfers between devices  1640 us (54%)
  blocking collectives  647 us (21%)
  matrix products  278 us (9%)
  local copies, waits for them, and re-layouts  247 us (8%)
  other arithmetic  214 us (7%)
    reduce_scatter x1, waiting for transfers between devices, per_device(): lax.psum_scatter(all_grads[1], 'wide', scatter_dimension=2, tiled=True)  884 us
    all_gather x1, waiting for transfers between devices, per_device(): lax.all_gather(atrous_part, 'wide', axis=2, tiled=True)  417 us
    psum x3, blocking collectives, moments(): seconds = lax.psum(square_sums(blocks, [mean_row]), ('wide', 'narrow'))  122 us
    unnamed x592, local copies, waits for them, and re-layouts  121 us
    psum x3, blocking collectives, gradient_sums(): return unpack_pairs(lax.psum(pack_pairs(pairs), ('wide', 'narrow')), pairs)  119 us
    psum x3, blocking collectives, moments(): firsts = lax.psum(first_sums(blocks), ('wide', 'narrow'))  118 us
    reduce_scatter x1, waiting for transfers between devices, per_device(): lax.psum_scatter(all_grads[0], 'wide', scatter_dimension=1, tiled=True)  90 us
    reduce_scatter x1, waiting for transfers between devices, per_device(): lax.psum_scatter(all_grads[4], 'wide', scatter_dimension=2, tiled=True)  86.8 us
  transfers between devices with their start and end apart: 17, of which 11 were waited for; matrix products, arithmetic and copies ran while one was open for 14% of the time, Pallas kernels for 0%

commit v1 on v0

--- a/solution.py
+++ b/solution.py
@@ -1,11 +1,593 @@
+import functools
+
 import jax
 import jax.numpy as jnp
 from jax import lax
+from jax.experimental import pallas as pl
+from jax.experimental.pallas import tpu as pltpu
 from jax.sharding import PartitionSpec as P
 
 epsilon = 1e-05
 highest = lax.Precision.HIGHEST
 dilations = (6, 12, 18)
+ROUNDS = 4
+CHUNKS = (8, 6, 6, 9)
+VMEM_BYTES = 48 * 1024 * 1024
+
+
+def exchange(values, axis, bit):
+    size = lax.axis_size(axis)
+    return lax.ppermute(values, axis, [(place, place ^ bit) for place in range(size)])
+
+
+def rotate(values, axis, step, stride):
+    size = lax.axis_size(axis)
+    rounds = size // stride
+    pairs = []
+    for place in range(size):
+        outer, inner = place // stride, place % stride
+        pairs.append((place, ((outer + step) % rounds) * stride + inner))
+    return lax.ppermute(values, axis, pairs)
+
+
+def bits_of(axis):
+    size = lax.axis_size(axis)
+    bits = []
+    bit = 1
+    while bit < size:
+        bits.append((axis, bit))
+        bit = bit * 2
+    return bits
+
+
+def sum_all(values):
+    for axis, bit in bits_of("narrow") + bits_of("wide"):
+        values = values + exchange(values, axis, bit)
+    return values
+
+
+def merge_all(counts, means, squares):
+    for axis, bit in bits_of("narrow") + bits_of("wide"):
+        other = exchange(jnp.stack([counts, means, squares]), axis, bit)
+        total = counts + other[0]
+        gap = means - other[1]
+        squares = squares + other[2] + gap * gap * (counts * other[0] / total)
+        means = (counts * means + other[0] * other[1]) / total
+        counts = total
+    return (counts, means, squares)
+
+
+def local_moments(values, valid_map, count):
+    axes = tuple(range(values.ndim - 1))
+    mean = jnp.sum(values * valid_map, axis=axes) / count
+    centered = values - mean
+    return (jnp.full_like(mean, 1.0) * count, mean, jnp.sum(centered * centered * valid_map, axis=axes))
+
+
+def place():
+    wide = lax.axis_index("wide")
+    narrow = lax.axis_index("narrow")
+    return (wide // 2, wide % 2, narrow // 2, narrow % 2)
+
+
+def share_core(shard):
+    core = place()[3]
+    half = shard.shape[1] // 2
+    parts = shard.reshape(shard.shape[0], 2, half, shard.shape[2])
+    kept = lax.dynamic_index_in_dim(parts, core, 1, keepdims=False)
+    given = lax.dynamic_index_in_dim(parts, 1 - core, 1, keepdims=False)
+    got = exchange(given, "narrow", 1)
+    lower = jnp.where(core == 0, kept, got)
+    upper = jnp.where(core == 0, got, kept)
+    return jnp.concatenate([lower, upper], axis=2)
+
+
+def depth_groups():
+    size = lax.axis_size("wide")
+    return [list(range(inner, size, 2)) for inner in range(2)]
+
+
+def gather_depth(block):
+    rounds = lax.axis_size("wide") // 2
+    if rounds > 4:
+        stack = lax.all_gather(block, "wide", axis_index_groups=depth_groups())
+        return jnp.take(stack, (place()[0] - jnp.arange(rounds)) % rounds, axis=0)
+    parts = [block] + [rotate(block, "wide", step, 2) for step in range(1, rounds)]
+    return jnp.stack(parts)
+
+
+def tuned():
+    return lax.axis_size("wide") == 2 * ROUNDS and lax.axis_size("narrow") == 4
+
+
+def kernel_place():
+    values = jnp.stack(place()).astype(jnp.int32)
+    return values if tuned() else jnp.zeros_like(values)
+
+
+def gather_chunk(block, x_first):
+    order = [("wide", 1), ("narrow", 2)]
+    if not x_first:
+        order = order[::-1]
+    stack = gather_depth(block)
+    stack = jnp.stack([stack, exchange(stack, *order[0])])
+    stack = jnp.stack([stack, exchange(stack, *order[1])])
+    return (stack, exchange(stack, "narrow", 1))
+
+
+def gather_taps(weights, sizes):
+    chunks = []
+    start = 0
+    if tuned():
+        shared = share_core(weights)
+    else:
+        full = lax.all_gather(weights, "narrow", axis=2, tiled=True)
+        full = lax.all_gather(full, "wide", axis=1, tiled=True)
+        rows = full.shape[1] // (4 * ROUNDS)
+        full = full.reshape(full.shape[0], ROUNDS, 2, 2, rows, 2, full.shape[2] // 2)
+    for index, size in enumerate(sizes):
+        x_first = index % 2 == 0
+        if tuned():
+            chunks.append(gather_chunk(shared[start : start + size], x_first))
+        else:
+            part = full[start : start + size]
+            part = part[:, [0] + list(range(ROUNDS - 1, 0, -1))]
+            part = part.transpose((3, 5, 2, 1, 0, 4, 6) if x_first else (3, 2, 5, 1, 0, 4, 6))
+            chunks.append((part[0], part[1]))
+        start += size
+    return chunks
+
+
+def add_wide(first, second):
+    return first.astype(jnp.float32) + second.astype(jnp.float32)
+
+
+def scatter_chunk(keep, give, x_first):
+    order = [("wide", 1), ("narrow", 2)]
+    if not x_first:
+        order = order[::-1]
+    got = exchange(give, "narrow", 1)
+    sent = add_wide(keep[1], got[1]).astype(jnp.bfloat16)
+    total = add_wide(keep[0], got[0]) + exchange(sent, *order[0]).astype(jnp.float32)
+    sent = total[1].astype(jnp.bfloat16)
+    total = total[0] + exchange(sent, *order[1]).astype(jnp.float32)
+    sent = total[1:].astype(jnp.bfloat16)
+    total = total[0]
+    for step in range(1, sent.shape[0] + 1):
+        total = total + rotate(sent[step - 1], "wide", step, 2).astype(jnp.float32)
+    return total
+
+
+def scatter_taps(chunks, shape):
+    if tuned():
+        owned = [scatter_chunk(*pair, index % 2 == 0) for index, pair in enumerate(chunks)]
+        return settle_core(jnp.concatenate(owned))
+    parts = []
+    for index, pair in enumerate(chunks):
+        x_first = index % 2 == 0
+        part = jnp.stack(pair)
+        part = part.transpose((4, 3, 1, 0, 5, 2, 6) if x_first else (4, 3, 2, 0, 5, 1, 6))
+        taps = part.shape[0]
+        parts.append(part.reshape(taps, -1, 2 * part.shape[6]))
+    full = jnp.concatenate(parts)
+    full = lax.psum_scatter(full, "wide", scatter_dimension=1, tiled=True)
+    return lax.psum_scatter(full, "narrow", scatter_dimension=2, tiled=True).astype(jnp.float32)
+
+
+def row_span(dilation, row, height):
+    step = (row - 1) * dilation
+    return (max(step, 0), max(-step, 0), height - abs(step))
+
+
+def tap_matrix(pair, tap, place_ref, x_first):
+    row, core = place_ref[2], place_ref[3]
+
+    def half(ref):
+        if x_first:
+            return jnp.concatenate([ref[row, 0, 0, tap], ref[1 - row, 0, 0, tap]], axis=1)
+        return jnp.concatenate([ref[0, row, 0, tap], ref[0, 1 - row, 0, tap]], axis=1)
+
+    mine = half(pair[0])
+    other = half(pair[1])
+    lower = jnp.where(core == 0, mine, other)
+    upper = jnp.where(core == 0, other, mine)
+    return jnp.concatenate([lower, upper], axis=0)
+
+
+def weight_specs(chunk, x_first):
+    taps, rows, cols = chunk[0].shape[3:]
+    shape = (2, 1, 1, taps, rows, cols) if x_first else (1, 2, 1, taps, rows, cols)
+
+    def index_map(step, place_ref):
+        flip = lax.rem(step + place_ref[1], 2)
+        slot = lax.rem(place_ref[0] - step // 2 + ROUNDS, ROUNDS)
+        return (0, flip, slot, 0, 0, 0) if x_first else (flip, 0, slot, 0, 0, 0)
+
+    return [pl.BlockSpec(shape, index_map)] * 2
+
+
+def full_spec(array):
+    return pl.BlockSpec(array.shape, lambda step, place_ref: (0,) * array.ndim)
+
+
+def lane_spec(array):
+    return pl.BlockSpec(
+        (array.shape[0], array.shape[1] // (2 * ROUNDS)), lambda step, place_ref: (0, step)
+    )
+
+
+def store_moments(z_ref, mask_ref, stats_ref):
+    mask = mask_ref[...]
+    count = jnp.sum(mask)
+    values = z_ref[...]
+    mean = jnp.sum(values * mask, axis=0, keepdims=True) / count
+    centered = (values - mean) * mask
+    stats_ref[0:1, :] = mean
+    stats_ref[1:2, :] = jnp.sum(centered * centered, axis=0, keepdims=True)
+
+
+def coarse_forward_kernel(plan, place_ref, *refs):
+    refs = list(refs)
+    mask_ref = refs.pop(0)
+    sides = [refs.pop(0) for _ in range(3)]
+    if plan["pool"]:
+        member_ref = refs.pop(0)
+        sizes_ref = refs.pop(0)
+    pairs = {}
+    for index in plan["chunks"]:
+        pairs[index] = (refs.pop(0), refs.pop(0))
+    z_ref = refs.pop(0)
+    stats_ref = refs.pop(0)
+    step = pl.program_id(0)
+
+    @pl.when(step == 0)
+    def _():
+        z_ref[...] = jnp.zeros_like(z_ref)
+
+    columns = plan["columns"]
+    for row, chunk, tap in plan["rows"]:
+        x_first = chunk % 2 == 0
+        source, target, extent = row_span(plan["dilation"], row, plan["height"])
+        matrix = jnp.concatenate(
+            [tap_matrix(pairs[chunk], tap + k, place_ref, x_first) for k in range(3)], axis=0
+        )
+        rows_in = pl.ds(source * columns, extent * columns)
+        rows_out = pl.ds(target * columns, extent * columns)
+        values = jnp.concatenate([side[rows_in, :] for side in sides], axis=1)
+        z_ref[rows_out, :] += jnp.dot(values, matrix, preferred_element_type=jnp.float32)
+    if plan["pool"]:
+        point_ref, point_stats_ref, pool_ref, pooled_ref = refs
+
+        @pl.when(step == 0)
+        def _():
+            point_ref[...] = jnp.zeros_like(point_ref)
+            pool_ref[...] = jnp.zeros_like(pool_ref)
+
+        center = sides[1][...]
+        point_ref[...] += jnp.dot(
+            center, tap_matrix(pairs[0], 0, place_ref, True), preferred_element_type=jnp.float32
+        )
+        pooled = jnp.dot(member_ref[...], center, preferred_element_type=jnp.float32)
+        pooled = (pooled * sizes_ref[...]).astype(jnp.bfloat16)
+        pooled_ref[...] = pooled
+        pool_ref[...] += jnp.dot(
+            pooled, tap_matrix(pairs[0], 1, place_ref, True), preferred_element_type=jnp.float32
+        )
+
+    @pl.when(step == 2 * ROUNDS - 1)
+    def _():
+        store_moments(z_ref, mask_ref, stats_ref)
+        if plan["pool"]:
+            store_moments(point_ref, mask_ref, point_stats_ref)
+
+
+def coarse_forward(branch, mask, sides, chunks, shape, pool=None):
+    height, columns, channels = shape
+    positions = height * columns
+    layout = atrous_layout()[branch]
+    used = sorted({chunk for _, chunk, _ in layout} | ({0} if pool else set()))
+    plan = {
+        "pool": pool is not None,
+        "chunks": used,
+        "columns": columns,
+        "height": height,
+        "dilation": dilations[branch],
+        "rows": layout,
+    }
+    args = [mask] + list(sides)
+    specs = [full_spec(mask)] + [lane_spec(side) for side in sides]
+    if pool:
+        args += list(pool)
+        specs += [full_spec(item) for item in pool]
+    for index in used:
+        args += list(chunks[index])
+        specs += weight_specs(chunks[index], index % 2 == 0)
+    outs = [
+        jax.ShapeDtypeStruct((positions, channels), jnp.float32),
+        jax.ShapeDtypeStruct((8, channels), jnp.float32),
+    ]
+    if pool:
+        outs += outs
+        outs += [
+            jax.ShapeDtypeStruct((8, channels), jnp.float32),
+            jax.ShapeDtypeStruct((8, sides[1].shape[1]), jnp.bfloat16),
+        ]
+    out_specs = [full_spec(item) for item in outs]
+    if pool:
+        out_specs[-1] = lane_spec(outs[-1])
+    return pl.pallas_call(
+        functools.partial(coarse_forward_kernel, plan),
+        out_shape=outs,
+        grid_spec=pltpu.PrefetchScalarGridSpec(
+            num_scalar_prefetch=1, grid=(2 * ROUNDS,), in_specs=specs, out_specs=out_specs
+        ),
+        compiler_params=pltpu.CompilerParams(vmem_limit_bytes=VMEM_BYTES),
+        name="coarse_forward",
+    )(kernel_place(), *args)
+
+
+def coarse_weight_kernel(plan, place_ref, *refs):
+    refs = list(refs)
+    sides = {branch: [refs.pop(0) for _ in range(3)] for branch in plan["branches"]}
+    grads = {branch: refs.pop(0) for branch in plan["branches"]}
+    if plan["pool"]:
+        point_ref, pooled_ref, pool_ref = refs.pop(0), refs.pop(0), refs.pop(0)
+    keep_ref, give_ref = refs
+    row, core = place_ref[2], place_ref[3]
+    rows = keep_ref.shape[-2]
+    cols = keep_ref.shape[-1]
+    columns = plan["columns"]
+
+    def store(tap, value):
+        value = value.astype(jnp.bfloat16)
+        lower, upper = value[:rows], value[rows:]
+        mine = jnp.where(core == 0, lower, upper)
+        other = jnp.where(core == 0, upper, lower)
+        for ref, part in ((keep_ref, mine), (give_ref, other)):
+            for side, lane_part in ((row, part[:, :cols]), (1 - row, part[:, cols:])):
+                if plan["x_first"]:
+                    ref[0, side, 0, tap] = lane_part
+                else:
+                    ref[side, 0, 0, tap] = lane_part
+
+    across = (((0,), (0,)), ((), ()))
+    for branch, line, tap in plan["rows"]:
+        source, target, extent = row_span(dilations[branch], line, plan["height"])
+        values = jnp.concatenate(
+            [side[pl.ds(source * columns, extent * columns), :] for side in sides[branch]], axis=1
+        )
+        result = lax.dot_general(
+            values,
+            grads[branch][pl.ds(target * columns, extent * columns), :],
+            across,
+            preferred_element_type=jnp.float32,
+        )
+        for k in range(3):
+            store(tap + k, result[2 * rows * k : 2 * rows * (k + 1)])
+    if plan["pool"]:
+        center = sides[plan["branches"][0]][1][...]
+        store(
+            0,
+            lax.dot_general(center, point_ref[...], across, preferred_element_type=jnp.float32),
+        )
+        store(
+            1,
+            lax.dot_general(
+                pooled_ref[...], pool_ref[...], across, preferred_element_type=jnp.float32
+            ),
+        )
+
+
+def coarse_weight(chunk, taps, sides, grads, shape, pool=None):
+    height, columns, channels = shape
+    entries = [
+        (branch, line, tap)
+        for branch, rows in enumerate(atrous_layout())
+        for line, own, tap in rows
+        if own == chunk
+    ]
+    branches = sorted({branch for branch, _, _ in entries})
+    x_first = chunk % 2 == 0
+    plan = {
+        "pool": pool is not None,
+        "branches": branches,
+        "rows": entries,
+        "columns": columns,
+        "height": height,
+        "x_first": x_first,
+    }
+    args = []
+    specs = []
+    for branch in branches:
+        args += list(sides[branch])
+        specs += [lane_spec(side) for side in sides[branch]]
+    for branch in branches:
+        args.append(grads[branch])
+        specs.append(full_spec(grads[branch]))
+    if pool:
+        args += list(pool)
+        specs += [full_spec(pool[0]), lane_spec(pool[1]), full_spec(pool[2])]
+    rows = sides[0][1].shape[1] // (4 * ROUNDS)
+    out = jax.ShapeDtypeStruct((2, 2, ROUNDS, taps, rows, channels // 2), jnp.bfloat16)
+    shape = (1, 2, 1, taps, rows, channels // 2) if x_first else (2, 1, 1, taps, rows, channels // 2)
+
+    def index_map(step, place_ref):
+        flip = lax.rem(step + place_ref[1], 2)
+        slot = lax.rem(step // 2 - place_ref[0] + ROUNDS, ROUNDS)
+        return (flip, 0, slot, 0, 0, 0) if x_first else (0, flip, slot, 0, 0, 0)
+
+    return pl.pallas_call(
+        functools.partial(coarse_weight_kernel, plan),
+        out_shape=[out, out],
+        grid_spec=pltpu.PrefetchScalarGridSpec(
+            num_scalar_prefetch=1,
+            grid=(2 * ROUNDS,),
+            in_specs=specs,
+            out_specs=[pl.BlockSpec(shape, index_map)] * 2,
+        ),
+        compiler_params=pltpu.CompilerParams(vmem_limit_bytes=VMEM_BYTES),
+        name="coarse_weight",
+    )(kernel_place(), *args)
+
+
+def coarse_input_kernel(plan, place_ref, *refs):
+    refs = list(refs)
+    point_ref, pool_ref, spread_ref = refs.pop(0), refs.pop(0), refs.pop(0)
+    grads = [refs.pop(0) for _ in range(3)]
+    pairs = [(refs.pop(0), refs.pop(0)) for _ in range(plan["chunks"])]
+    out_ref, total_ref = refs
+    columns = plan["columns"]
+    turned = (((1,), (1,)), ((), ()))
+    total_ref[...] = lax.dot_general(
+        point_ref[...],
+        tap_matrix(pairs[0], 0, place_ref, True),
+        turned,
+        preferred_element_type=jnp.float32,
+    )
+    pooled = lax.dot_general(
+        pool_ref[...],
+        tap_matrix(pairs[0], 1, place_ref, True),
+        turned,
+        preferred_element_type=jnp.float32,
+    )
+    total_ref[...] += jnp.dot(
+        spread_ref[...], pooled, preferred_element_type=jnp.float32, precision=highest
+    )
+    for branch, rows in enumerate(plan["rows"]):
+        for line, chunk, tap in rows:
+            source, target, extent = row_span(dilations[branch], line, plan["height"])
+            matrix = jnp.concatenate(
+                [tap_matrix(pairs[chunk], tap + k, place_ref, chunk % 2 == 0) for k in range(3)],
+                axis=1,
+            )
+            total_ref[pl.ds(source * columns, extent * columns), :] += lax.dot_general(
+                grads[branch][pl.ds(target * columns, extent * columns), :],
+                matrix,
+                turned,
+                preferred_element_type=jnp.float32,
+            )
+    out_ref[...] = total_ref[...].astype(jnp.bfloat16)
+
+
+def coarse_input(point_dz, pool_dz, spread, grads, chunks, shape, width):
+    height, columns, channels = shape
+    plan = {
+        "chunks": len(chunks),
+        "columns": columns,
+        "height": height,
+        "rows": atrous_layout(),
+    }
+    args = [point_dz, pool_dz, spread] + list(grads)
+    specs = [full_spec(item) for item in args]
+    for index, pair in enumerate(chunks):
+        args += list(pair)
+        specs += weight_specs(pair, index % 2 == 0)
+    out = jax.ShapeDtypeStruct((height * columns, width), jnp.bfloat16)
+    return pl.pallas_call(
+        functools.partial(coarse_input_kernel, plan),
+        out_shape=out,
+        grid_spec=pltpu.PrefetchScalarGridSpec(
+            num_scalar_prefetch=1,
+            grid=(2 * ROUNDS,),
+            in_specs=specs,
+            out_specs=lane_spec(out),
+            scratch_shapes=[pltpu.VMEM((height * columns, width // (2 * ROUNDS)), jnp.float32)],
+        ),
+        compiler_params=pltpu.CompilerParams(vmem_limit_bytes=VMEM_BYTES),
+        name="coarse_input",
+    )(kernel_place(), *args)
+
+
+def atrous_layout():
+    places = [(chunk, tap) for chunk, size in enumerate(CHUNKS) for tap in range(size)]
+    places = places[2:]
+    return [
+        [(line,) + places[9 * branch + 3 * line] for line in range(3)] for branch in range(3)
+    ]
+
+
+def side_values(values, image_ids, dilation):
+    result = []
+    for step in (-dilation, dilation):
+        mask = tap_mask(image_ids, values.shape[1], 0, step).astype(values.dtype)
+        result.append(mask * shifted(values, 0, step))
+    return [result[0], values, result[1]]
+
+
+def side_grads(values, image_ids, dilation):
+    result = []
+    for step in (-dilation, 0, dilation):
+        masked = tap_mask(image_ids, values.shape[1], 0, step).astype(values.dtype) * values
+        result.append(shifted(masked, 0, -step))
+    return jnp.concatenate(result, axis=-1)
+
+
+def cast_add(first, second):
+    return (first.astype(jnp.float32) + second.astype(jnp.float32)).astype(jnp.bfloat16)
+
+
+def reduce_half(values, dim, index, axis, bit):
+    kept = lax.dynamic_index_in_dim(values, index, dim, keepdims=False)
+    given = lax.dynamic_index_in_dim(values, 1 - index, dim, keepdims=False)
+    return cast_add(kept, exchange(given, axis, bit))
+
+
+def reduce_depth(values, dim, depth):
+    rounds = lax.axis_size("wide") // 2
+    if rounds > 4:
+        return lax.psum_scatter(
+            values.astype(jnp.float32),
+            "wide",
+            scatter_dimension=dim,
+            axis_index_groups=depth_groups(),
+        )
+    total = lax.dynamic_index_in_dim(values, depth, dim, keepdims=False).astype(jnp.float32)
+    for step in range(1, rounds):
+        given = lax.dynamic_index_in_dim(
+            values, lax.rem(depth + step, rounds), dim, keepdims=False
+        )
+        total = total + rotate(given, "wide", step, 2).astype(jnp.float32)
+    return total
+
+
+def settle_core(values):
+    core = place()[3]
+    taps, rows, cols = values.shape
+    parts = values.reshape(taps, rows, 2, cols // 2)
+    kept = lax.dynamic_index_in_dim(parts, core, 2, keepdims=False)
+    given = lax.dynamic_index_in_dim(parts, 1 - core, 2, keepdims=False).astype(jnp.bfloat16)
+    got = exchange(given, "narrow", 1).astype(jnp.float32)
+    lower = jnp.where(core == 0, kept, got)
+    upper = jnp.where(core == 0, got, kept)
+    return jnp.concatenate([lower, upper], axis=1)
+
+
+def gather_small(flat):
+    rounds = lax.axis_size("wide") // 2
+    depth, side, row, core = place()
+    stack = jnp.take(gather_depth(flat), (depth - jnp.arange(rounds)) % rounds, axis=0)
+
+    def both(values, index, axis, bit, dim):
+        other = exchange(values, axis, bit)
+        return jnp.stack(
+            [jnp.where(index == 0, values, other), jnp.where(index == 0, other, values)], axis=dim
+        )
+
+    stack = both(stack, row, "narrow", 2, 1)
+    stack = both(stack, side, "wide", 1, 1)
+    stack = both(stack, core, "narrow", 1, 3)
+    return stack.reshape((lax.axis_size("wide"), lax.axis_size("narrow")) + flat.shape)
+
+
+def scatter_small(values):
+    depth, side, row, core = place()
+    rounds = lax.axis_size("wide") // 2
+    shape = values.shape[2:]
+    values = values.reshape((rounds, 2, 2, 2) + shape)
+    values = reduce_half(values, 3, core, "narrow", 1)
+    values = reduce_half(values, 1, side, "wide", 1)
+    values = reduce_half(values, 1, row, "narrow", 2)
+    return reduce_depth(values, 0, depth)
 
 
 def band_ids(widths, columns):
@@ -131,58 +713,9 @@
     return (valid_map * gain_row * norm_scale * inner).astype(jnp.bfloat16)
 
 
-def first_sums(blocks):
-    return jnp.concatenate(
-        [
-            jnp.sum(values * valid_map, axis=tuple(range(values.ndim - 1)))
-            for values, valid_map in blocks
-        ]
-    )
-
-
-def square_sums(blocks, means_all):
-    pieces = []
-    for block_pair, mean_row in zip(blocks, means_all):
-        values, valid_map = block_pair
-        centered = values - mean_row
-        pieces.append(jnp.sum(centered * centered * valid_map, axis=tuple(range(values.ndim - 1))))
-    return jnp.concatenate(pieces)
-
-
-def split_channels(flat, blocks):
-    pieces = []
-    offset = 0
-    for values, valid_map in blocks:
-        pieces.append(flat[offset : offset + values.shape[-1]])
-        offset = offset + values.shape[-1]
-    return pieces
-
-
-def first_counts(pixel_total, images_total):
-    pixel_count = pixel_total[0]
-    return [pixel_count, pixel_count, pixel_count, pixel_count, images_total, 16.0 * pixel_count]
-
-
-def first_moments(blocks, local_count, images_total):
-    firsts, pixel_total = lax.psum((first_sums(blocks), local_count), ("wide", "narrow"))
-    counts = first_counts(pixel_total, images_total)
-    means_all = [
-        piece / count_all for piece, count_all in zip(split_channels(firsts, blocks), counts)
-    ]
-    seconds = lax.psum(square_sums(blocks, means_all), ("wide", "narrow"))
-    variances = [
-        piece / count_all for piece, count_all in zip(split_channels(seconds, blocks), counts)
-    ]
-    return (means_all, variances, pixel_total)
-
-
-def moments(values, valid_map, count_all):
-    blocks = [(values, valid_map)]
-    firsts = lax.psum(first_sums(blocks), ("wide", "narrow"))
-    mean_row = firsts / count_all
-    seconds = lax.psum(square_sums(blocks, [mean_row]), ("wide", "narrow"))
-    variance = seconds / count_all
-    return (mean_row, variance)
+def moments(values, valid_map, local_count, count_all):
+    counts, means, squares = merge_all(*local_moments(values, valid_map, local_count))
+    return (means, squares / count_all)
 
 
 def pack_pairs(pairs):
@@ -208,7 +741,61 @@
 
 
 def gradient_sums(pairs):
-    return unpack_pairs(lax.psum(pack_pairs(pairs), ("wide", "narrow")), pairs)
+    return unpack_pairs(sum_all(pack_pairs(pairs)), pairs)
+
+
+def gather_weights(small):
+    sizes = [item.size for item in small]
+    total = sum(sizes)
+    padded = -(-total // 2048) * 2048
+    flat = jnp.concatenate(
+        [item.reshape(-1) for item in small] + [jnp.zeros((padded - total,), jnp.bfloat16)]
+    ).reshape(-1, 128)
+    everything = gather_small(flat)
+    wide, narrow = everything.shape[:2]
+    everything = everything.reshape(wide, narrow, -1)
+    pieces = []
+    start = 0
+    for item in small:
+        pieces.append(
+            everything[:, :, start : start + item.size].reshape((wide, narrow) + item.shape)
+        )
+        start += item.size
+    proj, reduce, decode, refine = pieces
+    proj = proj.transpose(0, 2, 1, 3).reshape(wide * proj.shape[2], -1)
+    reduce = reduce.transpose(0, 2, 1, 3).reshape(wide * reduce.shape[2], -1)
+    decode = decode.transpose(2, 1, 3, 0, 4).reshape(decode.shape[2], narrow * decode.shape[3], -1)
+    refine = refine.transpose(2, 0, 3, 1, 4).reshape(refine.shape[2], wide * refine.shape[3], -1)
+    return (proj, reduce, decode, refine)
+
+
+def scatter_weights(grads, shapes):
+    wide = lax.axis_size("wide")
+    narrow = lax.axis_size("narrow")
+    proj, reduce, decode, refine = grads
+    shape_p, shape_r, shape_d, shape_f = shapes
+    proj = proj.reshape(wide, shape_p[0], narrow, shape_p[1]).transpose(0, 2, 1, 3)
+    reduce = reduce.reshape(wide, shape_r[0], narrow, shape_r[1]).transpose(0, 2, 1, 3)
+    decode = decode.reshape(shape_d[0], narrow, shape_d[1], wide, shape_d[2]).transpose(3, 1, 0, 2, 4)
+    refine = refine.reshape(shape_f[0], wide, shape_f[1], narrow, shape_f[2]).transpose(1, 3, 0, 2, 4)
+    flats = [
+        item.astype(jnp.bfloat16).reshape(wide, narrow, -1)
+        for item in (proj, reduce, decode, refine)
+    ]
+    total = sum(item.shape[2] for item in flats)
+    padded = -(-total // 2048) * 2048
+    flats.append(jnp.zeros((wide, narrow, padded - total), jnp.bfloat16))
+    packed = jnp.concatenate(flats, axis=2).reshape(wide, narrow, -1, 128)
+    owned = scatter_small(packed).reshape(-1)
+    pieces = []
+    start = 0
+    for shape in shapes:
+        size = 1
+        for extent in shape:
+            size *= extent
+        pieces.append(owned[start : start + size].reshape(shape))
+        start += size
+    return pieces
 
 
 def per_device(
@@ -236,43 +823,51 @@
     images = widths.shape[1] - 1
     channels = gains.shape[1]
     images_total = float(canvases * lax.axis_size("wide") * lax.axis_size("narrow") * images)
-    point_part, atrous_part, proj_part, reduce_part, decode_part, refine_part = (
-        lax.all_gather(w_point, "narrow", axis=2, tiled=True),
-        lax.all_gather(w_atrous, "narrow", axis=3, tiled=True),
-        lax.all_gather(w_proj, "narrow", axis=1, tiled=True),
-        lax.all_gather(w_low, "narrow", axis=1, tiled=True),
-        lax.all_gather(w_dec1, "narrow", axis=1, tiled=True),
-        lax.all_gather(w_dec2, "narrow", axis=2, tiled=True),
-    )
-    point_full, atrous_full, proj_full, reduce_full, decode_full, refine_full = (
-        lax.all_gather(point_part, "wide", axis=1, tiled=True),
-        lax.all_gather(atrous_part, "wide", axis=2, tiled=True),
-        lax.all_gather(proj_part, "wide", axis=0, tiled=True),
-        lax.all_gather(reduce_part, "wide", axis=0, tiled=True),
-        lax.all_gather(decode_part, "wide", axis=2, tiled=True),
-        lax.all_gather(refine_part, "wide", axis=1, tiled=True),
-    )
+    small = [w_proj, w_low, w_dec1, w_dec2]
+    proj_full, reduce_full, decode_full, refine_full = gather_weights(small)
+    all_taps = jnp.concatenate([w_point, w_atrous.reshape((-1,) + w_atrous.shape[2:])])
+    chunks = gather_taps(all_taps, CHUNKS)
     ids_coarse = band_ids(widths, columns)
     ids_fine = band_ids(4 * widths, fine_columns)
     valid_coarse = (ids_coarse >= 0).astype(jnp.float32)[:, None, :, None]
     valid_fine = (ids_fine >= 0).astype(jnp.float32)[:, None, :, None]
     all_ones = jnp.ones((1, 1, 1), jnp.float32)
-    local_count = (height * jnp.sum(widths[:, :images])).astype(jnp.float32).reshape(1)
+    local_count = (height * jnp.sum(widths[:, :images])).astype(jnp.float32)
     member = (ids_coarse[:, :, None] == jnp.arange(images, dtype=jnp.int32)[None, None, :]).astype(
         jnp.float32
     )
     member_low = member.astype(jnp.bfloat16)
     image_sizes = (height * widths[:, :images]).astype(jnp.float32)
+    flat_features = features.reshape(height * columns, -1)
+    coarse_shape = (height, columns, channels)
+    sides = [
+        [
+            item.reshape(height * columns, -1)
+            for item in side_values(features, ids_coarse, dilation)
+        ]
+        for dilation in dilations
+    ]
+    mask_column = jnp.broadcast_to(valid_coarse, (1, height, columns, 1)).reshape(-1, 1)
+    member_wide = jnp.pad(member[0], ((0, 0), (0, 8 - images)))
+    member_rows = jnp.tile(member_wide, (height, 1))
+    sizes_inverse = jnp.pad(1.0 / image_sizes[0], (0, 8 - images)).reshape(8, 1)
+    first = coarse_forward(
+        0,
+        mask_column,
+        sides[0],
+        chunks,
+        coarse_shape,
+        (member_rows.T.astype(jnp.bfloat16), sizes_inverse),
+    )
+    second = coarse_forward(1, mask_column, sides[1], chunks, coarse_shape)
+    third = coarse_forward(2, mask_column, sides[2], chunks, coarse_shape)
+    pool_z = first[4][None, :images]
+    pooled = first[5]
+    coarse_stats = [first[3], first[1], second[1], third[1]]
     coarse_z = [
-        jnp.einsum("nhwc,cd->nhwd", features, point_full[0], preferred_element_type=jnp.float32)
+        item.reshape(1, height, columns, channels)
+        for item in (first[2], first[0], second[0], third[0])
     ]
-    for branch in range(3):
-        coarse_z.append(conv_forward(features, atrous_full[branch], ids_coarse, dilations[branch]))
-    pooled = (
-        jnp.einsum("nhwc,nwk->nkc", features, member_low, preferred_element_type=jnp.float32)
-        / image_sizes[:, :, None]
-    ).astype(jnp.bfloat16)
-    pool_z = jnp.einsum("nkc,cd->nkd", pooled, point_full[1], preferred_element_type=jnp.float32)
     reduce_z = jnp.einsum(
         "nhwc,cd->nhwd", low_level, reduce_full, preferred_element_type=jnp.float32
     )
@@ -280,9 +875,28 @@
         (pool_z, all_ones),
         (reduce_z, valid_fine),
     ]
-    section_means, section_vars, pixel_total = first_moments(blocks, local_count, images_total)
-    pixel_count = pixel_total[0]
+    local_images = float(canvases * images)
+    local_counts = [local_count] * 4 + [local_images, 16.0 * local_count]
+    states = [
+        (jnp.full((channels,), 1.0) * local_count, item[0], item[1]) for item in coarse_stats
+    ] + [
+        local_moments(block[0], block[1], count)
+        for block, count in zip(blocks[4:], local_counts[4:])
+    ]
+    counts_flat, means_flat, squares_flat = merge_all(
+        *[jnp.concatenate([state[item] for state in states]) for item in range(3)]
+    )
+    vars_flat = squares_flat / counts_flat
+    section_means = []
+    section_vars = []
+    offset = 0
+    for block in blocks:
+        section_means.append(means_flat[offset : offset + block[0].shape[-1]])
+        section_vars.append(vars_flat[offset : offset + block[0].shape[-1]])
+        offset += block[0].shape[-1]
+    pixel_count = counts_flat[0]
     fine_count = 16.0 * pixel_count
+    fine_local = 16.0 * local_count
     gain_rows = [gains[0], gains[1], gains[2], gains[3], gains[4], low_gain]
     bias_rows = [biases[0], biases[1], biases[2], biases[3], biases[4], low_bias]
     kept = []
@@ -307,7 +921,7 @@
     proj_z = jnp.einsum(
         "nhwc,cd->nhwd", joined_coarse, proj_full, preferred_element_type=jnp.float32
     )
-    proj_mean, proj_var = moments(proj_z, valid_coarse, pixel_count)
+    proj_mean, proj_var = moments(proj_z, valid_coarse, local_count, pixel_count)
     proj_act, proj_centered, proj_shaped, proj_scale = normalize(
         proj_z, valid_coarse, proj_mean, proj_var, gains[5], biases[5]
     )
@@ -325,13 +939,13 @@
     )
     joined_fine = jnp.concatenate([upsampled, activations[5]], axis=-1)
     decode_z = conv_forward(joined_fine, decode_full, ids_fine, 1)
-    decode_mean, decode_var = moments(decode_z, valid_fine, fine_count)
+    decode_mean, decode_var = moments(decode_z, valid_fine, fine_local, fine_count)
     decode_act, decode_centered, decode_shaped, decode_scale = normalize(
         decode_z, valid_fine, decode_mean, decode_var, gains[6], biases[6]
     )
     decode_act = decode_act.astype(jnp.bfloat16)
     refine_z = conv_forward(decode_act, refine_full, ids_fine, 1)
-    refine_mean, refine_var = moments(refine_z, valid_fine, fine_count)
+    refine_mean, refine_var = moments(refine_z, valid_fine, fine_local, fine_count)
     refine_act, refine_centered, refine_shaped, refine_scale = normalize(
         refine_z, valid_fine, refine_mean, refine_var, gains[7], biases[7]
     )
@@ -343,22 +957,6 @@
             + b_cls
         )
     ).astype(jnp.bfloat16)
-    point_again, atrous_again, proj_again, reduce_again, decode_again, refine_again = (
-        lax.all_gather(w_point, "narrow", axis=2, tiled=True),
-        lax.all_gather(w_atrous, "narrow", axis=3, tiled=True),
-        lax.all_gather(w_proj, "narrow", axis=1, tiled=True),
-        lax.all_gather(w_low, "narrow", axis=1, tiled=True),
-        lax.all_gather(w_dec1, "narrow", axis=1, tiled=True),
-        lax.all_gather(w_dec2, "narrow", axis=2, tiled=True),
-    )
-    point_back, atrous_back, proj_back, reduce_back, decode_back, refine_back = (
-        lax.all_gather(point_again, "wide", axis=1, tiled=True),
-        lax.all_gather(atrous_again, "wide", axis=2, tiled=True),
-        lax.all_gather(proj_again, "wide", axis=0, tiled=True),
-        lax.all_gather(reduce_again, "wide", axis=0, tiled=True),
-        lax.all_gather(decode_again, "wide", axis=2, tiled=True),
-        lax.all_gather(refine_again, "wide", axis=1, tiled=True),
-    )
     masked_grad = valid_fine.astype(jnp.bfloat16) * logit_grad
     cls_weight_grad = jnp.einsum(
         "nhwc,nhwk->ck", refine_act, masked_grad, preferred_element_type=jnp.float32
@@ -379,7 +977,7 @@
         refine_bias,
         fine_count,
     )
-    decode_up, refine_kernel_grad = conv_backward(decode_act, refine_back, refine_dz, ids_fine, 1)
+    decode_up, refine_kernel_grad = conv_backward(decode_act, refine_full, refine_dz, ids_fine, 1)
     decode_local, decode_gain, decode_bias = norm_grad_terms(
         decode_up, valid_fine, decode_centered, decode_shaped
     )
@@ -395,7 +993,7 @@
         fine_count,
     )
     joined_grad, decode_kernel_grad = conv_backward(
-        joined_fine, decode_back, decode_dz, ids_fine, 1
+        joined_fine, decode_full, decode_dz, ids_fine, 1
     )
     up_grad = joined_grad[..., :channels].astype(jnp.bfloat16)
     reduce_up = joined_grad[..., channels:]
@@ -439,13 +1037,13 @@
         "nhwc,nhwd->cd", low_level, reduce_dz, preferred_element_type=jnp.float32
     )
     low_level_grad = jnp.einsum(
-        "nhwd,cd->nhwc", reduce_dz, reduce_back, preferred_element_type=jnp.float32
+        "nhwd,cd->nhwc", reduce_dz, reduce_full, preferred_element_type=jnp.float32
     ).astype(jnp.bfloat16)
     proj_kernel_grad = jnp.einsum(
         "nhwc,nhwd->cd", joined_coarse, proj_dz, preferred_element_type=jnp.float32
     )
     concat_grad = jnp.einsum(
-        "nhwd,cd->nhwc", proj_dz, proj_back, preferred_element_type=jnp.float32
+        "nhwd,cd->nhwc", proj_dz, proj_full, preferred_element_type=jnp.float32
     )
     branch_terms = []
     for index in range(4):
@@ -456,9 +1054,14 @@
     )
     branch_terms.append(norm_grad_terms(pool_up, all_ones, kept[4][0], kept[4][1]))
     local_pairs = [(term_item[1], term_item[2]) for term_item in branch_terms]
-    flat_sums, cls_weight_grad, cls_bias_grad = lax.psum(
-        (pack_pairs(local_pairs), cls_weight_grad, cls_bias_grad), ("wide", "narrow")
-    )
+    flat_pairs = pack_pairs(local_pairs)
+    flat_sums = sum_all(
+        jnp.concatenate([flat_pairs, cls_bias_grad, cls_weight_grad.reshape(-1)])
+    )
+    classes = cls_bias_grad.shape[0]
+    cls_weight_grad = flat_sums[flat_pairs.shape[0] + classes :].reshape(cls_weight_grad.shape)
+    cls_bias_grad = flat_sums[flat_pairs.shape[0] : flat_pairs.shape[0] + classes]
+    flat_sums = flat_sums[: flat_pairs.shape[0]]
     last_pairs = unpack_pairs(flat_sums, local_pairs)
     valid_list = [valid_coarse, valid_coarse, valid_coarse, valid_coarse, all_ones]
     count_list = [pixel_count, pixel_count, pixel_count, pixel_count, images_total]
@@ -475,66 +1078,43 @@
         )
         for index in range(5)
     ]
-    point_grad = jnp.stack(
+    flat_dz = [item.reshape(height * columns, channels) for item in branch_dz[:4]]
+    pool_dz = jnp.pad(branch_dz[4][0], ((0, 8 - images), (0, 0)))
+    grad_chunks = []
+    for index, size in enumerate(CHUNKS):
+        grad_chunks.append(
+            coarse_weight(
+                index,
+                size,
+                sides,
+                flat_dz[1:],
+                coarse_shape,
+                (flat_dz[0], pooled, pool_dz) if index == 0 else None,
+            )
+        )
+    big_owned = scatter_taps(grad_chunks, all_taps.shape)
+    point_owned = big_owned[: w_point.shape[0]]
+    atrous_owned = big_owned[w_point.shape[0] :].reshape(w_atrous.shape)
+    spread_rows = member_rows * sizes_inverse.reshape(1, 8)
+    features_grad = coarse_input(
+        flat_dz[0],
+        pool_dz,
+        spread_rows,
         [
-            jnp.einsum("nhwc,nhwd->cd", features, branch_dz[0], preferred_element_type=jnp.float32),
-            jnp.einsum("nkc,nkd->cd", pooled, branch_dz[4], preferred_element_type=jnp.float32),
-        ]
-    )
-    features_grad = jnp.einsum(
-        "nhwd,cd->nhwc", branch_dz[0], point_back[0], preferred_element_type=jnp.float32
-    )
-    atrous_list = []
-    for branch in range(3):
-        input_part, kernel_part = conv_backward(
-            features, atrous_back[branch], branch_dz[branch + 1], ids_coarse, dilations[branch]
-        )
-        features_grad = features_grad + input_part
-        atrous_list.append(kernel_part)
-    pooled_grad = (
-        jnp.einsum("nkd,cd->nkc", branch_dz[4], point_back[1], preferred_element_type=jnp.float32)
-        / image_sizes[:, :, None]
-    )
-    features_grad = (
-        features_grad + jnp.einsum("nwk,nkc->nwc", member, pooled_grad, precision=highest)[:, None]
-    )
-    atrous_grad = jnp.stack(atrous_list)
-    all_grads = (
-        point_grad,
-        atrous_grad,
-        proj_kernel_grad,
-        reduce_kernel_grad,
-        decode_kernel_grad,
-        refine_kernel_grad,
-    )
-    point_wide, atrous_wide, proj_wide, reduce_wide, decode_wide, refine_wide = (
-        lax.psum_scatter(all_grads[0], "wide", scatter_dimension=1, tiled=True),
-        lax.psum_scatter(all_grads[1], "wide", scatter_dimension=2, tiled=True),
-        lax.psum_scatter(all_grads[2], "wide", scatter_dimension=0, tiled=True),
-        lax.psum_scatter(all_grads[3], "wide", scatter_dimension=0, tiled=True),
-        lax.psum_scatter(all_grads[4], "wide", scatter_dimension=2, tiled=True),
-        lax.psum_scatter(all_grads[5], "wide", scatter_dimension=1, tiled=True),
-    )
-    point_owned, atrous_owned, proj_owned, reduce_owned, decode_owned, refine_owned = (
-        lax.psum_scatter(
-            point_wide.astype(jnp.bfloat16), "narrow", scatter_dimension=2, tiled=True
-        ).astype(jnp.float32),
-        lax.psum_scatter(
-            atrous_wide.astype(jnp.bfloat16), "narrow", scatter_dimension=3, tiled=True
-        ).astype(jnp.float32),
-        lax.psum_scatter(
-            proj_wide.astype(jnp.bfloat16), "narrow", scatter_dimension=1, tiled=True
-        ).astype(jnp.float32),
-        lax.psum_scatter(
-            reduce_wide.astype(jnp.bfloat16), "narrow", scatter_dimension=1, tiled=True
-        ).astype(jnp.float32),
-        lax.psum_scatter(
-            decode_wide.astype(jnp.bfloat16), "narrow", scatter_dimension=1, tiled=True
-        ).astype(jnp.float32),
-        lax.psum_scatter(
-            refine_wide.astype(jnp.bfloat16), "narrow", scatter_dimension=2, tiled=True
-        ).astype(jnp.float32),
-    )
+            side_grads(branch_dz[branch + 1], ids_coarse, dilations[branch]).reshape(
+                height * columns, -1
+            )
+            for branch in range(3)
+        ],
+        chunks,
+        coarse_shape,
+        flat_features.shape[1],
+    ).reshape(features.shape)
+    small_owned = scatter_weights(
+        (proj_kernel_grad, reduce_kernel_grad, decode_kernel_grad, refine_kernel_grad),
+        [item.shape for item in small],
+    )
+    proj_owned, reduce_owned, decode_owned, refine_owned = small_owned
     gains_grad = jnp.stack(
         [
             last_pairs[0][0],
@@ -561,7 +1141,7 @@
     )
     return (
         logits,
-        features_grad.astype(jnp.bfloat16),
+        features_grad,
         low_level_grad,
         point_owned,
         atrous_owned,

time: 3060 us -> 1320 us (0.43)
  waiting for transfers between devices: 1640 us -> 280 us
  blocking collectives: 647 us -> 0 us
  starting transfers between devices: 5.05 us -> 177 us
  Pallas kernels: 0 us -> 94.9 us
  matrix products: 278 us -> 189 us
  local copies, waits for them, and re-layouts: 247 us -> 334 us
    reduce_scatter x7 -> x0, waiting for transfers between devices: 1120 us -> none  [the longest x1 884 us: per_device(): lax.psum_scatter(all_grads[1], 'wide', scatter_dimension=2, tiled=True)]
    psum x12 -> x0, blocking collectives: 484 us -> none  [the longest x3 122 us: moments(): seconds = lax.psum(square_sums(blocks, [mean_row]), ('wide', 'narrow'))]
    all_gather x5 -> x0, waiting for transfers between devices: 443 us -> none  [the longest x1 417 us: per_device(): lax.all_gather(atrous_part, 'wide', axis=2, tiled=True)]
    ppermute x0 -> x102, waiting for transfers between devices: none -> 280 us  [the longest x72 212 us: exchange(): lax.ppermute(values, axis, [(place, place ^ bit) for place in range(size)])]
    ppermute x0 -> x102, starting transfers between devices: none -> 177 us  [the longest x72 101 us: exchange(): lax.ppermute(values, axis, [(place, place ^ bit) for place in range(size)])]
    all_gather x7 -> x0, blocking collectives: 156 us -> none  [the longest x1 59.7 us: per_device(): lax.all_gather(reduce_part, 'wide', axis=0, tiled=True)]
    pallas_call x0 -> x8, Pallas kernels: none -> 94.9 us  [the longest x4 38.7 us: coarse_weight(): pl.pallas_call(functools.partial(coarse_weight_kernel, plan), out_shape=[...]
    unnamed x21 -> x0, waiting for transfers between devices: 75 us -> none
  transfers between devices with their start and end apart: 17 -> 102, of which waited for: 11 -> 47; matrix products, arithmetic and copies ran while one was open for 14% -> 24% of each run, Pallas kernels for 0% -> 7%
where the time goes in v1:
time: 1320 us; the launch traced here: 1300 us
  local copies, waits for them, and re-layouts  334 us (25%)
  waiting for transfers between devices  280 us (21%)
  other arithmetic  221 us (17%)
  matrix products  189 us (14%)
  starting transfers between devices  177 us (13%)
  Pallas kernels  94.9 us (7%)
    ppermute x72, waiting for transfers between devices, exchange(): lax.ppermute(values, axis, [(place, place ^ bit) for place in range(size)])  212 us
    ppermute x72, starting transfers between devices, exchange(): lax.ppermute(values, axis, [(place, place ^ bit) for place in range(size)])  101 us
    unnamed x555, local copies, waits for them, and re-layouts  100 us
    squeeze x3, local copies, waits for them, and re-layouts, conv_forward(): products[tap_index]  84.6 us
    ppermute x30, starting transfers between devices, rotate(): return lax.ppermute(values, axis, pairs)  75.7 us
    ppermute x30, waiting for transfers between devices, rotate(): return lax.ppermute(values, axis, pairs)  68.2 us
    dot_general x2, matrix products, conv_forward(): jnp.einsum('nhwc,tcd->tnhwd', values, kernel, preferred_element_type=jnp....  60.2 us
    reduce_sum x3, other arithmetic, local_moments(): mean = jnp.sum(values * valid_map, axis=axes) / count  50.5 us
  transfers between devices with their start and end apart: 102, of which 47 were waited for; matrix products, arithmetic and copies ran while one was open for 24% of the time, Pallas kernels for 7%

profile of v1, /device:TPU:1, one launch (start us, length us, event | category | flops | bytes accessed | tf_op | source)
XLA Modules:
  0.0 1301.6 jit_solution(17008904108651013703)
XLA Ops:
  25.5 10.3 collective-permute-done.8
  42.0 18.4 %collective-permute-done.26 = bf16[9,128,128]{2,1,0:T(8,128)(2,1)S(1)} collective-permute-done((bf16[9,128,128]{2,1,0:T(8,128)(2,1)S(1)}, bf16[9,128,128]{2,1,0:T(8,128)(2,1)S(1)}, u32[]{:S(2)}, u32[]{:S(2)}) %collective-permute-start.26) | collective-permute-done | bytes 294944 | tf_op jit(solution)/shard_map/ppermute | solution.py:30
  63.4 6.7 collective-permute-start.13
  72.2 7.6 collective-permute-start.19
  113.4 37.6 %collective-permute-done.16 = bf16[4,6,128,128]{3,2,1,0:T(8,128)(2,1)S(1)} collective-permute-done((bf16[4,6,128,128]{3,2,1,0:T(8,128)(2,1)}, bf16[4,6,128,128]{3,2,1,0:T(8,128)(2,1)S(1)}, u32[]{:S(2)}, u32[]{:S(2)}) %collective-permute-start.16) | collective-permute-done | bytes 786464 | tf_op jit(solution)/shard_map/ppermute | solution.py:20
  151.0 5.6 collective-permute-start.1
  175.6 33.3 %collective-permute-done.3 = bf16[4,400,128]{2,1,0:T(8,128)(2,1)S(1)} collective-permute-done((bf16[4,400,128]{2,1,0:T(8,128)(2,1)S(1)}, bf16[4,400,128]{2,1,0:T(8,128)(2,1)S(1)}, u32[]{:S(2)}, u32[]{:S(2)}) %collective-permute-start.3) | collective-permute-done | bytes 409632 | tf_op jit(solution)/shard_map/ppermute | solution.py:20
  231.9 6.0 fusion.106
  250.8 11.0 coarse_forward.4
  263.0 13.7 %coarse_forward.3 = (f32[480,256]{1,0:T(8,128)S(1)}, f32[8,256]{1,0:T(8,128)S(1)}, f32[480,256]{1,0:T(8,128)S(1)}, f32[8,256]{1,0:T(8,128)S(1)}, f32[8,256]{1,0:T(8,128)S(1)}, /*index=5*/bf16[8,2048]{1,0:T(8,128)(2,1)S(1)}) custom-call(s32[4]{0:T(128)S(1)} %pad_add_fusion.place_ref, f32[480,1]{1,0:T(8,128)S(1)} %copy-done.22, ...), custom_call_target="tpu_custom_call" | custom-call | tf_op jit(solution)/shard_map/coarse_forward/pallas_call | solution.py:318
  277.0 9.9 coarse_forward.5
  337.0 7.3 reshape.3900
  344.4 7.7 copy.197
  373.3 8.6 convert_bitcast_fusion.1
  382.0 31.3 %fusion.93 = f32[9,256,80,96]{1,3,2,0:T(8,128)} fusion(bf16[1,80,96,48]{3,2,1,0:T(8,128)(2,1)} %copy.215, bf16[1,80,96,256]{3,2,1,0:T(8,128)(2,1)} %convert_bitcast_fusion.1, bf16[9,304,256]{1,2,0:T(8,128)(2,1)} %reshape.3901), kind=kOutput, calls=%fused_computation.177 | convolution fusion | flops 10767728640 | bytes 76849152 | tf_op jit(solution)/shard_map/nhwc,tcd->tnhwd/dot_general | solution.py:631
  413.3 36.2 %slice_bitcast_fusion.17 = (f32[1,80,96,256]{3,2,1,0:T(8,128)}, f32[1,80,96,256]{3,2,1,0:T(8,128)}, f32[1,80,96,256]{3,2,1,0:T(8,128)}, f32[1,80,96,256]{3,2,1,0...) fusion(f32[9,1,80,96,256]{4,3,2,1,0:T(8,128)} %bitcast.140), kind=kLoop, calls=%fused_computation.78 | loop fusion | bytes 110100480 | tf_op jit(solution)/shard_map/squeeze | solution.py:636
  449.6 7.4 slice_bitcast_fusion.9
  457.1 25.2 %multiply_reduce_fusion.5 = (f32[256]{0:T(256)S(1)}, f32[1,80,96,256]{3,2,1,0:T(8,128)}) fusion(f32[96]{0:T(128)S(1)} %copy-done.85, f32[1,80,96,256]{3,2,1,0:T(8,128)} %slice_bitcast_fusion.9, f32[80,96]{1,0:T(8,128)S(1)} %copy-done.62, f32[1,80,96,256]{3,2,1,0:T(8,128)} %get-tuple-element.226, f32[80]{0:T(128)S(1)} %copy-done.190, ...), kind=kLoop, calls=%fused_computation.99 | loop fusion | flops 37355264 | bytes 78829888 | tf_op jit(solution)/shard_map/reduce_sum | solution.py:62
  504.8 6.2 copy.196
  515.4 28.9 %convolution_bitcast_fusion = f32[9,1,80,96,256]{4,3,2,1,0:T(8,128)} fusion(bf16[9,256,256,1]{2,1,0,3:T(8,128)(2,1)S(1)} %reshape.3977, f32[1,80,96,256]{3,2,1,0:T(8,128)} %get-tuple-element.197, f32[256]{0:T(256)} %bitcast.1097, f32[256]{0:T(256)S(1)} %bitcast.1037, f32[256]{0:T(256)S(1)} %bitcast.1043, f32[256]{0:T(256)S(1)} %add_divide_fusion.29, ...), kind=kOutput, calls=%fused_computation.9 | convolution fusion | flops 9079357440 | bytes 79827328 | tf_op jit(solution)/shard_map/nhwc,tcd->tnhwd/dot_general | solution.py:631
  544.3 41.0 %slice_bitcast_fusion.8 = (f32[1,80,96,256]{3,2,1,0:T(8,128)}, f32[1,80,96,256]{3,2,1,0:T(8,128)}, f32[1,80,96,256]{3,2,1,0:T(8,128)}, f32[1,80,96,256]{3,2,1,0:...) fusion(f32[9,1,80,96,256]{4,3,2,1,0:T(8,128)} %convolution_bitc, ...), kind=kLoop, calls=%fused_computation.68 | loop fusion | bytes 125829120 | tf_op jit(solution)/shard_map/squeeze | solution.py:636
  585.3 25.3 %multiply_reduce_fusion.3 = (f32[256]{0:T(256)S(1)}, f32[1,80,96,256]{3,2,1,0:T(8,128)}) fusion(f32[96]{0:T(128)S(1)} %copy-done.85, f32[1,80,96,256]{3,2,1,0:T(8,128)} %get-tuple-element.218, f32[80,96]{1,0:T(8,128)S(1)} %copy-done.62, f32[1,80,96,256]{3,2,1,0:T(8,128)} %get-tuple-element.219, f32[80]{0:T(128)S(1)} %copy-done.190, ...), kind=kLoop, calls=%fused_computation.93 | loop fusion | flops 37355264 | bytes 78829888 | tf_op jit(solution)/shard_map/reduce_sum | solution.py:62
  631.8 7.2 multiply_reduce_fusion.1
  658.8 7.7 broadcast_multiply_fusion.3
  703.3 22.5 %multiply_reduce_fusion = (f32[256]{0:T(256)S(1)}, f32[256]{0:T(256)S(1)}, f32[1,80,96,256]{3,2,1,0:T(8,128)}) fusion(f32[1,80,96,256]{3,2,1,0:T(8,128)} %get-tuple-element.197, f32[256]{0:T(256)S(1)} %bitcast.1044, f32[256]{0:T(256)S(1)} %copy-done.199, f32[256]{0:T(256)S(1)} %bitcast.1098, f32[256]{0:T(256)S(1)} %bitcast.1039, ...), kind=kOutput, calls=%fused_computation.85 | convolution fusion | flops 9091153920 | bytes 52304256 | tf_op jit(solution)/shard_map/tnhwd,tcd->nhwc/dot_general | solution.py:650
  740.0 8.2 copy.209
  748.9 7.0 broadcast_multiply_fusion
  755.9 8.0 broadcast_multiply_fusion.2
  800.7 18.9 %fusion.50 = f32[1,80,96,304]{2,3,1,0:T(8,128)S(1)} fusion(bf16[9,1,80,96,256]{4,3,2,1,0:T(8,128)(2,1)} %fusion.84, bf16[9,304,256]{1,2,0:T(8,128)(2,1)S(1)} %copy-done.39), kind=kOutput, calls=%fused_computation.125 | convolution fusion | flops 10758389760 | bytes 46129152 | tf_op jit(solution)/shard_map/tnhwd,tcd->nhwc/dot_general | solution.py:650
  846.1 19.5 %fusion.140 = bf16[9,256,256]{1,2,0:T(8,128)(2,1)} fusion(bf16[9,1,80,96,256]{4,3,2,1,0:T(8,128)(2,1)} %fusion.76, f32[1,80,96,256]{3,2,1,0:T(8,128)} %get-tuple-element.197, f32[256]{0:T(256)S(1)} %bitcast.1099, f32[256]{0:T(256)S(1)} %bitcast.1040, f32[256]{0:T(256)S(1)} %bitcast.1046, f32[256]{0:T(256)S(1)} %copy-done.200, f32[96]{0:T(128)S(1)} %copy-done.86), kind=kOutput, calls=%fused_computation.276 | convolution fusion | flops 9079947264 | bytes 44437888 | tf_op jit(solution)/shard_map/nhwc,tnhwd->tcd/dot_general | solution.py:651
  879.3 18.5 %fusion.137 = bf16[9,304,256]{2,1,0:T(8,128)(2,1)S(1)} fusion(bf16[1,80,96,48]{3,2,1,0:T(8,128)(2,1)} %copy.215, bf16[1,80,96,256]{3,2,1,0:T(8,128)(2,1)} %convert_bitcast_fusion.1, bf16[9,1,80,96,256]{4,3,2,1,0:T(8,128)(2,1)} %fusion.84), kind=kOutput, calls=%fused_computation.275 | convolution fusion | flops 10768429056 | bytes 41459712 | tf_op jit(solution)/shard_map/nhwc,tnhwd->tcd/dot_general | solution.py:651
  900.1 5.5 convert_element_type.1239
  905.6 8.5 copy.245
  914.1 6.9 reshape.3944
  953.4 7.5 fusion.179
  986.1 11.1 coarse_weight.5
  1001.2 8.9 coarse_weight.7
  1010.9 10.8 coarse_weight.4
  1025.3 8.0 coarse_weight.6
  1051.6 10.1 collective-permute-done.97
  1082.7 23.8 %collective-permute-done.78 = bf16[2,4,6,128,128]{4,3,2,1,0:T(8,128)(2,1)S(1)} collective-permute-done((bf16[2,4,6,128,128]{4,3,2,1,0:T(8,128)(2,1)S(1)}, bf16[2,4,6,128,128]{4,3,2,1,0:T(8,128)(2,1)S(1)}, u32[]{:S(2)}, u32[]{:S(2)}) %collective-permute-start.78) | collective-permute-done | bytes 1572896 | tf_op jit(solution)/shard_map/ppermute | solution.py:20
  1113.9 54.8 %collective-permute-done.79 = bf16[4,6,128,128]{3,2,1,0:T(8,128)(2,1)S(1)} collective-permute-done((bf16[4,6,128,128]{3,2,1,0:T(8,128)(2,1)S(1)}, bf16[4,6,128,128]{3,2,1,0:T(8,128)(2,1)S(1)}, u32[]{:S(2)}, u32[]{:S(2)}) %collective-permute-start.79) | collective-permute-done | bytes 786464 | tf_op jit(solution)/shard_map/ppermute | solution.py:20
  1186.8 7.5 collective-permute-done.73
  1205.1 8.0 collective-permute-start.93
  1216.8 15.8 %collective-permute-done.75 = bf16[8,128,128]{2,1,0:T(8,128)(2,1)S(1)} collective-permute-done((bf16[8,128,128]{2,1,0:T(8,128)(2,1)S(1)}, bf16[8,128,128]{2,1,0:T(8,128)(2,1)S(1)}, u32[]{:S(2)}, u32[]{:S(2)}) %collective-permute-start.75) | collective-permute-done | bytes 262176 | tf_op jit(solution)/shard_map/ppermute | solution.py:30
  1232.6 8.0 collective-permute-start.101
  1240.8 5.9 collective-permute-start.99
  1262.0 21.5 %coarse_input.1 = bf16[480,2048]{1,0:T(8,128)(2,1)} custom-call(s32[4]{0:T(128)S(1)} %pad_add_fusion.place_ref, bf16[480,256]{1,0:T(8,128)(2,1)S(1)} %bitcast.893, bf16[8,256]{1,0:T(8,128)(2,1)S(1)} %pad.239.refs_1_.refs_6_, f32[480,8]{1,0:T(8,128)S(1)} %bitcast_multiply_fusion.10.refs_2_, bf16[480,768]{1,0:T(8,128)(2,1)S(1)} %bitcast.891, ...), custom_call_target="tpu_custom_call" | custom-call | tf_op jit(solution)/shard_map/coarse_input/pallas_call | solution.py:486
  (1079 shorter events, 569.7 us)
Async XLA Ops:
  15.6 20.3 %collective-permute-start.8 = (bf16[8,128,128]{2,1,0:T(8,128)(2,1)S(1)}, bf16[8,128,128]{2,1,0:T(8,128)(2,1)S(1)}, u32[]{:S(2)}, u32[]{:S(2)}) collective-permute-start(bf16[8,128,128]{2,1,0:T(8,128)(2,1)S(1)} %fusion.225), channel_id=1, source_target_pairs={{0,16},{4,20},{8,24},{12,28},{16,0},{20,4},{24,8},{28,12},{1,17},{... | collective-permute-start | bytes 786440 | tf_op jit(solution)/shard_map/ppermute | solution.py:30
  20.7 21.3 %collective-permute-start.25 = (bf16[9,128,128]{2,1,0:T(8,128)(2,1)S(1)}, bf16[9,128,128]{2,1,0:T(8,128)(2,1)S(1)}, u32[]{:S(2)}, u32[]{:S(2)}) collective-permute-start(bf16[9,128,128]{2,1,0:T(8,128)(2,1)S(1)} %pad_maximum_fusion.21), channel_id=1, source_target_pairs={{0,8},{4,12},{8,16},{12,20},{16,24},{20,28},{24,0},{28,4},{1,9},{5... | collective-permute-start | bytes 884744 | tf_op jit(solution)/shard_map/ppermute | solution.py:30
  21.1 39.2 %collective-permute-start.26 = (bf16[9,128,128]{2,1,0:T(8,128)(2,1)S(1)}, bf16[9,128,128]{2,1,0:T(8,128)(2,1)S(1)}, u32[]{:S(2)}, u32[]{:S(2)}) collective-permute-start(bf16[9,128,128]{2,1,0:T(8,128)(2,1)S(1)} %pad_maximum_fusion.21), channel_id=1, source_target_pairs={{0,16},{4,20},{8,24},{12,28},{16,0},{20,4},{24,8},{28,12},{1,17},{... | collective-permute-start | bytes 884744 | tf_op jit(solution)/shard_map/ppermute | solution.py:30
  24.4 36.0 %collective-permute-start.27 = (bf16[9,128,128]{2,1,0:T(8,128)(2,1)S(1)}, bf16[9,128,128]{2,1,0:T(8,128)(2,1)S(1)}, u32[]{:S(2)}, u32[]{:S(2)}) collective-permute-start(bf16[9,128,128]{2,1,0:T(8,128)(2,1)S(1)} %pad_maximum_fusion.21), channel_id=1, source_target_pairs={{0,24},{4,28},{8,0},{12,4},{16,8},{20,12},{24,16},{28,20},{1,25},{... | collective-permute-start | bytes 884744 | tf_op jit(solution)/shard_map/ppermute | solution.py:30
  37.0 35.2 %collective-permute-start.10 = (bf16[4,8,128,128]{3,2,1,0:T(8,128)(2,1)S(1)}, bf16[4,8,128,128]{3,2,1,0:T(8,128)(2,1)S(1)}, u32[]{:S(2)}, u32[]{:S(2)}) collective-permute-start(bf16[4,8,128,128]{3,2,1,0:T(8,128)(2,1)S(1)} %get-tuple-element.287), channel_id=1, source_target_pairs={{0,4},{4,0},{8,12},{12,8},{16,20},{20,16},{24,28},{28,24},{1,5},{5... | collective-permute-start | bytes 3145736 | tf_op jit(solution)/shard_map/ppermute | solution.py:20
  61.9 46.3 %collective-permute-start.28 = (bf16[4,9,128,128]{3,2,1,0:T(8,128)(2,1)}, bf16[4,9,128,128]{3,2,1,0:T(8,128)(2,1)}, u32[]{:S(2)}, u32[]{:S(2)}) collective-permute-start(bf16[4,9,128,128]{3,2,1,0:T(8,128)(2,1)} %get-tuple-element.282), channel_id=1, source_target_pairs={{0,2},{1,3},{2,0},{3,1},{4,6},{5,7},{6,4},{7,5},{8,10},{9,11},{10,... | collective-permute-start | bytes 3538952 | tf_op jit(solution)/shard_map/ppermute | solution.py:20
  82.1 86.0 %collective-permute-start.11 = (bf16[2,4,8,128,128]{4,3,2,1,0:T(8,128)(2,1)}, bf16[2,4,8,128,128]{4,3,2,1,0:T(8,128)(2,1)}, u32[]{:S(2)}, u32[]{:S(2)}) collective-permute-start(bf16[2,4,8,128,128]{4,3,2,1,0:T(8,128)(2,1)} %get-tuple-element.263), channel_id=1, source_target_pairs={{0,2},{1,3},{2,0},{3,1},{4,6},{5,7},{6,4},{7,5},{8,10},{9,11},{10,... | collective-permute-start | bytes 6291464 | tf_op jit(solution)/shard_map/ppermute | solution.py:20
  85.7 20.0 %collective-permute-start.21 = (bf16[6,128,128]{2,1,0:T(8,128)(2,1)S(1)}, bf16[6,128,128]{2,1,0:T(8,128)(2,1)S(1)}, u32[]{:S(2)}, u32[]{:S(2)}) collective-permute-start(bf16[6,128,128]{2,1,0:T(8,128)(2,1)S(1)} %get-tuple-element.270), channel_id=1, source_target_pairs={{0,24},{4,28},{8,0},{12,4},{16,8},{20,12},{24,16},{28,20},{1,25},{... | collective-permute-start | bytes 589832 | tf_op jit(solution)/shard_map/ppermute | solution.py:30
  90.7 60.3 %collective-permute-start.16 = (bf16[4,6,128,128]{3,2,1,0:T(8,128)(2,1)}, bf16[4,6,128,128]{3,2,1,0:T(8,128)(2,1)S(1)}, u32[]{:S(2)}, u32[]{:S(2)}) collective-permute-start(bf16[4,6,128,128]{3,2,1,0:T(8,128)(2,1)} %get-tuple-element.299), channel_id=1, source_target_pairs={{0,2},{1,3},{2,0},{3,1},{4,6},{5,7},{6,4},{7,5},{8,10},{9,11},{10,... | collective-permute-start | bytes 2359304 | tf_op jit(solution)/shard_map/ppermute | solution.py:20
  101.4 57.7 %collective-permute-start = (bf16[400,128]{1,0:T(8,128)(2,1)S(1)}, bf16[400,128]{1,0:T(8,128)(2,1)S(1)}, u32[]{:S(2)}, u32[]{:S(2)}) collective-permute-start(bf16[400,128]{1,0:T(8,128)(2,1)S(1)} %bitcast.939), channel_id=1, source_target_pairs={{0,8},{4,12},{8,16},{12,20},{16,24},{20,28},{24,0},{28,4},{1,9},{5... | collective-permute-start | bytes 307208 | tf_op jit(solution)/shard_map/ppermute | solution.py:30
  107.0 57.8 %collective-permute-start.22 = (bf16[4,6,128,128]{3,2,1,0:T(8,128)(2,1)}, bf16[4,6,128,128]{3,2,1,0:T(8,128)(2,1)}, u32[]{:S(2)}, u32[]{:S(2)}) collective-permute-start(bf16[4,6,128,128]{3,2,1,0:T(8,128)(2,1)} %get-tuple-element.297), channel_id=1, source_target_pairs={{0,4},{4,0},{8,12},{12,8},{16,20},{20,16},{24,28},{28,24},{1,5},{5... | collective-permute-start | bytes 2359304 | tf_op jit(solution)/shard_map/ppermute | solution.py:20
  112.0 105.2 %collective-permute-start.29 = (bf16[2,4,9,128,128]{4,3,2,1,0:T(8,128)(2,1)}, bf16[2,4,9,128,128]{4,3,2,1,0:T(8,128)(2,1)}, u32[]{:S(2)}, u32[]{:S(2)}) collective-permute-start(bf16[2,4,9,128,128]{4,3,2,1,0:T(8,128)(2,1)} %get-tuple-element.261), channel_id=1, source_target_pairs={{0,4},{4,0},{8,12},{12,8},{16,20},{20,16},{24,28},{28,24},{1,5},{5... | collective-permute-start | bytes 7077896 | tf_op jit(solution)/shard_map/ppermute | solution.py:20
  162.5 48.0 %collective-permute-start.17 = (bf16[2,4,6,128,128]{4,3,2,1,0:T(8,128)(2,1)}, bf16[2,4,6,128,128]{4,3,2,1,0:T(8,128)(2,1)}, u32[]{:S(2)}, u32[]{:S(2)}) collective-permute-start(bf16[2,4,6,128,128]{4,3,2,1,0:T(8,128)(2,1)} %get-tuple-element.277), channel_id=1, source_target_pairs={{0,4},{4,0},{8,12},{12,8},{16,20},{20,16},{24,28},{28,24},{1,5},{5... | collective-permute-start | bytes 4718600 | tf_op jit(solution)/shard_map/ppermute | solution.py:20
  166.4 55.0 %collective-permute-start.23 = (bf16[2,4,6,128,128]{4,3,2,1,0:T(8,128)(2,1)S(1)}, bf16[2,4,6,128,128]{4,3,2,1,0:T(8,128)(2,1)S(1)}, u32[]{:S(2)}, u32[]{:S(2)}) collective-permute-start(bf16[2,4,6,128,128]{4,3,2,1,0:T(8,128)(2,1)S(1)} %get-tuple-element.275), channel_id=1, source_target_pairs={{0,2},{1,3},{2,0},{3,1},{4,6},{5,7},{6,4},{7,5},{8,10},{9,11},{10,... | collective-permute-start | bytes 4718600 | tf_op jit(solution)/shard_map/ppermute | solution.py:20
  167.8 41.1 %collective-permute-start.3 = (bf16[4,400,128]{2,1,0:T(8,128)(2,1)S(1)}, bf16[4,400,128]{2,1,0:T(8,128)(2,1)S(1)}, u32[]{:S(2)}, u32[]{:S(2)}) collective-permute-start(bf16[4,400,128]{2,1,0:T(8,128)(2,1)S(1)} %broadcast_select_fusion.2), channel_id=1, source_target_pairs={{0,2},{1,3},{2,0},{3,1},{4,6},{5,7},{6,4},{7,5},{8,10},{9,11},{10,... | collective-permute-start | bytes 1228808 | tf_op jit(solution)/shard_map/ppermute | solution.py:20
  172.7 89.1 %collective-permute-start.12 = (bf16[2,2,4,8,128,128]{5,4,3,2,1,0:T(8,128)(2,1)}, bf16[2,2,4,8,128,128]{5,4,3,2,1,0:T(8,128)(2,1)}, u32[]{:S(2)}, u32[]{:S(2)}) collective-permute-start(bf16[2,2,4,8,128,128]{5,4,3,2,1,0:T(8,128)(2,1)} %pad_maximum_fusion.1.refs_6_), channel_id=1, source_target_pairs={{0,1},{1,0},{2,3},{3,2},{4,5},{5,4},{6,7},{7,6},{8,9},{9,8},{10,11... | collective-permute-start | bytes 12582920 | tf_op jit(solution)/shard_map/ppermute | solution.py:20
  213.7 37.0 %collective-permute-start.18 = (bf16[2,2,4,6,128,128]{5,4,3,2,1,0:T(8,128)(2,1)}, bf16[2,2,4,6,128,128]{5,4,3,2,1,0:T(8,128)(2,1)}, u32[]{:S(2)}, u32[]{:S(2)}) collective-permute-start(bf16[2,2,4,6,128,128]{5,4,3,2,1,0:T(8,128)(2,1)} %pad_maximum_fusion.4.refs_8_.refs_4_), channel_id=1, source_target_pairs={{0,1},{1,0},{2,3},{3,2},{4,5},{5,4},{6,7},{7,6},{8,9},{9,8},{10,11... | collective-permute-start | bytes 9437192 | tf_op jit(solution)/shard_map/ppermute | solution.py:20
  221.4 55.5 %collective-permute-start.30 = (bf16[2,2,4,9,128,128]{5,4,3,2,1,0:T(8,128)(2,1)}, bf16[2,2,4,9,128,128]{5,4,3,2,1,0:T(8,128)(2,1)}, u32[]{:S(2)}, u32[]{:S(2)}) collective-permute-start(bf16[2,2,4,9,128,128]{5,4,3,2,1,0:T(8,128)(2,1)} %pad_maximum_fusion.refs_4_.refs_12_), channel_id=1, source_target_pairs={{0,1},{1,0},{2,3},{3,2},{4,5},{5,4},{6,7},{7,6},{8,9},{9,8},{10,11... | collective-permute-start | bytes 14155784 | tf_op jit(solution)/shard_map/ppermute | solution.py:20
  223.4 27.3 %collective-permute-start.24 = (bf16[2,2,4,6,128,128]{5,4,3,2,1,0:T(8,128)(2,1)}, bf16[2,2,4,6,128,128]{5,4,3,2,1,0:T(8,128)(2,1)}, u32[]{:S(2)}, u32[]{:S(2)}) collective-permute-start(bf16[2,2,4,6,128,128]{5,4,3,2,1,0:T(8,128)(2,1)} %pad_maximum_fusion.5.refs_6_.refs_10_), channel_id=1, source_target_pairs={{0,1},{1,0},{2,3},{3,2},{4,5},{5,4},{6,7},{7,6},{8,9},{9,8},{10,11... | collective-permute-start | bytes 9437192 | tf_op jit(solution)/shard_map/ppermute | solution.py:20
  334.1 22.6 %collective-permute-start.38 = (f32[3,256]{1,0:T(4,128)S(1)}, f32[3,256]{1,0:T(4,128)S(1)}, u32[]{:S(2)}, u32[]{:S(2)}) collective-permute-start(f32[3,256]{1,0:T(4,128)S(1)} %pad_maximum_fusion.32), channel_id=1, source_target_pairs={{0,4},{4,0},{8,12},{12,8},{16,20},{20,16},{24,28},{28,24},{1,5},{5... | collective-permute-start | bytes 9224 | tf_op jit(solution)/shard_map/ppermute | solution.py:20
  844.9 32.1 %collective-permute-start.64 = (f32[608]{0:T(1024)S(1)}, f32[608]{0:T(1024)S(1)}, u32[]{:S(2)}, u32[]{:S(2)}) collective-permute-start(f32[608]{0:T(1024)S(1)} %add.2170), channel_id=1, source_target_pairs={{0,8},{4,12},{8,0},{12,4},{16,24},{20,28},{24,16},{28,20},{1,9},{5... | collective-permute-start | bytes 7304 | tf_op jit(solution)/shard_map/ppermute | solution.py:20
  877.0 44.0 %collective-permute-start.65 = (f32[608]{0:T(1024)S(1)}, f32[608]{0:T(1024)S(1)}, u32[]{:S(2)}, u32[]{:S(2)}) collective-permute-start(f32[608]{0:T(1024)S(1)} %add.2171), channel_id=1, source_target_pairs={{0,16},{4,20},{8,24},{12,28},{16,0},{20,4},{24,8},{28,12},{1,17},{... | collective-permute-start | bytes 7304 | tf_op jit(solution)/shard_map/ppermute | solution.py:20
  934.3 31.7 %collective-permute-start.66 = (f32[7957]{0:T(1024)S(1)}, f32[7957]{0:T(1024)}, u32[]{:S(2)}, u32[]{:S(2)}) collective-permute-start(f32[7957]{0:T(1024)S(1)} %concatenate.132), channel_id=1, source_target_pairs={{0,1},{1,0},{2,3},{3,2},{4,5},{5,4},{6,7},{7,6},{8,9},{9,8},{10,11... | collective-permute-start | bytes 95492 | tf_op jit(solution)/shard_map/ppermute | solution.py:20
  979.1 59.9 %collective-permute-start.96 = (bf16[4,2,2,400,128]{4,3,1,0,2:T(8,128)(2,1)}, bf16[4,2,2,400,128]{4,3,1,0,2:T(8,128)(2,1)}, u32[]{:S(2)}, u32[]{:S(2)}) collective-permute-start(bf16[4,2,2,400,128]{4,3,1,0,2:T(8,128)(2,1)} %dynamic-slice_bitcast_fusion), channel_id=1, source_target_pairs={{0,1},{1,0},{2,3},{3,2},{4,5},{5,4},{6,7},{7,6},{8,9},{9,8},{10,11... | collective-permute-start | bytes 4915208 | tf_op jit(solution)/shard_map/ppermute | solution.py:20
  997.2 66.9 %collective-permute-start.77 = (bf16[2,2,4,6,128,128]{5,4,3,2,1,0:T(8,128)(2,1)}, bf16[2,2,4,6,128,128]{5,4,3,2,1,0:T(8,128)(2,1)}, u32[]{:S(2)}, u32[]{:S(2)}) collective-permute-start(bf16[2,2,4,6,128,128]{5,4,3,2,1,0:T(8,128)(2,1)} %get-tuple-element.46), channel_id=1, source_target_pairs={{0,1},{1,0},{2,3},{3,2},{4,5},{5,4},{6,7},{7,6},{8,9},{9,8},{10,11... | collective-permute-start | bytes 9437192 | tf_op jit(solution)/shard_map/ppermute | solution.py:20
  1010.1 69.0 %collective-permute-start.89 = (bf16[2,2,4,9,128,128]{5,4,3,2,1,0:T(8,128)(2,1)}, bf16[2,2,4,9,128,128]{5,4,3,2,1,0:T(8,128)(2,1)}, u32[]{:S(2)}, u32[]{:S(2)}) collective-permute-start(bf16[2,2,4,9,128,128]{5,4,3,2,1,0:T(8,128)(2,1)} %get-tuple-element.50), channel_id=1, source_target_pairs={{0,1},{1,0},{2,3},{3,2},{4,5},{5,4},{6,7},{7,6},{8,9},{9,8},{10,11... | collective-permute-start | bytes 14155784 | tf_op jit(solution)/shard_map/ppermute | solution.py:20
  1021.7 54.6 %collective-permute-start.71 = (bf16[2,2,4,8,128,128]{5,4,3,2,1,0:T(8,128)(2,1)}, bf16[2,2,4,8,128,128]{5,4,3,2,1,0:T(8,128)(2,1)}, u32[]{:S(2)}, u32[]{:S(2)}) collective-permute-start(bf16[2,2,4,8,128,128]{5,4,3,2,1,0:T(8,128)(2,1)} %get-tuple-element.44), channel_id=1, source_target_pairs={{0,1},{1,0},{2,3},{3,2},{4,5},{5,4},{6,7},{7,6},{8,9},{9,8},{10,11... | collective-permute-start | bytes 12582920 | tf_op jit(solution)/shard_map/ppermute | solution.py:20
  1033.4 39.6 %collective-permute-start.83 = (bf16[2,2,4,6,128,128]{5,4,3,2,1,0:T(8,128)(2,1)}, bf16[2,2,4,6,128,128]{5,4,3,2,1,0:T(8,128)(2,1)}, u32[]{:S(2)}, u32[]{:S(2)}) collective-permute-start(bf16[2,2,4,6,128,128]{5,4,3,2,1,0:T(8,128)(2,1)} %get-tuple-element.48), channel_id=1, source_target_pairs={{0,1},{1,0},{2,3},{3,2},{4,5},{5,4},{6,7},{7,6},{8,9},{9,8},{10,11... | collective-permute-start | bytes 9437192 | tf_op jit(solution)/shard_map/ppermute | solution.py:20
  1042.0 19.7 %collective-permute-start.97 = (bf16[4,2,400,128]{3,2,0,1:T(8,128)(2,1)}, bf16[4,2,400,128]{3,2,0,1:T(8,128)(2,1)}, u32[]{:S(2)}, u32[]{:S(2)}) collective-permute-start(bf16[4,2,400,128]{3,2,0,1:T(8,128)(2,1)} %dynamic-slice_bitcast_fusion.1), channel_id=1, source_target_pairs={{0,4},{4,0},{8,12},{12,8},{16,20},{20,16},{24,28},{28,24},{1,5},{5... | collective-permute-start | bytes 2457608 | tf_op jit(solution)/shard_map/ppermute | solution.py:20
  1066.3 40.2 %collective-permute-start.78 = (bf16[2,4,6,128,128]{4,3,2,1,0:T(8,128)(2,1)S(1)}, bf16[2,4,6,128,128]{4,3,2,1,0:T(8,128)(2,1)S(1)}, u32[]{:S(2)}, u32[]{:S(2)}) collective-permute-start(bf16[2,4,6,128,128]{4,3,2,1,0:T(8,128)(2,1)S(1)} %fusion.131), channel_id=1, source_target_pairs={{0,2},{1,3},{2,0},{3,1},{4,6},{5,7},{6,4},{7,5},{8,10},{9,11},{10,... | collective-permute-start | bytes 4718600 | tf_op jit(solution)/shard_map/ppermute | solution.py:20
  1075.0 35.7 %collective-permute-start.84 = (bf16[2,4,6,128,128]{4,3,2,1,0:T(8,128)(2,1)S(1)}, bf16[2,4,6,128,128]{4,3,2,1,0:T(8,128)(2,1)S(1)}, u32[]{:S(2)}, u32[]{:S(2)}) collective-permute-start(bf16[2,4,6,128,128]{4,3,2,1,0:T(8,128)(2,1)S(1)} %fusion.132), channel_id=1, source_target_pairs={{0,4},{4,0},{8,12},{12,8},{16,20},{20,16},{24,28},{28,24},{1,5},{5... | collective-permute-start | bytes 4718600 | tf_op jit(solution)/shard_map/ppermute | solution.py:20
  1078.6 92.0 %collective-permute-start.72 = (bf16[2,4,8,128,128]{4,3,2,1,0:T(8,128)(2,1)S(1)}, bf16[2,4,8,128,128]{4,3,2,1,0:T(8,128)(2,1)S(1)}, u32[]{:S(2)}, u32[]{:S(2)}) collective-permute-start(bf16[2,4,8,128,128]{4,3,2,1,0:T(8,128)(2,1)S(1)} %fusion.99), channel_id=1, source_target_pairs={{0,4},{4,0},{8,12},{12,8},{16,20},{20,16},{24,28},{28,24},{1,5},{5... | collective-permute-start | bytes 6291464 | tf_op jit(solution)/shard_map/ppermute | solution.py:20
  1081.6 93.4 %collective-permute-start.90 = (bf16[2,4,9,128,128]{4,3,2,1,0:T(8,128)(2,1)S(1)}, bf16[2,4,9,128,128]{4,3,2,1,0:T(8,128)(2,1)S(1)}, u32[]{:S(2)}, u32[]{:S(2)}) collective-permute-start(bf16[2,4,9,128,128]{4,3,2,1,0:T(8,128)(2,1)S(1)} %fusion.97), channel_id=1, source_target_pairs={{0,2},{1,3},{2,0},{3,1},{4,6},{5,7},{6,4},{7,5},{8,10},{9,11},{10,... | collective-permute-start | bytes 7077896 | tf_op jit(solution)/shard_map/ppermute | solution.py:20
  1108.7 60.0 %collective-permute-start.79 = (bf16[4,6,128,128]{3,2,1,0:T(8,128)(2,1)S(1)}, bf16[4,6,128,128]{3,2,1,0:T(8,128)(2,1)S(1)}, u32[]{:S(2)}, u32[]{:S(2)}) collective-permute-start(bf16[4,6,128,128]{3,2,1,0:T(8,128)(2,1)S(1)} %fusion.192), channel_id=1, source_target_pairs={{0,4},{4,0},{8,12},{12,8},{16,20},{20,16},{24,28},{28,24},{1,5},{5... | collective-permute-start | bytes 2359304 | tf_op jit(solution)/shard_map/ppermute | solution.py:20
  1112.8 66.2 %collective-permute-start.85 = (bf16[4,6,128,128]{3,2,1,0:T(8,128)(2,1)S(1)}, bf16[4,6,128,128]{3,2,1,0:T(8,128)(2,1)S(1)}, u32[]{:S(2)}, u32[]{:S(2)}) collective-permute-start(bf16[4,6,128,128]{3,2,1,0:T(8,128)(2,1)S(1)} %fusion.193), channel_id=1, source_target_pairs={{0,2},{1,3},{2,0},{3,1},{4,6},{5,7},{6,4},{7,5},{8,10},{9,11},{10,... | collective-permute-start | bytes 2359304 | tf_op jit(solution)/shard_map/ppermute | solution.py:20
  1175.1 19.2 %collective-permute-start.73 = (bf16[4,8,128,128]{3,2,1,0:T(8,128)(2,1)S(1)}, bf16[4,8,128,128]{3,2,1,0:T(8,128)(2,1)S(1)}, u32[]{:S(2)}, u32[]{:S(2)}) collective-permute-start(bf16[4,8,128,128]{3,2,1,0:T(8,128)(2,1)S(1)} %fusion.185), channel_id=1, source_target_pairs={{0,2},{1,3},{2,0},{3,1},{4,6},{5,7},{6,4},{7,5},{8,10},{9,11},{10,... | collective-permute-start | bytes 3145736 | tf_op jit(solution)/shard_map/ppermute | solution.py:20
  1179.0 21.7 %collective-permute-start.91 = (bf16[4,9,128,128]{3,2,1,0:T(8,128)(2,1)S(1)}, bf16[4,9,128,128]{3,2,1,0:T(8,128)(2,1)S(1)}, u32[]{:S(2)}, u32[]{:S(2)}) collective-permute-start(bf16[4,9,128,128]{3,2,1,0:T(8,128)(2,1)S(1)} %fusion.163), channel_id=1, source_target_pairs={{0,4},{4,0},{8,12},{12,8},{16,20},{20,16},{24,28},{28,24},{1,5},{5... | collective-permute-start | bytes 3538952 | tf_op jit(solution)/shard_map/ppermute | solution.py:20
  1180.6 21.7 %collective-permute-start.86 = (bf16[6,128,128]{2,1,0:T(8,128)(2,1)S(1)}, bf16[6,128,128]{2,1,0:T(8,128)(2,1)S(1)}, u32[]{:S(2)}, u32[]{:S(2)}) collective-permute-start(bf16[6,128,128]{2,1,0:T(8,128)(2,1)S(1)} %get-tuple-element.293), channel_id=1, source_target_pairs={{0,8},{4,12},{8,16},{12,20},{16,24},{20,28},{24,0},{28,4},{1,9},{5... | collective-permute-start | bytes 589832 | tf_op jit(solution)/shard_map/ppermute | solution.py:30
  1185.0 20.1 %collective-permute-start.88 = (bf16[6,128,128]{2,1,0:T(8,128)(2,1)S(1)}, bf16[6,128,128]{2,1,0:T(8,128)(2,1)S(1)}, u32[]{:S(2)}, u32[]{:S(2)}) collective-permute-start(bf16[6,128,128]{2,1,0:T(8,128)(2,1)S(1)} %get-tuple-element.294), channel_id=1, source_target_pairs={{0,24},{4,28},{8,0},{12,4},{16,8},{20,12},{24,16},{28,20},{1,25},{... | collective-permute-start | bytes 589832 | tf_op jit(solution)/shard_map/ppermute | solution.py:30
  1200.7 31.9 %collective-permute-start.75 = (bf16[8,128,128]{2,1,0:T(8,128)(2,1)S(1)}, bf16[8,128,128]{2,1,0:T(8,128)(2,1)S(1)}, u32[]{:S(2)}, u32[]{:S(2)}) collective-permute-start(bf16[8,128,128]{2,1,0:T(8,128)(2,1)S(1)} %get-tuple-element.285), channel_id=1, source_target_pairs={{0,16},{4,20},{8,24},{12,28},{16,0},{20,4},{24,8},{28,12},{1,17},{... | collective-permute-start | bytes 786440 | tf_op jit(solution)/shard_map/ppermute | solution.py:30
  1202.4 30.3 %collective-permute-start.76 = (bf16[8,128,128]{2,1,0:T(8,128)(2,1)S(1)}, bf16[8,128,128]{2,1,0:T(8,128)(2,1)S(1)}, u32[]{:S(2)}, u32[]{:S(2)}) collective-permute-start(bf16[8,128,128]{2,1,0:T(8,128)(2,1)S(1)} %get-tuple-element.284), channel_id=1, source_target_pairs={{0,24},{4,28},{8,0},{12,4},{16,8},{20,12},{24,16},{28,20},{1,25},{... | collective-permute-start | bytes 786440 | tf_op jit(solution)/shard_map/ppermute | solution.py:30
  1203.7 37.1 %collective-permute-start.92 = (bf16[9,128,128]{2,1,0:T(8,128)(2,1)S(1)}, bf16[9,128,128]{2,1,0:T(8,128)(2,1)S(1)}, u32[]{:S(2)}, u32[]{:S(2)}) collective-permute-start(bf16[9,128,128]{2,1,0:T(8,128)(2,1)S(1)} %get-tuple-element.278), channel_id=1, source_target_pairs={{0,8},{4,12},{8,16},{12,20},{16,24},{20,28},{24,0},{28,4},{1,9},{5... | collective-permute-start | bytes 884744 | tf_op jit(solution)/shard_map/ppermute | solution.py:30
  1205.1 44.3 %collective-permute-start.93 = (bf16[9,128,128]{2,1,0:T(8,128)(2,1)S(1)}, bf16[9,128,128]{2,1,0:T(8,128)(2,1)S(1)}, u32[]{:S(2)}, u32[]{:S(2)}) collective-permute-start(bf16[9,128,128]{2,1,0:T(8,128)(2,1)S(1)} %get-tuple-element.280), channel_id=1, source_target_pairs={{0,16},{4,20},{8,24},{12,28},{16,0},{20,4},{24,8},{28,12},{1,17},{... | collective-permute-start | bytes 884744 | tf_op jit(solution)/shard_map/ppermute | solution.py:30
  1213.1 36.3 %collective-permute-start.94 = (bf16[9,128,128]{2,1,0:T(8,128)(2,1)S(1)}, bf16[9,128,128]{2,1,0:T(8,128)(2,1)S(1)}, u32[]{:S(2)}, u32[]{:S(2)}) collective-permute-start(bf16[9,128,128]{2,1,0:T(8,128)(2,1)S(1)} %get-tuple-element.279), channel_id=1, source_target_pairs={{0,24},{4,28},{8,0},{12,4},{16,8},{20,12},{24,16},{28,20},{1,25},{... | collective-permute-start | bytes 884744 | tf_op jit(solution)/shard_map/ppermute | solution.py:30
  1232.6 50.9 %collective-permute-start.100 = (bf16[400,128]{1,0:T(8,128)(2,1)}, bf16[400,128]{1,0:T(8,128)(2,1)}, u32[]{:S(2)}, u32[]{:S(2)}) collective-permute-start(bf16[400,128]{1,0:T(8,128)(2,1)} %get-tuple-element.302), channel_id=1, source_target_pairs={{0,16},{4,20},{8,24},{12,28},{16,0},{20,4},{24,8},{28,12},{1,17},{... | collective-permute-start | bytes 307208 | tf_op jit(solution)/shard_map/ppermute | solution.py:30
  1232.6 50.9 %collective-permute-start.101 = (bf16[400,128]{1,0:T(8,128)(2,1)}, bf16[400,128]{1,0:T(8,128)(2,1)}, u32[]{:S(2)}, u32[]{:S(2)}) collective-permute-start(bf16[400,128]{1,0:T(8,128)(2,1)} %get-tuple-element.301), channel_id=1, source_target_pairs={{0,24},{4,28},{8,0},{12,4},{16,8},{20,12},{24,16},{28,20},{1,25},{... | collective-permute-start | bytes 307208 | tf_op jit(solution)/shard_map/ppermute | solution.py:30
  1240.8 42.8 %collective-permute-start.99 = (bf16[400,128]{1,0:T(8,128)(2,1)}, bf16[400,128]{1,0:T(8,128)(2,1)}, u32[]{:S(2)}, u32[]{:S(2)}) collective-permute-start(bf16[400,128]{1,0:T(8,128)(2,1)} %get-tuple-element.300), channel_id=1, source_target_pairs={{0,8},{4,12},{8,16},{12,20},{16,24},{20,28},{24,0},{28,4},{1,9},{5... | collective-permute-start | bytes 307208 | tf_op jit(solution)/shard_map/ppermute | solution.py:30
  1255.9 35.2 %collective-permute-start.95 = (bf16[29,128,64]{1,2,0:T(8,128)(2,1)}, bf16[29,128,64]{1,2,0:T(8,128)(2,1)}, u32[]{:S(2)}, u32[]{:S(2)}) collective-permute-start(bf16[29,128,64]{1,2,0:T(8,128)(2,1)} %fusion.215), channel_id=1, source_target_pairs={{0,1},{1,0},{2,3},{3,2},{4,5},{5,4},{6,7},{7,6},{8,9},{9,8},{10,11... | collective-permute-start | bytes 1425416 | tf_op jit(solution)/shard_map/ppermute | solution.py:20
  (303 other events, 4522.7 us)

commit v2 on v1

v2 whole, which is shorter than its diff:
```python
import functools

import jax
import jax.numpy as jnp
from jax import lax
from jax.experimental import pallas as pl
from jax.experimental.pallas import tpu as pltpu
from jax.sharding import PartitionSpec as P

epsilon = 1e-05
highest = lax.Precision.HIGHEST
dilations = (6, 12, 18)
ROUNDS = 4
CHUNKS = (3, 3, 5, 6, 6, 6)
PARTS = ((0, 1), (2, 3), (4, 5))
POINT_CHUNK = 2
VMEM_BYTES = 48 * 1024 * 1024


def exchange(values, axis, bit):
    size = lax.axis_size(axis)
    return lax.ppermute(values, axis, [(place, place ^ bit) for place in range(size)])


def rotate(values, axis, step, stride):
    size = lax.axis_size(axis)
    rounds = size // stride
    pairs = []
    for place in range(size):
        outer, inner = place // stride, place % stride
        pairs.append((place, ((outer + step) % rounds) * stride + inner))
    return lax.ppermute(values, axis, pairs)


def bits_of(axis):
    size = lax.axis_size(axis)
    bits = []
    bit = 1
    while bit < size:
        bits.append((axis, bit))
        bit = bit * 2
    return bits


def sum_all(values):
    for axis, bit in bits_of("narrow") + bits_of("wide"):
        values = values + exchange(values, axis, bit)
    return values


def merge_all(counts, means, squares):
    for axis, bit in bits_of("narrow") + bits_of("wide"):
        other = exchange(jnp.stack([counts, means, squares]), axis, bit)
        total = counts + other[0]
        gap = means - other[1]
        squares = squares + other[2] + gap * gap * (counts * other[0] / total)
        means = (counts * means + other[0] * other[1]) / total
        counts = total
    return (counts, means, squares)


def local_moments(values, valid_map, count):
    axes = tuple(range(values.ndim - 1))
    mean = jnp.sum(values * valid_map, axis=axes) / count
    centered = values - mean
    return (jnp.full_like(mean, 1.0) * count, mean, jnp.sum(centered * centered * valid_map, axis=axes))


def place():
    wide = lax.axis_index("wide")
    narrow = lax.axis_index("narrow")
    return (wide // 2, wide % 2, narrow // 2, narrow % 2)


def share_core(shard):
    core = place()[3]
    half = shard.shape[1] // 2
    parts = shard.reshape(shard.shape[0], 2, half, shard.shape[2])
    kept = lax.dynamic_index_in_dim(parts, core, 1, keepdims=False)
    given = lax.dynamic_index_in_dim(parts, 1 - core, 1, keepdims=False)
    got = exchange(given, "narrow", 1)
    lower = jnp.where(core == 0, kept, got)
    upper = jnp.where(core == 0, got, kept)
    return jnp.concatenate([lower, upper], axis=2)


def tuned():
    return lax.axis_size("wide") == 2 * ROUNDS and lax.axis_size("narrow") == 4


def kernel_place():
    values = jnp.stack(place()).astype(jnp.int32)
    return values if tuned() else jnp.zeros_like(values)


class Order:
    def __init__(self):
        self.last = None

    def take(self, values):
        if self.last is None:
            return values
        values, self.last = lax.optimization_barrier((values, self.last))
        return values

    def give(self, values):
        self.last = values
        return values

    def run(self, function, *values):
        return self.give(function(*self.take(values)))


def chunk_order(index):
    return [("wide", 1), ("narrow", 2)] if index % 2 == 0 else [("narrow", 2), ("wide", 1)]


def gather_taps(weights, small, fillers, kernels):
    rounds = ROUNDS
    sizes = [[CHUNKS[index] for index in part] for part in PARTS]
    shapes = [item.shape for item in small]
    if not tuned():
        chunks = []
        for part, values in zip(PARTS, weights):
            full = lax.all_gather(values, "narrow", axis=2, tiled=True)
            full = lax.all_gather(full, "wide", axis=1, tiled=True)
            rows = full.shape[1] // (4 * rounds)
            full = full.reshape(full.shape[0], rounds, 2, 2, rows, 2, full.shape[2] // 2)
            start = 0
            for index in part:
                piece = full[start : start + CHUNKS[index]]
                start += CHUNKS[index]
                piece = piece[:, [0] + list(range(rounds - 1, 0, -1))]
                order = (3, 5, 2, 1, 0, 4, 6) if index % 2 == 0 else (3, 2, 5, 1, 0, 4, 6)
                piece = piece.transpose(order)
                chunks.append((piece[0], piece[1]))
        flat = pack_small(small)
        everything = lax.all_gather(flat, ("wide", "narrow"))
        everything = everything.reshape(lax.axis_size("wide"), lax.axis_size("narrow"), -1)
        unpacked = unpack_small(everything, small)
        ready = fillers[0]()
        results = fillers[1](*unpacked)
        result = None
        for part, kernel in zip(PARTS, kernels):
            own = [chunks[index][0] for index in part]
            other = [chunks[index][1] for index in part]
            result = kernel(ready, own, other, result)
        return (chunks, unpacked, ready, results, result)

    def depth(values):
        return [rotate(values, "wide", step, 2) for step in range(1, rounds)]

    def split(part, own, others):
        values = jnp.stack([own] + list(others))
        result = []
        start = 0
        for size in sizes[part]:
            result.append(values[:, start : start + size])
            start += size
        return result

    def along(part, stacks, turn):
        return [
            exchange(stack, *chunk_order(index)[turn]) for stack, index in zip(stacks, PARTS[part])
        ]

    def pair(values, others):
        return [jnp.stack(item) for item in zip(values, others)]

    def across(stacks):
        return [exchange(stack, "narrow", 1) for stack in stacks]

    order = Order()
    shared = [None, None, None]
    shared[0] = order.run(share_core, weights[0])
    z0 = depth(shared[0])
    small = order.run(small_block, list(small))
    xs = exchange(small, "wide", 1)
    shared[1] = order.run(share_core, weights[1])
    z1 = depth(shared[1])
    small = order.run(lambda *items: jnp.stack(items), small, xs)
    ys = exchange(small, "narrow", 2)
    s0 = order.run(functools.partial(split, 0), shared[0], z0)
    f0 = along(0, s0, 0)
    shared[2] = order.run(share_core, weights[2])
    z2 = depth(shared[2])
    small = order.run(lambda *items: jnp.stack(items), small, ys)
    zs = depth(small)
    s0 = order.run(pair, s0, f0)
    g0 = along(0, s0, 1)
    ready = order.run(fillers[0])
    s1 = order.run(functools.partial(split, 1), shared[1], z1)
    f1 = along(1, s1, 0)
    s0 = order.run(pair, s0, g0)
    c0 = across(s0)
    s1 = order.run(pair, s1, f1)
    g1 = along(1, s1, 1)
    result = order.run(kernels[0], ready, s0, c0, None)
    s2 = order.run(functools.partial(split, 2), shared[2], z2)
    f2 = along(2, s2, 0)
    s1 = order.run(pair, s1, g1)
    c1 = across(s1)
    s2 = order.run(pair, s2, f2)
    g2 = along(2, s2, 1)
    small = order.run(lambda own, others: jnp.stack([own] + others), small, zs)
    cs = exchange(small, "narrow", 1)
    result = order.run(kernels[1], ready, s1, c1, result)
    unpacked = order.run(functools.partial(unpack_block, shapes=shapes), small, cs)
    results = order.run(fillers[1], *unpacked)
    s2 = order.run(pair, s2, g2)
    c2 = across(s2)
    result = order.run(kernels[2], ready, s2, c2, result)
    chunks = list(zip(s0 + s1 + s2, c0 + c1 + c2))
    return (chunks, unpacked, ready, results, result)


def add_wide(first, second):
    return first.astype(jnp.float32) + second.astype(jnp.float32)


def narrow(values):
    return values.astype(jnp.bfloat16)


def scatter_taps(grads, shapes, kernels, pack, fillers):
    rounds = ROUNDS
    if not tuned():
        owned = []
        for part, kernel in zip(PARTS, kernels):
            pieces = []
            for index, pair in zip(part, kernel(grads)):
                piece = jnp.stack(pair)
                order = (4, 3, 1, 0, 5, 2, 6) if index % 2 == 0 else (4, 3, 2, 0, 5, 1, 6)
                piece = piece.transpose(order)
                pieces.append(piece.reshape(piece.shape[0], -1, 2 * piece.shape[6]))
            full = jnp.concatenate(pieces)
            full = lax.psum_scatter(full, "wide", scatter_dimension=1, tiled=True)
            full = lax.psum_scatter(full, "narrow", scatter_dimension=2, tiled=True)
            owned.append(full.astype(jnp.float32))
        low, low_weight = fillers[0](grads[0])
        small = pack_grads(low_weight, *pack, shapes)
        small = lax.psum_scatter(small, "wide", scatter_dimension=0, tiled=True)
        small = lax.psum_scatter(small, "narrow", scatter_dimension=1, tiled=True)
        small = unpack_grads(small[0, 0].astype(jnp.float32), shapes)
        return (owned, small, low, fillers[1](None))

    def across(pairs):
        return [exchange(pair[1], "narrow", 1) for pair in pairs]

    def first(pairs, others):
        return [narrow(add_wide(pair[0][1], other[1])) for pair, other in zip(pairs, others)]

    def second(pairs, others, values):
        sent = []
        kept = []
        for pair, other, value in zip(pairs, others, values):
            total = add_wide(pair[0][0], other[0]) + value.astype(jnp.float32)
            kept.append(total[0])
            sent.append(narrow(total[1]))
        return (kept, sent)

    def along(indices, values, turn):
        return [
            exchange(value, *chunk_order(index)[turn]) for value, index in zip(values, indices)
        ]

    def deep(kept, values):
        total = jnp.concatenate(
            [own + value.astype(jnp.float32) for own, value in zip(kept, values)], axis=1
        )
        return (total[0], [narrow(total[step]) for step in range(1, rounds)])

    def turned(values):
        return [rotate(value, "wide", step + 1, 2) for step, value in enumerate(values)]

    def finish(total, values):
        for value in values:
            total = total + value.astype(jnp.float32)
        return total

    def settle(total, values):
        return settle_core(finish(total, values))

    order = Order()
    a, b, c = 2, 1, 0
    pairs_a = kernels[a](grads)
    core_a = across(pairs_a)
    pairs_b = kernels[b](grads, tie=pairs_a[0][0])
    core_b = across(pairs_b)
    sent_a = first(pairs_a, core_a)
    first_a = along(PARTS[a], sent_a, 0)
    pairs_c = kernels[c](grads, tie=sent_a[1])
    core_c = across(pairs_c)
    sent_b = first(pairs_b, core_b)
    first_b = along(PARTS[b], sent_b, 0)
    low, low_weight = fillers[0](sent_b[0])
    pairs_s = [pack_block(pack[0], low_weight, *pack[1:], shapes=shapes, tie=sent_b[1])]
    core_s = across(pairs_s)
    filled = fillers[1](sent_b[1])
    kept_a, sent = order.run(second, pairs_a, core_a, first_a)
    second_a = along(PARTS[a], sent, 1)
    first_c = along(PARTS[c], order.run(first, pairs_c, core_c), 0)
    first_s = along((0,), order.run(first, pairs_s, core_s), 0)
    kept_b, sent = order.run(second, pairs_b, core_b, first_b)
    second_b = along(PARTS[b], sent, 1)
    total_a, sent = order.run(deep, kept_a, second_a)
    deep_a = turned(sent)
    kept_c, sent = order.run(second, pairs_c, core_c, first_c)
    second_c = along(PARTS[c], sent, 1)
    kept_s, sent = order.run(second, pairs_s, core_s, first_s)
    second_s = along((0,), sent, 1)
    total_b, sent = order.run(deep, kept_b, second_b)
    deep_b = turned(sent)
    total_c, sent = order.run(deep, kept_c, second_c)
    deep_c = turned(sent)
    total_s, sent = order.run(deep, kept_s, second_s)
    deep_s = turned(sent)
    owned = [None, None, None]
    owned[a] = settle_core(order.run(finish, total_a, deep_a))
    owned[b] = settle_core(order.run(finish, total_b, deep_b))
    owned[c] = settle_core(order.run(finish, total_c, deep_c))
    small = settle_small(order.run(finish, total_s, deep_s), shapes)
    return (owned, small, low, filled)


def row_span(dilation, row, height):
    step = (row - 1) * dilation
    return (max(step, 0), max(-step, 0), height - abs(step))


def tap_matrix(pair, tap, place_ref, x_first):
    row, core = place_ref[2], place_ref[3]

    def half(ref):
        if x_first:
            return jnp.concatenate([ref[row, 0, 0, tap], ref[1 - row, 0, 0, tap]], axis=1)
        return jnp.concatenate([ref[0, row, 0, tap], ref[0, 1 - row, 0, tap]], axis=1)

    mine = half(pair[0])
    other = half(pair[1])
    lower = jnp.where(core == 0, mine, other)
    upper = jnp.where(core == 0, other, mine)
    return jnp.concatenate([lower, upper], axis=0)


def weight_specs(chunk, x_first):
    taps, rows, cols = chunk[0].shape[3:]
    shape = (2, 1, 1, taps, rows, cols) if x_first else (1, 2, 1, taps, rows, cols)

    def index_map(step, place_ref):
        flip = lax.rem(step + place_ref[1], 2)
        slot = lax.rem(place_ref[0] - step // 2 + ROUNDS, ROUNDS)
        return (0, flip, slot, 0, 0, 0) if x_first else (flip, 0, slot, 0, 0, 0)

    return [pl.BlockSpec(shape, index_map)] * 2


def cost(flops, arrays):
    return pl.CostEstimate(flops=1, bytes_accessed=1, transcendentals=0)


def coarse_flops(rows, shape, width):
    height, columns, channels = shape
    extents = sum(row_span(dilations[branch], line, height)[2] for branch, line in rows)
    return 2 * 3 * extents * columns * channels * width


def full_spec(array):
    return pl.BlockSpec(array.shape, lambda step, place_ref: (0,) * array.ndim)


def lane_spec(array):
    return pl.BlockSpec(
        (array.shape[0], array.shape[1] // (2 * ROUNDS)), lambda step, place_ref: (0, step)
    )


def store_moments(z_ref, mask_ref, stats_ref):
    mask = mask_ref[...]
    count = jnp.sum(mask)
    values = z_ref[...]
    mean = jnp.sum(values * mask, axis=0, keepdims=True) / count
    centered = (values - mean) * mask
    stats_ref[0:1, :] = mean
    stats_ref[1:2, :] = jnp.sum(centered * centered, axis=0, keepdims=True)


def behind_tie(kernel):
    def run(place_ref, tie_ref, *refs):
        kernel(place_ref, *refs)

    return run


def coarse_forward_kernel(plan, place_ref, *refs):
    refs = list(refs)
    mask_ref = refs.pop(0)
    center = refs.pop(0)
    outer = {branch: (refs.pop(0), refs.pop(0)) for branch in plan["branches"]}
    before = {branch: refs.pop(0) for branch in plan["begun"]}
    if plan["pool"]:
        member_ref = refs.pop(0)
        sizes_ref = refs.pop(0)
    pairs = {index: (refs.pop(0), refs.pop(0)) for index in plan["chunks"]}
    results = {branch: refs.pop(0) for branch in plan["branches"]}
    stats = {branch: refs.pop(0) for branch in plan["done"]}
    step = pl.program_id(0)

    @pl.when(step == 0)
    def _():
        for branch in plan["branches"]:
            if branch in before:
                results[branch][...] = before[branch][...]
            else:
                results[branch][...] = jnp.zeros_like(results[branch])

    columns = plan["columns"]
    for branch, row, chunk, tap in plan["rows"]:
        source, target, extent = row_span(dilations[branch], row, plan["height"])
        matrix = jnp.concatenate(
            [tap_matrix(pairs[chunk], tap + k, place_ref, chunk % 2 == 0) for k in range(3)],
            axis=0,
        )
        rows_in = pl.ds(source * columns, extent * columns)
        rows_out = pl.ds(target * columns, extent * columns)
        sides = (outer[branch][0], center, outer[branch][1])
        values = jnp.concatenate([side[rows_in, :] for side in sides], axis=1)
        results[branch][rows_out, :] += jnp.dot(
            values, matrix, preferred_element_type=jnp.float32
        )
    if plan["pool"]:
        point_ref, point_stats_ref, pool_ref, pooled_ref = refs

        @pl.when(step == 0)
        def _():
            point_ref[...] = jnp.zeros_like(point_ref)
            pool_ref[...] = jnp.zeros_like(pool_ref)

        values = center[...]
        x_first = POINT_CHUNK % 2 == 0
        pair = pairs[POINT_CHUNK]
        point_ref[...] += jnp.dot(
            values, tap_matrix(pair, 0, place_ref, x_first), preferred_element_type=jnp.float32
        )
        pooled = jnp.dot(member_ref[...], values, preferred_element_type=jnp.float32)
        pooled = (pooled * sizes_ref[...]).astype(jnp.bfloat16)
        pooled_ref[...] = pooled
        pool_ref[...] += jnp.dot(
            pooled, tap_matrix(pair, 1, place_ref, x_first), preferred_element_type=jnp.float32
        )

    @pl.when(step == 2 * ROUNDS - 1)
    def _():
        for branch in plan["done"]:
            store_moments(results[branch], mask_ref, stats[branch])
        if plan["pool"]:
            store_moments(point_ref, mask_ref, point_stats_ref)


def coarse_forward(part, mask, sides, chunks, shape, begun, pool=None):
    height, columns, channels = shape
    positions = height * columns
    rows = part_rows(part)
    branches = sorted({row[0] for row in rows})
    done = [branch for branch in branches if atrous_layout()[branch][-1][1] in PARTS[part]]
    plan = {
        "pool": pool is not None,
        "chunks": PARTS[part],
        "branches": branches,
        "begun": [branch for branch in branches if branch in begun],
        "done": done,
        "columns": columns,
        "height": height,
        "rows": rows,
    }
    center = sides[0][1]
    args = [mask, center]
    specs = [full_spec(mask), lane_spec(center)]
    for branch in branches:
        args += [sides[branch][0], sides[branch][2]]
        specs += [lane_spec(center)] * 2
    for branch in plan["begun"]:
        args.append(begun[branch])
        specs.append(full_spec(begun[branch]))
    if pool:
        args += list(pool)
        specs += [full_spec(item) for item in pool]
    for index in PARTS[part]:
        args += list(chunks[index])
        specs += weight_specs(chunks[index], index % 2 == 0)
    flat = jax.ShapeDtypeStruct((positions, channels), jnp.float32)
    small = jax.ShapeDtypeStruct((8, channels), jnp.float32)
    outs = [flat] * len(branches) + [small] * len(done)
    if pool:
        outs += [flat, small, small, jax.ShapeDtypeStruct((8, center.shape[1]), jnp.bfloat16)]
    out_specs = [full_spec(item) for item in outs]
    if pool:
        out_specs[-1] = lane_spec(outs[-1])
    results = pl.pallas_call(
        functools.partial(coarse_forward_kernel, plan),
        out_shape=outs,
        grid_spec=pltpu.PrefetchScalarGridSpec(
            num_scalar_prefetch=1, grid=(2 * ROUNDS,), in_specs=specs, out_specs=out_specs
        ),
        compiler_params=pltpu.CompilerParams(vmem_limit_bytes=VMEM_BYTES),
        cost_estimate=cost(
            coarse_flops([row[:2] for row in rows], shape, center.shape[1])
            + (2 * positions * channels * center.shape[1] if pool else 0),
            args + outs,
        ),
        name="coarse_forward",
    )(kernel_place(), *args)
    sums = dict(zip(branches, results))
    stats = dict(zip(done, results[len(branches) :]))
    return (sums, stats, results[len(branches) + len(done) :])


def coarse_weight_kernel(plan, place_ref, *refs):
    refs = list(refs)
    center = refs.pop(0)
    outer = {branch: (refs.pop(0), refs.pop(0)) for branch in plan["branches"]}
    grads = {branch: refs.pop(0) for branch in plan["branches"]}
    if plan["pool"]:
        point_ref, pooled_ref, pool_ref = refs.pop(0), refs.pop(0), refs.pop(0)
    outs = {index: (refs.pop(0), refs.pop(0)) for index in plan["chunks"]}
    row, core = place_ref[2], place_ref[3]
    rows, cols = outs[plan["chunks"][0]][0].shape[-2:]
    columns = plan["columns"]

    def store(chunk, tap, value):
        value = value.astype(jnp.bfloat16)
        lower, upper = value[:rows], value[rows:]
        mine = jnp.where(core == 0, lower, upper)
        other = jnp.where(core == 0, upper, lower)
        for ref, part in zip(outs[chunk], (mine, other)):
            for side, lane_part in ((row, part[:, :cols]), (1 - row, part[:, cols:])):
                if chunk % 2 == 0:
                    ref[0, side, 0, tap] = lane_part
                else:
                    ref[side, 0, 0, tap] = lane_part

    across = (((0,), (0,)), ((), ()))
    for branch, line, chunk, tap in plan["rows"]:
        source, target, extent = row_span(dilations[branch], line, plan["height"])
        sides = (outer[branch][0], center, outer[branch][1])
        values = jnp.concatenate(
            [side[pl.ds(source * columns, extent * columns), :] for side in sides], axis=1
        )
        result = lax.dot_general(
            values,
            grads[branch][pl.ds(target * columns, extent * columns), :],
            across,
            preferred_element_type=jnp.float32,
        )
        for k in range(3):
            store(chunk, tap + k, result[2 * rows * k : 2 * rows * (k + 1)])
    if plan["pool"]:
        for tap, left, right in ((0, center, point_ref), (1, pooled_ref, pool_ref)):
            store(
                POINT_CHUNK,
                tap,
                lax.dot_general(
                    left[...], right[...], across, preferred_element_type=jnp.float32
                ),
            )


def coarse_weight(part, sides, grads, shape, pool=None, tie=None):
    height, columns, channels = shape
    rows = part_rows(part)
    branches = sorted({row[0] for row in rows})
    plan = {
        "pool": pool is not None,
        "branches": branches,
        "chunks": PARTS[part],
        "rows": rows,
        "columns": columns,
        "height": height,
    }
    center = sides[0][1]
    args = [center]
    specs = [lane_spec(center)]
    for branch in branches:
        args += [sides[branch][0], sides[branch][2]]
        specs += [lane_spec(center)] * 2
    for branch in branches:
        args.append(grads[branch])
        specs.append(full_spec(grads[branch]))
    if pool:
        args += list(pool)
        specs += [full_spec(pool[0]), lane_spec(pool[1]), full_spec(pool[2])]
    kernel = functools.partial(coarse_weight_kernel, plan)
    if tie is not None:
        kernel = behind_tie(kernel)
        args.insert(0, tie)
        specs.insert(0, pl.BlockSpec(memory_space=pl.ANY))
    height_now = center.shape[1] // (4 * ROUNDS)
    outs = []
    out_specs = []
    for index in PARTS[part]:
        tail = (CHUNKS[index], height_now, channels // 2)
        block = (1, 2, 1) if index % 2 == 0 else (2, 1, 1)

        def index_map(step, place_ref, x_first=index % 2 == 0):
            flip = lax.rem(step + place_ref[1], 2)
            slot = lax.rem(step // 2 - place_ref[0] + ROUNDS, ROUNDS)
            return (flip, 0, slot, 0, 0, 0) if x_first else (0, flip, slot, 0, 0, 0)

        outs += [jax.ShapeDtypeStruct((2, 2, ROUNDS) + tail, jnp.bfloat16)] * 2
        out_specs += [pl.BlockSpec(block + tail, index_map)] * 2
    results = pl.pallas_call(
        kernel,
        out_shape=outs,
        grid_spec=pltpu.PrefetchScalarGridSpec(
            num_scalar_prefetch=1, grid=(2 * ROUNDS,), in_specs=specs, out_specs=out_specs
        ),
        compiler_params=pltpu.CompilerParams(vmem_limit_bytes=VMEM_BYTES),
        cost_estimate=cost(
            coarse_flops([row[:2] for row in rows], shape, center.shape[1])
            + (2 * height * columns * channels * center.shape[1] if pool else 0),
            args + outs,
        ),
        name="coarse_weight",
    )(kernel_place(), *args)
    return [(results[0], results[1]), (results[2], results[3])]


def coarse_input_kernel(plan, place_ref, *refs):
    refs = list(refs)
    point_ref, pool_ref, spread_ref = refs.pop(0), refs.pop(0), refs.pop(0)
    grads = [refs.pop(0) for _ in range(3)]
    pairs = [(refs.pop(0), refs.pop(0)) for _ in range(plan["chunks"])]
    out_ref, total_ref = refs
    columns = plan["columns"]
    turned = (((1,), (1,)), ((), ()))
    total_ref[...] = lax.dot_general(
        point_ref[...],
        tap_matrix(pairs[POINT_CHUNK], 0, place_ref, POINT_CHUNK % 2 == 0),
        turned,
        preferred_element_type=jnp.float32,
    )
    pooled = lax.dot_general(
        pool_ref[...],
        tap_matrix(pairs[POINT_CHUNK], 1, place_ref, POINT_CHUNK % 2 == 0),
        turned,
        preferred_element_type=jnp.float32,
    )
    total_ref[...] += jnp.dot(
        spread_ref[...], pooled, preferred_element_type=jnp.float32, precision=highest
    )
    for branch, rows in enumerate(plan["rows"]):
        for line, chunk, tap in rows:
            source, target, extent = row_span(dilations[branch], line, plan["height"])
            matrix = jnp.concatenate(
                [tap_matrix(pairs[chunk], tap + k, place_ref, chunk % 2 == 0) for k in range(3)],
                axis=1,
            )
            total_ref[pl.ds(source * columns, extent * columns), :] += lax.dot_general(
                grads[branch][pl.ds(target * columns, extent * columns), :],
                matrix,
                turned,
                preferred_element_type=jnp.float32,
            )
    out_ref[...] = total_ref[...].astype(jnp.bfloat16)


def coarse_input(point_dz, pool_dz, spread, grads, chunks, shape, width, tie=None):
    height, columns, channels = shape
    plan = {
        "chunks": len(chunks),
        "columns": columns,
        "height": height,
        "rows": atrous_layout(),
    }
    args = [point_dz, pool_dz, spread] + list(grads)
    specs = [full_spec(item) for item in args]
    for index, pair in enumerate(chunks):
        args += list(pair)
        specs += weight_specs(pair, index % 2 == 0)
    kernel = functools.partial(coarse_input_kernel, plan)
    if tie is not None:
        kernel = behind_tie(kernel)
        args.insert(0, tie)
        specs.insert(0, pl.BlockSpec(memory_space=pl.ANY))
    out = jax.ShapeDtypeStruct((height * columns, width), jnp.bfloat16)
    return pl.pallas_call(
        kernel,
        out_shape=out,
        grid_spec=pltpu.PrefetchScalarGridSpec(
            num_scalar_prefetch=1,
            grid=(2 * ROUNDS,),
            in_specs=specs,
            out_specs=lane_spec(out),
            scratch_shapes=[pltpu.VMEM((height * columns, width // (2 * ROUNDS)), jnp.float32)],
        ),
        compiler_params=pltpu.CompilerParams(vmem_limit_bytes=VMEM_BYTES),
        cost_estimate=cost(
            coarse_flops([(b, k) for b in range(3) for k in range(3)], shape, width)
            + 2 * height * columns * channels * width,
            args + [out],
        ),
        name="coarse_input",
    )(kernel_place(), *args)


STRIP = 8


def norm_vectors(mean, variance, gain, bias, *more):
    rows = [mean, lax.rsqrt(variance + epsilon), gain, bias] + list(more)
    rows += [jnp.zeros_like(mean)] * (8 - len(rows))
    return jnp.stack(rows)


def sigmoid(values):
    return 0.5 * jnp.tanh(0.5 * values) + 0.5


def vector(ref, index):
    return ref[index : index + 1, :]


def shaped_of(values, vector_ref):
    centered = (values - vector(vector_ref, 0)) * vector(vector_ref, 1)
    return (centered, centered * vector(vector_ref, 2) + vector(vector_ref, 3))


def slope_of(shaped, gate):
    return gate * (1.0 + shaped * (1.0 - gate))


def lag_specs(steps):
    def ahead(array, block):
        return pl.BlockSpec(block, lambda step: (jnp.minimum(step, steps - 1), 0))

    def behind(array, block):
        return pl.BlockSpec(block, lambda step: (jnp.maximum(step - 1, 0), 0))

    return (ahead, behind)


def whole(array):
    return pl.BlockSpec(array.shape, lambda step: (0,) * len(array.shape))


def window(ref, start, step, columns):
    return ref[pl.ds(pl.multiple_of((start + step) * columns, columns), STRIP * columns), :]


def run_moments(values, mask, stats_ref, step):
    count = jnp.sum(mask)
    mean = jnp.sum(values * mask, axis=0, keepdims=True) / count
    centered = (values - mean) * mask
    squares = jnp.sum(centered * centered, axis=0, keepdims=True)
    done = (step - 1).astype(jnp.float32)
    old_mean = jnp.where(step > 1, stats_ref[0:1, :], mean)
    old_squares = jnp.where(step > 1, stats_ref[1:2, :], 0.0)
    gap = mean - old_mean
    stats_ref[0:1, :] = old_mean + gap / (done + 1.0)
    stats_ref[1:2, :] = old_squares + squares + gap * gap * (count * done / (done + 1.0))


def spread_columns(products, masks_ref):
    size = products.shape[0]
    width = products.shape[1] // 3
    result = products[:, width : 2 * width]
    result = result + masks_ref[:, 1:2] * pltpu.roll(products[:, :width], 1, 0)
    return result + masks_ref[:, 2:3] * pltpu.roll(products[:, 2 * width :], size - 1, 0)


def clear_edges(ref, columns):
    ref[:columns, :] = jnp.zeros((columns, ref.shape[1]), ref.dtype)
    ref[ref.shape[0] - columns :, :] = jnp.zeros((columns, ref.shape[1]), ref.dtype)


def row_taps(w_ref, row, start, stop):
    return jnp.concatenate([w_ref[3 * row + k, start:stop, :] for k in range(3)], axis=1)


def low_lanes(width):
    return lax.broadcasted_iota(jnp.int32, (1, width), 1)


def decode_forward_kernel(
    steps, act_ref, table_ref, low_ref, wide_ref, vector_ref, masks_ref, w_ref, z_ref, stats_ref,
    up_ref, joined_ref, reduced_ref
):
    step = pl.program_id(0)
    columns = table_ref.shape[0]
    channels = act_ref.shape[2]
    rows = act_ref.shape[0]

    @pl.when(step == 0)
    def _():
        clear_edges(joined_ref, columns)
        clear_edges(reduced_ref, columns)

    @pl.when(step < steps)
    def _():
        for offset in range(STRIP):
            base = step * (STRIP // 4) + offset // 4 + (offset % 4 - 2) // 2
            fraction = ((2 * (offset % 4) - 3) % 8) / 8.0
            lower = act_ref[jnp.maximum(base, 0)]
            upper = act_ref[jnp.minimum(base + 1, rows - 1)]
            mixed = (1.0 - fraction) * lower + fraction * upper
            coarse = mixed.astype(jnp.bfloat16)
            fine = (mixed - coarse.astype(jnp.float32)).astype(jnp.bfloat16)
            value = jnp.dot(
                table_ref[...],
                jnp.concatenate([coarse, fine], axis=0),
                preferred_element_type=jnp.float32,
            ).astype(jnp.bfloat16)
            up_ref[offset * columns : (offset + 1) * columns, :] = value
            start = pl.multiple_of((step * STRIP + offset + 1) * columns, columns)
            joined_ref[pl.ds(start, columns), :] = value
        reduced = jnp.dot(low_ref[...], wide_ref[...], preferred_element_type=jnp.float32)
        _, shaped = shaped_of(reduced, vector_ref)
        value = masks_ref[:, 0:1] * (shaped * sigmoid(shaped))
        start = pl.multiple_of((step * STRIP + 1) * columns, columns)
        reduced_ref[pl.ds(start, STRIP * columns), :] = value.astype(jnp.bfloat16)

    @pl.when(step > 0)
    def _():
        start = (step - 1) * STRIP
        lane = low_lanes(reduced_ref.shape[1])
        lows = [window(reduced_ref, start, k, columns) for k in range(3)]
        low = jnp.where(lane < 64, lows[0], jnp.where(lane < 128, lows[1], lows[2]))
        values = jnp.concatenate(
            [window(joined_ref, start, k, columns) for k in range(3)] + [low], axis=1
        )
        extra = w_ref.shape[1] - channels
        parts = [row_taps(w_ref, k, 0, channels) for k in range(3)]
        for k in range(3):
            parts.append(row_taps(w_ref, k, channels, channels + extra))
            parts.append(jnp.zeros((64 - extra, 3 * channels), jnp.bfloat16))
        parts.append(jnp.zeros((64, 3 * channels), jnp.bfloat16))
        products = jnp.dot(
            values, jnp.concatenate(parts, axis=0), preferred_element_type=jnp.float32
        )
        result = spread_columns(products, masks_ref)
        z_ref[...] = result
        run_moments(result, masks_ref[:, 0:1], stats_ref, step)


def decode_forward(act, table, low, wide, vectors, masks, weights):
    positions = low.shape[0]
    columns = table.shape[0]
    block = STRIP * columns
    steps = positions // block
    channels = act.shape[2]
    ahead, behind = lag_specs(steps)
    flat = jax.ShapeDtypeStruct((positions, channels), jnp.float32)
    stats = jax.ShapeDtypeStruct((8, channels), jnp.float32)
    up = jax.ShapeDtypeStruct((positions, channels), jnp.bfloat16)
    return pl.pallas_call(
        functools.partial(decode_forward_kernel, steps),
        out_shape=[flat, stats, up],
        grid=(steps + 1,),
        in_specs=[
            whole(act),
            whole(table),
            ahead(low, (block, low.shape[1])),
            whole(wide),
            whole(vectors),
            whole(masks),
            whole(weights),
        ],
        out_specs=[
            behind(flat, (block, channels)),
            whole(stats),
            ahead(up, (block, channels)),
        ],
        scratch_shapes=[
            pltpu.VMEM((positions + 2 * columns, channels), jnp.bfloat16),
            pltpu.VMEM((positions + 2 * columns, wide.shape[1]), jnp.bfloat16),
        ],
        compiler_params=pltpu.CompilerParams(vmem_limit_bytes=VMEM_BYTES),
        cost_estimate=cost(2 * positions * 3 * channels * 4 * channels, [low, flat, up]),
        name="decode_forward",
    )(act, table, low, wide, vectors, masks, weights)


def refine_forward_kernel(
    steps, columns, z_in_ref, vector_ref, masks_ref, w_ref, z_ref, stats_ref, act_ref
):
    step = pl.program_id(0)
    channels = w_ref.shape[1]

    @pl.when(step == 0)
    def _():
        clear_edges(act_ref, columns)

    @pl.when(step < steps)
    def _():
        _, shaped = shaped_of(z_in_ref[...], vector_ref)
        value = masks_ref[:, 0:1] * (shaped * sigmoid(shaped))
        start = pl.multiple_of((step * STRIP + 1) * columns, columns)
        act_ref[pl.ds(start, STRIP * columns), :] = value.astype(jnp.bfloat16)

    @pl.when(step > 0)
    def _():
        start = (step - 1) * STRIP
        values = jnp.concatenate([window(act_ref, start, k, columns) for k in range(3)], axis=1)
        matrix = jnp.concatenate([row_taps(w_ref, k, 0, channels) for k in range(3)], axis=0)
        products = jnp.dot(values, matrix, preferred_element_type=jnp.float32)
        result = spread_columns(products, masks_ref)
        z_ref[...] = result
        run_moments(result, masks_ref[:, 0:1], stats_ref, step)


def refine_forward(z_in, vectors, masks, weights):
    positions, channels = z_in.shape
    block = masks.shape[0]
    columns = block // STRIP
    steps = positions // block
    ahead, behind = lag_specs(steps)
    flat = jax.ShapeDtypeStruct((positions, channels), jnp.float32)
    stats = jax.ShapeDtypeStruct((8, channels), jnp.float32)
    return pl.pallas_call(
        functools.partial(refine_forward_kernel, steps, columns),
        out_shape=[flat, stats],
        grid=(steps + 1,),
        in_specs=[ahead(z_in, (block, channels)), whole(vectors), whole(masks), whole(weights)],
        out_specs=[behind(flat, (block, channels)), whole(stats)],
        scratch_shapes=[pltpu.VMEM((positions + 2 * columns, channels), jnp.bfloat16)],
        compiler_params=pltpu.CompilerParams(vmem_limit_bytes=VMEM_BYTES),
        cost_estimate=cost(2 * positions * 9 * channels * channels, [z_in, flat]),
        name="refine_forward",
    )(z_in, vectors, masks, weights)


def class_kernel(
    z_ref, grad_ref, vector_ref, masks_ref, w_ref, b_ref, logits_ref, sums_ref, weight_ref, bias_ref
):
    step = pl.program_id(0)

    @pl.when(step == 0)
    def _():
        sums_ref[...] = jnp.zeros_like(sums_ref)
        weight_ref[...] = jnp.zeros_like(weight_ref)
        bias_ref[...] = jnp.zeros_like(bias_ref)

    mask = masks_ref[:, 0:1]
    centered, shaped = shaped_of(z_ref[...], vector_ref)
    gate = sigmoid(shaped)
    act = (mask * (shaped * gate)).astype(jnp.bfloat16)
    logits = jnp.dot(act, w_ref[...], preferred_element_type=jnp.float32) + b_ref[...]
    logits_ref[...] = (mask * logits).astype(jnp.bfloat16)
    grad = (mask * grad_ref[...].astype(jnp.float32)).astype(jnp.bfloat16)
    upstream = lax.dot_general(
        grad, w_ref[...], (((1,), (1,)), ((), ())), preferred_element_type=jnp.float32
    )
    local = mask * upstream * slope_of(shaped, gate)
    sums_ref[0:1, :] += jnp.sum(local * centered, axis=0, keepdims=True)
    sums_ref[1:2, :] += jnp.sum(local, axis=0, keepdims=True)
    weight_ref[...] += lax.dot_general(
        grad, act, (((0,), (0,)), ((), ())), preferred_element_type=jnp.float32
    )
    bias_ref[...] += jnp.sum(grad.astype(jnp.float32), axis=0, keepdims=True)


def classify(z, grad, vectors, masks, weights, bias):
    positions, channels = z.shape
    block = masks.shape[0]
    classes = grad.shape[1]
    outs = [
        jax.ShapeDtypeStruct((positions, classes), jnp.bfloat16),
        jax.ShapeDtypeStruct((8, channels), jnp.float32),
        jax.ShapeDtypeStruct((classes, channels), jnp.float32),
        jax.ShapeDtypeStruct((1, classes), jnp.float32),
    ]

    def strip(width):
        return pl.BlockSpec((block, width), lambda step: (step, 0))

    return pl.pallas_call(
        class_kernel,
        out_shape=outs,
        grid=(positions // block,),
        in_specs=[
            strip(channels),
            strip(classes),
            whole(vectors),
            whole(masks),
            whole(weights),
            whole(bias),
        ],
        out_specs=[strip(classes)] + [whole(item) for item in outs[1:]],
        compiler_params=pltpu.CompilerParams(vmem_limit_bytes=VMEM_BYTES),
        cost_estimate=cost(6 * positions * channels * 128, [z, grad, grad]),
        name="classify",
    )(z, grad, vectors, masks, weights, bias)


def finish_grad(local, centered, mask, vector_ref):
    inner = local - vector(vector_ref, 5) - centered * vector(vector_ref, 4)
    return mask * vector(vector_ref, 2) * vector(vector_ref, 1) * inner


def store_sides(grad, masks_ref, side_ref, start):
    size, width = grad.shape
    grad = grad.astype(jnp.bfloat16).astype(jnp.float32)
    rows = pl.ds(start, size)
    side_ref[rows, :width] = pltpu.roll(masks_ref[:, 1:2] * grad, size - 1, 0).astype(jnp.bfloat16)
    side_ref[rows, width : 2 * width] = grad.astype(jnp.bfloat16)
    side_ref[rows, 2 * width :] = pltpu.roll(masks_ref[:, 2:3] * grad, 1, 0).astype(jnp.bfloat16)


def refine_backward_kernel(
    steps, columns, z_ref, grad_ref, vector_ref, cls_ref, z_in_ref, vector_in_ref, masks_ref, w_ref,
    local_ref, sums_ref, weight_ref, side_ref
):
    step = pl.program_id(0)
    channels = w_ref.shape[1]
    mask = masks_ref[:, 0:1]

    @pl.when(step == 0)
    def _():
        clear_edges(side_ref, columns)
        sums_ref[...] = jnp.zeros_like(sums_ref)
        weight_ref[...] = jnp.zeros_like(weight_ref)

    @pl.when(step < steps)
    def _():
        centered, shaped = shaped_of(z_ref[...], vector_ref)
        grad = (mask * grad_ref[...].astype(jnp.float32)).astype(jnp.bfloat16)
        upstream = lax.dot_general(
            grad, cls_ref[...], (((1,), (1,)), ((), ())), preferred_element_type=jnp.float32
        )
        local = mask * upstream * slope_of(shaped, sigmoid(shaped))
        start = pl.multiple_of((step * STRIP + 1) * columns, columns)
        store_sides(finish_grad(local, centered, mask, vector_ref), masks_ref, side_ref, start)

    @pl.when(step > 0)
    def _():
        start = (step - 1) * STRIP
        centered, shaped = shaped_of(z_in_ref[...], vector_in_ref)
        gate = sigmoid(shaped)
        act = (mask * (shaped * gate)).astype(jnp.bfloat16)
        sides = [window(side_ref, start, 2 - k, columns) for k in range(3)]
        upstream = lax.dot_general(
            jnp.concatenate(sides, axis=1),
            jnp.concatenate([w_ref[tap] for tap in range(9)], axis=1),
            (((1,), (1,)), ((), ())),
            preferred_element_type=jnp.float32,
        )
        local = mask * upstream * slope_of(shaped, gate)
        local_ref[...] = local
        sums_ref[0:1, :] += jnp.sum(local * centered, axis=0, keepdims=True)
        sums_ref[1:2, :] += jnp.sum(local, axis=0, keepdims=True)
        turned = act.T
        for k in range(3):
            weight_ref[k] += jnp.dot(turned, sides[k], preferred_element_type=jnp.float32)


def refine_backward(z, grad, vectors, classes, z_in, vectors_in, masks, weights):
    positions, channels = z.shape
    block = masks.shape[0]
    columns = block // STRIP
    steps = positions // block
    ahead, behind = lag_specs(steps)
    outs = [
        jax.ShapeDtypeStruct((positions, channels), jnp.float32),
        jax.ShapeDtypeStruct((8, channels), jnp.float32),
        jax.ShapeDtypeStruct((3, channels, 3 * channels), jnp.float32),
    ]
    return pl.pallas_call(
        functools.partial(refine_backward_kernel, steps, columns),
        out_shape=outs,
        grid=(steps + 1,),
        in_specs=[
            ahead(z, (block, channels)),
            ahead(grad, (block, grad.shape[1])),
            whole(vectors),
            whole(classes),
            behind(z_in, (block, channels)),
            whole(vectors_in),
            whole(masks),
            whole(weights),
        ],
        out_specs=[behind(z, (block, channels)), whole(outs[1]), whole(outs[2])],
        scratch_shapes=[pltpu.VMEM((positions + 2 * columns, 3 * channels), jnp.bfloat16)],
        compiler_params=pltpu.CompilerParams(vmem_limit_bytes=VMEM_BYTES),
        cost_estimate=cost(4 * positions * 9 * channels * channels, [z, z_in, grad, outs[0], weights]),
        name="refine_backward",
    )(z, grad, vectors, classes, z_in, vectors_in, masks, weights)


def decode_backward_kernel(
    steps, columns, local_ref, z_ref, vector_ref, up_ref, low_ref, wide_ref, low_vector_ref,
    table_ref, masks_ref, w_ref, coarse_ref, low_local_ref, sums_ref, weight_ref, low_weight_ref,
    side_ref, total_ref
):
    step = pl.program_id(0)
    channels = w_ref.shape[2]
    extra = w_ref.shape[1] - channels
    mask = masks_ref[:, 0:1]

    @pl.when(step == 0)
    def _():
        clear_edges(side_ref, columns)
        sums_ref[...] = jnp.zeros_like(sums_ref)
        weight_ref[...] = jnp.zeros_like(weight_ref)
        low_weight_ref[...] = jnp.zeros_like(low_weight_ref)
        total_ref[...] = jnp.zeros_like(total_ref)

    @pl.when(step < steps)
    def _():
        centered, _ = shaped_of(z_ref[...], vector_ref)
        start = pl.multiple_of((step * STRIP + 1) * columns, columns)
        grad = finish_grad(local_ref[...], centered, mask, vector_ref)
        store_sides(grad, masks_ref, side_ref, start)

    @pl.when(step > 0)
    def _():
        start = (step - 1) * STRIP
        sides = [window(side_ref, start, 2 - k, columns) for k in range(3)]
        pieces = []
        for tap in range(9):
            pieces.append(
                jnp.concatenate(
                    [w_ref[tap], jnp.zeros((64 - extra, channels), jnp.bfloat16)], axis=0
                )
            )
        upstream = lax.dot_general(
            jnp.concatenate(sides, axis=1),
            jnp.concatenate(pieces, axis=1),
            (((1,), (1,)), ((), ())),
            preferred_element_type=jnp.float32,
        )
        for offset in range(STRIP):
            base = (step - 1) * (STRIP // 4) + offset // 4 + (offset % 4 - 2) // 2
            fraction = ((2 * (offset % 4) - 3) % 8) / 8.0
            value = upstream[offset * columns : (offset + 1) * columns, :channels]
            value = value.astype(jnp.bfloat16).astype(jnp.float32)
            total_ref[base + 1] += (1.0 - fraction) * value
            total_ref[base + 2] += fraction * value
        reduced = jnp.dot(low_ref[...], wide_ref[...], preferred_element_type=jnp.float32)
        centered, shaped = shaped_of(reduced, low_vector_ref)
        gate = sigmoid(shaped)
        low_act = (mask * (shaped * gate)).astype(jnp.bfloat16)
        low_up = upstream[:, channels:]
        local = mask * low_up * slope_of(shaped, gate)[:, :64]
        low_local_ref[...] = local
        sums_ref[0:1, :64] += jnp.sum(local * centered[:, :64], axis=0, keepdims=True)
        sums_ref[1:2, :64] += jnp.sum(local, axis=0, keepdims=True)
        turned = up_ref[...].T
        low_turned = low_act[:, :128].T[:64]
        for k in range(3):
            weight_ref[k] += jnp.dot(turned, sides[k], preferred_element_type=jnp.float32)
            low_weight_ref[k] += jnp.dot(low_turned, sides[k], preferred_element_type=jnp.float32)

    @pl.when(step == steps)
    def _():
        rows = coarse_ref.shape[0]
        total_ref[1] += total_ref[0]
        total_ref[rows] += total_ref[rows + 1]
        for row in range(rows):
            value = total_ref[row + 1]
            upper = value.astype(jnp.bfloat16)
            lower = (value - upper.astype(jnp.float32)).astype(jnp.bfloat16)
            coarse_ref[row] = jnp.dot(
                table_ref[...],
                jnp.concatenate([upper, lower], axis=0),
                preferred_element_type=jnp.float32,
            )


def decode_backward(local, z, vectors, up, low, wide, low_vectors, table, masks, weights, shape):
    positions, channels = z.shape
    block = masks.shape[0]
    columns = block // STRIP
    steps = positions // block
    height, coarse_columns, _ = shape
    ahead, behind = lag_specs(steps)
    outs = [
        jax.ShapeDtypeStruct((height, coarse_columns, channels), jnp.float32),
        jax.ShapeDtypeStruct((positions, 64), jnp.float32),
        jax.ShapeDtypeStruct((8, channels), jnp.float32),
        jax.ShapeDtypeStruct((3, channels, 3 * channels), jnp.float32),
        jax.ShapeDtypeStruct((3, 64, 3 * channels), jnp.float32),
    ]
    return pl.pallas_call(
        functools.partial(decode_backward_kernel, steps, columns),
        out_shape=outs,
        grid=(steps + 1,),
        in_specs=[
            ahead(local, (block, channels)),
            ahead(z, (block, channels)),
            whole(vectors),
            behind(up, (block, channels)),
            behind(low, (block, low.shape[1])),
            whole(wide),
            whole(low_vectors),
            whole(table),
            whole(masks),
            whole(weights),
        ],
        out_specs=[whole(outs[0]), behind(outs[1], (block, 64))]
        + [whole(item) for item in outs[2:]],
        scratch_shapes=[
            pltpu.VMEM((positions + 2 * columns, 3 * channels), jnp.bfloat16),
            pltpu.VMEM((height + 2, columns, channels), jnp.float32),
        ],
        compiler_params=pltpu.CompilerParams(vmem_limit_bytes=VMEM_BYTES),
        cost_estimate=cost(4 * positions * 9 * channels * (channels + 64), [local, z, up, low, outs[1], weights]),
        name="decode_backward",
    )(local, z, vectors, up, low, wide, low_vectors, table, masks, weights)


def low_backward_kernel(
    vector_ref, local_ref, low_ref, wide_ref, masks_ref, out_ref, weight_ref
):
    @pl.when(pl.program_id(0) == 0)
    def _():
        weight_ref[...] = jnp.zeros_like(weight_ref)

    low = low_ref[...]
    weights = wide_ref[:, :128]
    reduced = jnp.dot(low, weights, preferred_element_type=jnp.float32)
    mean, scale, gain = (vector_ref[k : k + 1, :64] for k in range(3))
    centered = (reduced[:, :64] - mean) * scale
    inner = local_ref[...] - vector_ref[5:6, :64] - centered * vector_ref[4:5, :64]
    grad = (masks_ref[:, 0:1] * gain * scale * inner).astype(jnp.bfloat16)
    out_ref[...] = lax.dot_general(
        grad, weights[:, :64], (((1,), (1,)), ((), ())), preferred_element_type=jnp.float32
    ).astype(jnp.bfloat16)
    weight_ref[...] += lax.dot_general(
        grad, low, (((0,), (0,)), ((), ())), preferred_element_type=jnp.float32
    )


def low_backward(local, low, wide, vectors, masks, tie):
    positions, width = low.shape
    block = masks.shape[0]
    outs = [
        jax.ShapeDtypeStruct((positions, width), jnp.bfloat16),
        jax.ShapeDtypeStruct((64, width), jnp.float32),
    ]
    return pl.pallas_call(
        behind_tie(low_backward_kernel),
        out_shape=outs,
        grid=(positions // block,),
        in_specs=[
            whole(vectors),
            pl.BlockSpec(memory_space=pl.ANY),
            pl.BlockSpec((block, 64), lambda step: (step, 0)),
            pl.BlockSpec((block, width), lambda step: (step, 0)),
            whole(wide),
            whole(masks),
        ],
        out_specs=[pl.BlockSpec((block, width), lambda step: (step, 0)), whole(outs[1])],
        compiler_params=pltpu.CompilerParams(vmem_limit_bytes=VMEM_BYTES),
        cost_estimate=cost(6 * positions * width * 128, [local, low, low]),
        name="low_backward",
    )(vectors, tie, local, low, wide, masks)


def atrous_layout():
    places = []
    for chunk, size in enumerate(CHUNKS):
        places += [(chunk, tap) for tap in range(2 if chunk == POINT_CHUNK else 0, size)]
    return [
        [(line,) + places[9 * branch + 3 * line] for line in range(3)] for branch in range(3)
    ]


def part_rows(part):
    return [
        (branch, line, chunk, tap)
        for branch, rows in enumerate(atrous_layout())
        for line, chunk, tap in rows
        if chunk in PARTS[part]
    ]


def order_taps(point, atrous):
    flat = atrous.reshape((-1,) + atrous.shape[2:])
    before = sum(CHUNKS[:POINT_CHUNK])
    flat = jnp.concatenate([flat[:before], point, flat[before:]])
    parts = []
    start = 0
    for part in PARTS:
        size = sum(CHUNKS[index] for index in part)
        parts.append(flat[start : start + size])
        start += size
    return parts


def restore_taps(parts, shape):
    flat = jnp.concatenate(parts)
    before = sum(CHUNKS[:POINT_CHUNK])
    atrous = jnp.concatenate([flat[:before], flat[before + 2 :]])
    return (flat[before : before + 2], atrous.reshape(shape))


def side_values(values, image_ids, dilation):
    result = []
    for step in (-dilation, dilation):
        mask = tap_mask(image_ids, values.shape[1], 0, step).astype(values.dtype)
        result.append(mask * shifted(values, 0, step))
    return [result[0], values, result[1]]


def side_grads(values, image_ids, dilation):
    result = []
    for step in (-dilation, 0, dilation):
        masked = tap_mask(image_ids, values.shape[1], 0, step).astype(values.dtype) * values
        result.append(shifted(masked, 0, -step))
    return jnp.concatenate(result, axis=-1)


def settle_core(values):
    core = place()[3]
    taps, rows, cols = values.shape
    parts = values.reshape(taps, rows, 2, cols // 2)
    kept = lax.dynamic_index_in_dim(parts, core, 2, keepdims=False)
    given = lax.dynamic_index_in_dim(parts, 1 - core, 2, keepdims=False).astype(jnp.bfloat16)
    got = exchange(given, "narrow", 1).astype(jnp.float32)
    lower = jnp.where(core == 0, kept, got)
    upper = jnp.where(core == 0, got, kept)
    return jnp.concatenate([lower, upper], axis=1)


def band_ids(widths, columns):
    ends_all = jnp.cumsum(widths, axis=1)
    position = jnp.arange(columns, dtype=jnp.int32)
    band_index = jnp.sum(
        (position[None, :, None] >= ends_all[:, None, :]).astype(jnp.int32), axis=2
    )
    return jnp.where(band_index < widths.shape[1] - 1, band_index, -1)


def shifted(values, row_shift, col_shift):
    height = values.shape[1]
    columns = values.shape[2]
    padded = jnp.pad(
        values, ((0, 0), (abs(row_shift), abs(row_shift)), (abs(col_shift), abs(col_shift)), (0, 0))
    )
    row_start = abs(row_shift) + row_shift
    col_start = abs(col_shift) + col_shift
    return padded[:, row_start : row_start + height, col_start : col_start + columns, :]


def tap_mask(image_ids, height, row_shift, col_shift):
    columns = image_ids.shape[1]
    padded = jnp.pad(image_ids, ((0, 0), (abs(col_shift), abs(col_shift))), constant_values=-2)
    col_start = abs(col_shift) + col_shift
    other_ids = padded[:, col_start : col_start + columns]
    same_image = (other_ids == image_ids).astype(jnp.float32)
    row_place = jnp.arange(height) + row_shift
    inside = ((row_place >= 0) & (row_place < height)).astype(jnp.float32)
    return (inside[None, :, None] * same_image[:, None, :])[..., None]


def tap_offsets(dilation):
    return [
        ((tap_index // 3 - 1) * dilation, (tap_index % 3 - 1) * dilation) for tap_index in range(9)
    ]


def linear_weights(out_count, in_count):
    position = jnp.arange(out_count, dtype=jnp.int32)
    scaled = 2 * position - 3
    left_index = jnp.floor_divide(scaled, 8)
    fraction = (scaled - 8 * left_index).astype(jnp.float32) / 8.0
    lower_index = jnp.clip(left_index, 0, in_count - 1)
    upper_index = jnp.clip(left_index + 1, 0, in_count - 1)
    return (position, lower_index, upper_index, fraction)


def column_table(image_ids):
    columns = image_ids.shape[1]
    position, lower_index, upper_index, fraction = linear_weights(4 * columns, columns)
    source = jnp.arange(columns, dtype=jnp.int32)[None, :]

    def picker(index_row):
        return (source == index_row[:, None]).astype(jnp.int32)

    def lookup(index_row):
        return jnp.sum(image_ids[:, None, :] * picker(index_row)[None], axis=2)

    own_index = position // 4
    own_id = lookup(own_index)
    weight_lower = (1.0 - fraction)[None, :] * (lookup(lower_index) == own_id).astype(jnp.float32)
    weight_upper = fraction[None, :] * (lookup(upper_index) == own_id).astype(jnp.float32)
    weight_own = 1.0 - weight_lower - weight_upper
    table = weight_lower[:, :, None] * picker(lower_index)[None].astype(jnp.float32)
    table = table + weight_upper[:, :, None] * picker(upper_index)[None].astype(jnp.float32)
    table = table + weight_own[:, :, None] * picker(own_index)[None].astype(jnp.float32)
    return table


def normalize(values, valid_map, mean_row, variance, gain_row, bias_row):
    norm_scale = lax.rsqrt(variance + epsilon)
    centered = (values - mean_row) * norm_scale
    shaped = centered * gain_row + bias_row
    return (valid_map * jax.nn.silu(shaped), centered, shaped, norm_scale)


def norm_grad_terms(upstream, valid_map, centered, shaped):
    sigmoid_value = jax.nn.sigmoid(shaped)
    local_term = valid_map * upstream * sigmoid_value * (1.0 + shaped * (1.0 - sigmoid_value))
    axes = tuple(range(local_term.ndim - 1))
    return (local_term, jnp.sum(local_term * centered, axis=axes), jnp.sum(local_term, axis=axes))


def norm_grad_finish(
    local_term, valid_map, centered, norm_scale, gain_row, gain_sum, bias_sum, count_all
):
    inner = local_term - bias_sum / count_all - centered * gain_sum / count_all
    return (valid_map * gain_row * norm_scale * inner).astype(jnp.bfloat16)


def moments(values, valid_map, local_count, count_all):
    counts, means, squares = merge_all(*local_moments(values, valid_map, local_count))
    return (means, squares / count_all)


def merged(stats, local_count, count_all):
    counts = jnp.full((stats.shape[1],), 1.0) * local_count
    counts, means, squares = merge_all(counts, stats[0], stats[1])
    return (means, squares / count_all)


def pack_pairs(pairs):
    return jnp.concatenate(
        [pair_item[0] for pair_item in pairs] + [pair_item[1] for pair_item in pairs]
    )


def unpack_pairs(flat, pairs):
    lengths = [pair_item[0].shape[0] for pair_item in pairs]
    half_point = sum(lengths)
    result_pairs = []
    offset = 0
    for length_now in lengths:
        result_pairs.append(
            (
                flat[offset : offset + length_now],
                flat[half_point + offset : half_point + offset + length_now],
            )
        )
        offset = offset + length_now
    return result_pairs


def gradient_sums(pairs):
    return unpack_pairs(sum_all(pack_pairs(pairs)), pairs)


def small_block(items):
    proj, reduce, decode, refine = items
    taps, rows, cols = refine.shape
    count = proj.shape[0] // rows
    proj = proj.reshape(2, count, rows // 2, cols).swapaxes(0, 1).reshape(count, rows, cols)
    reduce = jnp.pad(reduce, ((0, 0), (0, cols - reduce.shape[1])))[None]
    shared = share_core(jnp.concatenate([refine, proj, reduce]))
    lanes = shared.shape[2]
    decode = decode.swapaxes(1, 2)
    decode = jnp.pad(decode, ((0, 0), (0, 0), (0, lanes - decode.shape[2])))
    return jnp.concatenate([shared, decode.reshape(-1, shared.shape[1], lanes)])


def settle_small(owned, shapes):
    shape_p, shape_r, shape_d, shape_f = shapes
    taps, rows, cols = shape_f
    count = shape_p[0] // rows
    first = taps + count + 1
    settled = settle_core(owned[:first])
    proj = settled[taps : taps + count].reshape(count, 2, rows // 2, cols)
    proj = proj.swapaxes(0, 1).reshape(shape_p)
    reduce = settled[taps + count, :, : shape_r[1]]
    decode = owned[first:].reshape(taps, shape_d[2], -1)[:, :, : shape_d[1]].swapaxes(1, 2)
    return (proj, reduce, decode, settled[:taps])


def reduce_lanes(width, row, core, half):
    start = (2 * row + core) * width
    return start, core * half


def unpack_kernel(shapes, place_ref, own_ref, other_ref, proj_ref, wide_ref, decode_ref, refine_ref):
    deep, side, row, core = (place_ref[index] for index in range(4))
    shape_p, shape_r, shape_d, shape_f = shapes
    taps = shape_f[0]
    rows = shape_f[1] // 2
    count = shape_p[0] // (2 * rows)
    lanes = own_ref.shape[-1]

    def load(ref, z, x, y, start, size):
        slot = lax.rem(deep - z + ROUNDS, ROUNDS)
        return ref[slot, lax.rem(y + row, 2), lax.rem(x + side, 2), start : start + size]

    def both(z, x, y, start, size):
        mine = load(own_ref, z, x, y, start, size)
        others = load(other_ref, z, x, y, start, size)
        return (jnp.where(core == 0, mine, others), jnp.where(core == 0, others, mine))

    lane = lax.broadcasted_iota(jnp.int32, (1, lanes), 1)
    for z in range(ROUNDS):
        for x in range(2):
            wide = 2 * z + x
            halves = [both(z, x, y, 0, taps + count + 1) for y in range(2)]
            for h in range(2):
                joined = jnp.concatenate([halves[0][h], halves[1][h]], axis=-1)
                base = (2 * wide + h) * rows
                refine_ref[:, base : base + rows, :] = joined[:taps]
                base = (2 * wide + h) * rows * count
                proj_ref[base : base + rows * count, :] = joined[taps : taps + count].reshape(
                    rows * count, 2 * lanes
                )
                total = jnp.zeros((rows, lanes), jnp.float32)
                for y in range(2):
                    value = halves[y][h][taps + count].astype(jnp.float32)
                    for c in range(2):
                        start, held = reduce_lanes(shape_r[1], y, c, lanes // 2)
                        moved = pltpu.roll(value, (start - held) % lanes, 1)
                        inside = (lane >= start) & (lane < start + shape_r[1])
                        total = total + jnp.where(inside, moved, 0.0)
                base = (2 * wide + h) * rows
                left = total + pltpu.roll(total, 64, 1)
                wide_ref[base : base + rows, :] = jnp.concatenate([left, total], axis=1).astype(
                    jnp.bfloat16
                )
    height, width = shape_d[1], shape_d[2]
    blocks = width // rows
    for tap in range(taps):
        start = taps + count + 1 + tap * blocks
        pieces = []
        for y in range(2):
            columns = ([], [])
            for z in range(ROUNDS):
                for x in range(2):
                    for c, value in enumerate(both(z, x, y, start, blocks)):
                        columns[c].append(value.reshape(width, lanes))
            for c in range(2):
                joined = jnp.concatenate(columns[c], axis=0).astype(jnp.float32)
                pieces.append(joined.T[:height])
        decode_ref[tap] = jnp.concatenate(pieces, axis=0).astype(jnp.bfloat16)


def unpack_block(own, other, shapes):
    wide = 2 * ROUNDS
    shape_p, shape_r, shape_d, shape_f = shapes
    outs = [
        jax.ShapeDtypeStruct((wide * shape_p[0], 4 * shape_p[1]), jnp.bfloat16),
        jax.ShapeDtypeStruct((wide * shape_r[0], 256), jnp.bfloat16),
        jax.ShapeDtypeStruct((shape_d[0], 4 * shape_d[1], wide * shape_d[2]), jnp.bfloat16),
        jax.ShapeDtypeStruct((shape_f[0], wide * shape_f[1], 4 * shape_f[2]), jnp.bfloat16),
    ]
    return pl.pallas_call(
        functools.partial(unpack_kernel, shapes),
        out_shape=outs,
        in_specs=[pl.BlockSpec(memory_space=pltpu.SMEM)]
        + [pl.BlockSpec(memory_space=pltpu.VMEM)] * 2,
        out_specs=[pl.BlockSpec(memory_space=pltpu.VMEM)] * 4,
        compiler_params=pltpu.CompilerParams(vmem_limit_bytes=VMEM_BYTES),
        cost_estimate=cost(0, [own, other] + outs + outs),
        name="unpack_weights",
    )(kernel_place(), own, other)


def pack_kernel(
    shapes, place_ref, proj_ref, reduce_ref, decode_ref, low_ref, refine_ref, keep_ref, give_ref
):
    deep, side, row, core = (place_ref[index] for index in range(4))
    shape_p, shape_r, shape_d, shape_f = shapes
    taps = shape_f[0]
    rows = shape_f[1] // 2
    count = shape_p[0] // (2 * rows)
    lanes = keep_ref.shape[-1]
    channels = 2 * lanes

    def store(z, x, y, start, size, values):
        values = [value.astype(jnp.bfloat16) for value in values]
        index = (
            lax.rem(x + side, 2),
            lax.rem(y + row, 2),
            lax.rem(z - deep + ROUNDS, ROUNDS),
            pl.ds(start, size),
        )
        keep_ref[index] = jnp.where(core == 0, values[0], values[1])
        give_ref[index] = jnp.where(core == 0, values[1], values[0])

    lane = lax.broadcasted_iota(jnp.int32, (1, lanes), 1)
    reduce = jnp.concatenate(
        [reduce_ref[...], jnp.zeros((lanes - reduce_ref.shape[0], reduce_ref.shape[1]), jnp.float32)]
    ).T
    moved = []
    for y in range(2):
        total = jnp.zeros_like(reduce)
        for c in range(2):
            start, held = reduce_lanes(shape_r[1], y, c, lanes // 2)
            inside = (lane >= held) & (lane < held + shape_r[1])
            total = total + jnp.where(inside, pltpu.roll(reduce, (held - start) % lanes, 1), 0.0)
        moved.append(total)
    for z in range(ROUNDS):
        for x in range(2):
            wide = 2 * z + x
            for y in range(2):
                columns = slice(y * lanes, (y + 1) * lanes)
                for tap in range(taps):
                    line, k = tap // 3, tap % 3
                    left = k * channels + y * lanes
                    values = []
                    for h in range(2):
                        base = (2 * wide + h) * rows
                        values.append(
                            refine_ref[line, base : base + rows, left : left + lanes][None]
                        )
                    store(z, x, y, tap, 1, values)
                values = []
                for h in range(2):
                    base = (2 * wide + h) * rows * count
                    values.append(
                        proj_ref[base : base + rows * count, columns].reshape(count, rows, lanes)
                    )
                store(z, x, y, taps, count, values)
                values = [
                    moved[y][(2 * wide + h) * rows : (2 * wide + h + 1) * rows][None]
                    for h in range(2)
                ]
                store(z, x, y, taps + count, 1, values)
    height, width = shape_d[1], shape_d[2]
    blocks = width // rows
    for tap in range(taps):
        line, k = tap // 3, tap % 3
        columns = slice(k * channels, (k + 1) * channels)
        whole_tap = jnp.concatenate(
            [
                decode_ref[line, :, columns],
                low_ref[line, :, columns],
                jnp.zeros((lanes, channels), jnp.float32),
            ],
            axis=0,
        )
        turned = [whole_tap[n * height : n * height + lanes].T for n in range(4)]
        for z in range(ROUNDS):
            for x in range(2):
                base = (2 * z + x) * width
                for y in range(2):
                    values = [
                        turned[2 * y + c][base : base + width].reshape(blocks, rows, lanes)
                        for c in range(2)
                    ]
                    store(z, x, y, taps + count + 1 + tap * blocks, blocks, values)


def pack_block(proj, reduce, decode, low, refine, shapes, tie):
    shape_p, shape_r, shape_d, shape_f = shapes
    rows = shape_f[1] // 2
    total = shape_f[0] + shape_p[0] // (2 * rows) + 1 + shape_d[0] * shape_d[2] // rows
    out = jax.ShapeDtypeStruct((2, 2, ROUNDS, total, rows, 2 * shape_f[2]), jnp.bfloat16)
    return pl.pallas_call(
        behind_tie(functools.partial(pack_kernel, shapes)),
        out_shape=[out, out],
        in_specs=[pl.BlockSpec(memory_space=pltpu.SMEM), pl.BlockSpec(memory_space=pl.ANY)]
        + [pl.BlockSpec(memory_space=pltpu.VMEM)] * 5,
        out_specs=[pl.BlockSpec(memory_space=pltpu.VMEM)] * 2,
        compiler_params=pltpu.CompilerParams(vmem_limit_bytes=VMEM_BYTES),
        cost_estimate=cost(0, [proj, decode, low, refine, out, out, out]),
        name="pack_gradients",
    )(kernel_place(), tie, proj, reduce, decode, low, refine)


def low_moments_kernel(low_ref, wide_ref, masks_ref, stats_ref):
    reduced = jnp.dot(low_ref[...], wide_ref[...], preferred_element_type=jnp.float32)
    run_moments(reduced, masks_ref[:, 0:1], stats_ref, pl.program_id(0) + 1)


def low_moments(low, wide, masks):
    block = masks.shape[0]
    out = jax.ShapeDtypeStruct((8, wide.shape[1]), jnp.float32)
    return pl.pallas_call(
        low_moments_kernel,
        out_shape=out,
        grid=(low.shape[0] // block,),
        in_specs=[
            pl.BlockSpec((block, low.shape[1]), lambda step: (step, 0)),
            whole(wide),
            whole(masks),
        ],
        out_specs=whole(out),
        compiler_params=pltpu.CompilerParams(vmem_limit_bytes=VMEM_BYTES),
        cost_estimate=cost(2 * low.shape[0] * low.shape[1] * 256, [low]),
        name="low_moments",
    )(low, wide, masks)


def by_tap(values):
    width = values.shape[2] // 3
    split = values.reshape(3, values.shape[1], 3, width)
    return split.transpose(0, 2, 1, 3).reshape(9, values.shape[1], width)


def widen(values):
    padded = jnp.pad(values, ((0, 0), (0, 64 - values.shape[1])))
    return jnp.concatenate([padded, padded, padded, jnp.zeros_like(padded)], axis=1)


def pack_small(items):
    total = sum(item.size for item in items)
    padded = -(-total // 2048) * 2048
    flats = [item.reshape(-1) for item in items]
    return jnp.concatenate(flats + [jnp.zeros((padded - total,), jnp.bfloat16)]).reshape(-1, 128)


def unpack_small(everything, items):
    wide, narrow = everything.shape[:2]
    everything = everything.reshape(wide, narrow, -1)
    pieces = []
    start = 0
    for item in items:
        pieces.append(
            everything[:, :, start : start + item.size].reshape((wide, narrow) + item.shape)
        )
        start += item.size
    proj, reduce, decode, refine = pieces
    proj = proj.transpose(0, 2, 1, 3).reshape(wide * proj.shape[2], -1)
    reduce = reduce.transpose(0, 2, 1, 3).reshape(wide * reduce.shape[2], -1)
    decode = decode.transpose(2, 1, 3, 0, 4).reshape(decode.shape[2], narrow * decode.shape[3], -1)
    refine = refine.transpose(2, 0, 3, 1, 4).reshape(refine.shape[2], wide * refine.shape[3], -1)
    return (proj, widen(reduce), decode, refine)


def pack_grads(reduce, proj, decode, low, refine, shapes):
    wide = lax.axis_size("wide")
    narrow = lax.axis_size("narrow")
    extra = narrow * shapes[1][1]
    reduce = reduce[:extra].T
    decode = jnp.concatenate([by_tap(decode), by_tap(low)[:, :extra]], axis=1)
    refine = by_tap(refine)
    shape_p, shape_r, shape_d, shape_f = shapes
    proj = proj.reshape(wide, shape_p[0], narrow, shape_p[1]).transpose(0, 2, 1, 3)
    reduce = reduce.reshape(wide, shape_r[0], narrow, shape_r[1]).transpose(0, 2, 1, 3)
    decode = decode.reshape(shape_d[0], narrow, shape_d[1], wide, shape_d[2]).transpose(3, 1, 0, 2, 4)
    refine = refine.reshape(shape_f[0], wide, shape_f[1], narrow, shape_f[2]).transpose(1, 3, 0, 2, 4)
    flats = [
        item.astype(jnp.bfloat16).reshape(wide, narrow, -1)
        for item in (proj, reduce, decode, refine)
    ]
    total = sum(item.shape[2] for item in flats)
    padded = -(-total // 2048) * 2048
    flats.append(jnp.zeros((wide, narrow, padded - total), jnp.bfloat16))
    return jnp.concatenate(flats, axis=2).reshape(wide, narrow, -1, 128)


def unpack_grads(owned, shapes):
    owned = owned.reshape(-1)
    pieces = []
    start = 0
    for shape in shapes:
        size = 1
        for extent in shape:
            size *= extent
        pieces.append(owned[start : start + size].reshape(shape))
        start += size
    return pieces


def per_device(
    features,
    low_level,
    widths,
    w_point,
    w_atrous,
    w_proj,
    w_low,
    w_dec1,
    w_dec2,
    w_cls,
    b_cls,
    gains,
    biases,
    low_gain,
    low_bias,
    logit_grad,
):
    canvases = features.shape[0]
    height = features.shape[1]
    columns = features.shape[2]
    fine_columns = low_level.shape[2]
    images = widths.shape[1] - 1
    channels = gains.shape[1]
    images_total = float(canvases * lax.axis_size("wide") * lax.axis_size("narrow") * images)
    small = [w_proj, w_low, w_dec1, w_dec2]
    ids_coarse = band_ids(widths, columns)
    ids_fine = band_ids(4 * widths, fine_columns)
    valid_coarse = (ids_coarse >= 0).astype(jnp.float32)[:, None, :, None]
    valid_fine = (ids_fine >= 0).astype(jnp.float32)[:, None, :, None]
    all_ones = jnp.ones((1, 1, 1), jnp.float32)
    local_count = (height * jnp.sum(widths[:, :images])).astype(jnp.float32)
    member = (ids_coarse[:, :, None] == jnp.arange(images, dtype=jnp.int32)[None, None, :]).astype(
        jnp.float32
    )
    member_low = member.astype(jnp.bfloat16)
    image_sizes = (height * widths[:, :images]).astype(jnp.float32)
    positions = low_level.shape[1] * fine_columns
    low_flat = low_level.reshape(positions, -1)
    extra = low_gain.shape[0]
    side_masks = [tap_mask(ids_fine, STRIP, 0, step) for step in (-1, 1)]
    masks = jnp.concatenate([valid_fine * jnp.ones((1, STRIP, 1, 1))] + side_masks, axis=-1)
    masks = masks.reshape(STRIP * fine_columns, 3)
    coarse_shape = (height, columns, channels)
    mask_column = jnp.broadcast_to(valid_coarse, (1, height, columns, 1)).reshape(-1, 1)
    member_wide = jnp.pad(member[0], ((0, 0), (0, 8 - images)))
    member_rows = jnp.tile(member_wide, (height, 1))
    sizes_inverse = jnp.pad(1.0 / image_sizes[0], (0, 8 - images)).reshape(8, 1)
    pool_inputs = (member_rows.T.astype(jnp.bfloat16), sizes_inverse)

    def all_sides():
        sides = [
            [
                item.reshape(height * columns, -1)
                for item in side_values(features, ids_coarse, dilation)
            ]
            for dilation in dilations
        ]
        return (sides, logit_grad.reshape(-1, logit_grad.shape[-1]))

    def low_part(proj, wide, decode, refine):
        return low_moments(low_flat, wide, masks)

    def forward(part, ready, own, other, before):
        sums, stats, pooling = ({}, {}, ()) if before is None else before
        pair = dict(zip(PARTS[part], zip(own, other)))
        more, more_stats, more_pooling = coarse_forward(
            part,
            mask_column,
            ready[0],
            pair,
            coarse_shape,
            sums,
            pool_inputs if POINT_CHUNK in PARTS[part] else None,
        )
        return ({**sums, **more}, {**stats, **more_stats}, tuple(pooling) + tuple(more_pooling))

    chunks, unpacked, ready, low_stats, coarse = gather_taps(
        order_taps(w_point, w_atrous),
        small,
        [all_sides, low_part],
        [functools.partial(forward, part) for part in range(3)],
    )
    proj_full, low_wide, decode_full, refine_full = unpacked
    sides, grad_flat = ready
    sums, stats, pool_results = coarse
    point_z, point_stats, pool_z, pooled = pool_results
    pool_z = pool_z[None, :images]
    coarse_stats = [point_stats, stats[0], stats[1], stats[2]]
    coarse_z = [
        item.reshape(1, height, columns, channels) for item in (point_z, sums[0], sums[1], sums[2])
    ]
    blocks = [(item_z, valid_coarse) for item_z in coarse_z] + [(pool_z, all_ones)]
    local_images = float(canvases * images)
    states = [
        (jnp.full((channels,), 1.0) * local_count, item[0], item[1]) for item in coarse_stats
    ] + [
        local_moments(pool_z, all_ones, local_images),
        (
            jnp.full((extra,), 16.0) * local_count,
            low_stats[0, :extra],
            low_stats[1, :extra],
        ),
    ]
    counts_flat, means_flat, squares_flat = merge_all(
        *[jnp.concatenate([state[item] for state in states]) for item in range(3)]
    )
    vars_flat = squares_flat / counts_flat
    section_means = []
    section_vars = []
    offset = 0
    for width in [channels] * 5 + [extra]:
        section_means.append(means_flat[offset : offset + width])
        section_vars.append(vars_flat[offset : offset + width])
        offset += width
    pixel_count = counts_flat[0]
    fine_count = 16.0 * pixel_count
    fine_local = 16.0 * local_count
    gain_rows = [gains[0], gains[1], gains[2], gains[3], gains[4], low_gain]
    bias_rows = [biases[0], biases[1], biases[2], biases[3], biases[4], low_bias]
    kept = []
    activations = []
    for index in range(5):
        block_values, block_valid = blocks[index]
        result = normalize(
            block_values,
            block_valid,
            section_means[index],
            section_vars[index],
            gain_rows[index],
            bias_rows[index],
        )
        kept.append(result[1:])
        activations.append(result[0].astype(jnp.bfloat16))
    spread = jnp.einsum(
        "nwk,nkd->nwd", member_low, activations[4], preferred_element_type=jnp.float32
    ).astype(jnp.bfloat16)
    spread = jnp.broadcast_to(spread[:, None], (canvases, height, columns, channels))
    joined_coarse = jnp.concatenate(activations[:4] + [spread], axis=-1)
    proj_z = jnp.einsum(
        "nhwc,cd->nhwd", joined_coarse, proj_full, preferred_element_type=jnp.float32
    )
    proj_mean, proj_var = moments(proj_z, valid_coarse, local_count, pixel_count)
    proj_act, proj_centered, proj_shaped, proj_scale = normalize(
        proj_z, valid_coarse, proj_mean, proj_var, gains[5], biases[5]
    )
    proj_act = proj_act.astype(jnp.bfloat16).astype(jnp.float32)
    cols_table = column_table(ids_coarse)[0].astype(jnp.bfloat16)
    low_mean, low_var = section_means[5], section_vars[5]
    low_vectors = widen(norm_vectors(low_mean, low_var, low_gain, low_bias))
    decode_z, decode_stats, upsampled = decode_forward(
        proj_act[0],
        jnp.concatenate([cols_table, cols_table], axis=1),
        low_flat,
        low_wide,
        low_vectors,
        masks,
        decode_full,
    )
    decode_mean, decode_var = merged(decode_stats, fine_local, fine_count)
    decode_vectors = norm_vectors(decode_mean, decode_var, gains[6], biases[6])
    refine_z, refine_stats = refine_forward(decode_z, decode_vectors, masks, refine_full)
    refine_mean, refine_var = merged(refine_stats, fine_local, fine_count)
    refine_vectors = norm_vectors(refine_mean, refine_var, gains[7], biases[7])
    logits, refine_sums, cls_weight_grad, cls_bias_grad = classify(
        refine_z, grad_flat, refine_vectors, masks, w_cls, b_cls.reshape(1, -1)
    )
    logits = logits.reshape(logit_grad.shape)
    cls_weight_grad = cls_weight_grad.T
    cls_bias_grad = cls_bias_grad[0]
    refine_gain, refine_bias = gradient_sums([(refine_sums[0], refine_sums[1])])[0]
    refine_vectors = norm_vectors(
        refine_mean,
        refine_var,
        gains[7],
        biases[7],
        refine_gain / fine_count,
        refine_bias / fine_count,
    )
    decode_local, decode_sums, refine_kernel_grad = refine_backward(
        refine_z, grad_flat, refine_vectors, w_cls, decode_z, decode_vectors, masks, refine_full
    )
    decode_gain, decode_bias = gradient_sums([(decode_sums[0], decode_sums[1])])[0]
    decode_vectors = norm_vectors(
        decode_mean,
        decode_var,
        gains[6],
        biases[6],
        decode_gain / fine_count,
        decode_bias / fine_count,
    )
    proj_up, reduce_local, reduce_sums, decode_kernel_grad, low_kernel_grad = decode_backward(
        decode_local,
        decode_z,
        decode_vectors,
        upsampled,
        low_flat,
        low_wide,
        low_vectors,
        jnp.concatenate([cols_table.T, cols_table.T], axis=1),
        masks,
        decode_full,
        coarse_shape,
    )
    proj_up = proj_up[None]
    reduce_gain, reduce_bias = reduce_sums[0, :extra], reduce_sums[1, :extra]

    proj_local, proj_gain, proj_bias = norm_grad_terms(
        proj_up, valid_coarse, proj_centered, proj_shaped
    )
    summed_pairs = gradient_sums([(proj_gain, proj_bias), (reduce_gain, reduce_bias)])
    proj_gain, proj_bias = summed_pairs[0]
    reduce_gain, reduce_bias = summed_pairs[1]
    proj_dz = norm_grad_finish(
        proj_local,
        valid_coarse,
        proj_centered,
        proj_scale,
        gains[5],
        proj_gain,
        proj_bias,
        pixel_count,
    )
    proj_kernel_grad = jnp.einsum(
        "nhwc,nhwd->cd", joined_coarse, proj_dz, preferred_element_type=jnp.float32
    )
    concat_grad = jnp.einsum(
        "nhwd,cd->nhwc", proj_dz, proj_full, preferred_element_type=jnp.float32
    )
    branch_terms = []
    for index in range(4):
        upstream = concat_grad[..., index * channels : (index + 1) * channels]
        branch_terms.append(norm_grad_terms(upstream, valid_coarse, kept[index][0], kept[index][1]))
    pool_up = jnp.einsum(
        "nhwd,nwk->nkd", concat_grad[..., 4 * channels :], member, precision=highest
    )
    branch_terms.append(norm_grad_terms(pool_up, all_ones, kept[4][0], kept[4][1]))
    local_pairs = [(term_item[1], term_item[2]) for term_item in branch_terms]
    flat_pairs = pack_pairs(local_pairs)
    flat_sums = sum_all(
        jnp.concatenate([flat_pairs, cls_bias_grad, cls_weight_grad.reshape(-1)])
    )
    classes = cls_bias_grad.shape[0]
    cls_weight_grad = flat_sums[flat_pairs.shape[0] + classes :].reshape(cls_weight_grad.shape)
    cls_bias_grad = flat_sums[flat_pairs.shape[0] : flat_pairs.shape[0] + classes]
    flat_sums = flat_sums[: flat_pairs.shape[0]]
    last_pairs = unpack_pairs(flat_sums, local_pairs)
    valid_list = [valid_coarse, valid_coarse, valid_coarse, valid_coarse, all_ones]
    count_list = [pixel_count, pixel_count, pixel_count, pixel_count, images_total]
    branch_dz = [
        norm_grad_finish(
            branch_terms[index][0],
            valid_list[index],
            kept[index][0],
            kept[index][2],
            gains[index],
            last_pairs[index][0],
            last_pairs[index][1],
            count_list[index],
        )
        for index in range(5)
    ]
    flat_dz = [item.reshape(height * columns, channels) for item in branch_dz[:4]]
    pool_dz = jnp.pad(branch_dz[4][0], ((0, 8 - images), (0, 0)))
    low_vectors = widen(
        norm_vectors(
            low_mean,
            low_var,
            low_gain,
            low_bias,
            reduce_gain / fine_count,
            reduce_bias / fine_count,
        )
    )

    def low_late(tie):
        return low_backward(reduce_local, low_flat, low_wide, low_vectors, masks, tie)

    def input_late(tie):
        side_dz = [
            side_grads(branch_dz[branch + 1], ids_coarse, dilations[branch]).reshape(
                height * columns, -1
            )
            for branch in range(3)
        ]
        return coarse_input(
            flat_dz[0],
            pool_dz,
            member_rows * sizes_inverse.reshape(1, 8),
            side_dz,
            chunks,
            coarse_shape,
            features.shape[3],
            tie,
        )

    def weight_part(part, grads, tie=None):
        return coarse_weight(
            part,
            sides,
            grads[1:4],
            coarse_shape,
            (grads[0], pooled, grads[4]) if POINT_CHUNK in PARTS[part] else None,
            tie,
        )

    owned, small_owned, low_level_grad, features_grad = scatter_taps(
        flat_dz + [pool_dz],
        [item.shape for item in small],
        [functools.partial(weight_part, part) for part in range(3)],
        (proj_kernel_grad, decode_kernel_grad, low_kernel_grad, refine_kernel_grad),
        [low_late, input_late],
    )
    low_level_grad = low_level_grad.reshape(low_level.shape)
    features_grad = features_grad.reshape(features.shape)
    proj_owned, reduce_owned, decode_owned, refine_owned = small_owned
    point_owned, atrous_owned = restore_taps(owned, w_atrous.shape)
    gains_grad = jnp.stack(
        [
            last_pairs[0][0],
            last_pairs[1][0],
            last_pairs[2][0],
            last_pairs[3][0],
            last_pairs[4][0],
            proj_gain,
            decode_gain,
            refine_gain,
        ]
    )
    biases_grad = jnp.stack(
        [
            last_pairs[0][1],
            last_pairs[1][1],
            last_pairs[2][1],
            last_pairs[3][1],
            last_pairs[4][1],
            proj_bias,
            decode_bias,
            refine_bias,
        ]
    )
    return (
        logits,
        features_grad,
        low_level_grad,
        point_owned,
        atrous_owned,
        proj_owned,
        reduce_owned,
        decode_owned,
        refine_owned,
        cls_weight_grad,
        cls_bias_grad,
        gains_grad,
        biases_grad,
        reduce_gain,
        reduce_bias,
    )


def solution(mesh):
    in_specs = (
        P(("wide", "narrow"), None, None, None),
        P(("wide", "narrow"), None, None, None),
        P(("wide", "narrow"), None),
        P(None, "wide", "narrow"),
        P(None, None, "wide", "narrow"),
        P("wide", "narrow"),
        P("wide", "narrow"),
        P(None, "narrow", "wide"),
        P(None, "wide", "narrow"),
        P(),
        P(),
        P(),
        P(),
        P(),
        P(),
        P(("wide", "narrow"), None, None, None),
    )
    out_specs = (
        P(("wide", "narrow"), None, None, None),
        P(("wide", "narrow"), None, None, None),
        P(("wide", "narrow"), None, None, None),
        P(None, "wide", "narrow"),
        P(None, None, "wide", "narrow"),
        P("wide", "narrow"),
        P("wide", "narrow"),
        P(None, "narrow", "wide"),
        P(None, "wide", "narrow"),
        P(),
        P(),
        P(),
        P(),
        P(),
        P(),
    )
    return jax.shard_map(
        per_device, mesh=mesh, in_specs=in_specs, out_specs=out_specs, check_vma=False
    )
```

time: 1320 us -> 902 us (0.68)
  local copies, waits for them, and re-layouts: 334 us -> 97.8 us
  matrix products: 189 us -> 6.82 us
  Pallas kernels: 94.9 us -> 247 us
  other arithmetic: 221 us -> 120 us
  waiting for transfers between devices: 280 us -> 207 us
  starting transfers between devices: 177 us -> 205 us
    dot_general x16 -> x0, matrix products: 181 us -> none  [the longest x2 60.2 us: conv_forward(): jnp.einsum('nhwc,tcd->tnhwd', values, kernel, preferred_element_type=jnp....]
    pallas_call x5 -> x13, Pallas kernels: 60.3 us -> 214 us  [the longest x1 45.9 us: decode_backward(): pl.pallas_call(functools.partial(decode_backward_kernel, steps, columns),...]
    squeeze x11 -> x10, local copies, waits for them, and re-layouts: 87.8 us -> 0.74 us  [the longest x7 0.7 us: second(): kept.append(total[0])]
    ppermute x72 -> x90, waiting for transfers between devices: 212 us -> 158 us  [exchange(): lax.ppermute(values, axis, [(place, place ^ bit) for place in range(size)])]
    reduce_sum x3 -> x1, other arithmetic: 50.5 us -> 0.02 us  [local_moments(): mean = jnp.sum(values * valid_map, axis=axes) / count]
    reshape x20 -> x5, local copies, waits for them, and re-layouts: 44.9 us -> 0.43 us  [the longest x3 0.24 us: share_core(): parts = shard.reshape(shard.shape[0], 2, half, shard.shape[2])]
    ppermute x72 -> x90, starting transfers between devices: 101 us -> 134 us  [exchange(): lax.ppermute(values, axis, [(place, place ^ bit) for place in range(size)])]
    unnamed x555 -> x531, local copies, waits for them, and re-layouts: 100 us -> 67.5 us
  transfers between devices with their start and end apart: 102 -> 114, of which waited for: 47 -> 61; matrix products, arithmetic and copies ran while one was open for 24% -> 14% of each run, Pallas kernels for 7% -> 10%
where the time goes in v2:
time: 902 us; the launch traced here: 890 us
  Pallas kernels  247 us (27%)
  waiting for transfers between devices  207 us (23%)
  starting transfers between devices  205 us (23%)
  other arithmetic  120 us (13%)
  local copies, waits for them, and re-layouts  97.8 us (11%)
    ppermute x90, waiting for transfers between devices, exchange(): lax.ppermute(values, axis, [(place, place ^ bit) for place in range(size)])  158 us
    ppermute x90, starting transfers between devices, exchange(): lax.ppermute(values, axis, [(place, place ^ bit) for place in range(size)])  134 us
    ppermute x24, starting transfers between devices, rotate(): return lax.ppermute(values, axis, pairs)  71.5 us
    unnamed x531, local copies, waits for them, and re-layouts  67.5 us
    ppermute x24, waiting for transfers between devices, rotate(): return lax.ppermute(values, axis, pairs)  49.7 us
    pallas_call x1, Pallas kernels, decode_backward(): pl.pallas_call(functools.partial(decode_backward_kernel, steps, columns),...  45.9 us
    pallas_call x3, Pallas kernels, coarse_weight(): pl.pallas_call(kernel, out_shape=outs, grid_spec=pltpu.PrefetchScalarGrid...  35.9 us
    pallas_call x1, Pallas kernels, refine_backward(): pl.pallas_call(functools.partial(refine_backward_kernel, steps, columns),...  34.3 us
  transfers between devices with their start and end apart: 114, of which 61 were waited for; matrix products, arithmetic and copies ran while one was open for 14% of the time, Pallas kernels for 10%

profile of v2, /device:TPU:1, one launch (start us, length us, event | category | flops | bytes accessed | tf_op | source)
XLA Modules:
  0.0 890.3 jit_solution(2848188731718249194)
XLA Ops:
  19.1 8.3 collective-permute-done.2
  33.3 4.4 collective-permute-start.16
  53.7 6.1 fusion.9
  77.6 14.8 %collective-permute-done.21 = bf16[4,5,128,128]{3,2,1,0:T(8,128)(2,1)S(1)} collective-permute-done((bf16[4,5,128,128]{3,2,1,0:T(8,128)(2,1)S(1)}, bf16[4,5,128,128]{3,2,1,0:T(8,128)(2,1)S(1)}, u32[]{:S(2)}, u32[]{:S(2)}) %collective-permute-start.21) | collective-permute-done | bytes 655392 | tf_op jit(solution)/shard_map/ppermute | solution.py:22
  99.2 4.4 collective-permute-start.8
  110.2 8.6 coarse_forward.3.refs_6_
  118.8 12.6 %collective-permute-done.9 = bf16[12,128,128]{2,1,0:T(8,128)(2,1)} collective-permute-done((bf16[12,128,128]{2,1,0:T(8,128)(2,1)}, bf16[12,128,128]{2,1,0:T(8,128)(2,1)}, u32[]{:S(2)}, u32[]{:S(2)}) %collective-permute-start.9) | collective-permute-done | bytes 393248 | tf_op jit(solution)/shard_map/ppermute | solution.py:32
  134.7 3.9 pad_maximum_fusion.3.refs_11_.refs_12_
  139.7 8.6 collective-permute-start.29
  151.7 6.4 collective-permute-start.31
  158.0 3.5 pad_maximum_fusion.6.refs_9_.refs_10_
  167.3 17.7 %collective-permute-done.30 = bf16[2,2,33,16,128]{4,3,2,1,0:T(8,128)(2,1)S(1)} collective-permute-done((bf16[2,2,33,16,128]{4,3,2,1,0:T(8,128)(2,1)S(1)}, bf16[2,2,33,16,128]{4,3,2,1,0:T(8,128)(2,1)S(1)}, u32[]{:S(2)}, u32[]{:S(2)}) %collective-permute-start.30) | collective-permute-done | bytes 540704 | tf_op jit(solution)/shard_map/ppermute | solution.py:32
  192.1 13.7 %coarse_forward.4 = (f32[480,256]{1,0:T(8,128)S(1)}, f32[480,256]{1,0:T(8,128)S(1)}, f32[8,256]{1,0:T(8,128)S(1)}, f32[480,256]{1,0:T(8,128)S(1)}, f32[8,256]{1,...) custom-call(s32[4]{0:T(128)S(1)} %pad_add_fusion.place_ref, f32[480,1]{1,0:T(8,128)S(1)} %broadcast_in_dim.25.refs_0_, ...), custom_call_target="tpu_custom_call" | custom-call | flops 1 | bytes 1 | tf_op jit(solution)/shard_map/coarse_forward/pallas_call | solution.py:499
  208.7 3.7 unpack_weights.1
  212.5 4.7 low_moments.1
  217.2 6.6 collective-permute-done.27
  224.4 3.5 pad_maximum_fusion.4.refs_7_.refs_14_
  229.0 3.4 pad_maximum_fusion.5.refs_9_.refs_16_
  250.3 11.4 %coarse_forward.5 = (f32[480,256]{1,0:T(8,128)S(1)}, f32[480,256]{1,0:T(8,128)S(1)}, f32[8,256]{1,0:T(8,128)S(1)}, f32[8,256]{1,0:T(8,128)S(1)}) custom-call(s32[4]{0:T(128)S(1)} %pad_add_fusion.place_ref, f32[480,1]{1,0:T(8,128)S(1)} %copy-done.34, bf16[480,2048]{1,0:T(8,128)(2,1)S(1)} %bitcast.369, bf16[480,2048]{1,0:T(8,128)(2,1)S(1)} %bitcast.382, ...), custom_call_target="tpu_custom_call" | custom-call | flops 1 | bytes 1 | tf_op jit(solution)/shard_map/coarse_forward/pallas_call | solution.py:499
  270.3 11.2 %collective-permute-start.40 = (f32[3,1328]{1,0:T(4,128)S(1)}, f32[3,1328]{1,0:T(4,128)S(1)}, u32[]{:S(2)}, u32[]{:S(2)}) collective-permute-start(f32[3,1328]{1,0:T(4,128)S(1)} %pad_maximum_fusion.40), channel_id=1, source_target_pairs={{0,8},{4,12},{8,0},{12,4},{16,24},{20,28},{24,16},{28,20},{1,9},{5... | collective-permute-start | bytes 47816 | tf_op jit(solution)/shard_map/ppermute | solution.py:22
  290.6 4.7 collective-permute-start.42
  319.5 23.9 %decode_forward.1 = (f32[7680,256]{1,0:T(8,128)}, f32[8,256]{1,0:T(8,128)S(1)}, bf16[7680,256]{1,0:T(8,128)(2,1)}) custom-call(f32[20,24,256]{2,1,0:T(8,128)S(1)} %fusion.49.act_ref, bf16[96,48]{1,0:T(8,128)(2,1)S(1)} %copy-done.60, bf16[7680,256]{1,0:T(8,128)(2,1)} %bitcast.372, bf16[256,256]{1,0:T(8,128)(2,1)S(1)} %copy-done.42, ...), custom_call_target="tpu_custom_call" | custom-call | flops 1 | bytes 1 | tf_op jit(solution)/shard_map/decode_forward/pallas_call | solution.py:855
  343.5 4.6 collective-permute-start.47
  364.5 18.0 %refine_forward.1 = (f32[7680,256]{1,0:T(8,128)}, f32[8,256]{1,0:T(8,128)S(1)}) custom-call(f32[7680,256]{1,0:T(8,128)} %get-tuple-element.300.z_in_ref.z_ref, f32[8,256]{1,0:T(8,128)S(1)} %stack.579.vector_ref.vector_in_ref, f32[768,3]{1,0:T(8,128)S(1)} %copy.190.masks_ref.refs_3_, bf16[9,256,256]{2,1,0:T(8,128)(2,1)S(1)} %get-tuple-element.275.w_ref), custom_call_target="tpu_custom_call" | custom-call | flops 1 | bytes 1 | tf_op jit(solution)/shard_map/refine_forward/pallas_call | solution.py:919
  382.4 4.7 collective-permute-start.52
  407.3 10.0 %classify.1 = (bf16[7680,21]{1,0:T(8,128)(2,1)S(1)}, f32[8,256]{1,0:T(8,128)S(1)}, f32[21,256]{1,0:T(8,128)S(1)}, f32[1,21]{1,0:T(1,128)S(1)}) custom-call(f32[7680,256]{1,0:T(8,128)} %get-tuple-element.302.z_ref, bf16[7680,21]{1,0:T(8,128)(2,1)S(1)} %bitcast.384, f32[8,256]{1,0:T(8,128)S(1)} %copy-done.66, f32[768,3]{1,0:T(8,128)S(1)} %copy.190.masks_ref.refs_3_, ...), custom_call_target="tpu_custom_call" | custom-call | flops 1 | bytes 1 | tf_op jit(solution)/shard_map/classify/pallas_call | solution.py:976
  419.7 4.7 collective-permute-start.57
  441.8 34.3 %refine_backward.1 = (f32[7680,256]{1,0:T(8,128)}, f32[8,256]{1,0:T(8,128)S(1)}, f32[3,256,768]{2,1,0:T(8,128)S(1)}) custom-call(f32[7680,256]{1,0:T(8,128)} %get-tuple-element.302.z_ref, bf16[7680,21]{1,0:T(8,128)(2,1)S(1)} %bitcast.385, f32[8,256]{1,0:T(8,128)S(1)} %copy-done.65, bf16[256,21]{1,0:T(8,128)(2,1)S(1)} %copy-done.55, ...), custom_call_target="tpu_custom_call" | custom-call | flops 1 | bytes 1 | tf_op jit(solution)/shard_map/refine_backward/pallas_call | solution.py:1067
  477.6 4.7 collective-permute-start.62
  497.8 45.9 %decode_backward.1 = (f32[20,24,256]{2,1,0:T(8,128)S(1)}, f32[7680,64]{1,0:T(8,128)}, f32[8,256]{1,0:T(8,128)S(1)}, f32[3,256,768]{2,1,0:T(8,128)S(1)}, f32[3,64,768]{2,1,0:T(8,128)S(1)}) custom-call(f32[7680,256]{1,0:T(8,128)} %get-tuple-element.306.local_ref, f32[7680,256]{1,0:T(8,128)} %get-tuple-element.300.z_in_ref.z_ref, ...), custom_call_target="tpu_custom_call" | custom-call | flops 1 | bytes 1 | tf_op jit(solution)/shard_map/decode_backward/pallas_call | solution.py:1183
  546.4 4.7 collective-permute-start.67
  576.1 4.7 collective-permute-start.72
  599.5 12.6 %coarse_weight.3 = (bf16[2,2,4,6,128,128]{5,4,3,2,1,0:T(8,128)(2,1)}, bf16[2,2,4,6,128,128]{5,4,3,2,1,0:T(8,128)(2,1)}, bf16[2,2,4,6,128,128]{5,4,3,2,1,0:T(8,128)(2,1)}, bf16[2,2,4,6,128,128]{5,4,3,2,1,0:T(8,128)(2,1)}) custom-call(s32[4]{0:T(128)S(1)} %copy-done.62, bf16[480,2048]{1,0:T(8,128)(2,1)S(1)} %bitcast.370, bf16[480,2048]{1,0:T(8,128)(2,1)S(1)} %bitcast.383, ...), custom_call_target="tpu_custom_call" | custom-call | flops 1 | bytes 1 | tf_op jit(solution)/shard_map/coarse_weight/pallas_call | solution.py:611
  612.2 4.7 collective-permute-start.85
  625.3 12.8 %coarse_weight.4 = (bf16[2,2,4,5,128,128]{5,4,3,2,1,0:T(8,128)(2,1)}, bf16[2,2,4,5,128,128]{5,4,3,2,1,0:T(8,128)(2,1)}, bf16[2,2,4,6,128,128]{5,4,3,2,1,0:T(8,128)(2,1)}, bf16[2,2,4,6,128,128]{5,4,3,2,1,0:T(8,128)(2,1)}) custom-call(s32[4]{0:T(128)S(1)} %copy-done.62, bf16[2,2,4,6,128,128]{5,4,3,2,1,0:T(8,128)(2,1)} %get-tuple-element.313.tie_ref, ...), custom_call_target="tpu_custom_call" | custom-call | flops 1 | bytes 1 | tf_op jit(solution)/shard_map/coarse_weight/pallas_call | solution.py:611
  661.9 9.5 %low_backward.1 = (bf16[7680,256]{1,0:T(8,128)(2,1)}, f32[64,256]{1,0:T(8,128)S(1)}) custom-call(f32[8,256]{1,0:T(8,128)S(1)} %maximum_maximum_fusion.1.place_ref, bf16[2,4,5,128,128]{4,3,2,1,0:T(8,128)(2,1)S(1)} %fusion.14.tie_ref, f32[7680,64]{1,0:T(8,128)S(1)} %copy-done.29, bf16[7680,256]{1,0:T(8,128)(2,1)} %bitcast.374, ...), custom_call_target="tpu_custom_call" | custom-call | flops 1 | bytes 1 | tf_op jit(solution)/shard_map/low_backward/pallas_call | solution.py:1240
  671.5 10.5 %coarse_weight.5 = (bf16[2,2,4,3,128,128]{5,4,3,2,1,0:T(8,128)(2,1)S(1)}, bf16[2,2,4,3,128,128]{5,4,3,2,1,0:T(8,128)(2,1)S(1)}, bf16[2,2,4,3,128,128]{5,4,3,2,1,...) custom-call(s32[4]{0:T(128)S(1)} %copy-done.62, bf16[2,4,6,128,128]{4,3,2,1,0:T(8,128)(2,1)} %fusion.12.tie_ref, ...), custom_call_target="tpu_custom_call" | custom-call | flops 1 | bytes 1 | tf_op jit(solution)/shard_map/coarse_weight/pallas_call | solution.py:611
  685.8 5.3 pack_gradients.1
  692.1 22.4 %coarse_input.1 = bf16[480,2048]{1,0:T(8,128)(2,1)} custom-call(s32[4]{0:T(128)S(1)} %copy-done.62, bf16[2,4,6,128,128]{4,3,2,1,0:T(8,128)(2,1)S(1)} %fusion.11.tie_ref, bf16[480,256]{1,0:T(8,128)(2,1)S(1)} %bitcast.406, bf16[8,256]{1,0:T(8,128)(2,1)S(1)} %pad.103.refs_9_.refs_1_, f32[480,8]{1,0:T(8,128)S(1)} %copy-done.51, bf16[480,768]{1,0:T(8,128)(2,1)S(1)} %bitcast.402, ...), custom_call_target="tpu_custom_call" | custom-call | flops 1 | bytes 1 | tf_op jit(solution)/shard_map/coarse_input/pallas_call | solution.py:686
  728.6 25.8 %collective-permute-done.80 = bf16[2,4,6,128,128]{4,3,2,1,0:T(8,128)(2,1)S(1)} collective-permute-done((bf16[2,4,6,128,128]{4,3,2,1,0:T(8,128)(2,1)S(1)}, bf16[2,4,6,128,128]{4,3,2,1,0:T(8,128)(2,1)S(1)}, u32[]{:S(2)}, u32[]{:S(2)}) %collective-permute-start.80) | collective-permute-done | bytes 1572896 | tf_op jit(solution)/shard_map/ppermute | solution.py:22
  760.9 10.4 %collective-permute-done.93 = bf16[4,6,128,128]{3,2,1,0:T(8,128)(2,1)S(1)} collective-permute-done((bf16[4,6,128,128]{3,2,1,0:T(8,128)(2,1)S(1)}, bf16[4,6,128,128]{3,2,1,0:T(8,128)(2,1)S(1)}, u32[]{:S(2)}, u32[]{:S(2)}) %collective-permute-start.93) | collective-permute-done | bytes 786464 | tf_op jit(solution)/shard_map/ppermute | solution.py:22
  775.2 13.0 %collective-permute-done.92 = bf16[2,4,3,128,128]{4,3,2,1,0:T(8,128)(2,1)S(1)} collective-permute-done((bf16[2,4,3,128,128]{4,3,2,1,0:T(8,128)(2,1)S(1)}, bf16[2,4,3,128,128]{4,3,2,1,0:T(8,128)(2,1)S(1)}, u32[]{:S(2)}, u32[]{:S(2)}) %collective-permute-start.92) | collective-permute-done | bytes 786464 | tf_op jit(solution)/shard_map/ppermute | solution.py:22
  794.9 7.3 collective-permute-done.88
  804.2 7.8 collective-permute-done.102
  815.0 9.1 %collective-permute-done.101 = bf16[4,33,16,128]{3,2,1,0:T(8,128)(2,1)S(1)} collective-permute-done((bf16[4,33,16,128]{3,2,1,0:T(8,128)(2,1)S(1)}, bf16[4,33,16,128]{3,2,1,0:T(8,128)(2,1)S(1)}, u32[]{:S(2)}, u32[]{:S(2)}) %collective-permute-start.101) | collective-permute-done | bytes 540704 | tf_op jit(solution)/shard_map/ppermute | solution.py:22
  832.3 9.7 %collective-permute-done.96 = bf16[11,128,128]{2,1,0:T(8,128)(2,1)S(1)} collective-permute-done((bf16[11,128,128]{2,1,0:T(8,128)(2,1)S(1)}, bf16[11,128,128]{2,1,0:T(8,128)(2,1)S(1)}, u32[]{:S(2)}, u32[]{:S(2)}) %collective-permute-start.96) | collective-permute-done | bytes 360480 | tf_op jit(solution)/shard_map/ppermute | solution.py:32
  842.8 16.6 %collective-permute-start.110 = (bf16[33,16,128]{2,1,0:T(8,128)(2,1)}, bf16[33,16,128]{2,1,0:T(8,128)(2,1)}, u32[]{:S(2)}, u32[]{:S(2)}) collective-permute-start(bf16[33,16,128]{2,1,0:T(8,128)(2,1)} %get-tuple-element.580), channel_id=1, source_target_pairs={{0,8},{4,12},{8,16},{12,20},{16,24},{20,28},{24,0},{28,4},{1,9},{5... | collective-permute-start | bytes 405512 | tf_op jit(solution)/shard_map/ppermute | solution.py:32
  865.0 6.3 collective-permute-start.104
  (1072 shorter events, 377.9 us)
Async XLA Ops:
  33.3 28.4 %collective-permute-start.16 = (bf16[11,128,128]{2,1,0:T(8,128)(2,1)S(1)}, bf16[11,128,128]{2,1,0:T(8,128)(2,1)}, u32[]{:S(2)}, u32[]{:S(2)}) collective-permute-start(bf16[11,128,128]{2,1,0:T(8,128)(2,1)S(1)} %pad_maximum_fusion.29), channel_id=1, source_target_pairs={{0,8},{4,12},{8,16},{12,20},{16,24},{20,28},{24,0},{28,4},{1,9},{5... | collective-permute-start | bytes 1081352 | tf_op jit(solution)/shard_map/ppermute | solution.py:32
  38.1 25.0 %collective-permute-start.17 = (bf16[11,128,128]{2,1,0:T(8,128)(2,1)S(1)}, bf16[11,128,128]{2,1,0:T(8,128)(2,1)}, u32[]{:S(2)}, u32[]{:S(2)}) collective-permute-start(bf16[11,128,128]{2,1,0:T(8,128)(2,1)S(1)} %pad_maximum_fusion.29), channel_id=1, source_target_pairs={{0,16},{4,20},{8,24},{12,28},{16,0},{20,4},{24,8},{28,12},{1,17},{... | collective-permute-start | bytes 1081352 | tf_op jit(solution)/shard_map/ppermute | solution.py:32
  41.5 21.6 %collective-permute-start.18 = (bf16[11,128,128]{2,1,0:T(8,128)(2,1)S(1)}, bf16[11,128,128]{2,1,0:T(8,128)(2,1)}, u32[]{:S(2)}, u32[]{:S(2)}) collective-permute-start(bf16[11,128,128]{2,1,0:T(8,128)(2,1)S(1)} %pad_maximum_fusion.29), channel_id=1, source_target_pairs={{0,24},{4,28},{8,0},{12,4},{16,8},{20,12},{24,16},{28,20},{1,25},{... | collective-permute-start | bytes 1081352 | tf_op jit(solution)/shard_map/ppermute | solution.py:32
  49.2 18.5 %collective-permute-start.14 = (bf16[2,4,3,128,128]{4,3,2,1,0:T(8,128)(2,1)S(1)}, bf16[2,4,3,128,128]{4,3,2,1,0:T(8,128)(2,1)}, u32[]{:S(2)}, u32[]{:S(2)}) collective-permute-start(bf16[2,4,3,128,128]{4,3,2,1,0:T(8,128)(2,1)S(1)} %pad_maximum_fusion.20), channel_id=1, source_target_pairs={{0,2},{1,3},{2,0},{3,1},{4,6},{5,7},{6,4},{7,5},{8,10},{9,11},{10,... | collective-permute-start | bytes 2359304 | tf_op jit(solution)/shard_map/ppermute | solution.py:22
  52.4 18.4 %collective-permute-start.15 = (bf16[2,4,3,128,128]{4,3,2,1,0:T(8,128)(2,1)}, bf16[2,4,3,128,128]{4,3,2,1,0:T(8,128)(2,1)}, u32[]{:S(2)}, u32[]{:S(2)}) collective-permute-start(bf16[2,4,3,128,128]{4,3,2,1,0:T(8,128)(2,1)} %pad_maximum_fusion.21), channel_id=1, source_target_pairs={{0,4},{4,0},{8,12},{12,8},{16,20},{20,16},{24,28},{28,24},{1,5},{5... | collective-permute-start | bytes 2359304 | tf_op jit(solution)/shard_map/ppermute | solution.py:22
  72.1 31.5 %collective-permute-start.19 = (bf16[2,2,4,3,128,128]{5,4,3,2,1,0:T(8,128)(2,1)S(1)}, bf16[2,2,4,3,128,128]{5,4,3,2,1,0:T(8,128)(2,1)S(1)}, u32[]{:S(2)}, u32[]{:S(2)}) collective-permute-start(bf16[2,2,4,3,128,128]{5,4,3,2,1,0:T(8,128)(2,1)S(1)} %pad_maximum_fusion.9.refs_4_.refs_6_), channel_id=1, source_target_pairs={{0,1},{1,0},{2,3},{3,2},{4,5},{5,4},{6,7},{7,6},{8,9},{9,8},{10,11... | collective-permute-start | bytes 4718600 | tf_op jit(solution)/shard_map/ppermute | solution.py:22
  75.6 30.4 %collective-permute-start.20 = (bf16[2,2,4,3,128,128]{5,4,3,2,1,0:T(8,128)(2,1)S(1)}, bf16[2,2,4,3,128,128]{5,4,3,2,1,0:T(8,128)(2,1)S(1)}, u32[]{:S(2)}, u32[]{:S(2)}) collective-permute-start(bf16[2,2,4,3,128,128]{5,4,3,2,1,0:T(8,128)(2,1)S(1)} %pad_maximum_fusion.10.refs_6_.refs_8_), channel_id=1, source_target_pairs={{0,1},{1,0},{2,3},{3,2},{4,5},{5,4},{6,7},{7,6},{8,9},{9,8},{10,11... | collective-permute-start | bytes 4718600 | tf_op jit(solution)/shard_map/ppermute | solution.py:22
  76.1 19.1 %collective-permute-start.22 = (bf16[4,6,128,128]{3,2,1,0:T(8,128)(2,1)S(1)}, bf16[4,6,128,128]{3,2,1,0:T(8,128)(2,1)S(1)}, u32[]{:S(2)}, u32[]{:S(2)}) collective-permute-start(bf16[4,6,128,128]{3,2,1,0:T(8,128)(2,1)S(1)} %pad_maximum_fusion.16), channel_id=1, source_target_pairs={{0,2},{1,3},{2,0},{3,1},{4,6},{5,7},{6,4},{7,5},{8,10},{9,11},{10,... | collective-permute-start | bytes 2359304 | tf_op jit(solution)/shard_map/ppermute | solution.py:22
  96.6 38.1 %collective-permute-start.26 = (bf16[2,4,6,128,128]{4,3,2,1,0:T(8,128)(2,1)}, bf16[2,4,6,128,128]{4,3,2,1,0:T(8,128)(2,1)}, u32[]{:S(2)}, u32[]{:S(2)}) collective-permute-start(bf16[2,4,6,128,128]{4,3,2,1,0:T(8,128)(2,1)} %pad_maximum_fusion.11), channel_id=1, source_target_pairs={{0,4},{4,0},{8,12},{12,8},{16,20},{20,16},{24,28},{28,24},{1,5},{5... | collective-permute-start | bytes 4718600 | tf_op jit(solution)/shard_map/ppermute | solution.py:22
  98.9 35.8 %collective-permute-start.25 = (bf16[2,4,5,128,128]{4,3,2,1,0:T(8,128)(2,1)}, bf16[2,4,5,128,128]{4,3,2,1,0:T(8,128)(2,1)}, u32[]{:S(2)}, u32[]{:S(2)}) collective-permute-start(bf16[2,4,5,128,128]{4,3,2,1,0:T(8,128)(2,1)} %pad_maximum_fusion.15), channel_id=1, source_target_pairs={{0,2},{1,3},{2,0},{3,1},{4,6},{5,7},{6,4},{7,5},{8,10},{9,11},{10,... | collective-permute-start | bytes 3932168 | tf_op jit(solution)/shard_map/ppermute | solution.py:22
  99.2 19.6 %collective-permute-start.8 = (bf16[12,128,128]{2,1,0:T(8,128)(2,1)}, bf16[12,128,128]{2,1,0:T(8,128)(2,1)}, u32[]{:S(2)}, u32[]{:S(2)}) collective-permute-start(bf16[12,128,128]{2,1,0:T(8,128)(2,1)} %pad_maximum_fusion.27), channel_id=1, source_target_pairs={{0,8},{4,12},{8,16},{12,20},{16,24},{20,28},{24,0},{28,4},{1,9},{5... | collective-permute-start | bytes 1179656 | tf_op jit(solution)/shard_map/ppermute | solution.py:32
  104.7 26.7 %collective-permute-start.9 = (bf16[12,128,128]{2,1,0:T(8,128)(2,1)}, bf16[12,128,128]{2,1,0:T(8,128)(2,1)}, u32[]{:S(2)}, u32[]{:S(2)}) collective-permute-start(bf16[12,128,128]{2,1,0:T(8,128)(2,1)} %pad_maximum_fusion.27), channel_id=1, source_target_pairs={{0,16},{4,20},{8,24},{12,28},{16,0},{20,4},{24,8},{28,12},{1,17},{... | collective-permute-start | bytes 1179656 | tf_op jit(solution)/shard_map/ppermute | solution.py:32
  107.2 24.1 %collective-permute-start.10 = (bf16[12,128,128]{2,1,0:T(8,128)(2,1)}, bf16[12,128,128]{2,1,0:T(8,128)(2,1)}, u32[]{:S(2)}, u32[]{:S(2)}) collective-permute-start(bf16[12,128,128]{2,1,0:T(8,128)(2,1)} %pad_maximum_fusion.27), channel_id=1, source_target_pairs={{0,24},{4,28},{8,0},{12,4},{16,8},{20,12},{24,16},{28,20},{1,25},{... | collective-permute-start | bytes 1179656 | tf_op jit(solution)/shard_map/ppermute | solution.py:32
  133.1 18.6 %collective-permute-start.23 = (bf16[4,6,128,128]{3,2,1,0:T(8,128)(2,1)S(1)}, bf16[4,6,128,128]{3,2,1,0:T(8,128)(2,1)S(1)}, u32[]{:S(2)}, u32[]{:S(2)}) collective-permute-start(bf16[4,6,128,128]{3,2,1,0:T(8,128)(2,1)S(1)} %get-tuple-element.245), channel_id=1, source_target_pairs={{0,4},{4,0},{8,12},{12,8},{16,20},{20,16},{24,28},{28,24},{1,5},{5... | collective-permute-start | bytes 2359304 | tf_op jit(solution)/shard_map/ppermute | solution.py:22
  133.4 28.1 %collective-permute-start.24 = (bf16[4,6,128,128]{3,2,1,0:T(8,128)(2,1)S(1)}, bf16[4,6,128,128]{3,2,1,0:T(8,128)(2,1)S(1)}, u32[]{:S(2)}, u32[]{:S(2)}) collective-permute-start(bf16[4,6,128,128]{3,2,1,0:T(8,128)(2,1)S(1)} %get-tuple-element.247), channel_id=1, source_target_pairs={{0,2},{1,3},{2,0},{3,1},{4,6},{5,7},{6,4},{7,5},{8,10},{9,11},{10,... | collective-permute-start | bytes 2359304 | tf_op jit(solution)/shard_map/ppermute | solution.py:22
  138.6 51.9 %collective-permute-start.34 = (bf16[2,2,4,6,128,128]{5,4,3,2,1,0:T(8,128)(2,1)}, bf16[2,2,4,6,128,128]{5,4,3,2,1,0:T(8,128)(2,1)}, u32[]{:S(2)}, u32[]{:S(2)}) collective-permute-start(bf16[2,2,4,6,128,128]{5,4,3,2,1,0:T(8,128)(2,1)} %pad_maximum_fusion.3.refs_11_.refs_12_), channel_id=1, source_target_pairs={{0,1},{1,0},{2,3},{3,2},{4,5},{5,4},{6,7},{7,6},{8,9},{9,8},{10,11... | collective-permute-start | bytes 9437192 | tf_op jit(solution)/shard_map/ppermute | solution.py:22
  139.7 27.6 %collective-permute-start.29 = (bf16[2,2,33,16,128]{4,3,2,1,0:T(8,128)(2,1)S(1)}, bf16[2,2,33,16,128]{4,3,2,1,0:T(8,128)(2,1)S(1)}, u32[]{:S(2)}, u32[]{:S(2)}) collective-permute-start(bf16[2,2,33,16,128]{4,3,2,1,0:T(8,128)(2,1)S(1)} %copy-done.94), channel_id=1, source_target_pairs={{0,8},{4,12},{8,16},{12,20},{16,24},{20,28},{24,0},{28,4},{1,9},{5... | collective-permute-start | bytes 1622024 | tf_op jit(solution)/shard_map/ppermute | solution.py:32
  148.4 36.7 %collective-permute-start.30 = (bf16[2,2,33,16,128]{4,3,2,1,0:T(8,128)(2,1)S(1)}, bf16[2,2,33,16,128]{4,3,2,1,0:T(8,128)(2,1)S(1)}, u32[]{:S(2)}, u32[]{:S(2)}) collective-permute-start(bf16[2,2,33,16,128]{4,3,2,1,0:T(8,128)(2,1)S(1)} %copy-done.94), channel_id=1, source_target_pairs={{0,16},{4,20},{8,24},{12,28},{16,0},{20,4},{24,8},{28,12},{1,17},{... | collective-permute-start | bytes 1622024 | tf_op jit(solution)/shard_map/ppermute | solution.py:32
  151.7 33.3 %collective-permute-start.31 = (bf16[2,2,33,16,128]{4,3,2,1,0:T(8,128)(2,1)S(1)}, bf16[2,2,33,16,128]{4,3,2,1,0:T(8,128)(2,1)S(1)}, u32[]{:S(2)}, u32[]{:S(2)}) collective-permute-start(bf16[2,2,33,16,128]{4,3,2,1,0:T(8,128)(2,1)S(1)} %copy-done.94), channel_id=1, source_target_pairs={{0,24},{4,28},{8,0},{12,4},{16,8},{20,12},{24,16},{28,20},{1,25},{... | collective-permute-start | bytes 1622024 | tf_op jit(solution)/shard_map/ppermute | solution.py:32
  161.5 29.0 %collective-permute-start.33 = (bf16[2,2,4,5,128,128]{5,4,3,2,1,0:T(8,128)(2,1)}, bf16[2,2,4,5,128,128]{5,4,3,2,1,0:T(8,128)(2,1)}, u32[]{:S(2)}, u32[]{:S(2)}) collective-permute-start(bf16[2,2,4,5,128,128]{5,4,3,2,1,0:T(8,128)(2,1)} %pad_maximum_fusion.6.refs_9_.refs_10_), channel_id=1, source_target_pairs={{0,1},{1,0},{2,3},{3,2},{4,5},{5,4},{6,7},{7,6},{8,9},{9,8},{10,11... | collective-permute-start | bytes 7864328 | tf_op jit(solution)/shard_map/ppermute | solution.py:22
  186.6 21.4 %collective-permute-start.32 = (bf16[4,2,2,33,16,128]{5,4,3,2,1,0:T(8,128)(2,1)}, bf16[4,2,2,33,16,128]{5,4,3,2,1,0:T(8,128)(2,1)}, u32[]{:S(2)}, u32[]{:S(2)}) collective-permute-start(bf16[4,2,2,33,16,128]{5,4,3,2,1,0:T(8,128)(2,1)} %pad_maximum_fusion.7.own_ref), channel_id=1, source_target_pairs={{0,1},{1,0},{2,3},{3,2},{4,5},{5,4},{6,7},{7,6},{8,9},{9,8},{10,11... | collective-permute-start | bytes 6488072 | tf_op jit(solution)/shard_map/ppermute | solution.py:22
  187.4 36.4 %collective-permute-start.27 = (bf16[2,4,6,128,128]{4,3,2,1,0:T(8,128)(2,1)}, bf16[2,4,6,128,128]{4,3,2,1,0:T(8,128)(2,1)}, u32[]{:S(2)}, u32[]{:S(2)}) collective-permute-start(bf16[2,4,6,128,128]{4,3,2,1,0:T(8,128)(2,1)} %pad_maximum_fusion.13), channel_id=1, source_target_pairs={{0,2},{1,3},{2,0},{3,1},{4,6},{5,7},{6,4},{7,5},{8,10},{9,11},{10,... | collective-permute-start | bytes 4718600 | tf_op jit(solution)/shard_map/ppermute | solution.py:22
  188.3 36.0 %collective-permute-start.28 = (bf16[2,4,6,128,128]{4,3,2,1,0:T(8,128)(2,1)}, bf16[2,4,6,128,128]{4,3,2,1,0:T(8,128)(2,1)}, u32[]{:S(2)}, u32[]{:S(2)}) collective-permute-start(bf16[2,4,6,128,128]{4,3,2,1,0:T(8,128)(2,1)} %pad_maximum_fusion.14), channel_id=1, source_target_pairs={{0,4},{4,0},{8,12},{12,8},{16,20},{20,16},{24,28},{28,24},{1,5},{5... | collective-permute-start | bytes 4718600 | tf_op jit(solution)/shard_map/ppermute | solution.py:22
  612.2 32.3 %collective-permute-start.85 = (bf16[2,2,4,6,128,128]{5,4,3,2,1,0:T(8,128)(2,1)}, bf16[2,2,4,6,128,128]{5,4,3,2,1,0:T(8,128)(2,1)}, u32[]{:S(2)}, u32[]{:S(2)}) collective-permute-start(bf16[2,2,4,6,128,128]{5,4,3,2,1,0:T(8,128)(2,1)} %get-tuple-element.333), channel_id=1, source_target_pairs={{0,1},{1,0},{2,3},{3,2},{4,5},{5,4},{6,7},{7,6},{8,9},{9,8},{10,11... | collective-permute-start | bytes 9437192 | tf_op jit(solution)/shard_map/ppermute | solution.py:22
  616.9 32.9 %collective-permute-start.82 = (bf16[2,2,4,6,128,128]{5,4,3,2,1,0:T(8,128)(2,1)}, bf16[2,2,4,6,128,128]{5,4,3,2,1,0:T(8,128)(2,1)}, u32[]{:S(2)}, u32[]{:S(2)}) collective-permute-start(bf16[2,2,4,6,128,128]{5,4,3,2,1,0:T(8,128)(2,1)} %get-tuple-element.328), channel_id=1, source_target_pairs={{0,1},{1,0},{2,3},{3,2},{4,5},{5,4},{6,7},{7,6},{8,9},{9,8},{10,11... | collective-permute-start | bytes 9437192 | tf_op jit(solution)/shard_map/ppermute | solution.py:22
  638.0 45.1 %collective-permute-start.77 = (bf16[2,2,4,6,128,128]{5,4,3,2,1,0:T(8,128)(2,1)}, bf16[2,2,4,6,128,128]{5,4,3,2,1,0:T(8,128)(2,1)}, u32[]{:S(2)}, u32[]{:S(2)}) collective-permute-start(bf16[2,2,4,6,128,128]{5,4,3,2,1,0:T(8,128)(2,1)} %get-tuple-element.316), channel_id=1, source_target_pairs={{0,1},{1,0},{2,3},{3,2},{4,5},{5,4},{6,7},{7,6},{8,9},{9,8},{10,11... | collective-permute-start | bytes 9437192 | tf_op jit(solution)/shard_map/ppermute | solution.py:22
  639.9 19.1 %collective-permute-start.78 = (bf16[2,2,4,5,128,128]{5,4,3,2,1,0:T(8,128)(2,1)}, bf16[2,2,4,5,128,128]{5,4,3,2,1,0:T(8,128)(2,1)}, u32[]{:S(2)}, u32[]{:S(2)}) collective-permute-start(bf16[2,2,4,5,128,128]{5,4,3,2,1,0:T(8,128)(2,1)} %get-tuple-element.318), channel_id=1, source_target_pairs={{0,1},{1,0},{2,3},{3,2},{4,5},{5,4},{6,7},{7,6},{8,9},{9,8},{10,11... | collective-permute-start | bytes 7864328 | tf_op jit(solution)/shard_map/ppermute | solution.py:22
  648.5 66.0 %collective-permute-start.86 = (bf16[2,4,6,128,128]{4,3,2,1,0:T(8,128)(2,1)}, bf16[2,4,6,128,128]{4,3,2,1,0:T(8,128)(2,1)}, u32[]{:S(2)}, u32[]{:S(2)}) collective-permute-start(bf16[2,4,6,128,128]{4,3,2,1,0:T(8,128)(2,1)} %fusion.13), channel_id=1, source_target_pairs={{0,4},{4,0},{8,12},{12,8},{16,20},{20,16},{24,28},{28,24},{1,5},{5... | collective-permute-start | bytes 4718600 | tf_op jit(solution)/shard_map/ppermute | solution.py:22
  654.8 63.5 %collective-permute-start.87 = (bf16[2,4,6,128,128]{4,3,2,1,0:T(8,128)(2,1)}, bf16[2,4,6,128,128]{4,3,2,1,0:T(8,128)(2,1)}, u32[]{:S(2)}, u32[]{:S(2)}) collective-permute-start(bf16[2,4,6,128,128]{4,3,2,1,0:T(8,128)(2,1)} %fusion.12.tie_ref), channel_id=1, source_target_pairs={{0,2},{1,3},{2,0},{3,1},{4,6},{5,7},{6,4},{7,5},{8,10},{9,11},{10,... | collective-permute-start | bytes 4718600 | tf_op jit(solution)/shard_map/ppermute | solution.py:22
  661.4 67.0 %collective-permute-start.79 = (bf16[2,4,5,128,128]{4,3,2,1,0:T(8,128)(2,1)S(1)}, bf16[2,4,5,128,128]{4,3,2,1,0:T(8,128)(2,1)}, u32[]{:S(2)}, u32[]{:S(2)}) collective-permute-start(bf16[2,4,5,128,128]{4,3,2,1,0:T(8,128)(2,1)S(1)} %fusion.14.tie_ref), channel_id=1, source_target_pairs={{0,4},{4,0},{8,12},{12,8},{16,20},{20,16},{24,28},{28,24},{1,5},{5... | collective-permute-start | bytes 3932168 | tf_op jit(solution)/shard_map/ppermute | solution.py:22
  691.1 35.2 %collective-permute-start.81 = (bf16[2,2,4,33,16,128]{5,4,3,2,1,0:T(8,128)(2,1)}, bf16[2,2,4,33,16,128]{5,4,3,2,1,0:T(8,128)(2,1)}, u32[]{:S(2)}, u32[]{:S(2)}) collective-permute-start(bf16[2,2,4,33,16,128]{5,4,3,2,1,0:T(8,128)(2,1)} %get-tuple-element.326), channel_id=1, source_target_pairs={{0,1},{1,0},{2,3},{3,2},{4,5},{5,4},{6,7},{7,6},{8,9},{9,8},{10,11... | collective-permute-start | bytes 6488072 | tf_op jit(solution)/shard_map/ppermute | solution.py:22
  692.1 31.1 %collective-permute-start.83 = (bf16[2,2,4,3,128,128]{5,4,3,2,1,0:T(8,128)(2,1)S(1)}, bf16[2,2,4,3,128,128]{5,4,3,2,1,0:T(8,128)(2,1)S(1)}, u32[]{:S(2)}, u32[]{:S(2)}) collective-permute-start(bf16[2,2,4,3,128,128]{5,4,3,2,1,0:T(8,128)(2,1)S(1)} %copy-done.78), channel_id=1, source_target_pairs={{0,1},{1,0},{2,3},{3,2},{4,5},{5,4},{6,7},{7,6},{8,9},{9,8},{10,11... | collective-permute-start | bytes 4718600 | tf_op jit(solution)/shard_map/ppermute | solution.py:22
  718.4 36.1 %collective-permute-start.80 = (bf16[2,4,6,128,128]{4,3,2,1,0:T(8,128)(2,1)S(1)}, bf16[2,4,6,128,128]{4,3,2,1,0:T(8,128)(2,1)S(1)}, u32[]{:S(2)}, u32[]{:S(2)}) collective-permute-start(bf16[2,4,6,128,128]{4,3,2,1,0:T(8,128)(2,1)S(1)} %fusion.11.tie_ref), channel_id=1, source_target_pairs={{0,2},{1,3},{2,0},{3,1},{4,6},{5,7},{6,4},{7,5},{8,10},{9,11},{10,... | collective-permute-start | bytes 4718600 | tf_op jit(solution)/shard_map/ppermute | solution.py:22
  723.2 48.1 %collective-permute-start.93 = (bf16[4,6,128,128]{3,2,1,0:T(8,128)(2,1)S(1)}, bf16[4,6,128,128]{3,2,1,0:T(8,128)(2,1)S(1)}, u32[]{:S(2)}, u32[]{:S(2)}) collective-permute-start(bf16[4,6,128,128]{3,2,1,0:T(8,128)(2,1)S(1)} %fusion.22), channel_id=1, source_target_pairs={{0,2},{1,3},{2,0},{3,1},{4,6},{5,7},{6,4},{7,5},{8,10},{9,11},{10,... | collective-permute-start | bytes 2359304 | tf_op jit(solution)/shard_map/ppermute | solution.py:22
  724.7 48.8 %collective-permute-start.91 = (bf16[2,4,3,128,128]{4,3,2,1,0:T(8,128)(2,1)S(1)}, bf16[2,4,3,128,128]{4,3,2,1,0:T(8,128)(2,1)S(1)}, u32[]{:S(2)}, u32[]{:S(2)}) collective-permute-start(bf16[2,4,3,128,128]{4,3,2,1,0:T(8,128)(2,1)S(1)} %fusion.20), channel_id=1, source_target_pairs={{0,4},{4,0},{8,12},{12,8},{16,20},{20,16},{24,28},{28,24},{1,5},{5... | collective-permute-start | bytes 2359304 | tf_op jit(solution)/shard_map/ppermute | solution.py:22
  726.3 61.8 %collective-permute-start.92 = (bf16[2,4,3,128,128]{4,3,2,1,0:T(8,128)(2,1)S(1)}, bf16[2,4,3,128,128]{4,3,2,1,0:T(8,128)(2,1)S(1)}, u32[]{:S(2)}, u32[]{:S(2)}) collective-permute-start(bf16[2,4,3,128,128]{4,3,2,1,0:T(8,128)(2,1)S(1)} %fusion.21), channel_id=1, source_target_pairs={{0,2},{1,3},{2,0},{3,1},{4,6},{5,7},{6,4},{7,5},{8,10},{9,11},{10,... | collective-permute-start | bytes 2359304 | tf_op jit(solution)/shard_map/ppermute | solution.py:22
  728.3 43.1 %collective-permute-start.94 = (bf16[4,6,128,128]{3,2,1,0:T(8,128)(2,1)S(1)}, bf16[4,6,128,128]{3,2,1,0:T(8,128)(2,1)S(1)}, u32[]{:S(2)}, u32[]{:S(2)}) collective-permute-start(bf16[4,6,128,128]{3,2,1,0:T(8,128)(2,1)S(1)} %fusion.23), channel_id=1, source_target_pairs={{0,4},{4,0},{8,12},{12,8},{16,20},{20,16},{24,28},{28,24},{1,5},{5... | collective-permute-start | bytes 2359304 | tf_op jit(solution)/shard_map/ppermute | solution.py:22
  754.4 35.9 %collective-permute-start.90 = (bf16[2,4,33,16,128]{4,3,2,1,0:T(8,128)(2,1)S(1)}, bf16[2,4,33,16,128]{4,3,2,1,0:T(8,128)(2,1)S(1)}, u32[]{:S(2)}, u32[]{:S(2)}) collective-permute-start(bf16[2,4,33,16,128]{4,3,2,1,0:T(8,128)(2,1)S(1)} %fusion.19), channel_id=1, source_target_pairs={{0,4},{4,0},{8,12},{12,8},{16,20},{20,16},{24,28},{28,24},{1,5},{5... | collective-permute-start | bytes 3244040 | tf_op jit(solution)/shard_map/ppermute | solution.py:22
  771.3 30.9 %collective-permute-start.88 = (bf16[4,5,128,128]{3,2,1,0:T(8,128)(2,1)S(1)}, bf16[4,5,128,128]{3,2,1,0:T(8,128)(2,1)S(1)}, u32[]{:S(2)}, u32[]{:S(2)}) collective-permute-start(bf16[4,5,128,128]{3,2,1,0:T(8,128)(2,1)S(1)} %fusion.29), channel_id=1, source_target_pairs={{0,2},{1,3},{2,0},{3,1},{4,6},{5,7},{6,4},{7,5},{8,10},{9,11},{10,... | collective-permute-start | bytes 1966088 | tf_op jit(solution)/shard_map/ppermute | solution.py:22
  771.5 30.9 %collective-permute-start.89 = (bf16[4,6,128,128]{3,2,1,0:T(8,128)(2,1)S(1)}, bf16[4,6,128,128]{3,2,1,0:T(8,128)(2,1)S(1)}, u32[]{:S(2)}, u32[]{:S(2)}) collective-permute-start(bf16[4,6,128,128]{3,2,1,0:T(8,128)(2,1)S(1)} %fusion.24), channel_id=1, source_target_pairs={{0,4},{4,0},{8,12},{12,8},{16,20},{20,16},{24,28},{28,24},{1,5},{5... | collective-permute-start | bytes 2359304 | tf_op jit(solution)/shard_map/ppermute | solution.py:22
  773.5 52.8 %collective-permute-start.98 = (bf16[12,128,128]{2,1,0:T(8,128)(2,1)S(1)}, bf16[12,128,128]{2,1,0:T(8,128)(2,1)S(1)}, u32[]{:S(2)}, u32[]{:S(2)}) collective-permute-start(bf16[12,128,128]{2,1,0:T(8,128)(2,1)S(1)} %get-tuple-element.557), channel_id=1, source_target_pairs={{0,8},{4,12},{8,16},{12,20},{16,24},{20,28},{24,0},{28,4},{1,9},{5... | collective-permute-start | bytes 1179656 | tf_op jit(solution)/shard_map/ppermute | solution.py:32
  788.1 40.6 %collective-permute-start.99 = (bf16[12,128,128]{2,1,0:T(8,128)(2,1)S(1)}, bf16[12,128,128]{2,1,0:T(8,128)(2,1)S(1)}, u32[]{:S(2)}, u32[]{:S(2)}) collective-permute-start(bf16[12,128,128]{2,1,0:T(8,128)(2,1)S(1)} %get-tuple-element.556), channel_id=1, source_target_pairs={{0,16},{4,20},{8,24},{12,28},{16,0},{20,4},{24,8},{28,12},{1,17},{... | collective-permute-start | bytes 1179656 | tf_op jit(solution)/shard_map/ppermute | solution.py:32
  790.4 38.4 %collective-permute-start.100 = (bf16[12,128,128]{2,1,0:T(8,128)(2,1)S(1)}, bf16[12,128,128]{2,1,0:T(8,128)(2,1)S(1)}, u32[]{:S(2)}, u32[]{:S(2)}) collective-permute-start(bf16[12,128,128]{2,1,0:T(8,128)(2,1)S(1)} %get-tuple-element.555), channel_id=1, source_target_pairs={{0,24},{4,28},{8,0},{12,4},{16,8},{20,12},{24,16},{28,20},{1,25},{... | collective-permute-start | bytes 1179656 | tf_op jit(solution)/shard_map/ppermute | solution.py:32
  828.7 36.2 %collective-permute-start.105 = (bf16[6,128,128]{2,1,0:T(8,128)(2,1)}, bf16[6,128,128]{2,1,0:T(8,128)(2,1)}, u32[]{:S(2)}, u32[]{:S(2)}) collective-permute-start(bf16[6,128,128]{2,1,0:T(8,128)(2,1)} %get-tuple-element.569), channel_id=1, source_target_pairs={{0,8},{4,12},{8,16},{12,20},{16,24},{20,28},{24,0},{28,4},{1,9},{5... | collective-permute-start | bytes 589832 | tf_op jit(solution)/shard_map/ppermute | solution.py:32
  828.8 36.2 %collective-permute-start.106 = (bf16[6,128,128]{2,1,0:T(8,128)(2,1)}, bf16[6,128,128]{2,1,0:T(8,128)(2,1)}, u32[]{:S(2)}, u32[]{:S(2)}) collective-permute-start(bf16[6,128,128]{2,1,0:T(8,128)(2,1)} %get-tuple-element.568), channel_id=1, source_target_pairs={{0,16},{4,20},{8,24},{12,28},{16,0},{20,4},{24,8},{28,12},{1,17},{... | collective-permute-start | bytes 589832 | tf_op jit(solution)/shard_map/ppermute | solution.py:32
  829.6 41.8 %collective-permute-start.107 = (bf16[6,128,128]{2,1,0:T(8,128)(2,1)S(1)}, bf16[6,128,128]{2,1,0:T(8,128)(2,1)}, u32[]{:S(2)}, u32[]{:S(2)}) collective-permute-start(bf16[6,128,128]{2,1,0:T(8,128)(2,1)S(1)} %get-tuple-element.567), channel_id=1, source_target_pairs={{0,24},{4,28},{8,0},{12,4},{16,8},{20,12},{24,16},{28,20},{1,25},{... | collective-permute-start | bytes 589832 | tf_op jit(solution)/shard_map/ppermute | solution.py:32
  842.8 32.8 %collective-permute-start.110 = (bf16[33,16,128]{2,1,0:T(8,128)(2,1)}, bf16[33,16,128]{2,1,0:T(8,128)(2,1)}, u32[]{:S(2)}, u32[]{:S(2)}) collective-permute-start(bf16[33,16,128]{2,1,0:T(8,128)(2,1)} %get-tuple-element.580), channel_id=1, source_target_pairs={{0,8},{4,12},{8,16},{12,20},{16,24},{20,28},{24,0},{28,4},{1,9},{5... | collective-permute-start | bytes 405512 | tf_op jit(solution)/shard_map/ppermute | solution.py:32
  865.0 18.1 %collective-permute-start.104 = (bf16[11,128,64]{2,1,0:T(8,128)(2,1)}, bf16[11,128,64]{2,1,0:T(8,128)(2,1)}, u32[]{:S(2)}, u32[]{:S(2)}) collective-permute-start(bf16[11,128,64]{2,1,0:T(8,128)(2,1)} %bitcast.465), channel_id=1, source_target_pairs={{0,1},{1,0},{2,3},{3,2},{4,5},{5,4},{6,7},{7,6},{8,9},{9,8},{10,11... | collective-permute-start | bytes 540680 | tf_op jit(solution)/shard_map/ppermute | solution.py:22
  (314 other events, 3907.5 us)

commit v3 on v2

--- a/solution.py
+++ b/solution.py
@@ -32,38 +32,30 @@
     return lax.ppermute(values, axis, pairs)
 
 
-def bits_of(axis):
-    size = lax.axis_size(axis)
-    bits = []
-    bit = 1
-    while bit < size:
-        bits.append((axis, bit))
-        bit = bit * 2
-    return bits
-
-
-def sum_all(values):
-    for axis, bit in bits_of("narrow") + bits_of("wide"):
-        values = values + exchange(values, axis, bit)
-    return values
-
-
-def merge_all(counts, means, squares):
-    for axis, bit in bits_of("narrow") + bits_of("wide"):
-        other = exchange(jnp.stack([counts, means, squares]), axis, bit)
-        total = counts + other[0]
-        gap = means - other[1]
-        squares = squares + other[2] + gap * gap * (counts * other[0] / total)
-        means = (counts * means + other[0] * other[1]) / total
-        counts = total
-    return (counts, means, squares)
+def device_count():
+    return lax.axis_size("wide") * lax.axis_size("narrow")
+
+
+def hand_out(rows):
+    return lax.all_to_all(rows, ("wide", "narrow"), 0, 0, tiled=True)
+
+
+def from_all(values):
+    return hand_out(jnp.broadcast_to(values[None], (device_count(),) + values.shape))
+
+
+def merge_rows(counts, means, squares):
+    total = jnp.sum(counts, axis=0)
+    mean = jnp.sum(counts * means, axis=0) / total
+    gap = means - mean[None]
+    return (total, mean, jnp.sum(squares + counts * gap * gap, axis=0))
 
 
 def local_moments(values, valid_map, count):
     axes = tuple(range(values.ndim - 1))
     mean = jnp.sum(values * valid_map, axis=axes) / count
     centered = values - mean
-    return (jnp.full_like(mean, 1.0) * count, mean, jnp.sum(centered * centered * valid_map, axis=axes))
+    return (mean, jnp.sum(centered * centered * valid_map, axis=axes))
 
 
 def place():
@@ -109,6 +101,111 @@
 
     def run(self, function, *values):
         return self.give(function(*self.take(values)))
+
+
+def one_step(body, outs, args, specs=None, tie=None):
+    def whole_spec(array):
+        return pl.BlockSpec(array.shape, lambda step: (0,) * len(array.shape))
+
+    specs = list(specs or [None] * len(args))
+    run = body
+    if tie is not None:
+        args = [tie] + list(args)
+        specs = [pl.BlockSpec(memory_space=pl.ANY)] + specs
+
+        def run(tie_ref, *refs):
+            body(*refs)
+
+    return pl.pallas_call(
+        run,
+        out_shape=outs,
+        grid=(1,),
+        in_specs=[spec or whole_spec(arg) for spec, arg in zip(specs, args)],
+        out_specs=[whole_spec(out) for out in outs],
+        compiler_params=pltpu.CompilerParams(vmem_limit_bytes=VMEM_BYTES),
+        cost_estimate=cost(0, args),
+        name="move",
+    )(*args)
+
+
+def entry_spec(array, index):
+    block = (1,) + array.shape[1:]
+    return pl.BlockSpec(block, lambda step: (index,) + (0,) * (len(block) - 1))
+
+
+def cut(sizes):
+    return [slice(sum(sizes[:index]), sum(sizes[: index + 1])) for index in range(len(sizes))]
+
+
+def first_sums(sizes, keep, got, tie=None):
+    tail = keep.shape[4:]
+    outs = [jax.ShapeDtypeStruct((2, ROUNDS, size) + tail, jnp.bfloat16) for size in sizes]
+
+    def body(keep_ref, got_ref, *targets):
+        for target, taps in zip(targets, cut(sizes)):
+            total = keep_ref[0, :, :, taps].astype(jnp.float32)
+            total = total + got_ref[0, :, :, taps].astype(jnp.float32)
+            target[...] = total.astype(jnp.bfloat16)
+
+    return one_step(body, outs, [keep, got], [entry_spec(keep, 1), entry_spec(got, 1)], tie)
+
+
+def second_sums(sizes, keep, got, values, tie=None):
+    tail = keep.shape[4:]
+    outs = [jax.ShapeDtypeStruct((ROUNDS, sum(sizes)) + tail, jnp.float32)]
+    outs += [jax.ShapeDtypeStruct((ROUNDS, size) + tail, jnp.bfloat16) for size in sizes]
+    count = len(sizes)
+
+    def body(keep_ref, got_ref, *refs):
+        kept = refs[count]
+        for index, taps in enumerate(cut(sizes)):
+            for half in range(2):
+                total = keep_ref[0, half, :, taps].astype(jnp.float32)
+                total = total + got_ref[0, half, :, taps].astype(jnp.float32)
+                total = total + refs[index][half].astype(jnp.float32)
+                if half:
+                    refs[count + 1 + index][...] = total.astype(jnp.bfloat16)
+                else:
+                    kept[:, taps] = total
+
+    specs = [entry_spec(keep, 0), entry_spec(got, 0)] + [None] * count
+    results = one_step(body, outs, [keep, got] + list(values), specs, tie)
+    return (results[0], results[1:])
+
+
+def deep_sums(sizes, kept, values, tie=None):
+    shape = (2,) + kept.shape[1:]
+    outs = [jax.ShapeDtypeStruct(shape, dtype) for dtype in (jnp.float32, jnp.bfloat16)]
+    count = len(sizes)
+
+    def body(kept_ref, *refs):
+        for slot in range(ROUNDS):
+            target = refs[count + slot // 2]
+            for value, taps in zip(refs, cut(sizes)):
+                total = kept_ref[slot, taps] + value[slot].astype(jnp.float32)
+                target[slot % 2, taps] = total.astype(target.dtype)
+
+    return one_step(body, outs, [kept] + list(values), None, tie)
+
+
+def near_sums(kept, far, tie=None):
+    shape = kept.shape[1:]
+    outs = [jax.ShapeDtypeStruct(shape, dtype) for dtype in (jnp.float32, jnp.bfloat16)]
+
+    def body(kept_ref, far_ref, *targets):
+        for slot, target in enumerate(targets):
+            total = kept_ref[slot] + far_ref[slot].astype(jnp.float32)
+            target[...] = total.astype(target.dtype)
+
+    return one_step(body, outs, [kept, far], None, tie)
+
+
+def last_sums(kept, near, tie=None):
+    def body(kept_ref, near_ref, target):
+        target[...] = kept_ref[...] + near_ref[...].astype(jnp.float32)
+
+    outs = [jax.ShapeDtypeStruct(kept.shape, jnp.float32)]
+    return one_step(body, outs, [kept, near], None, tie)[0]
 
 
 def chunk_order(index):
@@ -227,9 +324,10 @@
     if not tuned():
         owned = []
         for part, kernel in zip(PARTS, kernels):
+            joined = jnp.stack(kernel(grads))
             pieces = []
-            for index, pair in zip(part, kernel(grads)):
-                piece = jnp.stack(pair)
+            for index, taps in zip(part, cut([CHUNKS[index] for index in part])):
+                piece = joined[:, :, :, :, taps]
                 order = (4, 3, 1, 0, 5, 2, 6) if index % 2 == 0 else (4, 3, 2, 0, 5, 1, 6)
                 piece = piece.transpose(order)
                 pieces.append(piece.reshape(piece.shape[0], -1, 2 * piece.shape[6]))
@@ -244,82 +342,68 @@
         small = unpack_grads(small[0, 0].astype(jnp.float32), shapes)
         return (owned, small, low, fillers[1](None))
 
-    def across(pairs):
-        return [exchange(pair[1], "narrow", 1) for pair in pairs]
-
-    def first(pairs, others):
-        return [narrow(add_wide(pair[0][1], other[1])) for pair, other in zip(pairs, others)]
-
-    def second(pairs, others, values):
-        sent = []
-        kept = []
-        for pair, other, value in zip(pairs, others, values):
-            total = add_wide(pair[0][0], other[0]) + value.astype(jnp.float32)
-            kept.append(total[0])
-            sent.append(narrow(total[1]))
-        return (kept, sent)
+    sizes = [[CHUNKS[index] for index in part] for part in PARTS]
+
+    def across(pair):
+        return (pair[0], exchange(pair[1], "narrow", 1))
 
     def along(indices, values, turn):
         return [
             exchange(value, *chunk_order(index)[turn]) for value, index in zip(values, indices)
         ]
 
-    def deep(kept, values):
-        total = jnp.concatenate(
-            [own + value.astype(jnp.float32) for own, value in zip(kept, values)], axis=1
-        )
-        return (total[0], [narrow(total[step]) for step in range(1, rounds)])
-
-    def turned(values):
-        return [rotate(value, "wide", step + 1, 2) for step, value in enumerate(values)]
-
-    def finish(total, values):
-        for value in values:
-            total = total + value.astype(jnp.float32)
-        return total
-
-    def settle(total, values):
-        return settle_core(finish(total, values))
-
-    order = Order()
+    def far(sent):
+        return exchange(sent, "wide", 4)
+
+    def near(sent):
+        return exchange(sent, "wide", 2)
+
     a, b, c = 2, 1, 0
-    pairs_a = kernels[a](grads)
-    core_a = across(pairs_a)
-    pairs_b = kernels[b](grads, tie=pairs_a[0][0])
-    core_b = across(pairs_b)
-    sent_a = first(pairs_a, core_a)
-    first_a = along(PARTS[a], sent_a, 0)
-    pairs_c = kernels[c](grads, tie=sent_a[1])
-    core_c = across(pairs_c)
-    sent_b = first(pairs_b, core_b)
-    first_b = along(PARTS[b], sent_b, 0)
-    low, low_weight = fillers[0](sent_b[0])
-    pairs_s = [pack_block(pack[0], low_weight, *pack[1:], shapes=shapes, tie=sent_b[1])]
-    core_s = across(pairs_s)
-    filled = fillers[1](sent_b[1])
-    kept_a, sent = order.run(second, pairs_a, core_a, first_a)
+    pair_a = across(kernels[a](grads))
+    pair_b = across(kernels[b](grads, tie=pair_a[0]))
+    sent = first_sums(sizes[a], *pair_a, pair_b[0])
+    first_a = along(PARTS[a], sent, 0)
+    low, low_weight = fillers[0](sent[0])
+    pair_s = across(pack_block(pack[0], low_weight, *pack[1:], shapes=shapes, tie=low_weight))
+    sizes_s = [pair_s[0].shape[3]]
+    pair_c = across(kernels[c](grads, tie=pair_s[0]))
+    kept_a, sent = second_sums(sizes[a], *pair_a, first_a, pair_c[0])
     second_a = along(PARTS[a], sent, 1)
-    first_c = along(PARTS[c], order.run(first, pairs_c, core_c), 0)
-    first_s = along((0,), order.run(first, pairs_s, core_s), 0)
-    kept_b, sent = order.run(second, pairs_b, core_b, first_b)
+    sent = first_sums(sizes[b], *pair_b, sent[0])
+    first_b = along(PARTS[b], sent, 0)
+    kept_a, sent = deep_sums(sizes[a], kept_a, second_a, sent[0])
+    far_a = far(sent)
+    sent = first_sums(sizes_s, *pair_s, sent)
+    first_s = along((0,), sent, 0)
+    filled = fillers[1](sent[0])
+    kept_b, sent = second_sums(sizes[b], *pair_b, first_b, filled)
     second_b = along(PARTS[b], sent, 1)
-    total_a, sent = order.run(deep, kept_a, second_a)
-    deep_a = turned(sent)
-    kept_c, sent = order.run(second, pairs_c, core_c, first_c)
+    sent = first_sums(sizes[c], *pair_c, sent[0])
+    first_c = along(PARTS[c], sent, 0)
+    kept_s, sent = second_sums(sizes_s, *pair_s, first_s, sent[0])
+    second_s = along((0,), sent, 1)
+    total_a, sent = near_sums(kept_a, far_a, sent[0])
+    near_a = near(sent)
+    kept_b, sent = deep_sums(sizes[b], kept_b, second_b, sent)
+    far_b = far(sent)
+    kept_c, sent = second_sums(sizes[c], *pair_c, first_c, sent)
     second_c = along(PARTS[c], sent, 1)
-    kept_s, sent = order.run(second, pairs_s, core_s, first_s)
-    second_s = along((0,), sent, 1)
-    total_b, sent = order.run(deep, kept_b, second_b)
-    deep_b = turned(sent)
-    total_c, sent = order.run(deep, kept_c, second_c)
-    deep_c = turned(sent)
-    total_s, sent = order.run(deep, kept_s, second_s)
-    deep_s = turned(sent)
-    owned = [None, None, None]
-    owned[a] = settle_core(order.run(finish, total_a, deep_a))
-    owned[b] = settle_core(order.run(finish, total_b, deep_b))
-    owned[c] = settle_core(order.run(finish, total_c, deep_c))
-    small = settle_small(order.run(finish, total_s, deep_s), shapes)
+    kept_s, sent = deep_sums(sizes_s, kept_s, second_s, sent[0])
+    far_s = far(sent)
+    total_a = last_sums(total_a, near_a, sent)
+    kept_c, sent = deep_sums(sizes[c], kept_c, second_c, total_a)
+    far_c = far(sent)
+    total_b, sent = near_sums(kept_b, far_b, sent)
+    near_b = near(sent)
+    total_s, sent = near_sums(kept_s, far_s, sent)
+    near_s = near(sent)
+    total_c, sent = near_sums(kept_c, far_c, sent)
+    near_c = near(sent)
+    total_b = last_sums(total_b, near_b, sent)
+    total_s = last_sums(total_s, near_s, total_b)
+    total_c = last_sums(total_c, near_c, total_s)
+    owned = [settle_core(total) for total in (total_c, total_b, total_a)]
+    small = settle_small(total_s, shapes)
     return (owned, small, low, filled)
 
 
@@ -355,6 +439,16 @@
     return [pl.BlockSpec(shape, index_map)] * 2
 
 
+def whole_cost(flops, arrays):
+    total = 0
+    for array in arrays:
+        size = array.dtype.itemsize
+        for extent in array.shape:
+            size *= extent
+        total += size
+    return pl.CostEstimate(flops=int(flops), bytes_accessed=total, transcendentals=0)
+
+
 def cost(flops, arrays):
     return pl.CostEstimate(flops=1, bytes_accessed=1, transcendentals=0)
 
@@ -363,6 +457,22 @@
     height, columns, channels = shape
     extents = sum(row_span(dilations[branch], line, height)[2] for branch, line in rows)
     return 2 * 3 * extents * columns * channels * width
+
+
+def chunk_part(chunk):
+    return [index for index, part in enumerate(PARTS) if chunk in part][0]
+
+
+def chunk_start(chunk):
+    part = PARTS[chunk_part(chunk)]
+    return sum(CHUNKS[index] for index in part[: part.index(chunk)])
+
+
+def part_spec(array):
+    def index_map(step, place_ref):
+        return (0, 0, lax.bitwise_xor(step // 2, place_ref[0]), 0, 0, 0)
+
+    return pl.BlockSpec((2, 2, 1) + array.shape[3:], index_map)
 
 
 def full_spec(array):
@@ -522,9 +632,10 @@
     grads = {branch: refs.pop(0) for branch in plan["branches"]}
     if plan["pool"]:
         point_ref, pooled_ref, pool_ref = refs.pop(0), refs.pop(0), refs.pop(0)
-    outs = {index: (refs.pop(0), refs.pop(0)) for index in plan["chunks"]}
+    outs = (refs.pop(0), refs.pop(0))
     row, core = place_ref[2], place_ref[3]
-    rows, cols = outs[plan["chunks"][0]][0].shape[-2:]
+    flip = lax.rem(pl.program_id(0) + place_ref[1], 2)
+    rows, cols = outs[0].shape[-2:]
     columns = plan["columns"]
 
     def store(chunk, tap, value):
@@ -532,12 +643,13 @@
         lower, upper = value[:rows], value[rows:]
         mine = jnp.where(core == 0, lower, upper)
         other = jnp.where(core == 0, upper, lower)
-        for ref, part in zip(outs[chunk], (mine, other)):
+        place = chunk_start(chunk) + tap
+        for ref, part in zip(outs, (mine, other)):
             for side, lane_part in ((row, part[:, :cols]), (1 - row, part[:, cols:])):
                 if chunk % 2 == 0:
-                    ref[0, side, 0, tap] = lane_part
+                    ref[flip, side, 0, place] = lane_part
                 else:
-                    ref[side, 0, 0, tap] = lane_part
+                    ref[side, flip, 0, place] = lane_part
 
     across = (((0,), (0,)), ((), ()))
     for branch, line, chunk, tap in plan["rows"]:
@@ -594,20 +706,10 @@
         kernel = behind_tie(kernel)
         args.insert(0, tie)
         specs.insert(0, pl.BlockSpec(memory_space=pl.ANY))
-    height_now = center.shape[1] // (4 * ROUNDS)
-    outs = []
-    out_specs = []
-    for index in PARTS[part]:
-        tail = (CHUNKS[index], height_now, channels // 2)
-        block = (1, 2, 1) if index % 2 == 0 else (2, 1, 1)
-
-        def index_map(step, place_ref, x_first=index % 2 == 0):
-            flip = lax.rem(step + place_ref[1], 2)
-            slot = lax.rem(step // 2 - place_ref[0] + ROUNDS, ROUNDS)
-            return (flip, 0, slot, 0, 0, 0) if x_first else (0, flip, slot, 0, 0, 0)
-
-        outs += [jax.ShapeDtypeStruct((2, 2, ROUNDS) + tail, jnp.bfloat16)] * 2
-        out_specs += [pl.BlockSpec(block + tail, index_map)] * 2
+    total = sum(CHUNKS[index] for index in PARTS[part])
+    tail = (total, center.shape[1] // (4 * ROUNDS), channels // 2)
+    outs = [jax.ShapeDtypeStruct((2, 2, ROUNDS) + tail, jnp.bfloat16)] * 2
+    out_specs = [part_spec(item) for item in outs]
     results = pl.pallas_call(
         kernel,
         out_shape=outs,
@@ -622,7 +724,7 @@
         ),
         name="coarse_weight",
     )(kernel_place(), *args)
-    return [(results[0], results[1]), (results[2], results[3])]
+    return (results[0], results[1])
 
 
 def coarse_input_kernel(plan, place_ref, *refs):
@@ -1413,13 +1515,17 @@
 
 
 def moments(values, valid_map, local_count, count_all):
-    counts, means, squares = merge_all(*local_moments(values, valid_map, local_count))
-    return (means, squares / count_all)
+    mean, squares = local_moments(values, valid_map, local_count)
+    return merged(jnp.stack([mean, squares]), local_count, count_all)
 
 
 def merged(stats, local_count, count_all):
-    counts = jnp.full((stats.shape[1],), 1.0) * local_count
-    counts, means, squares = merge_all(counts, stats[0], stats[1])
+    width = stats.shape[1]
+    own = jnp.concatenate([stats[0], stats[1], jnp.full((1,), 1.0) * local_count])
+    rows = from_all(own)
+    counts, means, squares = merge_rows(
+        rows[:, 2 * width :], rows[:, :width], rows[:, width : 2 * width]
+    )
     return (means, squares / count_all)
 
 
@@ -1446,7 +1552,7 @@
 
 
 def gradient_sums(pairs):
-    return unpack_pairs(sum_all(pack_pairs(pairs)), pairs)
+    return unpack_pairs(jnp.sum(from_all(pack_pairs(pairs)), axis=0), pairs)
 
 
 def small_block(items):
@@ -1577,7 +1683,7 @@
         index = (
             lax.rem(x + side, 2),
             lax.rem(y + row, 2),
-            lax.rem(z - deep + ROUNDS, ROUNDS),
+            lax.bitwise_xor(deep, z),
             pl.ds(start, size),
         )
         keep_ref[index] = jnp.where(core == 0, values[0], values[1])
@@ -1659,7 +1765,7 @@
         + [pl.BlockSpec(memory_space=pltpu.VMEM)] * 5,
         out_specs=[pl.BlockSpec(memory_space=pltpu.VMEM)] * 2,
         compiler_params=pltpu.CompilerParams(vmem_limit_bytes=VMEM_BYTES),
-        cost_estimate=cost(0, [proj, decode, low, refine, out, out, out]),
+        cost_estimate=whole_cost(0, [proj, decode, low, refine, out, out, out]),
         name="pack_gradients",
     )(kernel_place(), tie, proj, reduce, decode, low, refine)
 
@@ -1853,24 +1959,28 @@
     ]
     blocks = [(item_z, valid_coarse) for item_z in coarse_z] + [(pool_z, all_ones)]
     local_images = float(canvases * images)
-    states = [
-        (jnp.full((channels,), 1.0) * local_count, item[0], item[1]) for item in coarse_stats
-    ] + [
+    states = [(item[0], item[1]) for item in coarse_stats] + [
         local_moments(pool_z, all_ones, local_images),
-        (
-            jnp.full((extra,), 16.0) * local_count,
-            low_stats[0, :extra],
-            low_stats[1, :extra],
-        ),
     ]
-    counts_flat, means_flat, squares_flat = merge_all(
-        *[jnp.concatenate([state[item] for state in states]) for item in range(3)]
+    own = [state[item] for item in range(2) for state in states]
+    rows = from_all(jnp.concatenate(own + [jnp.full((1,), 1.0) * local_count]))
+    width = 5 * channels
+    pixels = rows[:, 2 * width :]
+    count_rows = jnp.concatenate(
+        [
+            jnp.broadcast_to(pixels, (rows.shape[0], 4 * channels)),
+            jnp.full((rows.shape[0], channels), local_images),
+        ],
+        axis=1,
+    )
+    counts_flat, means_flat, squares_flat = merge_rows(
+        count_rows, rows[:, :width], rows[:, width : 2 * width]
     )
     vars_flat = squares_flat / counts_flat
     section_means = []
     section_vars = []
     offset = 0
-    for width in [channels] * 5 + [extra]:
+    for width in [channels] * 5:
         section_means.append(means_flat[offset : offset + width])
         section_vars.append(vars_flat[offset : offset + width])
         offset += width
@@ -1901,13 +2011,24 @@
     proj_z = jnp.einsum(
         "nhwc,cd->nhwd", joined_coarse, proj_full, preferred_element_type=jnp.float32
     )
-    proj_mean, proj_var = moments(proj_z, valid_coarse, local_count, pixel_count)
+    proj_moments = local_moments(proj_z, valid_coarse, local_count)
+    joint_mean, joint_var = merged(
+        jnp.stack(
+            [
+                jnp.concatenate([proj_moments[0], low_stats[0, :extra]]),
+                jnp.concatenate([proj_moments[1], low_stats[1, :extra] / 16.0]),
+            ]
+        ),
+        local_count,
+        pixel_count,
+    )
+    proj_mean, low_mean = joint_mean[:channels], joint_mean[channels:]
+    proj_var, low_var = joint_var[:channels], joint_var[channels:]
     proj_act, proj_centered, proj_shaped, proj_scale = normalize(
         proj_z, valid_coarse, proj_mean, proj_var, gains[5], biases[5]
     )
     proj_act = proj_act.astype(jnp.bfloat16).astype(jnp.float32)
     cols_table = column_table(ids_coarse)[0].astype(jnp.bfloat16)
-    low_mean, low_var = section_means[5], section_vars[5]
     low_vectors = widen(norm_vectors(low_mean, low_var, low_gain, low_bias))
     decode_z, decode_stats, upsampled = decode_forward(
         proj_act[0],
@@ -1927,9 +2048,16 @@
         refine_z, grad_flat, refine_vectors, masks, w_cls, b_cls.reshape(1, -1)
     )
     logits = logits.reshape(logit_grad.shape)
-    cls_weight_grad = cls_weight_grad.T
     cls_bias_grad = cls_bias_grad[0]
-    refine_gain, refine_bias = gradient_sums([(refine_sums[0], refine_sums[1])])[0]
+    devices = device_count()
+    cls_flat = jnp.concatenate([cls_bias_grad, cls_weight_grad.reshape(-1)])
+    share = -(-cls_flat.shape[0] // devices)
+    cls_rows = jnp.pad(cls_flat, (0, share * devices - cls_flat.shape[0])).reshape(devices, share)
+    own = jnp.concatenate([refine_sums[0], refine_sums[1]])
+    own = jnp.broadcast_to(own[None], (devices, 2 * channels))
+    summed = jnp.sum(hand_out(jnp.concatenate([own, cls_rows], axis=1)), axis=0)
+    refine_gain, refine_bias = summed[:channels], summed[channels : 2 * channels]
+    cls_share = summed[2 * channels :]
     refine_vectors = norm_vectors(
         refine_mean,
         refine_var,
@@ -1941,7 +2069,13 @@
     decode_local, decode_sums, refine_kernel_grad = refine_backward(
         refine_z, grad_flat, refine_vectors, w_cls, decode_z, decode_vectors, masks, refine_full
     )
-    decode_gain, decode_bias = gradient_sums([(decode_sums[0], decode_sums[1])])[0]
+    rows = from_all(jnp.concatenate([decode_sums[0], decode_sums[1], cls_share]))
+    summed = jnp.sum(rows[:, : 2 * channels], axis=0)
+    decode_gain, decode_bias = summed[:channels], summed[channels:]
+    cls_flat = rows[:, 2 * channels :].reshape(-1)[: cls_flat.shape[0]]
+    classes = cls_bias_grad.shape[0]
+    cls_bias_grad = cls_flat[:classes]
+    cls_weight_grad = cls_flat[classes:].reshape(cls_weight_grad.shape).T
     decode_vectors = norm_vectors(
         decode_mean,
         decode_var,
@@ -1997,15 +2131,7 @@
     )
     branch_terms.append(norm_grad_terms(pool_up, all_ones, kept[4][0], kept[4][1]))
     local_pairs = [(term_item[1], term_item[2]) for term_item in branch_terms]
-    flat_pairs = pack_pairs(local_pairs)
-    flat_sums = sum_all(
-        jnp.concatenate([flat_pairs, cls_bias_grad, cls_weight_grad.reshape(-1)])
-    )
-    classes = cls_bias_grad.shape[0]
-    cls_weight_grad = flat_sums[flat_pairs.shape[0] + classes :].reshape(cls_weight_grad.shape)
-    cls_bias_grad = flat_sums[flat_pairs.shape[0] : flat_pairs.shape[0] + classes]
-    flat_sums = flat_sums[: flat_pairs.shape[0]]
-    last_pairs = unpack_pairs(flat_sums, local_pairs)
+    last_pairs = gradient_sums(local_pairs)
     valid_list = [valid_coarse, valid_coarse, valid_coarse, valid_coarse, all_ones]
     count_list = [pixel_count, pixel_count, pixel_count, pixel_count, images_total]
     branch_dz = [

time: 902 us -> 842 us (0.933)
  starting transfers between devices: 205 us -> 120 us
  Pallas kernels: 247 us -> 290 us
  waiting for transfers between devices: 207 us -> 178 us
  blocking collectives: 0 us -> 24.2 us
  other arithmetic: 120 us -> 96.4 us
  local copies, waits for them, and re-layouts: 97.8 us -> 110 us
    ppermute x90 -> x55, starting transfers between devices: 134 us -> 50.9 us  [exchange(): lax.ppermute(values, axis, [(place, place ^ bit) for place in range(size)])]
    ppermute x90 -> x55, waiting for transfers between devices: 158 us -> 99.9 us  [exchange(): lax.ppermute(values, axis, [(place, place ^ bit) for place in range(size)])]
    pallas_call x0 -> x20, Pallas kernels: none -> 41 us  [one_step(): pl.pallas_call(run, out_shape=outs, grid=(1,), in_specs=[spec or whole_sp...]
    all_to_all x0 -> x6, waiting for transfers between devices: none -> 38.3 us  [hand_out(): return lax.all_to_all(rows, ('wide', 'narrow'), 0, 0, tiled=True)]
    ppermute x24 -> x12, starting transfers between devices: 71.5 us -> 37.6 us  [rotate(): return lax.ppermute(values, axis, pairs)]
    all_to_all x0 -> x6, starting transfers between devices: none -> 31.1 us  [hand_out(): return lax.all_to_all(rows, ('wide', 'narrow'), 0, 0, tiled=True)]
    all_to_all x0 -> x2, blocking collectives: none -> 24.2 us  [hand_out(): return lax.all_to_all(rows, ('wide', 'narrow'), 0, 0, tiled=True)]
    add x49 -> x0, other arithmetic: 18.7 us -> none  [the longest x7 12.9 us: second(): total = add_wide(pair[0][0], other[0]) + value.astype(jnp.float32)]
  transfers between devices with their start and end apart: 114 -> 73, of which waited for: 61 -> 33; matrix products, arithmetic and copies ran while one was open for 14% -> 10% of each run, Pallas kernels for 10% -> 16%
where the time goes in v3:
time: 842 us; the launch traced here: 830 us
  Pallas kernels  290 us (34%)
  waiting for transfers between devices  178 us (21%)
  starting transfers between devices  120 us (14%)
  local copies, waits for them, and re-layouts  110 us (13%)
  other arithmetic  96.4 us (11%)
  blocking collectives  24.2 us (3%)
    ppermute x55, waiting for transfers between devices, exchange(): lax.ppermute(values, axis, [(place, place ^ bit) for place in range(size)])  99.9 us
    unnamed x467, local copies, waits for them, and re-layouts  68.1 us
    ppermute x55, starting transfers between devices, exchange(): lax.ppermute(values, axis, [(place, place ^ bit) for place in range(size)])  50.9 us
    pallas_call x1, Pallas kernels, decode_backward(): pl.pallas_call(functools.partial(decode_backward_kernel, steps, columns),...  45.2 us
    pallas_call x20, Pallas kernels, one_step(): pl.pallas_call(run, out_shape=outs, grid=(1,), in_specs=[spec or whole_sp...  41 us
    ppermute x12, waiting for transfers between devices, rotate(): return lax.ppermute(values, axis, pairs)  40.2 us
    all_to_all x6, waiting for transfers between devices, hand_out(): return lax.all_to_all(rows, ('wide', 'narrow'), 0, 0, tiled=True)  38.3 us
    pallas_call x3, Pallas kernels, coarse_weight(): pl.pallas_call(kernel, out_shape=outs, grid_spec=pltpu.PrefetchScalarGrid...  38.2 us
  transfers between devices with their start and end apart: 73, of which 33 were waited for; matrix products, arithmetic and copies ran while one was open for 10% of the time, Pallas kernels for 16%

profile of v3, /device:TPU:1, one launch (start us, length us, event | category | flops | bytes accessed | tf_op | source)
XLA Modules:
  0.0 829.7 jit_solution(10061418836280421477)
XLA Ops:
  18.6 8.2 collective-permute-done.2
  33.5 4.5 collective-permute-start.16
  52.9 6.1 fusion.7
  76.4 14.8 %collective-permute-done.21 = bf16[4,5,128,128]{3,2,1,0:T(8,128)(2,1)S(1)} collective-permute-done((bf16[4,5,128,128]{3,2,1,0:T(8,128)(2,1)S(1)}, bf16[4,5,128,128]{3,2,1,0:T(8,128)(2,1)S(1)}, u32[]{:S(2)}, u32[]{:S(2)}) %collective-permute-start.21) | collective-permute-done | bytes 655392 | tf_op jit(solution)/shard_map/ppermute | solution.py:22
  97.9 4.6 collective-permute-start.8
  108.8 8.6 %coarse_forward.3.refs_6_ = f32[480,256]{1,0:T(8,128)S(1)} custom-call(s32[4]{0:T(128)S(1)} %pad_add_fusion.place_ref, f32[480,1]{1,0:T(8,128)S(1)} %broadcast_in_dim.55.refs_0_, bf16[480,2048]{1,0:T(8,128)(2,1)} %bitcast.283, bf16[480,2048]{1,0:T(8,128)(2,1)} %bitcast.297, bf16[480,2048]{1,0:T(8,128)(2,1)} %bitcast.293, ...), custom_call_target="tpu_custom_call" | custom-call | flops 1 | bytes 1 | tf_op jit(solution)/shard_map/coarse_forward/pallas_call | solution.py:609
  117.5 12.8 %collective-permute-done.9 = bf16[12,128,128]{2,1,0:T(8,128)(2,1)} collective-permute-done((bf16[12,128,128]{2,1,0:T(8,128)(2,1)}, bf16[12,128,128]{2,1,0:T(8,128)(2,1)}, u32[]{:S(2)}, u32[]{:S(2)}) %collective-permute-start.9) | collective-permute-done | bytes 393248 | tf_op jit(solution)/shard_map/ppermute | solution.py:32
  133.6 3.9 pad_maximum_fusion.1.refs_11_.refs_12_
  138.6 8.6 %collective-permute-start.29 = (bf16[2,2,33,16,128]{4,3,2,1,0:T(8,128)(2,1)S(1)}, bf16[2,2,33,16,128]{4,3,2,1,0:T(8,128)(2,1)S(1)}, u32[]{:S(2)}, u32[]{:S(2)}) collective-permute-start(bf16[2,2,33,16,128]{4,3,2,1,0:T(8,128)(2,1)S(1)} %copy-done.95), channel_id=1, source_target_pairs={{0,8},{4,12},{8,16},{12,20},{16,24},{20,28},{24,0},{28,4},{1,9},{5... | collective-permute-start | bytes 1622024 | tf_op jit(solution)/shard_map/ppermute | solution.py:32
  150.6 6.5 collective-permute-start.31
  166.4 17.5 %collective-permute-done.30 = bf16[2,2,33,16,128]{4,3,2,1,0:T(8,128)(2,1)S(1)} collective-permute-done((bf16[2,2,33,16,128]{4,3,2,1,0:T(8,128)(2,1)S(1)}, bf16[2,2,33,16,128]{4,3,2,1,0:T(8,128)(2,1)S(1)}, u32[]{:S(2)}, u32[]{:S(2)}) %collective-permute-start.30) | collective-permute-done | bytes 540704 | tf_op jit(solution)/shard_map/ppermute | solution.py:32
  191.0 13.7 %coarse_forward.4 = (f32[480,256]{1,0:T(8,128)S(1)}, f32[480,256]{1,0:T(8,128)S(1)}, f32[8,256]{1,0:T(8,128)S(1)}, f32[480,256]{1,0:T(8,128)S(1)}, f32[8,256]{1,...) custom-call(s32[4]{0:T(128)S(1)} %pad_add_fusion.place_ref, f32[480,1]{1,0:T(8,128)S(1)} %broadcast_in_dim.55.refs_0_, ...), custom_call_target="tpu_custom_call" | custom-call | flops 1 | bytes 1 | tf_op jit(solution)/shard_map/coarse_forward/pallas_call | solution.py:609
  212.0 4.7 low_moments.1
  216.8 5.9 collective-permute-done.27
  245.0 11.4 %coarse_forward.5 = (f32[480,256]{1,0:T(8,128)S(1)}, f32[480,256]{1,0:T(8,128)S(1)}, f32[8,256]{1,0:T(8,128)S(1)}, f32[8,256]{1,0:T(8,128)S(1)}) custom-call(s32[4]{0:T(128)S(1)} %pad_add_fusion.place_ref, f32[480,1]{1,0:T(8,128)S(1)} %copy-done.40, bf16[480,2048]{1,0:T(8,128)(2,1)S(1)} %bitcast.285, bf16[480,2048]{1,0:T(8,128)(2,1)S(1)} %bitcast.303, ...), custom_call_target="tpu_custom_call" | custom-call | flops 1 | bytes 1 | tf_op jit(solution)/shard_map/coarse_forward/pallas_call | solution.py:609
  259.1 14.8 %all-to-all-start = ((f32[32,1,2561]{2,1,0:T(1,128)}), f32[32,1,2561]{2,1,0:T(1,128)}, u32[]{:S(2)}, u32[]{:S(2)}) async-start(f32[32,1,2561]{2,1,0:T(1,128)} %broadcast_in_dim.44), calls=%async_computation | async-start | bytes 688128 | tf_op jit(solution)/shard_map/all_to_all | solution.py:40
  278.1 7.4 all-to-all-done
  294.5 4.4 all-to-all-start.1
  302.4 4.0 all-to-all-done.1
  318.8 23.8 %decode_forward.1 = (f32[7680,256]{1,0:T(8,128)}, f32[8,256]{1,0:T(8,128)S(1)}, bf16[7680,256]{1,0:T(8,128)(2,1)}) custom-call(f32[20,24,256]{2,1,0:T(8,128)S(1)} %copy-done.49, bf16[96,48]{1,0:T(8,128)(2,1)S(1)} %copy-done.68, bf16[7680,256]{1,0:T(8,128)(2,1)} %bitcast.289, bf16[256,256]{1,0:T(8,128)(2,1)S(1)} %copy-done.44, ...), custom_call_target="tpu_custom_call" | custom-call | flops 1 | bytes 1 | tf_op jit(solution)/shard_map/decode_forward/pallas_call | solution.py:957
  347.2 7.0 all-to-all-done.2
  358.4 18.0 %refine_forward.1 = (f32[7680,256]{1,0:T(8,128)}, f32[8,256]{1,0:T(8,128)S(1)}) custom-call(f32[7680,256]{1,0:T(8,128)} %get-tuple-element.276.z_in_ref.z_ref, f32[8,256]{1,0:T(8,128)S(1)} %stack.434.vector_ref.vector_in_ref, f32[768,3]{1,0:T(8,128)S(1)} %copy.268.masks_ref.refs_3_, bf16[9,256,256]{2,1,0:T(8,128)(2,1)S(1)} %get-tuple-element.251.w_ref), custom_call_target="tpu_custom_call" | custom-call | flops 1 | bytes 1 | tf_op jit(solution)/shard_map/refine_forward/pallas_call | solution.py:1021
  381.7 6.2 all-to-all-done.3
  396.4 10.0 %classify.1 = (bf16[7680,21]{1,0:T(8,128)(2,1)S(1)}, f32[8,256]{1,0:T(8,128)S(1)}, f32[21,256]{1,0:T(8,128)S(1)}, f32[1,21]{1,0:T(1,128)S(1)}) custom-call(f32[7680,256]{1,0:T(8,128)} %get-tuple-element.278.z_ref, bf16[7680,21]{1,0:T(8,128)(2,1)S(1)} %bitcast.305, f32[8,256]{1,0:T(8,128)S(1)} %copy-done.74, f32[768,3]{1,0:T(8,128)S(1)} %copy.268.masks_ref.refs_3_, ...), custom_call_target="tpu_custom_call" | custom-call | flops 1 | bytes 1 | tf_op jit(solution)/shard_map/classify/pallas_call | solution.py:1078
  415.3 10.2 %all_to_all.66 = f32[32,1,681]{2,1,0:T(1,128)} all-to-all(f32[32,1,681]{2,1,0:T(1,128)S(1)} %all_to_all.52), channel_id=1, replica_groups=mesh['wide'=8,'narrow'=4] {'wide','narrow'}, dimensions={0} | all-to-all | bytes 174336 | tf_op jit(solution)/shard_map/all_to_all | solution.py:40
  434.2 33.8 %refine_backward.1 = (f32[7680,256]{1,0:T(8,128)}, f32[8,256]{1,0:T(8,128)S(1)}, f32[3,256,768]{2,1,0:T(8,128)S(1)}) custom-call(f32[7680,256]{1,0:T(8,128)} %get-tuple-element.278.z_ref, bf16[7680,21]{1,0:T(8,128)(2,1)S(1)} %bitcast.306, f32[8,256]{1,0:T(8,128)S(1)} %copy-done.73, bf16[256,21]{1,0:T(8,128)(2,1)S(1)} %copy-done.59, ...), custom_call_target="tpu_custom_call" | custom-call | flops 1 | bytes 1 | tf_op jit(solution)/shard_map/refine_backward/pallas_call | solution.py:1169
  473.8 6.9 all-to-all-done.5
  484.4 45.2 %decode_backward.1 = (f32[20,24,256]{2,1,0:T(8,128)S(1)}, f32[7680,64]{1,0:T(8,128)}, f32[8,256]{1,0:T(8,128)S(1)}, f32[3,256,768]{2,1,0:T(8,128)S(1)}, f32[3,64,768]{2,1,0:T(8,128)S(1)}) custom-call(f32[7680,256]{1,0:T(8,128)} %get-tuple-element.284.local_ref, f32[7680,256]{1,0:T(8,128)} %get-tuple-element.276.z_in_ref.z_ref, ...), custom_call_target="tpu_custom_call" | custom-call | flops 1 | bytes 1 | tf_op jit(solution)/shard_map/decode_backward/pallas_call | solution.py:1285
  536.4 6.8 all-to-all-done.6
  553.3 14.0 %all_to_all.67 = f32[32,1,2560]{2,1,0:T(1,128)} all-to-all(f32[32,1,2560]{2,1,0:T(1,128)S(1)} %broadcast_in_dim.54), channel_id=1, replica_groups=mesh['wide'=8,'narrow'=4] {'wide','narrow'}, dimensions={0} | all-to-all | bytes 655360 | tf_op jit(solution)/shard_map/all_to_all | solution.py:40
  575.3 14.3 %coarse_weight.3 = (bf16[2,2,4,12,128,128]{5,4,3,2,1,0:T(8,128)(2,1)}, bf16[2,2,4,12,128,128]{5,4,3,2,1,0:T(8,128)(2,1)}) custom-call(s32[4]{0:T(128)S(1)} %copy-done.70, bf16[480,2048]{1,0:T(8,128)(2,1)S(1)} %bitcast.286, bf16[480,2048]{1,0:T(8,128)(2,1)S(1)} %bitcast.304, bf16[480,2048]{1,0:T(8,128)(2,1)} %bitcast.334, bf16[480,2048]{1,0:T(8,128)(2,1)} %bitcast.339, ...), custom_call_target="tpu_custom_call" | custom-call | flops 1 | bytes 1 | tf_op jit(solution)/shard_map/coarse_weight/pallas_call | solution.py:713
  593.1 14.8 %coarse_weight.4 = (bf16[2,2,4,11,128,128]{5,4,3,2,1,0:T(8,128)(2,1)}, bf16[2,2,4,11,128,128]{5,4,3,2,1,0:T(8,128)(2,1)}) custom-call(s32[4]{0:T(128)S(1)} %copy-done.70, bf16[2,2,4,12,128,128]{5,4,3,2,1,0:T(8,128)(2,1)} %get-tuple-element.289.tie_ref.refs_0_, bf16[480,2048]{1,0:T(8,128)(2,1)S(1)} %bitcast.287, bf16[480,2048]{1,0:T(8,128)(2,1)S(1)} %bitcast.299, ...), custom_call_target="tpu_custom_call" | custom-call | flops 1 | bytes 1 | tf_op jit(solution)/shard_map/coarse_weight/pallas_call | solution.py:713
  610.7 4.9 move.20
  620.9 9.6 %low_backward.1 = (bf16[7680,256]{1,0:T(8,128)(2,1)}, f32[64,256]{1,0:T(8,128)S(1)}) custom-call(f32[8,256]{1,0:T(8,128)S(1)} %maximum_maximum_fusion.1.place_ref, bf16[2,4,6,128,128]{4,3,2,1,0:T(8,128)(2,1)} %get-tuple-element.293.tie_ref, f32[7680,64]{1,0:T(8,128)S(1)} %copy-done.36, bf16[7680,256]{1,0:T(8,128)(2,1)} %bitcast.291, ...), custom_call_target="tpu_custom_call" | custom-call | flops 1 | bytes 1 | tf_op jit(solution)/shard_map/low_backward/pallas_call | solution.py:1342
  630.5 5.2 pack_gradients.1
  638.0 9.2 %coarse_weight.5 = (bf16[2,2,4,6,128,128]{5,4,3,2,1,0:T(8,128)(2,1)}, bf16[2,2,4,6,128,128]{5,4,3,2,1,0:T(8,128)(2,1)}) custom-call(s32[4]{0:T(128)S(1)} %copy-done.70, bf16[2,2,4,33,16,128]{5,4,3,2,1,0:T(8,128)(2,1)} %copy-done.10, bf16[480,2048]{1,0:T(8,128)(2,1)S(1)} %bitcast.288, bf16[480,2048]{1,0:T(8,128)(2,1)S(1)} %bitcast.300, ...), custom_call_target="tpu_custom_call" | custom-call | flops 1 | bytes 1 | tf_op jit(solution)/shard_map/coarse_weight/pallas_call | solution.py:713
  647.2 4.4 collective-permute-done.38.refs_2_
  651.8 5.9 move.21
  659.3 4.2 move.22
  664.4 10.8 %collective-permute-done.41.refs_1_ = bf16[4,6,128,128]{3,2,1,0:T(8,128)(2,1)S(1)} collective-permute-done((bf16[4,6,128,128]{3,2,1,0:T(8,128)(2,1)S(1)}, bf16[4,6,128,128]{3,2,1,0:T(8,128)(2,1)S(1)}, u32[]{:S(2)}, u32[]{:S(2)}) %collective-permute-start.41) | collective-permute-done | bytes 786464 | tf_op jit(solution)/shard_map/ppermute | solution.py:22
  684.1 22.4 %coarse_input.1.tie_ref = bf16[480,2048]{1,0:T(8,128)(2,1)} custom-call(s32[4]{0:T(128)S(1)} %copy-done.70, bf16[2,4,33,16,128]{4,3,2,1,0:T(8,128)(2,1)S(1)} %move.24.tie_ref, bf16[480,256]{1,0:T(8,128)(2,1)S(1)} %bitcast.328, bf16[8,256]{1,0:T(8,128)(2,1)S(1)} %pad.108.refs_9_.refs_1_, f32[480,8]{1,0:T(8,128)S(1)} %bitcast_multiply_fusion.refs_2_, ...), custom_call_target="tpu_custom_call" | custom-call | flops 1 | bytes 1 | tf_op jit(solution)/shard_map/coarse_input/pallas_call | solution.py:788
  709.0 5.6 move.25
  718.5 5.9 collective-permute-done.47.refs_2_
  729.2 11.9 %collective-permute-done.50.refs_2_ = bf16[4,6,128,128]{3,2,1,0:T(8,128)(2,1)S(1)} collective-permute-done((bf16[4,6,128,128]{3,2,1,0:T(8,128)(2,1)S(1)}, bf16[4,6,128,128]{3,2,1,0:T(8,128)(2,1)S(1)}, u32[]{:S(2)}, u32[]{:S(2)}) %collective-permute-start.50) | collective-permute-done | bytes 786464 | tf_op jit(solution)/shard_map/ppermute | solution.py:22
  746.2 11.8 %collective-permute-done.51.refs_2_ = bf16[2,4,3,128,128]{4,3,2,1,0:T(8,128)(2,1)S(1)} collective-permute-done((bf16[2,4,3,128,128]{4,3,2,1,0:T(8,128)(2,1)S(1)}, bf16[2,4,3,128,128]{4,3,2,1,0:T(8,128)(2,1)S(1)}, u32[]{:S(2)}, u32[]{:S(2)}) %collective-permute-start.51) | collective-permute-done | bytes 786464 | tf_op jit(solution)/shard_map/ppermute | solution.py:22
  771.6 7.3 collective-permute-start.65
  797.2 10.1 %collective-permute-done.59.refs_1_ = bf16[2,6,128,128]{3,2,1,0:T(8,128)(2,1)} collective-permute-done((bf16[2,6,128,128]{3,2,1,0:T(8,128)(2,1)S(1)}, bf16[2,6,128,128]{3,2,1,0:T(8,128)(2,1)}, u32[]{:S(2)}, u32[]{:S(2)}) %collective-permute-start.59) | collective-permute-done | bytes 393248 | tf_op jit(solution)/shard_map/ppermute | solution.py:22
  811.0 3.9 collective-permute-done.63.refs_1_
  (859 shorter events, 317.9 us)
Async XLA Ops:
  33.5 28.2 %collective-permute-start.16 = (bf16[11,128,128]{2,1,0:T(8,128)(2,1)S(1)}, bf16[11,128,128]{2,1,0:T(8,128)(2,1)S(1)}, u32[]{:S(2)}, u32[]{:S(2)}) collective-permute-start(bf16[11,128,128]{2,1,0:T(8,128)(2,1)S(1)} %pad_maximum_fusion.26), channel_id=1, source_target_pairs={{0,8},{4,12},{8,16},{12,20},{16,24},{20,28},{24,0},{28,4},{1,9},{5... | collective-permute-start | bytes 1081352 | tf_op jit(solution)/shard_map/ppermute | solution.py:32
  38.5 24.9 %collective-permute-start.17 = (bf16[11,128,128]{2,1,0:T(8,128)(2,1)S(1)}, bf16[11,128,128]{2,1,0:T(8,128)(2,1)}, u32[]{:S(2)}, u32[]{:S(2)}) collective-permute-start(bf16[11,128,128]{2,1,0:T(8,128)(2,1)S(1)} %pad_maximum_fusion.26), channel_id=1, source_target_pairs={{0,16},{4,20},{8,24},{12,28},{16,0},{20,4},{24,8},{28,12},{1,17},{... | collective-permute-start | bytes 1081352 | tf_op jit(solution)/shard_map/ppermute | solution.py:32
  41.8 21.7 %collective-permute-start.18 = (bf16[11,128,128]{2,1,0:T(8,128)(2,1)S(1)}, bf16[11,128,128]{2,1,0:T(8,128)(2,1)S(1)}, u32[]{:S(2)}, u32[]{:S(2)}) collective-permute-start(bf16[11,128,128]{2,1,0:T(8,128)(2,1)S(1)} %pad_maximum_fusion.26), channel_id=1, source_target_pairs={{0,24},{4,28},{8,0},{12,4},{16,8},{20,12},{24,16},{28,20},{1,25},{... | collective-permute-start | bytes 1081352 | tf_op jit(solution)/shard_map/ppermute | solution.py:32
  49.2 18.4 %collective-permute-start.14 = (bf16[2,4,3,128,128]{4,3,2,1,0:T(8,128)(2,1)S(1)}, bf16[2,4,3,128,128]{4,3,2,1,0:T(8,128)(2,1)}, u32[]{:S(2)}, u32[]{:S(2)}) collective-permute-start(bf16[2,4,3,128,128]{4,3,2,1,0:T(8,128)(2,1)S(1)} %pad_maximum_fusion.17), channel_id=1, source_target_pairs={{0,2},{1,3},{2,0},{3,1},{4,6},{5,7},{6,4},{7,5},{8,10},{9,11},{10,... | collective-permute-start | bytes 2359304 | tf_op jit(solution)/shard_map/ppermute | solution.py:22
  51.6 18.1 %collective-permute-start.15 = (bf16[2,4,3,128,128]{4,3,2,1,0:T(8,128)(2,1)S(1)}, bf16[2,4,3,128,128]{4,3,2,1,0:T(8,128)(2,1)}, u32[]{:S(2)}, u32[]{:S(2)}) collective-permute-start(bf16[2,4,3,128,128]{4,3,2,1,0:T(8,128)(2,1)S(1)} %pad_maximum_fusion.18), channel_id=1, source_target_pairs={{0,4},{4,0},{8,12},{12,8},{16,20},{20,16},{24,28},{28,24},{1,5},{5... | collective-permute-start | bytes 2359304 | tf_op jit(solution)/shard_map/ppermute | solution.py:22
  71.0 31.6 %collective-permute-start.19 = (bf16[2,2,4,3,128,128]{5,4,3,2,1,0:T(8,128)(2,1)S(1)}, bf16[2,2,4,3,128,128]{5,4,3,2,1,0:T(8,128)(2,1)S(1)}, u32[]{:S(2)}, u32[]{:S(2)}) collective-permute-start(bf16[2,2,4,3,128,128]{5,4,3,2,1,0:T(8,128)(2,1)S(1)} %pad_maximum_fusion.6.refs_4_.refs_6_), channel_id=1, source_target_pairs={{0,1},{1,0},{2,3},{3,2},{4,5},{5,4},{6,7},{7,6},{8,9},{9,8},{10,11... | collective-permute-start | bytes 4718600 | tf_op jit(solution)/shard_map/ppermute | solution.py:22
  74.3 30.6 %collective-permute-start.20 = (bf16[2,2,4,3,128,128]{5,4,3,2,1,0:T(8,128)(2,1)S(1)}, bf16[2,2,4,3,128,128]{5,4,3,2,1,0:T(8,128)(2,1)S(1)}, u32[]{:S(2)}, u32[]{:S(2)}) collective-permute-start(bf16[2,2,4,3,128,128]{5,4,3,2,1,0:T(8,128)(2,1)S(1)} %pad_maximum_fusion.7.refs_6_.refs_8_), channel_id=1, source_target_pairs={{0,1},{1,0},{2,3},{3,2},{4,5},{5,4},{6,7},{7,6},{8,9},{9,8},{10,11... | collective-permute-start | bytes 4718600 | tf_op jit(solution)/shard_map/ppermute | solution.py:22
  74.9 19.1 %collective-permute-start.22 = (bf16[4,6,128,128]{3,2,1,0:T(8,128)(2,1)S(1)}, bf16[4,6,128,128]{3,2,1,0:T(8,128)(2,1)S(1)}, u32[]{:S(2)}, u32[]{:S(2)}) collective-permute-start(bf16[4,6,128,128]{3,2,1,0:T(8,128)(2,1)S(1)} %pad_maximum_fusion.13), channel_id=1, source_target_pairs={{0,2},{1,3},{2,0},{3,1},{4,6},{5,7},{6,4},{7,5},{8,10},{9,11},{10,... | collective-permute-start | bytes 2359304 | tf_op jit(solution)/shard_map/ppermute | solution.py:22
  95.3 38.2 %collective-permute-start.26 = (bf16[2,4,6,128,128]{4,3,2,1,0:T(8,128)(2,1)}, bf16[2,4,6,128,128]{4,3,2,1,0:T(8,128)(2,1)}, u32[]{:S(2)}, u32[]{:S(2)}) collective-permute-start(bf16[2,4,6,128,128]{4,3,2,1,0:T(8,128)(2,1)} %pad_maximum_fusion.8), channel_id=1, source_target_pairs={{0,4},{4,0},{8,12},{12,8},{16,20},{20,16},{24,28},{28,24},{1,5},{5... | collective-permute-start | bytes 4718600 | tf_op jit(solution)/shard_map/ppermute | solution.py:22
  97.7 35.9 %collective-permute-start.25 = (bf16[2,4,5,128,128]{4,3,2,1,0:T(8,128)(2,1)}, bf16[2,4,5,128,128]{4,3,2,1,0:T(8,128)(2,1)}, u32[]{:S(2)}, u32[]{:S(2)}) collective-permute-start(bf16[2,4,5,128,128]{4,3,2,1,0:T(8,128)(2,1)} %pad_maximum_fusion.12), channel_id=1, source_target_pairs={{0,2},{1,3},{2,0},{3,1},{4,6},{5,7},{6,4},{7,5},{8,10},{9,11},{10,... | collective-permute-start | bytes 3932168 | tf_op jit(solution)/shard_map/ppermute | solution.py:22
  97.9 19.5 %collective-permute-start.8 = (bf16[12,128,128]{2,1,0:T(8,128)(2,1)}, bf16[12,128,128]{2,1,0:T(8,128)(2,1)}, u32[]{:S(2)}, u32[]{:S(2)}) collective-permute-start(bf16[12,128,128]{2,1,0:T(8,128)(2,1)} %pad_maximum_fusion.24), channel_id=1, source_target_pairs={{0,8},{4,12},{8,16},{12,20},{16,24},{20,28},{24,0},{28,4},{1,9},{5... | collective-permute-start | bytes 1179656 | tf_op jit(solution)/shard_map/ppermute | solution.py:32
  103.7 26.6 %collective-permute-start.9 = (bf16[12,128,128]{2,1,0:T(8,128)(2,1)}, bf16[12,128,128]{2,1,0:T(8,128)(2,1)}, u32[]{:S(2)}, u32[]{:S(2)}) collective-permute-start(bf16[12,128,128]{2,1,0:T(8,128)(2,1)} %pad_maximum_fusion.24), channel_id=1, source_target_pairs={{0,16},{4,20},{8,24},{12,28},{16,0},{20,4},{24,8},{28,12},{1,17},{... | collective-permute-start | bytes 1179656 | tf_op jit(solution)/shard_map/ppermute | solution.py:32
  106.1 24.2 %collective-permute-start.10 = (bf16[12,128,128]{2,1,0:T(8,128)(2,1)}, bf16[12,128,128]{2,1,0:T(8,128)(2,1)}, u32[]{:S(2)}, u32[]{:S(2)}) collective-permute-start(bf16[12,128,128]{2,1,0:T(8,128)(2,1)} %pad_maximum_fusion.24), channel_id=1, source_target_pairs={{0,24},{4,28},{8,0},{12,4},{16,8},{20,12},{24,16},{28,20},{1,25},{... | collective-permute-start | bytes 1179656 | tf_op jit(solution)/shard_map/ppermute | solution.py:32
  132.0 18.6 %collective-permute-start.23 = (bf16[4,6,128,128]{3,2,1,0:T(8,128)(2,1)S(1)}, bf16[4,6,128,128]{3,2,1,0:T(8,128)(2,1)S(1)}, u32[]{:S(2)}, u32[]{:S(2)}) collective-permute-start(bf16[4,6,128,128]{3,2,1,0:T(8,128)(2,1)S(1)} %get-tuple-element.221), channel_id=1, source_target_pairs={{0,4},{4,0},{8,12},{12,8},{16,20},{20,16},{24,28},{28,24},{1,5},{5... | collective-permute-start | bytes 2359304 | tf_op jit(solution)/shard_map/ppermute | solution.py:22
  132.3 28.2 %collective-permute-start.24 = (bf16[4,6,128,128]{3,2,1,0:T(8,128)(2,1)S(1)}, bf16[4,6,128,128]{3,2,1,0:T(8,128)(2,1)S(1)}, u32[]{:S(2)}, u32[]{:S(2)}) collective-permute-start(bf16[4,6,128,128]{3,2,1,0:T(8,128)(2,1)S(1)} %get-tuple-element.223), channel_id=1, source_target_pairs={{0,2},{1,3},{2,0},{3,1},{4,6},{5,7},{6,4},{7,5},{8,10},{9,11},{10,... | collective-permute-start | bytes 2359304 | tf_op jit(solution)/shard_map/ppermute | solution.py:22
  137.4 52.0 %collective-permute-start.34 = (bf16[2,2,4,6,128,128]{5,4,3,2,1,0:T(8,128)(2,1)}, bf16[2,2,4,6,128,128]{5,4,3,2,1,0:T(8,128)(2,1)}, u32[]{:S(2)}, u32[]{:S(2)}) collective-permute-start(bf16[2,2,4,6,128,128]{5,4,3,2,1,0:T(8,128)(2,1)} %pad_maximum_fusion.1.refs_11_.refs_12_), channel_id=1, source_target_pairs={{0,1},{1,0},{2,3},{3,2},{4,5},{5,4},{6,7},{7,6},{8,9},{9,8},{10,11... | collective-permute-start | bytes 9437192 | tf_op jit(solution)/shard_map/ppermute | solution.py:22
  138.6 27.8 %collective-permute-start.29 = (bf16[2,2,33,16,128]{4,3,2,1,0:T(8,128)(2,1)S(1)}, bf16[2,2,33,16,128]{4,3,2,1,0:T(8,128)(2,1)S(1)}, u32[]{:S(2)}, u32[]{:S(2)}) collective-permute-start(bf16[2,2,33,16,128]{4,3,2,1,0:T(8,128)(2,1)S(1)} %copy-done.95), channel_id=1, source_target_pairs={{0,8},{4,12},{8,16},{12,20},{16,24},{20,28},{24,0},{28,4},{1,9},{5... | collective-permute-start | bytes 1622024 | tf_op jit(solution)/shard_map/ppermute | solution.py:32
  147.2 36.8 %collective-permute-start.30 = (bf16[2,2,33,16,128]{4,3,2,1,0:T(8,128)(2,1)S(1)}, bf16[2,2,33,16,128]{4,3,2,1,0:T(8,128)(2,1)S(1)}, u32[]{:S(2)}, u32[]{:S(2)}) collective-permute-start(bf16[2,2,33,16,128]{4,3,2,1,0:T(8,128)(2,1)S(1)} %copy-done.95), channel_id=1, source_target_pairs={{0,16},{4,20},{8,24},{12,28},{16,0},{20,4},{24,8},{28,12},{1,17},{... | collective-permute-start | bytes 1622024 | tf_op jit(solution)/shard_map/ppermute | solution.py:32
  150.6 33.4 %collective-permute-start.31 = (bf16[2,2,33,16,128]{4,3,2,1,0:T(8,128)(2,1)S(1)}, bf16[2,2,33,16,128]{4,3,2,1,0:T(8,128)(2,1)S(1)}, u32[]{:S(2)}, u32[]{:S(2)}) collective-permute-start(bf16[2,2,33,16,128]{4,3,2,1,0:T(8,128)(2,1)S(1)} %copy-done.95), channel_id=1, source_target_pairs={{0,24},{4,28},{8,0},{12,4},{16,8},{20,12},{24,16},{28,20},{1,25},{... | collective-permute-start | bytes 1622024 | tf_op jit(solution)/shard_map/ppermute | solution.py:32
  160.5 28.9 %collective-permute-start.33 = (bf16[2,2,4,5,128,128]{5,4,3,2,1,0:T(8,128)(2,1)}, bf16[2,2,4,5,128,128]{5,4,3,2,1,0:T(8,128)(2,1)}, u32[]{:S(2)}, u32[]{:S(2)}) collective-permute-start(bf16[2,2,4,5,128,128]{5,4,3,2,1,0:T(8,128)(2,1)} %pad_maximum_fusion.4.refs_9_.refs_10_), channel_id=1, source_target_pairs={{0,1},{1,0},{2,3},{3,2},{4,5},{5,4},{6,7},{7,6},{8,9},{9,8},{10,11... | collective-permute-start | bytes 7864328 | tf_op jit(solution)/shard_map/ppermute | solution.py:22
  185.6 22.6 %collective-permute-start.32 = (bf16[4,2,2,33,16,128]{5,4,3,2,1,0:T(8,128)(2,1)}, bf16[4,2,2,33,16,128]{5,4,3,2,1,0:T(8,128)(2,1)}, u32[]{:S(2)}, u32[]{:S(2)}) collective-permute-start(bf16[4,2,2,33,16,128]{5,4,3,2,1,0:T(8,128)(2,1)} %pad_maximum_fusion.5.own_ref), channel_id=1, source_target_pairs={{0,1},{1,0},{2,3},{3,2},{4,5},{5,4},{6,7},{7,6},{8,9},{9,8},{10,11... | collective-permute-start | bytes 6488072 | tf_op jit(solution)/shard_map/ppermute | solution.py:22
  186.3 36.4 %collective-permute-start.27 = (bf16[2,4,6,128,128]{4,3,2,1,0:T(8,128)(2,1)}, bf16[2,4,6,128,128]{4,3,2,1,0:T(8,128)(2,1)}, u32[]{:S(2)}, u32[]{:S(2)}) collective-permute-start(bf16[2,4,6,128,128]{4,3,2,1,0:T(8,128)(2,1)} %pad_maximum_fusion.10), channel_id=1, source_target_pairs={{0,2},{1,3},{2,0},{3,1},{4,6},{5,7},{6,4},{7,5},{8,10},{9,11},{10,... | collective-permute-start | bytes 4718600 | tf_op jit(solution)/shard_map/ppermute | solution.py:22
  187.2 36.0 %collective-permute-start.28 = (bf16[2,4,6,128,128]{4,3,2,1,0:T(8,128)(2,1)}, bf16[2,4,6,128,128]{4,3,2,1,0:T(8,128)(2,1)}, u32[]{:S(2)}, u32[]{:S(2)}) collective-permute-start(bf16[2,4,6,128,128]{4,3,2,1,0:T(8,128)(2,1)} %pad_maximum_fusion.11), channel_id=1, source_target_pairs={{0,4},{4,0},{8,12},{12,8},{16,20},{20,16},{24,28},{28,24},{1,5},{5... | collective-permute-start | bytes 4718600 | tf_op jit(solution)/shard_map/ppermute | solution.py:22
  259.1 26.5 %all-to-all-start = ((f32[32,1,2561]{2,1,0:T(1,128)}), f32[32,1,2561]{2,1,0:T(1,128)}, u32[]{:S(2)}, u32[]{:S(2)}) async-start(f32[32,1,2561]{2,1,0:T(1,128)} %broadcast_in_dim.44), calls=%async_computation | async-start | bytes 688128 | tf_op jit(solution)/shard_map/all_to_all | solution.py:40
  589.6 18.5 %collective-permute-start.37 = (bf16[2,2,4,12,128,128]{5,4,3,2,1,0:T(8,128)(2,1)}, bf16[2,2,4,12,128,128]{5,4,3,2,1,0:T(8,128)(2,1)S(1)}, u32[]{:S(2)}, u32[]{:S(2)}) collective-permute-start(bf16[2,2,4,12,128,128]{5,4,3,2,1,0:T(8,128)(2,1)} %get-tuple-element.292), channel_id=1, source_target_pairs={{0,1},{1,0},{2,3},{3,2},{4,5},{5,4},{6,7},{7,6},{8,9},{9,8},{10,11... | collective-permute-start | bytes 18874376 | tf_op jit(solution)/shard_map/ppermute | solution.py:22
  608.0 51.3 %collective-permute-start.40 = (bf16[2,2,4,11,128,128]{5,4,3,2,1,0:T(8,128)(2,1)}, bf16[2,2,4,11,128,128]{5,4,3,2,1,0:T(8,128)(2,1)}, u32[]{:S(2)}, u32[]{:S(2)}) collective-permute-start(bf16[2,2,4,11,128,128]{5,4,3,2,1,0:T(8,128)(2,1)} %get-tuple-element.303), channel_id=1, source_target_pairs={{0,1},{1,0},{2,3},{3,2},{4,5},{5,4},{6,7},{7,6},{8,9},{9,8},{10,11... | collective-permute-start | bytes 17301512 | tf_op jit(solution)/shard_map/ppermute | solution.py:22
  615.6 35.9 %collective-permute-start.38 = (bf16[2,4,6,128,128]{4,3,2,1,0:T(8,128)(2,1)}, bf16[2,4,6,128,128]{4,3,2,1,0:T(8,128)(2,1)}, u32[]{:S(2)}, u32[]{:S(2)}) collective-permute-start(bf16[2,4,6,128,128]{4,3,2,1,0:T(8,128)(2,1)} %get-tuple-element.293.tie_ref), channel_id=1, source_target_pairs={{0,4},{4,0},{8,12},{12,8},{16,20},{20,16},{24,28},{28,24},{1,5},{5... | collective-permute-start | bytes 4718600 | tf_op jit(solution)/shard_map/ppermute | solution.py:22
  616.2 35.6 %collective-permute-start.39 = (bf16[2,4,6,128,128]{4,3,2,1,0:T(8,128)(2,1)}, bf16[2,4,6,128,128]{4,3,2,1,0:T(8,128)(2,1)}, u32[]{:S(2)}, u32[]{:S(2)}) collective-permute-start(bf16[2,4,6,128,128]{4,3,2,1,0:T(8,128)(2,1)} %get-tuple-element.301), channel_id=1, source_target_pairs={{0,2},{1,3},{2,0},{3,1},{4,6},{5,7},{6,4},{7,5},{8,10},{9,11},{10,... | collective-permute-start | bytes 4718600 | tf_op jit(solution)/shard_map/ppermute | solution.py:22
  637.1 43.5 %collective-permute-start.43 = (bf16[2,2,4,33,16,128]{5,4,3,2,1,0:T(8,128)(2,1)}, bf16[2,2,4,33,16,128]{5,4,3,2,1,0:T(8,128)(2,1)S(1)}, u32[]{:S(2)}, u32[]{:S(2)}) collective-permute-start(bf16[2,2,4,33,16,128]{5,4,3,2,1,0:T(8,128)(2,1)} %get-tuple-element.308), channel_id=1, source_target_pairs={{0,1},{1,0},{2,3},{3,2},{4,5},{5,4},{6,7},{7,6},{8,9},{9,8},{10,11... | collective-permute-start | bytes 6488072 | tf_op jit(solution)/shard_map/ppermute | solution.py:22
  647.2 69.1 %collective-permute-start.46 = (bf16[2,2,4,6,128,128]{5,4,3,2,1,0:T(8,128)(2,1)}, bf16[2,2,4,6,128,128]{5,4,3,2,1,0:T(8,128)(2,1)}, u32[]{:S(2)}, u32[]{:S(2)}) collective-permute-start(bf16[2,2,4,6,128,128]{5,4,3,2,1,0:T(8,128)(2,1)} %get-tuple-element.312), channel_id=1, source_target_pairs={{0,1},{1,0},{2,3},{3,2},{4,5},{5,4},{6,7},{7,6},{8,9},{9,8},{10,11... | collective-permute-start | bytes 9437192 | tf_op jit(solution)/shard_map/ppermute | solution.py:22
  657.7 17.5 %collective-permute-start.41 = (bf16[4,6,128,128]{3,2,1,0:T(8,128)(2,1)S(1)}, bf16[4,6,128,128]{3,2,1,0:T(8,128)(2,1)S(1)}, u32[]{:S(2)}, u32[]{:S(2)}) collective-permute-start(bf16[4,6,128,128]{3,2,1,0:T(8,128)(2,1)S(1)} %get-tuple-element.302.tie_ref), channel_id=1, source_target_pairs={{0,2},{1,3},{2,0},{3,1},{4,6},{5,7},{6,4},{7,5},{8,10},{9,11},{10,... | collective-permute-start | bytes 2359304 | tf_op jit(solution)/shard_map/ppermute | solution.py:22
  658.3 19.0 %collective-permute-start.42 = (bf16[4,6,128,128]{3,2,1,0:T(8,128)(2,1)S(1)}, bf16[4,6,128,128]{3,2,1,0:T(8,128)(2,1)S(1)}, u32[]{:S(2)}, u32[]{:S(2)}) collective-permute-start(bf16[4,6,128,128]{3,2,1,0:T(8,128)(2,1)S(1)} %get-tuple-element.306), channel_id=1, source_target_pairs={{0,4},{4,0},{8,12},{12,8},{16,20},{20,16},{24,28},{28,24},{1,5},{5... | collective-permute-start | bytes 2359304 | tf_op jit(solution)/shard_map/ppermute | solution.py:22
  663.5 45.5 %collective-permute-start.45 = (bf16[2,4,6,128,128]{4,3,2,1,0:T(8,128)(2,1)}, bf16[2,4,6,128,128]{4,3,2,1,0:T(8,128)(2,1)S(1)}, u32[]{:S(2)}, u32[]{:S(2)}) collective-permute-start(bf16[2,4,6,128,128]{4,3,2,1,0:T(8,128)(2,1)} %get-tuple-element.310), channel_id=1, source_target_pairs={{0,2},{1,3},{2,0},{3,1},{4,6},{5,7},{6,4},{7,5},{8,10},{9,11},{10,... | collective-permute-start | bytes 4718600 | tf_op jit(solution)/shard_map/ppermute | solution.py:22
  675.2 31.3 %collective-permute-start.44 = (bf16[2,4,5,128,128]{4,3,2,1,0:T(8,128)(2,1)S(1)}, bf16[2,4,5,128,128]{4,3,2,1,0:T(8,128)(2,1)}, u32[]{:S(2)}, u32[]{:S(2)}) collective-permute-start(bf16[2,4,5,128,128]{4,3,2,1,0:T(8,128)(2,1)S(1)} %get-tuple-element.304.tie_ref), channel_id=1, source_target_pairs={{0,4},{4,0},{8,12},{12,8},{16,20},{20,16},{24,28},{28,24},{1,5},{5... | collective-permute-start | bytes 3932168 | tf_op jit(solution)/shard_map/ppermute | solution.py:22
  681.9 42.5 %collective-permute-start.47 = (bf16[2,4,33,16,128]{4,3,2,1,0:T(8,128)(2,1)S(1)}, bf16[2,4,33,16,128]{4,3,2,1,0:T(8,128)(2,1)S(1)}, u32[]{:S(2)}, u32[]{:S(2)}) collective-permute-start(bf16[2,4,33,16,128]{4,3,2,1,0:T(8,128)(2,1)S(1)} %move.24.tie_ref), channel_id=1, source_target_pairs={{0,4},{4,0},{8,12},{12,8},{16,20},{20,16},{24,28},{28,24},{1,5},{5... | collective-permute-start | bytes 3244040 | tf_op jit(solution)/shard_map/ppermute | solution.py:22
  682.8 44.2 %collective-permute-start.48 = (bf16[2,12,128,128]{3,2,1,0:T(8,128)(2,1)}, bf16[2,12,128,128]{3,2,1,0:T(8,128)(2,1)}, u32[]{:S(2)}, u32[]{:S(2)}) collective-permute-start(bf16[2,12,128,128]{3,2,1,0:T(8,128)(2,1)} %get-tuple-element.307.tie_ref), channel_id=1, source_target_pairs={{0,16},{4,20},{8,24},{12,28},{16,0},{20,4},{24,8},{28,12},{1,17},{... | collective-permute-start | bytes 2359304 | tf_op jit(solution)/shard_map/ppermute | solution.py:22
  714.6 26.5 %collective-permute-start.50 = (bf16[4,6,128,128]{3,2,1,0:T(8,128)(2,1)S(1)}, bf16[4,6,128,128]{3,2,1,0:T(8,128)(2,1)S(1)}, u32[]{:S(2)}, u32[]{:S(2)}) collective-permute-start(bf16[4,6,128,128]{3,2,1,0:T(8,128)(2,1)S(1)} %get-tuple-element.318), channel_id=1, source_target_pairs={{0,4},{4,0},{8,12},{12,8},{16,20},{20,16},{24,28},{28,24},{1,5},{5... | collective-permute-start | bytes 2359304 | tf_op jit(solution)/shard_map/ppermute | solution.py:22
  718.1 39.9 %collective-permute-start.51 = (bf16[2,4,3,128,128]{4,3,2,1,0:T(8,128)(2,1)S(1)}, bf16[2,4,3,128,128]{4,3,2,1,0:T(8,128)(2,1)S(1)}, u32[]{:S(2)}, u32[]{:S(2)}) collective-permute-start(bf16[2,4,3,128,128]{4,3,2,1,0:T(8,128)(2,1)S(1)} %get-tuple-element.313.tie_ref), channel_id=1, source_target_pairs={{0,4},{4,0},{8,12},{12,8},{16,20},{20,16},{24,28},{28,24},{1,5},{5... | collective-permute-start | bytes 2359304 | tf_op jit(solution)/shard_map/ppermute | solution.py:22
  724.4 33.6 %collective-permute-start.52 = (bf16[2,4,3,128,128]{4,3,2,1,0:T(8,128)(2,1)S(1)}, bf16[2,4,3,128,128]{4,3,2,1,0:T(8,128)(2,1)S(1)}, u32[]{:S(2)}, u32[]{:S(2)}) collective-permute-start(bf16[2,4,3,128,128]{4,3,2,1,0:T(8,128)(2,1)S(1)} %get-tuple-element.320), channel_id=1, source_target_pairs={{0,2},{1,3},{2,0},{3,1},{4,6},{5,7},{6,4},{7,5},{8,10},{9,11},{10,... | collective-permute-start | bytes 2359304 | tf_op jit(solution)/shard_map/ppermute | solution.py:22
  727.1 37.3 %collective-permute-start.53 = (bf16[4,33,16,128]{3,2,1,0:T(8,128)(2,1)S(1)}, bf16[4,33,16,128]{3,2,1,0:T(8,128)(2,1)S(1)}, u32[]{:S(2)}, u32[]{:S(2)}) collective-permute-start(bf16[4,33,16,128]{3,2,1,0:T(8,128)(2,1)S(1)} %get-tuple-element.314.tie_ref), channel_id=1, source_target_pairs={{0,2},{1,3},{2,0},{3,1},{4,6},{5,7},{6,4},{7,5},{8,10},{9,11},{10,... | collective-permute-start | bytes 1622024 | tf_op jit(solution)/shard_map/ppermute | solution.py:22
  744.5 42.9 %collective-permute-start.57 = (bf16[2,11,128,128]{3,2,1,0:T(8,128)(2,1)S(1)}, bf16[2,11,128,128]{3,2,1,0:T(8,128)(2,1)}, u32[]{:S(2)}, u32[]{:S(2)}) collective-permute-start(bf16[2,11,128,128]{3,2,1,0:T(8,128)(2,1)S(1)} %get-tuple-element.319.tie_ref), channel_id=1, source_target_pairs={{0,16},{4,20},{8,24},{12,28},{16,0},{20,4},{24,8},{28,12},{1,17},{... | collective-permute-start | bytes 2162696 | tf_op jit(solution)/shard_map/ppermute | solution.py:22
  746.2 20.5 %collective-permute-start.54 = (bf16[12,128,128]{2,1,0:T(8,128)(2,1)S(1)}, bf16[12,128,128]{2,1,0:T(8,128)(2,1)S(1)}, u32[]{:S(2)}, u32[]{:S(2)}) collective-permute-start(bf16[12,128,128]{2,1,0:T(8,128)(2,1)S(1)} %get-tuple-element.316.tie_ref), channel_id=1, source_target_pairs={{0,8},{4,12},{8,0},{12,4},{16,24},{20,28},{24,16},{28,20},{1,9},{5... | collective-permute-start | bytes 1179656 | tf_op jit(solution)/shard_map/ppermute | solution.py:22
  762.1 21.9 %collective-permute-start.55 = (bf16[4,3,128,128]{3,2,1,0:T(8,128)(2,1)}, bf16[4,3,128,128]{3,2,1,0:T(8,128)(2,1)}, u32[]{:S(2)}, u32[]{:S(2)}) collective-permute-start(bf16[4,3,128,128]{3,2,1,0:T(8,128)(2,1)} %get-tuple-element.321.tie_ref), channel_id=1, source_target_pairs={{0,2},{1,3},{2,0},{3,1},{4,6},{5,7},{6,4},{7,5},{8,10},{9,11},{10,... | collective-permute-start | bytes 1179656 | tf_op jit(solution)/shard_map/ppermute | solution.py:22
  763.1 20.9 %collective-permute-start.56 = (bf16[4,3,128,128]{3,2,1,0:T(8,128)(2,1)}, bf16[4,3,128,128]{3,2,1,0:T(8,128)(2,1)}, u32[]{:S(2)}, u32[]{:S(2)}) collective-permute-start(bf16[4,3,128,128]{3,2,1,0:T(8,128)(2,1)} %get-tuple-element.326), channel_id=1, source_target_pairs={{0,4},{4,0},{8,12},{12,8},{16,20},{20,16},{24,28},{28,24},{1,5},{5... | collective-permute-start | bytes 1179656 | tf_op jit(solution)/shard_map/ppermute | solution.py:22
  766.0 27.5 %collective-permute-start.58 = (bf16[2,33,16,128]{3,2,1,0:T(8,128)(2,1)}, bf16[2,33,16,128]{3,2,1,0:T(8,128)(2,1)}, u32[]{:S(2)}, u32[]{:S(2)}) collective-permute-start(bf16[2,33,16,128]{3,2,1,0:T(8,128)(2,1)} %get-tuple-element.323.tie_ref), channel_id=1, source_target_pairs={{0,16},{4,20},{8,24},{12,28},{16,0},{20,4},{24,8},{28,12},{1,17},{... | collective-permute-start | bytes 811016 | tf_op jit(solution)/shard_map/ppermute | solution.py:22
  771.6 23.0 %collective-permute-start.65 = (bf16[12,128,64]{2,1,0:T(8,128)(2,1)}, bf16[12,128,64]{2,1,0:T(8,128)(2,1)}, u32[]{:S(2)}, u32[]{:S(2)}) collective-permute-start(bf16[12,128,64]{2,1,0:T(8,128)(2,1)} %bitcast.394), channel_id=1, source_target_pairs={{0,1},{1,0},{2,3},{3,2},{4,5},{5,4},{6,7},{7,6},{8,9},{9,8},{10,11... | collective-permute-start | bytes 589832 | tf_op jit(solution)/shard_map/ppermute | solution.py:22
  786.8 20.5 %collective-permute-start.59 = (bf16[2,6,128,128]{3,2,1,0:T(8,128)(2,1)S(1)}, bf16[2,6,128,128]{3,2,1,0:T(8,128)(2,1)}, u32[]{:S(2)}, u32[]{:S(2)}) collective-permute-start(bf16[2,6,128,128]{3,2,1,0:T(8,128)(2,1)S(1)} %get-tuple-element.327.tie_ref), channel_id=1, source_target_pairs={{0,16},{4,20},{8,24},{12,28},{16,0},{20,4},{24,8},{28,12},{1,17},{... | collective-permute-start | bytes 1179656 | tf_op jit(solution)/shard_map/ppermute | solution.py:22
  788.7 20.4 %collective-permute-start.60 = (bf16[11,128,128]{2,1,0:T(8,128)(2,1)S(1)}, bf16[11,128,128]{2,1,0:T(8,128)(2,1)S(1)}, u32[]{:S(2)}, u32[]{:S(2)}) collective-permute-start(bf16[11,128,128]{2,1,0:T(8,128)(2,1)S(1)} %get-tuple-element.329.tie_ref), channel_id=1, source_target_pairs={{0,8},{4,12},{8,0},{12,4},{16,24},{20,28},{24,16},{28,20},{1,9},{5... | collective-permute-start | bytes 1081352 | tf_op jit(solution)/shard_map/ppermute | solution.py:22
  (242 other events, 2343.0 us)

commit v4 on v3

--- a/solution.py
+++ b/solution.py
@@ -11,10 +11,64 @@
 highest = lax.Precision.HIGHEST
 dilations = (6, 12, 18)
 ROUNDS = 4
-CHUNKS = (3, 3, 5, 6, 6, 6)
-PARTS = ((0, 1), (2, 3), (4, 5))
-POINT_CHUNK = 2
 VMEM_BYTES = 48 * 1024 * 1024
+
+
+class Layout:
+    def __init__(self, chunks, point_chunk):
+        self.chunks = chunks
+        self.point_chunk = point_chunk
+        self.parts = [(index, index + 1) for index in range(0, len(chunks), 2)]
+        self.sizes = [[chunks[index] for index in part] for part in self.parts]
+        places = []
+        for chunk, size in enumerate(chunks):
+            places += [(chunk, tap) for tap in range(2 if chunk == point_chunk else 0, size)]
+        self.rows = [
+            [(line,) + places[9 * branch + 3 * line] for line in range(3)] for branch in range(3)
+        ]
+
+    def part_of(self, chunk):
+        return chunk // 2
+
+    def place(self, chunk, tap):
+        return tap + (self.chunks[chunk - 1] if chunk % 2 else 0)
+
+    def part_rows(self, part):
+        return [
+            (branch, line, chunk, tap)
+            for branch, rows in enumerate(self.rows)
+            for line, chunk, tap in rows
+            if chunk in self.parts[part]
+        ]
+
+    def has_point(self, part):
+        return self.point_chunk in self.parts[part]
+
+    def order(self, point, atrous):
+        flat = atrous.reshape((-1,) + atrous.shape[2:])
+        before = sum(self.chunks[: self.point_chunk])
+        parts = []
+        start = 0
+        for part, sizes in enumerate(self.sizes):
+            size = sum(sizes)
+            if self.has_point(part):
+                pieces = [flat[start:before], point, flat[before : start + size - 2]]
+                parts.append(jnp.concatenate([item for item in pieces if item.shape[0]]))
+                start += size - 2
+            else:
+                parts.append(flat[start : start + size])
+                start += size
+        return parts
+
+    def restore(self, parts, shape):
+        flat = jnp.concatenate(parts)
+        before = sum(self.chunks[: self.point_chunk])
+        atrous = jnp.concatenate([flat[:before], flat[before + 2 :]])
+        return (flat[before : before + 2], atrous.reshape(shape))
+
+
+GATHER = Layout((5, 6, 9, 9), 0)
+SCATTER = Layout((3, 3, 5, 6, 6, 6), 2)
 
 
 def exchange(values, axis, bit):
@@ -85,22 +139,9 @@
     return values if tuned() else jnp.zeros_like(values)
 
 
-class Order:
-    def __init__(self):
-        self.last = None
-
-    def take(self, values):
-        if self.last is None:
-            return values
-        values, self.last = lax.optimization_barrier((values, self.last))
-        return values
-
-    def give(self, values):
-        self.last = values
-        return values
-
-    def run(self, function, *values):
-        return self.give(function(*self.take(values)))
+def tied(values, earlier):
+    mark = earlier[(0,) * earlier.ndim]
+    return jnp.where(mark == mark, values, jnp.zeros_like(values))
 
 
 def one_step(body, outs, args, specs=None, tie=None):
@@ -135,6 +176,57 @@
 
 def cut(sizes):
     return [slice(sum(sizes[:index]), sum(sizes[: index + 1])) for index in range(len(sizes))]
+
+
+def pass_on(values, tie):
+    def body(source, target):
+        target[...] = source[...]
+
+    outs = [jax.ShapeDtypeStruct(values.shape, values.dtype)]
+    return one_step(body, outs, [values], None, tie)[0]
+
+
+def gather_depth(values):
+    return [exchange(values, "wide", 2 * flip) for flip in range(1, ROUNDS)]
+
+
+def lay_out(sizes, own, others, tie=None):
+    shape = own.shape[1:]
+    outs = [jax.ShapeDtypeStruct((ROUNDS, size) + shape, own.dtype) for size in sizes]
+
+    def body(*refs):
+        for target, taps in zip(refs[ROUNDS:], cut(sizes)):
+            for slot, source in enumerate(refs[:ROUNDS]):
+                target[slot] = source[taps]
+
+    return one_step(body, outs, [own] + list(others), tie=tie)
+
+
+def pair_up(values, others, tie=None):
+    outs = [jax.ShapeDtypeStruct((2,) + item.shape, item.dtype) for item in values]
+    count = len(outs)
+
+    def body(*refs):
+        for index in range(count):
+            refs[2 * count + index][0] = refs[index][...]
+            refs[2 * count + index][1] = refs[count + index][...]
+
+    return one_step(body, outs, list(values) + list(others), tie=tie)
+
+
+def pair_all(values, others, tie=None):
+    count = len(values)
+    shape = values[0].shape
+    sizes = [item.shape[2] for item in values]
+    outs = [jax.ShapeDtypeStruct((2,) + shape[:2] + (sum(sizes),) + shape[3:], values[0].dtype)]
+
+    def body(*refs):
+        target = refs[2 * count]
+        for index, taps in enumerate(cut(sizes)):
+            target[0, :, :, taps] = refs[index][...]
+            target[1, :, :, taps] = refs[count + index][...]
+
+    return one_step(body, outs, list(values) + list(others), tie=tie)[0]
 
 
 def first_sums(sizes, keep, got, tie=None):
@@ -214,23 +306,24 @@
 
 def gather_taps(weights, small, fillers, kernels):
     rounds = ROUNDS
-    sizes = [[CHUNKS[index] for index in part] for part in PARTS]
+    sizes = GATHER.sizes
     shapes = [item.shape for item in small]
     if not tuned():
-        chunks = []
-        for part, values in zip(PARTS, weights):
+        parts = []
+        for part, values in zip(GATHER.parts, weights):
             full = lax.all_gather(values, "narrow", axis=2, tiled=True)
             full = lax.all_gather(full, "wide", axis=1, tiled=True)
             rows = full.shape[1] // (4 * rounds)
             full = full.reshape(full.shape[0], rounds, 2, 2, rows, 2, full.shape[2] // 2)
             start = 0
+            pieces = []
             for index in part:
-                piece = full[start : start + CHUNKS[index]]
-                start += CHUNKS[index]
-                piece = piece[:, [0] + list(range(rounds - 1, 0, -1))]
+                piece = full[start : start + GATHER.chunks[index]]
+                start += GATHER.chunks[index]
                 order = (3, 5, 2, 1, 0, 4, 6) if index % 2 == 0 else (3, 2, 5, 1, 0, 4, 6)
-                piece = piece.transpose(order)
-                chunks.append((piece[0], piece[1]))
+                pieces.append(piece.transpose(order))
+            joined = jnp.concatenate(pieces, axis=4)
+            parts.append((joined[0], joined[1]))
         flat = pack_small(small)
         everything = lax.all_gather(flat, ("wide", "narrow"))
         everything = everything.reshape(lax.axis_size("wide"), lax.axis_size("narrow"), -1)
@@ -238,95 +331,55 @@
         ready = fillers[0]()
         results = fillers[1](*unpacked)
         result = None
-        for part, kernel in zip(PARTS, kernels):
-            own = [chunks[index][0] for index in part]
-            other = [chunks[index][1] for index in part]
-            result = kernel(ready, own, other, result)
-        return (chunks, unpacked, ready, results, result)
-
-    def depth(values):
-        return [rotate(values, "wide", step, 2) for step in range(1, rounds)]
-
-    def split(part, own, others):
-        values = jnp.stack([own] + list(others))
-        result = []
-        start = 0
-        for size in sizes[part]:
-            result.append(values[:, start : start + size])
-            start += size
-        return result
+        for pair, kernel in zip(parts, kernels):
+            result = kernel(ready, pair, result)
+        return (parts, unpacked, ready, results, result)
 
     def along(part, stacks, turn):
         return [
-            exchange(stack, *chunk_order(index)[turn]) for stack, index in zip(stacks, PARTS[part])
+            exchange(stack, *chunk_order(index)[turn]) for stack, index in zip(stacks, GATHER.parts[part])
         ]
 
-    def pair(values, others):
-        return [jnp.stack(item) for item in zip(values, others)]
-
-    def across(stacks):
-        return [exchange(stack, "narrow", 1) for stack in stacks]
-
-    order = Order()
-    shared = [None, None, None]
-    shared[0] = order.run(share_core, weights[0])
-    z0 = depth(shared[0])
-    small = order.run(small_block, list(small))
+    def across(values):
+        return (values, exchange(values, "narrow", 1))
+
+    shared = [share_core(values) for values in weights]
+    z0 = gather_depth(shared[0])
+    small = small_block(small)
     xs = exchange(small, "wide", 1)
-    shared[1] = order.run(share_core, weights[1])
-    z1 = depth(shared[1])
-    small = order.run(lambda *items: jnp.stack(items), small, xs)
+    small = pair_up([small], [xs], shared[1])[0]
     ys = exchange(small, "narrow", 2)
-    s0 = order.run(functools.partial(split, 0), shared[0], z0)
+    s0 = lay_out(sizes[0], shared[0], z0, small)
     f0 = along(0, s0, 0)
-    shared[2] = order.run(share_core, weights[2])
-    z2 = depth(shared[2])
-    small = order.run(lambda *items: jnp.stack(items), small, ys)
-    zs = depth(small)
-    s0 = order.run(pair, s0, f0)
+    z1 = gather_depth(shared[1])
+    s0 = pair_up(s0, f0, z1[0])
     g0 = along(0, s0, 1)
-    ready = order.run(fillers[0])
-    s1 = order.run(functools.partial(split, 1), shared[1], z1)
+    ready = fillers[0]()
+    small = pair_up([small], [ys], s0[0])[0]
+    zs = gather_depth(small)
+    s1 = lay_out(sizes[1], shared[1], z1, small)
     f1 = along(1, s1, 0)
-    s0 = order.run(pair, s0, g0)
-    c0 = across(s0)
-    s1 = order.run(pair, s1, f1)
+    p0 = across(pair_all(s0, g0, s1[0]))
+    s1 = pair_up(s1, f1, p0[0])
     g1 = along(1, s1, 1)
-    result = order.run(kernels[0], ready, s0, c0, None)
-    s2 = order.run(functools.partial(split, 2), shared[2], z2)
-    f2 = along(2, s2, 0)
-    s1 = order.run(pair, s1, g1)
-    c1 = across(s1)
-    s2 = order.run(pair, s2, f2)
-    g2 = along(2, s2, 1)
-    small = order.run(lambda own, others: jnp.stack([own] + others), small, zs)
+    result = kernels[0](ready, p0, None, s1[0])
+    small = lay_out([2], small, zs, result[0][0])[0]
     cs = exchange(small, "narrow", 1)
-    result = order.run(kernels[1], ready, s1, c1, result)
-    unpacked = order.run(functools.partial(unpack_block, shapes=shapes), small, cs)
-    results = order.run(fillers[1], *unpacked)
-    s2 = order.run(pair, s2, g2)
-    c2 = across(s2)
-    result = order.run(kernels[2], ready, s2, c2, result)
-    chunks = list(zip(s0 + s1 + s2, c0 + c1 + c2))
-    return (chunks, unpacked, ready, results, result)
-
-
-def add_wide(first, second):
-    return first.astype(jnp.float32) + second.astype(jnp.float32)
-
-
-def narrow(values):
-    return values.astype(jnp.bfloat16)
+    p1 = across(pair_all(s1, g1, small))
+    unpacked = unpack_block(small, cs, shapes=shapes)
+    results = fillers[1](*unpacked)
+    result = kernels[1](ready, p1, result)
+    return ([p0, p1], unpacked, ready, results, result)
 
 
 def scatter_taps(grads, shapes, kernels, pack, fillers):
     rounds = ROUNDS
     if not tuned():
         owned = []
-        for part, kernel in zip(PARTS, kernels):
+        for part, kernel in zip(SCATTER.parts, kernels):
             joined = jnp.stack(kernel(grads))
             pieces = []
-            for index, taps in zip(part, cut([CHUNKS[index] for index in part])):
+            for index, taps in zip(part, cut([SCATTER.chunks[index] for index in part])):
                 piece = joined[:, :, :, :, taps]
                 order = (4, 3, 1, 0, 5, 2, 6) if index % 2 == 0 else (4, 3, 2, 0, 5, 1, 6)
                 piece = piece.transpose(order)
@@ -342,7 +395,7 @@
         small = unpack_grads(small[0, 0].astype(jnp.float32), shapes)
         return (owned, small, low, fillers[1](None))
 
-    sizes = [[CHUNKS[index] for index in part] for part in PARTS]
+    sizes = SCATTER.sizes
 
     def across(pair):
         return (pair[0], exchange(pair[1], "narrow", 1))
@@ -362,24 +415,24 @@
     pair_a = across(kernels[a](grads))
     pair_b = across(kernels[b](grads, tie=pair_a[0]))
     sent = first_sums(sizes[a], *pair_a, pair_b[0])
-    first_a = along(PARTS[a], sent, 0)
+    first_a = along(SCATTER.parts[a], sent, 0)
     low, low_weight = fillers[0](sent[0])
     pair_s = across(pack_block(pack[0], low_weight, *pack[1:], shapes=shapes, tie=low_weight))
     sizes_s = [pair_s[0].shape[3]]
     pair_c = across(kernels[c](grads, tie=pair_s[0]))
     kept_a, sent = second_sums(sizes[a], *pair_a, first_a, pair_c[0])
-    second_a = along(PARTS[a], sent, 1)
+    second_a = along(SCATTER.parts[a], sent, 1)
     sent = first_sums(sizes[b], *pair_b, sent[0])
-    first_b = along(PARTS[b], sent, 0)
+    first_b = along(SCATTER.parts[b], sent, 0)
     kept_a, sent = deep_sums(sizes[a], kept_a, second_a, sent[0])
     far_a = far(sent)
     sent = first_sums(sizes_s, *pair_s, sent)
     first_s = along((0,), sent, 0)
     filled = fillers[1](sent[0])
     kept_b, sent = second_sums(sizes[b], *pair_b, first_b, filled)
-    second_b = along(PARTS[b], sent, 1)
+    second_b = along(SCATTER.parts[b], sent, 1)
     sent = first_sums(sizes[c], *pair_c, sent[0])
-    first_c = along(PARTS[c], sent, 0)
+    first_c = along(SCATTER.parts[c], sent, 0)
     kept_s, sent = second_sums(sizes_s, *pair_s, first_s, sent[0])
     second_s = along((0,), sent, 1)
     total_a, sent = near_sums(kept_a, far_a, sent[0])
@@ -387,7 +440,7 @@
     kept_b, sent = deep_sums(sizes[b], kept_b, second_b, sent)
     far_b = far(sent)
     kept_c, sent = second_sums(sizes[c], *pair_c, first_c, sent)
-    second_c = along(PARTS[c], sent, 1)
+    second_c = along(SCATTER.parts[c], sent, 1)
     kept_s, sent = deep_sums(sizes_s, kept_s, second_s, sent[0])
     far_s = far(sent)
     total_a = last_sums(total_a, near_a, sent)
@@ -412,13 +465,17 @@
     return (max(step, 0), max(-step, 0), height - abs(step))
 
 
-def tap_matrix(pair, tap, place_ref, x_first):
+def tap_matrix(pair, chunk, tap, place_ref):
     row, core = place_ref[2], place_ref[3]
+    flip = lax.rem(pl.program_id(0) + place_ref[1], 2)
+    place = GATHER.place(chunk, tap)
 
     def half(ref):
-        if x_first:
-            return jnp.concatenate([ref[row, 0, 0, tap], ref[1 - row, 0, 0, tap]], axis=1)
-        return jnp.concatenate([ref[0, row, 0, tap], ref[0, 1 - row, 0, tap]], axis=1)
+        if chunk % 2 == 0:
+            sides = [ref[y, flip, 0, place] for y in (row, 1 - row)]
+        else:
+            sides = [ref[flip, y, 0, place] for y in (row, 1 - row)]
+        return jnp.concatenate(sides, axis=1)
 
     mine = half(pair[0])
     other = half(pair[1])
@@ -427,16 +484,11 @@
     return jnp.concatenate([lower, upper], axis=0)
 
 
-def weight_specs(chunk, x_first):
-    taps, rows, cols = chunk[0].shape[3:]
-    shape = (2, 1, 1, taps, rows, cols) if x_first else (1, 2, 1, taps, rows, cols)
-
+def part_spec(array):
     def index_map(step, place_ref):
-        flip = lax.rem(step + place_ref[1], 2)
-        slot = lax.rem(place_ref[0] - step // 2 + ROUNDS, ROUNDS)
-        return (0, flip, slot, 0, 0, 0) if x_first else (flip, 0, slot, 0, 0, 0)
-
-    return [pl.BlockSpec(shape, index_map)] * 2
+        return (0, 0, lax.bitwise_xor(step // 2, place_ref[0]), 0, 0, 0)
+
+    return pl.BlockSpec((2, 2, 1) + array.shape[3:], index_map)
 
 
 def whole_cost(flops, arrays):
@@ -457,22 +509,6 @@
     height, columns, channels = shape
     extents = sum(row_span(dilations[branch], line, height)[2] for branch, line in rows)
     return 2 * 3 * extents * columns * channels * width
-
-
-def chunk_part(chunk):
-    return [index for index, part in enumerate(PARTS) if chunk in part][0]
-
-
-def chunk_start(chunk):
-    part = PARTS[chunk_part(chunk)]
-    return sum(CHUNKS[index] for index in part[: part.index(chunk)])
-
-
-def part_spec(array):
-    def index_map(step, place_ref):
-        return (0, 0, lax.bitwise_xor(step // 2, place_ref[0]), 0, 0, 0)
-
-    return pl.BlockSpec((2, 2, 1) + array.shape[3:], index_map)
 
 
 def full_spec(array):
@@ -511,7 +547,7 @@
     if plan["pool"]:
         member_ref = refs.pop(0)
         sizes_ref = refs.pop(0)
-    pairs = {index: (refs.pop(0), refs.pop(0)) for index in plan["chunks"]}
+    pair = (refs.pop(0), refs.pop(0))
     results = {branch: refs.pop(0) for branch in plan["branches"]}
     stats = {branch: refs.pop(0) for branch in plan["done"]}
     step = pl.program_id(0)
@@ -528,7 +564,7 @@
     for branch, row, chunk, tap in plan["rows"]:
         source, target, extent = row_span(dilations[branch], row, plan["height"])
         matrix = jnp.concatenate(
-            [tap_matrix(pairs[chunk], tap + k, place_ref, chunk % 2 == 0) for k in range(3)],
+            [tap_matrix(pair, chunk, tap + k, place_ref) for k in range(3)],
             axis=0,
         )
         rows_in = pl.ds(source * columns, extent * columns)
@@ -547,16 +583,14 @@
             pool_ref[...] = jnp.zeros_like(pool_ref)
 
         values = center[...]
-        x_first = POINT_CHUNK % 2 == 0
-        pair = pairs[POINT_CHUNK]
         point_ref[...] += jnp.dot(
-            values, tap_matrix(pair, 0, place_ref, x_first), preferred_element_type=jnp.float32
+            values, tap_matrix(pair, GATHER.point_chunk, 0, place_ref), preferred_element_type=jnp.float32
         )
         pooled = jnp.dot(member_ref[...], values, preferred_element_type=jnp.float32)
         pooled = (pooled * sizes_ref[...]).astype(jnp.bfloat16)
         pooled_ref[...] = pooled
         pool_ref[...] += jnp.dot(
-            pooled, tap_matrix(pair, 1, place_ref, x_first), preferred_element_type=jnp.float32
+            pooled, tap_matrix(pair, GATHER.point_chunk, 1, place_ref), preferred_element_type=jnp.float32
         )
 
     @pl.when(step == 2 * ROUNDS - 1)
@@ -567,15 +601,15 @@
             store_moments(point_ref, mask_ref, point_stats_ref)
 
 
-def coarse_forward(part, mask, sides, chunks, shape, begun, pool=None):
+def coarse_forward(part, mask, sides, pair, shape, begun, pool=None, tie=None):
     height, columns, channels = shape
     positions = height * columns
-    rows = part_rows(part)
+    rows = GATHER.part_rows(part)
     branches = sorted({row[0] for row in rows})
-    done = [branch for branch in branches if atrous_layout()[branch][-1][1] in PARTS[part]]
+    done = [branch for branch in branches if GATHER.rows[branch][-1][1] in GATHER.parts[part]]
     plan = {
         "pool": pool is not None,
-        "chunks": PARTS[part],
+        "chunks": GATHER.parts[part],
         "branches": branches,
         "begun": [branch for branch in branches if branch in begun],
         "done": done,
@@ -595,9 +629,13 @@
     if pool:
         args += list(pool)
         specs += [full_spec(item) for item in pool]
-    for index in PARTS[part]:
-        args += list(chunks[index])
-        specs += weight_specs(chunks[index], index % 2 == 0)
+    args += list(pair)
+    specs += [part_spec(item) for item in pair]
+    kernel = functools.partial(coarse_forward_kernel, plan)
+    if tie is not None:
+        kernel = behind_tie(kernel)
+        args.insert(0, tie)
+        specs.insert(0, pl.BlockSpec(memory_space=pl.ANY))
     flat = jax.ShapeDtypeStruct((positions, channels), jnp.float32)
     small = jax.ShapeDtypeStruct((8, channels), jnp.float32)
     outs = [flat] * len(branches) + [small] * len(done)
@@ -607,7 +645,7 @@
     if pool:
         out_specs[-1] = lane_spec(outs[-1])
     results = pl.pallas_call(
-        functools.partial(coarse_forward_kernel, plan),
+        kernel,
         out_shape=outs,
         grid_spec=pltpu.PrefetchScalarGridSpec(
             num_scalar_prefetch=1, grid=(2 * ROUNDS,), in_specs=specs, out_specs=out_specs
@@ -643,7 +681,7 @@
         lower, upper = value[:rows], value[rows:]
         mine = jnp.where(core == 0, lower, upper)
         other = jnp.where(core == 0, upper, lower)
-        place = chunk_start(chunk) + tap
+        place = SCATTER.place(chunk, tap)
         for ref, part in zip(outs, (mine, other)):
             for side, lane_part in ((row, part[:, :cols]), (1 - row, part[:, cols:])):
                 if chunk % 2 == 0:
@@ -669,7 +707,7 @@
     if plan["pool"]:
         for tap, left, right in ((0, center, point_ref), (1, pooled_ref, pool_ref)):
             store(
-                POINT_CHUNK,
+                SCATTER.point_chunk,
                 tap,
                 lax.dot_general(
                     left[...], right[...], across, preferred_element_type=jnp.float32
@@ -679,12 +717,12 @@
 
 def coarse_weight(part, sides, grads, shape, pool=None, tie=None):
     height, columns, channels = shape
-    rows = part_rows(part)
+    rows = SCATTER.part_rows(part)
     branches = sorted({row[0] for row in rows})
     plan = {
         "pool": pool is not None,
         "branches": branches,
-        "chunks": PARTS[part],
+        "chunks": SCATTER.parts[part],
         "rows": rows,
         "columns": columns,
         "height": height,
@@ -706,7 +744,7 @@
         kernel = behind_tie(kernel)
         args.insert(0, tie)
         specs.insert(0, pl.BlockSpec(memory_space=pl.ANY))
-    total = sum(CHUNKS[index] for index in PARTS[part])
+    total = sum(SCATTER.sizes[part])
     tail = (total, center.shape[1] // (4 * ROUNDS), channels // 2)
     outs = [jax.ShapeDtypeStruct((2, 2, ROUNDS) + tail, jnp.bfloat16)] * 2
     out_specs = [part_spec(item) for item in outs]
@@ -731,19 +769,20 @@
     refs = list(refs)
     point_ref, pool_ref, spread_ref = refs.pop(0), refs.pop(0), refs.pop(0)
     grads = [refs.pop(0) for _ in range(3)]
-    pairs = [(refs.pop(0), refs.pop(0)) for _ in range(plan["chunks"])]
+    pairs = [(refs.pop(0), refs.pop(0)) for _ in GATHER.parts]
+    point_pair = pairs[GATHER.part_of(GATHER.point_chunk)]
     out_ref, total_ref = refs
     columns = plan["columns"]
     turned = (((1,), (1,)), ((), ()))
     total_ref[...] = lax.dot_general(
         point_ref[...],
-        tap_matrix(pairs[POINT_CHUNK], 0, place_ref, POINT_CHUNK % 2 == 0),
+        tap_matrix(point_pair, GATHER.point_chunk, 0, place_ref),
         turned,
         preferred_element_type=jnp.float32,
     )
     pooled = lax.dot_general(
         pool_ref[...],
-        tap_matrix(pairs[POINT_CHUNK], 1, place_ref, POINT_CHUNK % 2 == 0),
+        tap_matrix(point_pair, GATHER.point_chunk, 1, place_ref),
         turned,
         preferred_element_type=jnp.float32,
     )
@@ -754,7 +793,10 @@
         for line, chunk, tap in rows:
             source, target, extent = row_span(dilations[branch], line, plan["height"])
             matrix = jnp.concatenate(
-                [tap_matrix(pairs[chunk], tap + k, place_ref, chunk % 2 == 0) for k in range(3)],
+                [
+                    tap_matrix(pairs[GATHER.part_of(chunk)], chunk, tap + k, place_ref)
+                    for k in range(3)
+                ],
                 axis=1,
             )
             total_ref[pl.ds(source * columns, extent * columns), :] += lax.dot_general(
@@ -766,19 +808,18 @@
     out_ref[...] = total_ref[...].astype(jnp.bfloat16)
 
 
-def coarse_input(point_dz, pool_dz, spread, grads, chunks, shape, width, tie=None):
+def coarse_input(point_dz, pool_dz, spread, grads, parts, shape, width, tie=None):
     height, columns, channels = shape
     plan = {
-        "chunks": len(chunks),
         "columns": columns,
         "height": height,
-        "rows": atrous_layout(),
+        "rows": GATHER.rows,
     }
     args = [point_dz, pool_dz, spread] + list(grads)
     specs = [full_spec(item) for item in args]
-    for index, pair in enumerate(chunks):
+    for pair in parts:
         args += list(pair)
-        specs += weight_specs(pair, index % 2 == 0)
+        specs += [part_spec(item) for item in pair]
     kernel = functools.partial(coarse_input_kernel, plan)
     if tie is not None:
         kernel = behind_tie(kernel)
@@ -831,6 +872,38 @@
     return gate * (1.0 + shaped * (1.0 - gate))
 
 
+def merge_vectors(rows_ref, params_ref, vector_ref, sums_ref=None):
+    width = vector_ref.shape[1]
+    means = rows_ref[:, :width]
+    squares = rows_ref[:, width : 2 * width]
+    counts = rows_ref[:, 2 * width : 2 * width + 1]
+    total = jnp.sum(counts, axis=0, keepdims=True)
+    mean = jnp.sum(counts * means, axis=0, keepdims=True) / total
+    gap = means - mean
+    variance = jnp.sum(squares + counts * gap * gap, axis=0, keepdims=True) / total
+    vector_ref[0:1, :] = mean
+    vector_ref[1:2, :] = lax.rsqrt(variance + epsilon)
+    vector_ref[2:4, :] = params_ref[...]
+    if sums_ref is not None:
+        for index in range(2):
+            part = sums_ref[:, index * width : (index + 1) * width]
+            vector_ref[6 + index : 7 + index, :] = jnp.sum(part, axis=0, keepdims=True)
+            vector_ref[4 + index : 5 + index, :] = vector_ref[6 + index : 7 + index, :] / total
+
+
+def send_rows(rows_ref, pieces):
+    joined = jnp.concatenate(pieces, axis=1)
+    rows_ref[...] = jnp.broadcast_to(joined, rows_ref.shape)
+
+
+def send_moments(rows_ref, stats_ref, masks_ref, steps):
+    count = jnp.sum(masks_ref[:, 0:1]) * steps
+    send_rows(
+        rows_ref,
+        [stats_ref[0:1, :], stats_ref[1:2, :], jnp.full((1, 128), 1.0, jnp.float32) * count],
+    )
+
+
 def lag_specs(steps):
     def ahead(array, block):
         return pl.BlockSpec(block, lambda step: (jnp.minimum(step, steps - 1), 0))
@@ -884,8 +957,8 @@
 
 
 def decode_forward_kernel(
-    steps, act_ref, table_ref, low_ref, wide_ref, vector_ref, masks_ref, w_ref, z_ref, stats_ref,
-    up_ref, joined_ref, reduced_ref
+    steps, act_ref, table_ref, low_ref, wide_ref, vector_ref, masks_ref, w_ref, z_ref, rows_ref,
+    up_ref, joined_ref, reduced_ref, stats_ref
 ):
     step = pl.program_id(0)
     columns = table_ref.shape[0]
@@ -943,8 +1016,12 @@
         z_ref[...] = result
         run_moments(result, masks_ref[:, 0:1], stats_ref, step)
 
-
-def decode_forward(act, table, low, wide, vectors, masks, weights):
+    @pl.when(step == steps)
+    def _():
+        send_moments(rows_ref, stats_ref, masks_ref, steps)
+
+
+def decode_forward(act, table, low, wide, vectors, masks, weights, devices):
     positions = low.shape[0]
     columns = table.shape[0]
     block = STRIP * columns
@@ -952,7 +1029,7 @@
     channels = act.shape[2]
     ahead, behind = lag_specs(steps)
     flat = jax.ShapeDtypeStruct((positions, channels), jnp.float32)
-    stats = jax.ShapeDtypeStruct((8, channels), jnp.float32)
+    stats = jax.ShapeDtypeStruct((devices, 2 * channels + 128), jnp.float32)
     up = jax.ShapeDtypeStruct((positions, channels), jnp.bfloat16)
     return pl.pallas_call(
         functools.partial(decode_forward_kernel, steps),
@@ -975,6 +1052,7 @@
         scratch_shapes=[
             pltpu.VMEM((positions + 2 * columns, channels), jnp.bfloat16),
             pltpu.VMEM((positions + 2 * columns, wide.shape[1]), jnp.bfloat16),
+            pltpu.VMEM((8, channels), jnp.float32),
         ],
         compiler_params=pltpu.CompilerParams(vmem_limit_bytes=VMEM_BYTES),
         cost_estimate=cost(2 * positions * 3 * channels * 4 * channels, [low, flat, up]),
@@ -983,7 +1061,8 @@
 
 
 def refine_forward_kernel(
-    steps, columns, z_in_ref, vector_ref, masks_ref, w_ref, z_ref, stats_ref, act_ref
+    steps, columns, z_in_ref, rows_in_ref, params_ref, masks_ref, w_ref, z_ref, rows_ref, act_ref,
+    vector_ref, stats_ref
 ):
     step = pl.program_id(0)
     channels = w_ref.shape[1]
@@ -991,6 +1070,7 @@
     @pl.when(step == 0)
     def _():
         clear_edges(act_ref, columns)
+        merge_vectors(rows_in_ref, params_ref, vector_ref)
 
     @pl.when(step < steps)
     def _():
@@ -1009,35 +1089,51 @@
         z_ref[...] = result
         run_moments(result, masks_ref[:, 0:1], stats_ref, step)
 
-
-def refine_forward(z_in, vectors, masks, weights):
+    @pl.when(step == steps)
+    def _():
+        send_moments(rows_ref, stats_ref, masks_ref, steps)
+
+
+def refine_forward(z_in, rows, params, masks, weights):
     positions, channels = z_in.shape
     block = masks.shape[0]
     columns = block // STRIP
     steps = positions // block
     ahead, behind = lag_specs(steps)
     flat = jax.ShapeDtypeStruct((positions, channels), jnp.float32)
-    stats = jax.ShapeDtypeStruct((8, channels), jnp.float32)
+    stats = jax.ShapeDtypeStruct(rows.shape, jnp.float32)
     return pl.pallas_call(
         functools.partial(refine_forward_kernel, steps, columns),
         out_shape=[flat, stats],
         grid=(steps + 1,),
-        in_specs=[ahead(z_in, (block, channels)), whole(vectors), whole(masks), whole(weights)],
+        in_specs=[
+            ahead(z_in, (block, channels)),
+            whole(rows),
+            whole(params),
+            whole(masks),
+            whole(weights),
+        ],
         out_specs=[behind(flat, (block, channels)), whole(stats)],
-        scratch_shapes=[pltpu.VMEM((positions + 2 * columns, channels), jnp.bfloat16)],
+        scratch_shapes=[
+            pltpu.VMEM((positions + 2 * columns, channels), jnp.bfloat16),
+            pltpu.VMEM((8, channels), jnp.float32),
+            pltpu.VMEM((8, channels), jnp.float32),
+        ],
         compiler_params=pltpu.CompilerParams(vmem_limit_bytes=VMEM_BYTES),
         cost_estimate=cost(2 * positions * 9 * channels * channels, [z_in, flat]),
         name="refine_forward",
-    )(z_in, vectors, masks, weights)
+    )(z_in, rows, params, masks, weights)
 
 
 def class_kernel(
-    z_ref, grad_ref, vector_ref, masks_ref, w_ref, b_ref, logits_ref, sums_ref, weight_ref, bias_ref
+    steps, z_ref, grad_ref, rows_ref, params_ref, masks_ref, w_ref, b_ref, logits_ref, out_ref,
+    vector_ref, sums_ref, weight_ref, bias_ref
 ):
     step = pl.program_id(0)
 
     @pl.when(step == 0)
     def _():
+        merge_vectors(rows_ref, params_ref, vector_ref)
         sums_ref[...] = jnp.zeros_like(sums_ref)
         weight_ref[...] = jnp.zeros_like(weight_ref)
         bias_ref[...] = jnp.zeros_like(bias_ref)
@@ -1060,38 +1156,61 @@
     )
     bias_ref[...] += jnp.sum(grad.astype(jnp.float32), axis=0, keepdims=True)
 
-
-def classify(z, grad, vectors, masks, weights, bias):
+    @pl.when(step == steps - 1)
+    def _():
+        width = vector_ref.shape[1]
+        classes = bias_ref.shape[1]
+        shape = (classes, width)
+        place = lax.broadcasted_iota(jnp.int32, shape, 0) == lax.broadcasted_iota(jnp.int32, shape, 1)
+        wide_bias = jnp.dot(
+            bias_ref[...],
+            jnp.where(place, 1.0, 0.0),
+            preferred_element_type=jnp.float32,
+            precision=highest,
+        )
+        out_ref[...] = jnp.zeros_like(out_ref)
+        send_rows(out_ref.at[:, : 2 * width], [sums_ref[0:1, :], sums_ref[1:2, :]])
+        out_ref[:classes, 2 * width :] = weight_ref[...]
+        out_ref[classes : classes + 1, 2 * width :] = wide_bias
+
+
+def classify(z, grad, rows, params, masks, weights, bias):
     positions, channels = z.shape
     block = masks.shape[0]
     classes = grad.shape[1]
+    steps = positions // block
     outs = [
         jax.ShapeDtypeStruct((positions, classes), jnp.bfloat16),
-        jax.ShapeDtypeStruct((8, channels), jnp.float32),
-        jax.ShapeDtypeStruct((classes, channels), jnp.float32),
-        jax.ShapeDtypeStruct((1, classes), jnp.float32),
+        jax.ShapeDtypeStruct((rows.shape[0], 3 * channels), jnp.float32),
     ]
 
     def strip(width):
         return pl.BlockSpec((block, width), lambda step: (step, 0))
 
     return pl.pallas_call(
-        class_kernel,
+        functools.partial(class_kernel, steps),
         out_shape=outs,
-        grid=(positions // block,),
+        grid=(steps,),
         in_specs=[
             strip(channels),
             strip(classes),
-            whole(vectors),
+            whole(rows),
+            whole(params),
             whole(masks),
             whole(weights),
             whole(bias),
         ],
-        out_specs=[strip(classes)] + [whole(item) for item in outs[1:]],
+        out_specs=[strip(classes), whole(outs[1])],
+        scratch_shapes=[
+            pltpu.VMEM((8, channels), jnp.float32),
+            pltpu.VMEM((8, channels), jnp.float32),
+            pltpu.VMEM((classes, channels), jnp.float32),
+            pltpu.VMEM((1, classes), jnp.float32),
+        ],
         compiler_params=pltpu.CompilerParams(vmem_limit_bytes=VMEM_BYTES),
         cost_estimate=cost(6 * positions * channels * 128, [z, grad, grad]),
         name="classify",
-    )(z, grad, vectors, masks, weights, bias)
+    )(z, grad, rows, params, masks, weights, bias)
 
 
 def finish_grad(local, centered, mask, vector_ref):
@@ -1109,8 +1228,9 @@
 
 
 def refine_backward_kernel(
-    steps, columns, z_ref, grad_ref, vector_ref, cls_ref, z_in_ref, vector_in_ref, masks_ref, w_ref,
-    local_ref, sums_ref, weight_ref, side_ref
+    steps, columns, z_ref, grad_ref, rows_ref, sums_in_ref, params_ref, cls_ref, z_in_ref,
+    rows_in_ref, params_in_ref, masks_ref, w_ref, local_ref, out_ref, totals_ref, weight_ref,
+    side_ref, vector_ref, vector_in_ref, sums_ref
 ):
     step = pl.program_id(0)
     channels = w_ref.shape[1]
@@ -1119,6 +1239,9 @@
     @pl.when(step == 0)
     def _():
         clear_edges(side_ref, columns)
+        merge_vectors(rows_ref, params_ref, vector_ref, sums_in_ref)
+        merge_vectors(rows_in_ref, params_in_ref, vector_in_ref)
+        totals_ref[...] = vector_ref[...]
         sums_ref[...] = jnp.zeros_like(sums_ref)
         weight_ref[...] = jnp.zeros_like(weight_ref)
 
@@ -1154,8 +1277,15 @@
         for k in range(3):
             weight_ref[k] += jnp.dot(turned, sides[k], preferred_element_type=jnp.float32)
 
-
-def refine_backward(z, grad, vectors, classes, z_in, vectors_in, masks, weights):
+    @pl.when(step == steps)
+    def _():
+        share = jnp.sum(sums_in_ref[:, 2 * channels :], axis=0, keepdims=True)
+        send_rows(out_ref, [sums_ref[0:1, :], sums_ref[1:2, :], share])
+
+
+def refine_backward(
+    z, grad, rows, sums, params, classes, z_in, rows_in, params_in, masks, weights
+):
     positions, channels = z.shape
     block = masks.shape[0]
     columns = block // STRIP
@@ -1163,6 +1293,7 @@
     ahead, behind = lag_specs(steps)
     outs = [
         jax.ShapeDtypeStruct((positions, channels), jnp.float32),
+        jax.ShapeDtypeStruct(sums.shape, jnp.float32),
         jax.ShapeDtypeStruct((8, channels), jnp.float32),
         jax.ShapeDtypeStruct((3, channels, 3 * channels), jnp.float32),
     ]
@@ -1173,25 +1304,33 @@
         in_specs=[
             ahead(z, (block, channels)),
             ahead(grad, (block, grad.shape[1])),
-            whole(vectors),
+            whole(rows),
+            whole(sums),
+            whole(params),
             whole(classes),
             behind(z_in, (block, channels)),
-            whole(vectors_in),
+            whole(rows_in),
+            whole(params_in),
             whole(masks),
             whole(weights),
         ],
-        out_specs=[behind(z, (block, channels)), whole(outs[1]), whole(outs[2])],
-        scratch_shapes=[pltpu.VMEM((positions + 2 * columns, 3 * channels), jnp.bfloat16)],
+        out_specs=[behind(z, (block, channels))] + [whole(item) for item in outs[1:]],
+        scratch_shapes=[
+            pltpu.VMEM((positions + 2 * columns, 3 * channels), jnp.bfloat16),
+            pltpu.VMEM((8, channels), jnp.float32),
+            pltpu.VMEM((8, channels), jnp.float32),
+            pltpu.VMEM((8, channels), jnp.float32),
+        ],
         compiler_params=pltpu.CompilerParams(vmem_limit_bytes=VMEM_BYTES),
         cost_estimate=cost(4 * positions * 9 * channels * channels, [z, z_in, grad, outs[0], weights]),
         name="refine_backward",
-    )(z, grad, vectors, classes, z_in, vectors_in, masks, weights)
+    )(z, grad, rows, sums, params, classes, z_in, rows_in, params_in, masks, weights)
 
 
 def decode_backward_kernel(
-    steps, columns, local_ref, z_ref, vector_ref, up_ref, low_ref, wide_ref, low_vector_ref,
-    table_ref, masks_ref, w_ref, coarse_ref, low_local_ref, sums_ref, weight_ref, low_weight_ref,
-    side_ref, total_ref
+    steps, columns, local_ref, z_ref, rows_ref, sums_in_ref, params_ref, up_ref, low_ref, wide_ref,
+    low_vector_ref, table_ref, masks_ref, w_ref, coarse_ref, low_local_ref, sums_ref, totals_ref,
+    weight_ref, low_weight_ref, side_ref, total_ref, vector_ref
 ):
     step = pl.program_id(0)
     channels = w_ref.shape[2]
@@ -1201,6 +1340,8 @@
     @pl.when(step == 0)
     def _():
         clear_edges(side_ref, columns)
+        merge_vectors(rows_ref, params_ref, vector_ref, sums_in_ref)
+        totals_ref[...] = vector_ref[...]
         sums_ref[...] = jnp.zeros_like(sums_ref)
         weight_ref[...] = jnp.zeros_like(weight_ref)
         low_weight_ref[...] = jnp.zeros_like(low_weight_ref)
@@ -1268,7 +1409,9 @@
             )
 
 
-def decode_backward(local, z, vectors, up, low, wide, low_vectors, table, masks, weights, shape):
+def decode_backward(
+    local, z, rows, sums, params, up, low, wide, low_vectors, table, masks, weights, shape
+):
     positions, channels = z.shape
     block = masks.shape[0]
     columns = block // STRIP
@@ -1278,6 +1421,7 @@
     outs = [
         jax.ShapeDtypeStruct((height, coarse_columns, channels), jnp.float32),
         jax.ShapeDtypeStruct((positions, 64), jnp.float32),
+        jax.ShapeDtypeStruct((8, channels), jnp.float32),
         jax.ShapeDtypeStruct((8, channels), jnp.float32),
         jax.ShapeDtypeStruct((3, channels, 3 * channels), jnp.float32),
         jax.ShapeDtypeStruct((3, 64, 3 * channels), jnp.float32),
@@ -1289,7 +1433,9 @@
         in_specs=[
             ahead(local, (block, channels)),
             ahead(z, (block, channels)),
-            whole(vectors),
+            whole(rows),
+            whole(sums),
+            whole(params),
             behind(up, (block, channels)),
             behind(low, (block, low.shape[1])),
             whole(wide),
@@ -1303,11 +1449,12 @@
         scratch_shapes=[
             pltpu.VMEM((positions + 2 * columns, 3 * channels), jnp.bfloat16),
             pltpu.VMEM((height + 2, columns, channels), jnp.float32),
+            pltpu.VMEM((8, channels), jnp.float32),
         ],
         compiler_params=pltpu.CompilerParams(vmem_limit_bytes=VMEM_BYTES),
         cost_estimate=cost(4 * positions * 9 * channels * (channels + 64), [local, z, up, low, outs[1], weights]),
         name="decode_backward",
-    )(local, z, vectors, up, low, wide, low_vectors, table, masks, weights)
+    )(local, z, rows, sums, params, up, low, wide, low_vectors, table, masks, weights)
 
 
 def low_backward_kernel(
@@ -1353,47 +1500,9 @@
         ],
         out_specs=[pl.BlockSpec((block, width), lambda step: (step, 0)), whole(outs[1])],
         compiler_params=pltpu.CompilerParams(vmem_limit_bytes=VMEM_BYTES),
-        cost_estimate=cost(6 * positions * width * 128, [local, low, low]),
+        cost_estimate=whole_cost(6 * positions * width * 128, [local, low, low]),
         name="low_backward",
     )(vectors, tie, local, low, wide, masks)
-
-
-def atrous_layout():
-    places = []
-    for chunk, size in enumerate(CHUNKS):
-        places += [(chunk, tap) for tap in range(2 if chunk == POINT_CHUNK else 0, size)]
-    return [
-        [(line,) + places[9 * branch + 3 * line] for line in range(3)] for branch in range(3)
-    ]
-
-
-def part_rows(part):
-    return [
-        (branch, line, chunk, tap)
-        for branch, rows in enumerate(atrous_layout())
-        for line, chunk, tap in rows
-        if chunk in PARTS[part]
-    ]
-
-
-def order_taps(point, atrous):
-    flat = atrous.reshape((-1,) + atrous.shape[2:])
-    before = sum(CHUNKS[:POINT_CHUNK])
-    flat = jnp.concatenate([flat[:before], point, flat[before:]])
-    parts = []
-    start = 0
-    for part in PARTS:
-        size = sum(CHUNKS[index] for index in part)
-        parts.append(flat[start : start + size])
-        start += size
-    return parts
-
-
-def restore_taps(parts, shape):
-    flat = jnp.concatenate(parts)
-    before = sum(CHUNKS[:POINT_CHUNK])
-    atrous = jnp.concatenate([flat[:before], flat[before + 2 :]])
-    return (flat[before : before + 2], atrous.reshape(shape))
 
 
 def side_values(values, image_ids, dilation):
@@ -1595,7 +1704,7 @@
     lanes = own_ref.shape[-1]
 
     def load(ref, z, x, y, start, size):
-        slot = lax.rem(deep - z + ROUNDS, ROUNDS)
+        slot = lax.bitwise_xor(deep, z)
         return ref[slot, lax.rem(y + row, 2), lax.rem(x + side, 2), start : start + size]
 
     def both(z, x, y, start, size):
@@ -1662,7 +1771,7 @@
         + [pl.BlockSpec(memory_space=pltpu.VMEM)] * 2,
         out_specs=[pl.BlockSpec(memory_space=pltpu.VMEM)] * 4,
         compiler_params=pltpu.CompilerParams(vmem_limit_bytes=VMEM_BYTES),
-        cost_estimate=cost(0, [own, other] + outs + outs),
+        cost_estimate=whole_cost(0, [own, other] + outs + outs),
         name="unpack_weights",
     )(kernel_place(), own, other)
 
@@ -1789,7 +1898,7 @@
         ],
         out_specs=whole(out),
         compiler_params=pltpu.CompilerParams(vmem_limit_bytes=VMEM_BYTES),
-        cost_estimate=cost(2 * low.shape[0] * low.shape[1] * 256, [low]),
+        cost_estimate=whole_cost(2 * low.shape[0] * low.shape[1] * 256, [low]),
         name="low_moments",
     )(low, wide, masks)
 
@@ -1928,9 +2037,8 @@
     def low_part(proj, wide, decode, refine):
         return low_moments(low_flat, wide, masks)
 
-    def forward(part, ready, own, other, before):
+    def forward(part, ready, pair, before, tie=None):
         sums, stats, pooling = ({}, {}, ()) if before is None else before
-        pair = dict(zip(PARTS[part], zip(own, other)))
         more, more_stats, more_pooling = coarse_forward(
             part,
             mask_column,
@@ -1938,15 +2046,16 @@
             pair,
             coarse_shape,
             sums,
-            pool_inputs if POINT_CHUNK in PARTS[part] else None,
+            pool_inputs if GATHER.has_point(part) else None,
+            tie,
         )
         return ({**sums, **more}, {**stats, **more_stats}, tuple(pooling) + tuple(more_pooling))
 
-    chunks, unpacked, ready, low_stats, coarse = gather_taps(
-        order_taps(w_point, w_atrous),
+    parts, unpacked, ready, low_stats, coarse = gather_taps(
+        GATHER.order(w_point, w_atrous),
         small,
         [all_sides, low_part],
-        [functools.partial(forward, part) for part in range(3)],
+        [functools.partial(forward, part) for part in range(len(GATHER.parts))],
     )
     proj_full, low_wide, decode_full, refine_full = unpacked
     sides, grad_flat = ready
@@ -1986,7 +2095,6 @@
         offset += width
     pixel_count = counts_flat[0]
     fine_count = 16.0 * pixel_count
-    fine_local = 16.0 * local_count
     gain_rows = [gains[0], gains[1], gains[2], gains[3], gains[4], low_gain]
     bias_rows = [biases[0], biases[1], biases[2], biases[3], biases[4], low_bias]
     kept = []
@@ -2030,7 +2138,10 @@
     proj_act = proj_act.astype(jnp.bfloat16).astype(jnp.float32)
     cols_table = column_table(ids_coarse)[0].astype(jnp.bfloat16)
     low_vectors = widen(norm_vectors(low_mean, low_var, low_gain, low_bias))
-    decode_z, decode_stats, upsampled = decode_forward(
+    devices = device_count()
+    decode_params = jnp.stack([gains[6], biases[6]])
+    refine_params = jnp.stack([gains[7], biases[7]])
+    decode_z, rows, upsampled = decode_forward(
         proj_act[0],
         jnp.concatenate([cols_table, cols_table], axis=1),
         low_flat,
@@ -2038,56 +2149,47 @@
         low_vectors,
         masks,
         decode_full,
-    )
-    decode_mean, decode_var = merged(decode_stats, fine_local, fine_count)
-    decode_vectors = norm_vectors(decode_mean, decode_var, gains[6], biases[6])
-    refine_z, refine_stats = refine_forward(decode_z, decode_vectors, masks, refine_full)
-    refine_mean, refine_var = merged(refine_stats, fine_local, fine_count)
-    refine_vectors = norm_vectors(refine_mean, refine_var, gains[7], biases[7])
-    logits, refine_sums, cls_weight_grad, cls_bias_grad = classify(
-        refine_z, grad_flat, refine_vectors, masks, w_cls, b_cls.reshape(1, -1)
+        devices,
+    )
+    decode_rows = hand_out(rows)
+    refine_z, rows = refine_forward(decode_z, decode_rows, decode_params, masks, refine_full)
+    refine_rows = hand_out(rows)
+    logits, rows = classify(
+        refine_z, grad_flat, refine_rows, refine_params, masks, w_cls, b_cls.reshape(1, -1)
     )
     logits = logits.reshape(logit_grad.shape)
-    cls_bias_grad = cls_bias_grad[0]
-    devices = device_count()
-    cls_flat = jnp.concatenate([cls_bias_grad, cls_weight_grad.reshape(-1)])
-    share = -(-cls_flat.shape[0] // devices)
-    cls_rows = jnp.pad(cls_flat, (0, share * devices - cls_flat.shape[0])).reshape(devices, share)
-    own = jnp.concatenate([refine_sums[0], refine_sums[1]])
-    own = jnp.broadcast_to(own[None], (devices, 2 * channels))
-    summed = jnp.sum(hand_out(jnp.concatenate([own, cls_rows], axis=1)), axis=0)
-    refine_gain, refine_bias = summed[:channels], summed[channels : 2 * channels]
-    cls_share = summed[2 * channels :]
-    refine_vectors = norm_vectors(
-        refine_mean,
-        refine_var,
-        gains[7],
-        biases[7],
-        refine_gain / fine_count,
-        refine_bias / fine_count,
-    )
-    decode_local, decode_sums, refine_kernel_grad = refine_backward(
-        refine_z, grad_flat, refine_vectors, w_cls, decode_z, decode_vectors, masks, refine_full
-    )
-    rows = from_all(jnp.concatenate([decode_sums[0], decode_sums[1], cls_share]))
-    summed = jnp.sum(rows[:, : 2 * channels], axis=0)
-    decode_gain, decode_bias = summed[:channels], summed[channels:]
-    cls_flat = rows[:, 2 * channels :].reshape(-1)[: cls_flat.shape[0]]
-    classes = cls_bias_grad.shape[0]
-    cls_bias_grad = cls_flat[:classes]
-    cls_weight_grad = cls_flat[classes:].reshape(cls_weight_grad.shape).T
-    decode_vectors = norm_vectors(
-        decode_mean,
-        decode_var,
-        gains[6],
-        biases[6],
-        decode_gain / fine_count,
-        decode_bias / fine_count,
-    )
-    proj_up, reduce_local, reduce_sums, decode_kernel_grad, low_kernel_grad = decode_backward(
+    refine_sums = hand_out(rows)
+    decode_local, rows, refine_totals, refine_kernel_grad = refine_backward(
+        refine_z,
+        grad_flat,
+        refine_rows,
+        refine_sums,
+        refine_params,
+        w_cls,
+        decode_z,
+        decode_rows,
+        decode_params,
+        masks,
+        refine_full,
+    )
+    decode_sums = hand_out(rows)
+    classes = w_cls.shape[1]
+    cls_weight_grad = decode_sums[:classes, 2 * channels :].T
+    cls_bias_grad = decode_sums[classes, 2 * channels : 2 * channels + classes]
+    refine_gain, refine_bias = refine_totals[6], refine_totals[7]
+    (
+        proj_up,
+        reduce_local,
+        reduce_sums,
+        decode_totals,
+        decode_kernel_grad,
+        low_kernel_grad,
+    ) = decode_backward(
         decode_local,
         decode_z,
-        decode_vectors,
+        decode_rows,
+        decode_sums,
+        decode_params,
         upsampled,
         low_flat,
         low_wide,
@@ -2097,6 +2199,7 @@
         decode_full,
         coarse_shape,
     )
+    decode_gain, decode_bias = decode_totals[6], decode_totals[7]
     proj_up = proj_up[None]
     reduce_gain, reduce_bias = reduce_sums[0, :extra], reduce_sums[1, :extra]
 
@@ -2175,7 +2278,7 @@
             pool_dz,
             member_rows * sizes_inverse.reshape(1, 8),
             side_dz,
-            chunks,
+            parts,
             coarse_shape,
             features.shape[3],
             tie,
@@ -2187,21 +2290,21 @@
             sides,
             grads[1:4],
             coarse_shape,
-            (grads[0], pooled, grads[4]) if POINT_CHUNK in PARTS[part] else None,
+            (grads[0], pooled, grads[4]) if SCATTER.has_point(part) else None,
             tie,
         )
 
     owned, small_owned, low_level_grad, features_grad = scatter_taps(
         flat_dz + [pool_dz],
         [item.shape for item in small],
-        [functools.partial(weight_part, part) for part in range(3)],
+        [functools.partial(weight_part, part) for part in range(len(SCATTER.parts))],
         (proj_kernel_grad, decode_kernel_grad, low_kernel_grad, refine_kernel_grad),
         [low_late, input_late],
     )
     low_level_grad = low_level_grad.reshape(low_level.shape)
     features_grad = features_grad.reshape(features.shape)
     proj_owned, reduce_owned, decode_owned, refine_owned = small_owned
-    point_owned, atrous_owned = restore_taps(owned, w_atrous.shape)
+    point_owned, atrous_owned = SCATTER.restore(owned, w_atrous.shape)
     gains_grad = jnp.stack(
         [
             last_pairs[0][0],

time: 842 us -> 809 us (0.961)
  other arithmetic: 96.4 us -> 53.4 us
  local copies, waits for them, and re-layouts: 110 us -> 80.2 us
  Pallas kernels: 290 us -> 315 us
  waiting for transfers between devices: 178 us -> 203 us
  starting transfers between devices: 120 us -> 110 us
    ppermute x55, waiting for transfers between devices: 99.9 us -> 175 us  [exchange(): lax.ppermute(values, axis, [(place, place ^ bit) for place in range(size)])]
    ppermute x12 -> x0, waiting for transfers between devices: 40.2 us -> none  [rotate(): return lax.ppermute(values, axis, pairs)]
    ppermute x12 -> x0, starting transfers between devices: 37.6 us -> none  [rotate(): return lax.ppermute(values, axis, pairs)]
    another operation x18 -> x2, other arithmetic: 31.2 us -> 1.85 us  [the longest x1 1.27 us: per_device(): refine_params = jnp.stack([gains[7], biases[7]])]
    ppermute x55, starting transfers between devices: 50.9 us -> 79.7 us  [exchange(): lax.ppermute(values, axis, [(place, place ^ bit) for place in range(size)])]
    pallas_call x20 -> x29, Pallas kernels: 41 us -> 62.6 us  [one_step(): pl.pallas_call(run, out_shape=outs, grid=(1,), in_specs=[spec or whole_sp...]
    unnamed x467 -> x485, local copies, waits for them, and re-layouts: 68.1 us -> 54.3 us
    all_to_all x6, waiting for transfers between devices: 38.3 us -> 27.7 us  [hand_out(): return lax.all_to_all(rows, ('wide', 'narrow'), 0, 0, tiled=True)]
  transfers between devices with their start and end apart: 73 -> 61, of which waited for: 33 -> 25; matrix products, arithmetic and copies ran while one was open for 10% -> 7% of each run, Pallas kernels for 16% -> 19%
where the time goes in v4:
time: 809 us; the launch traced here: 797 us
  Pallas kernels  315 us (39%)
  waiting for transfers between devices  203 us (25%)
  starting transfers between devices  110 us (14%)
  local copies, waits for them, and re-layouts  80.2 us (10%)
  other arithmetic  53.4 us (7%)
  blocking collectives  25.4 us (3%)
    ppermute x55, waiting for transfers between devices, exchange(): lax.ppermute(values, axis, [(place, place ^ bit) for place in range(size)])  175 us
    ppermute x55, starting transfers between devices, exchange(): lax.ppermute(values, axis, [(place, place ^ bit) for place in range(size)])  79.7 us
    pallas_call x29, Pallas kernels, one_step(): pl.pallas_call(run, out_shape=outs, grid=(1,), in_specs=[spec or whole_sp...  62.6 us
    unnamed x485, local copies, waits for them, and re-layouts  54.3 us
    pallas_call x1, Pallas kernels, decode_backward(): pl.pallas_call(functools.partial(decode_backward_kernel, steps, columns),...  46.1 us
    pallas_call x3, Pallas kernels, coarse_weight(): pl.pallas_call(kernel, out_shape=outs, grid_spec=pltpu.PrefetchScalarGrid...  38.2 us
    pallas_call x1, Pallas kernels, refine_backward(): pl.pallas_call(functools.partial(refine_backward_kernel, steps, columns),...  35.6 us
    pallas_call x2, Pallas kernels, coarse_forward(): pl.pallas_call(kernel, out_shape=outs, grid_spec=pltpu.PrefetchScalarGrid...  31.7 us
  transfers between devices with their start and end apart: 61, of which 25 were waited for; matrix products, arithmetic and copies ran while one was open for 7% of the time, Pallas kernels for 19%

profile of v4, /device:TPU:1, one launch (start us, length us, event | category | flops | bytes accessed | tf_op | source)
XLA Modules:
  0.0 796.8 jit_solution(2758771491624513938)
XLA Ops:
  18.2 9.7 %collective-permute-done.5.refs_1_ = bf16[11,128,128]{2,1,0:T(8,128)(2,1)S(1)} collective-permute-done((bf16[11,128,128]{2,1,0:T(8,128)(2,1)S(1)}, bf16[11,128,128]{2,1,0:T(8,128)(2,1)S(1)}, u32[]{:S(2)}, u32[]{:S(2)}) %collective-permute-start.5) | collective-permute-done | bytes 360480 | tf_op jit(solution)/shard_map/ppermute | solution.py:76
  27.9 10.4 %collective-permute-done.7.refs_3_ = bf16[11,128,128]{2,1,0:T(8,128)(2,1)S(1)} collective-permute-done((bf16[11,128,128]{2,1,0:T(8,128)(2,1)S(1)}, bf16[11,128,128]{2,1,0:T(8,128)(2,1)S(1)}, u32[]{:S(2)}, u32[]{:S(2)}) %collective-permute-start.7) | collective-permute-done | bytes 360480 | tf_op jit(solution)/shard_map/ppermute | solution.py:76
  39.9 7.9 collective-permute-start.1
  47.8 11.7 %collective-permute-done.1.tie_ref.refs_1_ = bf16[18,128,128]{2,1,0:T(8,128)(2,1)S(1)} collective-permute-done((bf16[18,128,128]{2,1,0:T(8,128)(2,1)S(1)}, bf16[18,128,128]{2,1,0:T(8,128)(2,1)S(1)}, u32[]{:S(2)}, u32[]{:S(2)}) %collective-permute-start.1) | collective-permute-done | bytes 589856 | tf_op jit(solution)/shard_map/ppermute | solution.py:76
  62.3 5.5 collective-permute-start.11
  69.1 26.1 %collective-permute-done.10.refs_1_ = bf16[2,33,16,128]{3,2,1,0:T(8,128)(2,1)S(1)} collective-permute-done((bf16[2,33,16,128]{3,2,1,0:T(8,128)(2,1)S(1)}, bf16[2,33,16,128]{3,2,1,0:T(8,128)(2,1)S(1)}, u32[]{:S(2)}, u32[]{:S(2)}) %collective-permute-start.10) | collective-permute-done | bytes 270368 | tf_op jit(solution)/shard_map/ppermute | solution.py:76
  95.3 10.5 %collective-permute-done.11.refs_2_ = bf16[18,128,128]{2,1,0:T(8,128)(2,1)S(1)} collective-permute-done((bf16[18,128,128]{2,1,0:T(8,128)(2,1)S(1)}, bf16[18,128,128]{2,1,0:T(8,128)(2,1)S(1)}, u32[]{:S(2)}, u32[]{:S(2)}) %collective-permute-start.11) | collective-permute-done | bytes 589856 | tf_op jit(solution)/shard_map/ppermute | solution.py:76
  117.4 26.0 %collective-permute-done.15.refs_2_ = bf16[4,9,128,128]{3,2,1,0:T(8,128)(2,1)} collective-permute-done((bf16[4,9,128,128]{3,2,1,0:T(8,128)(2,1)}, bf16[4,9,128,128]{3,2,1,0:T(8,128)(2,1)}, u32[]{:S(2)}, u32[]{:S(2)}) %collective-permute-start.15) | collective-permute-done | bytes 1179680 | tf_op jit(solution)/shard_map/ppermute | solution.py:76
  144.4 4.7 move.35
  150.7 11.8 %collective-permute-start.18 = (bf16[2,2,33,16,128]{4,3,2,1,0:T(8,128)(2,1)S(1)}, bf16[2,2,33,16,128]{4,3,2,1,0:T(8,128)(2,1)S(1)}, u32[]{:S(2)}, u32[]{:S(2)}) collective-permute-start(bf16[2,2,33,16,128]{4,3,2,1,0:T(8,128)(2,1)S(1)} %move.32.tie_ref.refs_0_), channel_id=1, source_target_pairs={{0,8},{4,12},{8,0},{12,4},{16,24},{20,28},{24,16},{28,20},{1,9},{5... | collective-permute-start | bytes 1622024 | tf_op jit(solution)/shard_map/ppermute | solution.py:76
  164.6 5.9 fusion.5
  170.6 15.0 %coarse_forward.2 = (f32[480,256]{1,0:T(8,128)S(1)}, f32[8,256]{1,0:T(8,128)S(1)}, f32[480,256]{1,0:T(8,128)S(1)}, f32[8,256]{1,0:T(8,128)S(1)}, f32[8,256]{1,0:T(8,128)S(1)}, /*index=5*/bf16[8,2048]{1,0:T(8,128)(2,1)S(1)}) custom-call(s32[4]{0:T(128)S(1)} %pad_add_fusion.place_ref, bf16[2,4,9,128,128]{4,3,2,1,0:T(8,128)(2,1)} %get-tuple-element.103.tie_ref.refs_0_, ...), custom_call_target="tpu_custom_call" | custom-call | flops 1 | bytes 1 | tf_op jit(solution)/shard_map/coarse_forward/pallas_call | solution.py:647
  186.2 11.2 %collective-permute-done.20.refs_3_ = bf16[2,2,33,16,128]{4,3,2,1,0:T(8,128)(2,1)S(1)} collective-permute-done((bf16[2,2,33,16,128]{4,3,2,1,0:T(8,128)(2,1)S(1)}, bf16[2,2,33,16,128]{4,3,2,1,0:T(8,128)(2,1)S(1)}, u32[]{:S(2)}, u32[]{:S(2)}) %collective-permute-start.20) | collective-permute-done | bytes 540704 | tf_op jit(solution)/shard_map/ppermute | solution.py:76
  201.0 7.3 move.37.refs_6_.refs_8_
  208.3 5.1 collective-permute-start.23
  216.9 11.2 %collective-permute-done.23.refs_7_.refs_9_ = bf16[2,2,4,18,128,128]{5,4,3,2,1,0:T(8,128)(2,1)} collective-permute-done((bf16[2,2,4,18,128,128]{5,4,3,2,1,0:T(8,128)(2,1)}, bf16[2,2,4,18,128,128]{5,4,3,2,1,0:T(8,128)(2,1)}, u32[]{:S(2)}, u32[]{:S(2)}) %collective-permute-start.23) | collective-permute-done | bytes 9437216 | tf_op jit(solution)/shard_map/ppermute | solution.py:76
  229.6 16.7 %coarse_forward.3 = (f32[480,256]{1,0:T(8,128)S(1)}, f32[480,256]{1,0:T(8,128)S(1)}, f32[8,256]{1,0:T(8,128)S(1)}, f32[8,256]{1,0:T(8,128)S(1)}) custom-call(s32[4]{0:T(128)S(1)} %pad_add_fusion.place_ref, f32[480,1]{1,0:T(8,128)S(1)} %broadcast_in_dim.43.refs_0_, bf16[480,2048]{1,0:T(8,128)(2,1)S(1)} %bitcast.231, bf16[480,2048]{1,0:T(8,128)(2,1)S(1)} %bitcast.246, ...), custom_call_target="tpu_custom_call" | custom-call | flops 1 | bytes 1 | tf_op jit(solution)/shard_map/coarse_forward/pallas_call | solution.py:647
  248.9 12.8 %all-to-all-start = ((f32[32,1,2561]{2,1,0:T(1,128)}), f32[32,1,2561]{2,1,0:T(1,128)}, u32[]{:S(2)}, u32[]{:S(2)}) async-start(f32[32,1,2561]{2,1,0:T(1,128)} %broadcast_in_dim.34), calls=%async_computation | async-start | bytes 688128 | tf_op jit(solution)/shard_map/all_to_all | solution.py:94
  267.4 4.6 low_moments.1
  280.8 5.3 all-to-all-start.1
  287.0 6.6 all-to-all-done.1
  299.5 24.1 %decode_forward.1 = (f32[7680,256]{1,0:T(8,128)}, f32[32,640]{1,0:T(8,128)S(1)}, bf16[7680,256]{1,0:T(8,128)(2,1)}) custom-call(f32[20,24,256]{2,1,0:T(8,128)S(1)} %fusion.31.act_ref, bf16[96,48]{1,0:T(8,128)(2,1)S(1)} %pad_maximum_fusion.10.table_ref, bf16[7680,256]{1,0:T(8,128)(2,1)} %bitcast.235, ...), custom_call_target="tpu_custom_call" | custom-call | flops 1 | bytes 1 | tf_op jit(solution)/shard_map/decode_forward/pallas_call | solution.py:1034
  328.2 7.1 all-to-all-done.2
  338.1 18.4 %refine_forward.1 = (f32[7680,256]{1,0:T(8,128)}, f32[32,640]{1,0:T(8,128)S(1)}) custom-call(f32[7680,256]{1,0:T(8,128)} %get-tuple-element.117.z_in_ref.z_ref, f32[32,640]{1,0:T(8,128)S(1)} %bitcast.273, f32[2,256]{1,0:T(2,128)S(1)} %copy-done.72, f32[768,3]{1,0:T(8,128)S(1)} %copy.258.masks_ref.refs_3_, bf16[9,256,256]{2,1,0:T(8,128)(2,1)S(1)} %copy-done.21), custom_call_target="tpu_custom_call" | custom-call | flops 1 | bytes 1 | tf_op jit(solution)/shard_map/refine_forward/pallas_call | solution.py:1105
  372.7 10.4 %classify.1 = (bf16[7680,21]{1,0:T(8,128)(2,1)S(1)}, f32[32,768]{1,0:T(8,128)S(1)}) custom-call(f32[7680,256]{1,0:T(8,128)} %get-tuple-element.120.z_ref, bf16[7680,21]{1,0:T(8,128)(2,1)S(1)} %bitcast.248, f32[32,640]{1,0:T(8,128)S(1)} %bitcast.276, f32[2,256]{1,0:T(2,128)S(1)} %copy-done.77, f32[768,3]{1,0:T(8,128)S(1)} %copy.258.masks_ref.refs_3_, ...), custom_call_target="tpu_custom_call" | custom-call | flops 1 | bytes 1 | tf_op jit(solution)/shard_map/classify/pallas_call | solution.py:1190
  384.6 11.4 %all_to_all.74 = f32[32,1,768]{2,1,0:T(1,128)S(1)} all-to-all(f32[32,1,768]{2,1,0:T(1,128)S(1)} %copy.267), channel_id=1, replica_groups=mesh['wide'=8,'narrow'=4] {'wide','narrow'}, dimensions={0} | all-to-all | bytes 196608 | tf_op jit(solution)/shard_map/all_to_all | solution.py:94
  396.0 35.6 %refine_backward.1 = (f32[7680,256]{1,0:T(8,128)}, f32[32,768]{1,0:T(8,128)S(1)}, f32[8,256]{1,0:T(8,128)S(1)}, f32[3,256,768]{2,1,0:T(8,128)}) custom-call(f32[7680,256]{1,0:T(8,128)} %get-tuple-element.120.z_ref, bf16[7680,21]{1,0:T(8,128)(2,1)S(1)} %bitcast.249, f32[32,640]{1,0:T(8,128)S(1)} %bitcast.277, f32[32,768]{1,0:T(8,128)S(1)} %bitcast.281, ...), custom_call_target="tpu_custom_call" | custom-call | flops 1 | bytes 1 | tf_op jit(solution)/shard_map/refine_backward/pallas_call | solution.py:1300
  438.9 5.1 all-to-all-done.5
  448.5 46.1 %decode_backward.1 = (f32[20,24,256]{2,1,0:T(8,128)S(1)}, f32[7680,64]{1,0:T(8,128)}, f32[8,256]{1,0:T(8,128)S(1)}, f32[8,256]{1,0:T(8,128)S(1)}, f32[3,256,768]{2,1,0:T(8,128)S(1)}, /*index=5*/f32[3,64,768]{2,1,0:T(8,128)S(1)}) custom-call(f32[7680,256]{1,0:T(8,128)} %get-tuple-element.124.local_ref, f32[7680,256]{1,0:T(8,128)} %get-tuple-element.117.z_in_ref.z_ref, ...), custom_call_target="tpu_custom_call" | custom-call | flops 1 | bytes 1 | tf_op jit(solution)/shard_map/decode_backward/pallas_call | solution.py:1429
  502.8 6.2 all-to-all-done.6
  520.7 14.0 %all_to_all.75 = f32[32,1,2560]{2,1,0:T(1,128)} all-to-all(f32[32,1,2560]{2,1,0:T(1,128)S(1)} %broadcast_in_dim.42), channel_id=1, replica_groups=mesh['wide'=8,'narrow'=4] {'wide','narrow'}, dimensions={0} | all-to-all | bytes 655360 | tf_op jit(solution)/shard_map/all_to_all | solution.py:94
  544.4 14.1 %coarse_weight.3 = (bf16[2,2,4,12,128,128]{5,4,3,2,1,0:T(8,128)(2,1)}, bf16[2,2,4,12,128,128]{5,4,3,2,1,0:T(8,128)(2,1)}) custom-call(s32[4]{0:T(128)S(1)} %copy-done.69, bf16[480,2048]{1,0:T(8,128)(2,1)S(1)} %bitcast.232, bf16[480,2048]{1,0:T(8,128)(2,1)S(1)} %bitcast.247, bf16[480,2048]{1,0:T(8,128)(2,1)} %bitcast.288, bf16[480,2048]{1,0:T(8,128)(2,1)} %bitcast.293, ...), custom_call_target="tpu_custom_call" | custom-call | flops 1 | bytes 1 | tf_op jit(solution)/shard_map/coarse_weight/pallas_call | solution.py:751
  562.1 14.8 %coarse_weight.4 = (bf16[2,2,4,11,128,128]{5,4,3,2,1,0:T(8,128)(2,1)}, bf16[2,2,4,11,128,128]{5,4,3,2,1,0:T(8,128)(2,1)}) custom-call(s32[4]{0:T(128)S(1)} %copy-done.69, bf16[2,2,4,12,128,128]{5,4,3,2,1,0:T(8,128)(2,1)} %get-tuple-element.129.tie_ref.refs_0_, bf16[480,2048]{1,0:T(8,128)(2,1)S(1)} %bitcast.233, bf16[480,2048]{1,0:T(8,128)(2,1)S(1)} %bitcast.243, ...), custom_call_target="tpu_custom_call" | custom-call | flops 1 | bytes 1 | tf_op jit(solution)/shard_map/coarse_weight/pallas_call | solution.py:751
  587.1 9.6 %low_backward.1 = (bf16[7680,256]{1,0:T(8,128)(2,1)}, f32[64,256]{1,0:T(8,128)S(1)}) custom-call(f32[8,256]{1,0:T(8,128)S(1)} %maximum_maximum_fusion.1.place_ref, bf16[2,4,6,128,128]{4,3,2,1,0:T(8,128)(2,1)S(1)} %get-tuple-element.133.tie_ref, f32[7680,64]{1,0:T(8,128)S(1)} %copy-done.31, bf16[7680,256]{1,0:T(8,128)(2,1)} %bitcast.237, ...), custom_call_target="tpu_custom_call" | custom-call | flops 1509949440 | bytes 9830400 | tf_op jit(solution)/shard_map/low_backward/pallas_call | solution.py:1489
  596.7 5.2 pack_gradients.1
  604.3 9.3 %coarse_weight.5 = (bf16[2,2,4,6,128,128]{5,4,3,2,1,0:T(8,128)(2,1)}, bf16[2,2,4,6,128,128]{5,4,3,2,1,0:T(8,128)(2,1)}) custom-call(s32[4]{0:T(128)S(1)} %copy-done.69, bf16[2,2,4,33,16,128]{5,4,3,2,1,0:T(8,128)(2,1)} %copy-done.11, bf16[480,2048]{1,0:T(8,128)(2,1)S(1)} %bitcast.234, bf16[480,2048]{1,0:T(8,128)(2,1)S(1)} %bitcast.244, ...), custom_call_target="tpu_custom_call" | custom-call | flops 1 | bytes 1 | tf_op jit(solution)/shard_map/coarse_weight/pallas_call | solution.py:751
  613.6 5.6 collective-permute-done.26.refs_2_
  619.7 5.2 move.39
  631.7 10.8 %collective-permute-done.29.refs_1_ = bf16[4,6,128,128]{3,2,1,0:T(8,128)(2,1)S(1)} collective-permute-done((bf16[4,6,128,128]{3,2,1,0:T(8,128)(2,1)S(1)}, bf16[4,6,128,128]{3,2,1,0:T(8,128)(2,1)S(1)}, u32[]{:S(2)}, u32[]{:S(2)}) %collective-permute-start.29) | collective-permute-done | bytes 786464 | tf_op jit(solution)/shard_map/ppermute | solution.py:76
  652.0 25.2 %coarse_input.1.tie_ref = bf16[480,2048]{1,0:T(8,128)(2,1)} custom-call(s32[4]{0:T(128)S(1)} %copy-done.69, bf16[2,4,33,16,128]{4,3,2,1,0:T(8,128)(2,1)S(1)} %move.42.tie_ref, bf16[480,256]{1,0:T(8,128)(2,1)S(1)} %bitcast.271, bf16[8,256]{1,0:T(8,128)(2,1)S(1)} %pad.103.refs_9_.refs_1_, f32[480,8]{1,0:T(8,128)S(1)} %bitcast_multiply_fusion.refs_2_, ...), custom_call_target="tpu_custom_call" | custom-call | flops 1 | bytes 1 | tf_op jit(solution)/shard_map/coarse_input/pallas_call | solution.py:829
  677.2 5.4 move.43
  687.0 4.6 collective-permute-done.35.refs_2_
  701.3 7.2 collective-permute-done.38.refs_2_
  714.2 11.2 %collective-permute-done.39.refs_2_ = bf16[2,4,3,128,128]{4,3,2,1,0:T(8,128)(2,1)} collective-permute-done((bf16[2,4,3,128,128]{4,3,2,1,0:T(8,128)(2,1)}, bf16[2,4,3,128,128]{4,3,2,1,0:T(8,128)(2,1)}, u32[]{:S(2)}, u32[]{:S(2)}) %collective-permute-start.39) | collective-permute-done | bytes 786464 | tf_op jit(solution)/shard_map/ppermute | solution.py:76
  738.7 5.4 collective-permute-start.53
  756.4 7.0 collective-permute-done.46.refs_1_
  767.3 4.6 collective-permute-done.47.refs_1_
  780.4 6.4 collective-permute-start.49
  (797 shorter events, 235.4 us)
Async XLA Ops:
  11.0 16.9 %collective-permute-start.5 = (bf16[11,128,128]{2,1,0:T(8,128)(2,1)S(1)}, bf16[11,128,128]{2,1,0:T(8,128)(2,1)S(1)}, u32[]{:S(2)}, u32[]{:S(2)}) collective-permute-start(bf16[11,128,128]{2,1,0:T(8,128)(2,1)S(1)} %pad_maximum_fusion.6.refs_0_), channel_id=1, source_target_pairs={{0,8},{4,12},{8,0},{12,4},{16,24},{20,28},{24,16},{28,20},{1,9},{5... | collective-permute-start | bytes 1081352 | tf_op jit(solution)/shard_map/ppermute | solution.py:76
  12.4 15.6 %collective-permute-start.6 = (bf16[11,128,128]{2,1,0:T(8,128)(2,1)S(1)}, bf16[11,128,128]{2,1,0:T(8,128)(2,1)S(1)}, u32[]{:S(2)}, u32[]{:S(2)}) collective-permute-start(bf16[11,128,128]{2,1,0:T(8,128)(2,1)S(1)} %pad_maximum_fusion.6.refs_0_), channel_id=1, source_target_pairs={{0,16},{4,20},{8,24},{12,28},{16,0},{20,4},{24,8},{28,12},{1,17},{... | collective-permute-start | bytes 1081352 | tf_op jit(solution)/shard_map/ppermute | solution.py:76
  14.7 23.6 %collective-permute-start.7 = (bf16[11,128,128]{2,1,0:T(8,128)(2,1)S(1)}, bf16[11,128,128]{2,1,0:T(8,128)(2,1)S(1)}, u32[]{:S(2)}, u32[]{:S(2)}) collective-permute-start(bf16[11,128,128]{2,1,0:T(8,128)(2,1)S(1)} %pad_maximum_fusion.6.refs_0_), channel_id=1, source_target_pairs={{0,24},{4,28},{8,16},{12,20},{16,8},{20,12},{24,0},{28,4},{1,25},{... | collective-permute-start | bytes 1081352 | tf_op jit(solution)/shard_map/ppermute | solution.py:76
  38.4 21.1 %collective-permute-start.9 = (bf16[4,6,128,128]{3,2,1,0:T(8,128)(2,1)S(1)}, bf16[4,6,128,128]{3,2,1,0:T(8,128)(2,1)S(1)}, u32[]{:S(2)}, u32[]{:S(2)}) collective-permute-start(bf16[4,6,128,128]{3,2,1,0:T(8,128)(2,1)S(1)} %get-tuple-element.98.refs_1_), channel_id=1, source_target_pairs={{0,2},{1,3},{2,0},{3,1},{4,6},{5,7},{6,4},{7,5},{8,10},{9,11},{10,... | collective-permute-start | bytes 2359304 | tf_op jit(solution)/shard_map/ppermute | solution.py:76
  39.7 19.8 %collective-permute-start.8 = (bf16[4,5,128,128]{3,2,1,0:T(8,128)(2,1)S(1)}, bf16[4,5,128,128]{3,2,1,0:T(8,128)(2,1)S(1)}, u32[]{:S(2)}, u32[]{:S(2)}) collective-permute-start(bf16[4,5,128,128]{3,2,1,0:T(8,128)(2,1)S(1)} %get-tuple-element.97.refs_0_), channel_id=1, source_target_pairs={{0,4},{4,0},{8,12},{12,8},{16,20},{20,16},{24,28},{28,24},{1,5},{5... | collective-permute-start | bytes 1966088 | tf_op jit(solution)/shard_map/ppermute | solution.py:76
  39.9 19.6 %collective-permute-start.1 = (bf16[18,128,128]{2,1,0:T(8,128)(2,1)S(1)}, bf16[18,128,128]{2,1,0:T(8,128)(2,1)S(1)}, u32[]{:S(2)}, u32[]{:S(2)}) collective-permute-start(bf16[18,128,128]{2,1,0:T(8,128)(2,1)S(1)} %pad_maximum_fusion.5.tie_ref.refs_0_), channel_id=1, source_target_pairs={{0,8},{4,12},{8,0},{12,4},{16,24},{20,28},{24,16},{28,20},{1,9},{5... | collective-permute-start | bytes 1769480 | tf_op jit(solution)/shard_map/ppermute | solution.py:76
  60.8 46.5 %collective-permute-start.14 = (bf16[2,4,6,128,128]{4,3,2,1,0:T(8,128)(2,1)}, bf16[2,4,6,128,128]{4,3,2,1,0:T(8,128)(2,1)S(1)}, u32[]{:S(2)}, u32[]{:S(2)}) collective-permute-start(bf16[2,4,6,128,128]{4,3,2,1,0:T(8,128)(2,1)} %get-tuple-element.101.refs_1_), channel_id=1, source_target_pairs={{0,4},{4,0},{8,12},{12,8},{16,20},{20,16},{24,28},{28,24},{1,5},{5... | collective-permute-start | bytes 4718600 | tf_op jit(solution)/shard_map/ppermute | solution.py:76
  62.1 45.2 %collective-permute-start.13 = (bf16[2,4,5,128,128]{4,3,2,1,0:T(8,128)(2,1)S(1)}, bf16[2,4,5,128,128]{4,3,2,1,0:T(8,128)(2,1)S(1)}, u32[]{:S(2)}, u32[]{:S(2)}) collective-permute-start(bf16[2,4,5,128,128]{4,3,2,1,0:T(8,128)(2,1)S(1)} %get-tuple-element.99.tie_ref.refs_0_), channel_id=1, source_target_pairs={{0,2},{1,3},{2,0},{3,1},{4,6},{5,7},{6,4},{7,5},{8,10},{9,11},{10,... | collective-permute-start | bytes 3932168 | tf_op jit(solution)/shard_map/ppermute | solution.py:76
  62.3 43.4 %collective-permute-start.11 = (bf16[18,128,128]{2,1,0:T(8,128)(2,1)S(1)}, bf16[18,128,128]{2,1,0:T(8,128)(2,1)S(1)}, u32[]{:S(2)}, u32[]{:S(2)}) collective-permute-start(bf16[18,128,128]{2,1,0:T(8,128)(2,1)S(1)} %pad_maximum_fusion.5.tie_ref.refs_0_), channel_id=1, source_target_pairs={{0,16},{4,20},{8,24},{12,28},{16,0},{20,4},{24,8},{28,12},{1,17},{... | collective-permute-start | bytes 1769480 | tf_op jit(solution)/shard_map/ppermute | solution.py:76
  67.8 37.9 %collective-permute-start.12 = (bf16[18,128,128]{2,1,0:T(8,128)(2,1)S(1)}, bf16[18,128,128]{2,1,0:T(8,128)(2,1)S(1)}, u32[]{:S(2)}, u32[]{:S(2)}) collective-permute-start(bf16[18,128,128]{2,1,0:T(8,128)(2,1)S(1)} %pad_maximum_fusion.5.tie_ref.refs_0_), channel_id=1, source_target_pairs={{0,24},{4,28},{8,16},{12,20},{16,8},{20,12},{24,0},{28,4},{1,25},{... | collective-permute-start | bytes 1769480 | tf_op jit(solution)/shard_map/ppermute | solution.py:76
  68.9 26.4 %collective-permute-start.10 = (bf16[2,33,16,128]{3,2,1,0:T(8,128)(2,1)S(1)}, bf16[2,33,16,128]{3,2,1,0:T(8,128)(2,1)S(1)}, u32[]{:S(2)}, u32[]{:S(2)}) collective-permute-start(bf16[2,33,16,128]{3,2,1,0:T(8,128)(2,1)S(1)} %move.29.tie_ref.refs_0_), channel_id=1, source_target_pairs={{0,2},{1,3},{2,0},{3,1},{4,6},{5,7},{6,4},{7,5},{8,10},{9,11},{10,... | collective-permute-start | bytes 811016 | tf_op jit(solution)/shard_map/ppermute | solution.py:76
  112.7 49.8 %collective-permute-start.17 = (bf16[2,2,4,11,128,128]{5,4,3,2,1,0:T(8,128)(2,1)}, bf16[2,2,4,11,128,128]{5,4,3,2,1,0:T(8,128)(2,1)}, u32[]{:S(2)}, u32[]{:S(2)}) collective-permute-start(bf16[2,2,4,11,128,128]{5,4,3,2,1,0:T(8,128)(2,1)} %move.34.tie_ref.refs_6_), channel_id=1, source_target_pairs={{0,1},{1,0},{2,3},{3,2},{4,5},{5,4},{6,7},{7,6},{8,9},{9,8},{10,11... | collective-permute-start | bytes 17301512 | tf_op jit(solution)/shard_map/ppermute | solution.py:76
  115.6 27.9 %collective-permute-start.15 = (bf16[4,9,128,128]{3,2,1,0:T(8,128)(2,1)}, bf16[4,9,128,128]{3,2,1,0:T(8,128)(2,1)}, u32[]{:S(2)}, u32[]{:S(2)}) collective-permute-start(bf16[4,9,128,128]{3,2,1,0:T(8,128)(2,1)} %get-tuple-element.100.tie_ref.refs_0_), channel_id=1, source_target_pairs={{0,4},{4,0},{8,12},{12,8},{16,20},{20,16},{24,28},{28,24},{1,5},{5... | collective-permute-start | bytes 3538952 | tf_op jit(solution)/shard_map/ppermute | solution.py:76
  116.8 27.6 %collective-permute-start.16 = (bf16[4,9,128,128]{3,2,1,0:T(8,128)(2,1)}, bf16[4,9,128,128]{3,2,1,0:T(8,128)(2,1)}, u32[]{:S(2)}, u32[]{:S(2)}) collective-permute-start(bf16[4,9,128,128]{3,2,1,0:T(8,128)(2,1)} %get-tuple-element.102.refs_1_), channel_id=1, source_target_pairs={{0,2},{1,3},{2,0},{3,1},{4,6},{5,7},{6,4},{7,5},{8,10},{9,11},{10,... | collective-permute-start | bytes 3538952 | tf_op jit(solution)/shard_map/ppermute | solution.py:76
  149.0 52.0 %collective-permute-start.21 = (bf16[2,4,9,128,128]{4,3,2,1,0:T(8,128)(2,1)}, bf16[2,4,9,128,128]{4,3,2,1,0:T(8,128)(2,1)}, u32[]{:S(2)}, u32[]{:S(2)}) collective-permute-start(bf16[2,4,9,128,128]{4,3,2,1,0:T(8,128)(2,1)} %get-tuple-element.103.tie_ref.refs_0_), channel_id=1, source_target_pairs={{0,2},{1,3},{2,0},{3,1},{4,6},{5,7},{6,4},{7,5},{8,10},{9,11},{10,... | collective-permute-start | bytes 7077896 | tf_op jit(solution)/shard_map/ppermute | solution.py:76
  149.3 51.7 %collective-permute-start.22 = (bf16[2,4,9,128,128]{4,3,2,1,0:T(8,128)(2,1)}, bf16[2,4,9,128,128]{4,3,2,1,0:T(8,128)(2,1)}, u32[]{:S(2)}, u32[]{:S(2)}) collective-permute-start(bf16[2,4,9,128,128]{4,3,2,1,0:T(8,128)(2,1)} %get-tuple-element.108.refs_1_), channel_id=1, source_target_pairs={{0,4},{4,0},{8,12},{12,8},{16,20},{20,16},{24,28},{28,24},{1,5},{5... | collective-permute-start | bytes 7077896 | tf_op jit(solution)/shard_map/ppermute | solution.py:76
  150.7 35.5 %collective-permute-start.18 = (bf16[2,2,33,16,128]{4,3,2,1,0:T(8,128)(2,1)S(1)}, bf16[2,2,33,16,128]{4,3,2,1,0:T(8,128)(2,1)S(1)}, u32[]{:S(2)}, u32[]{:S(2)}) collective-permute-start(bf16[2,2,33,16,128]{4,3,2,1,0:T(8,128)(2,1)S(1)} %move.32.tie_ref.refs_0_), channel_id=1, source_target_pairs={{0,8},{4,12},{8,0},{12,4},{16,24},{20,28},{24,16},{28,20},{1,9},{5... | collective-permute-start | bytes 1622024 | tf_op jit(solution)/shard_map/ppermute | solution.py:76
  162.5 23.8 %collective-permute-start.19 = (bf16[2,2,33,16,128]{4,3,2,1,0:T(8,128)(2,1)S(1)}, bf16[2,2,33,16,128]{4,3,2,1,0:T(8,128)(2,1)S(1)}, u32[]{:S(2)}, u32[]{:S(2)}) collective-permute-start(bf16[2,2,33,16,128]{4,3,2,1,0:T(8,128)(2,1)S(1)} %move.32.tie_ref.refs_0_), channel_id=1, source_target_pairs={{0,16},{4,20},{8,24},{12,28},{16,0},{20,4},{24,8},{28,12},{1,17},{... | collective-permute-start | bytes 1622024 | tf_op jit(solution)/shard_map/ppermute | solution.py:76
  162.5 35.0 %collective-permute-start.20 = (bf16[2,2,33,16,128]{4,3,2,1,0:T(8,128)(2,1)S(1)}, bf16[2,2,33,16,128]{4,3,2,1,0:T(8,128)(2,1)S(1)}, u32[]{:S(2)}, u32[]{:S(2)}) collective-permute-start(bf16[2,2,33,16,128]{4,3,2,1,0:T(8,128)(2,1)S(1)} %move.32.tie_ref.refs_0_), channel_id=1, source_target_pairs={{0,24},{4,28},{8,16},{12,20},{16,8},{20,12},{24,0},{28,4},{1,25},{... | collective-permute-start | bytes 1622024 | tf_op jit(solution)/shard_map/ppermute | solution.py:76
  208.3 19.7 %collective-permute-start.23 = (bf16[2,2,4,18,128,128]{5,4,3,2,1,0:T(8,128)(2,1)}, bf16[2,2,4,18,128,128]{5,4,3,2,1,0:T(8,128)(2,1)}, u32[]{:S(2)}, u32[]{:S(2)}) collective-permute-start(bf16[2,2,4,18,128,128]{5,4,3,2,1,0:T(8,128)(2,1)} %move.37.refs_6_.refs_8_), channel_id=1, source_target_pairs={{0,1},{1,0},{2,3},{3,2},{4,5},{5,4},{6,7},{7,6},{8,9},{9,8},{10,11... | collective-permute-start | bytes 28311560 | tf_op jit(solution)/shard_map/ppermute | solution.py:76
  216.7 45.9 %collective-permute-start.24 = (bf16[4,2,2,33,16,128]{5,4,3,2,1,0:T(8,128)(2,1)}, bf16[4,2,2,33,16,128]{5,4,3,2,1,0:T(8,128)(2,1)}, u32[]{:S(2)}, u32[]{:S(2)}) collective-permute-start(bf16[4,2,2,33,16,128]{5,4,3,2,1,0:T(8,128)(2,1)} %copy-done.9), channel_id=1, source_target_pairs={{0,1},{1,0},{2,3},{3,2},{4,5},{5,4},{6,7},{7,6},{8,9},{9,8},{10,11... | collective-permute-start | bytes 6488072 | tf_op jit(solution)/shard_map/ppermute | solution.py:76
  248.9 24.2 %all-to-all-start = ((f32[32,1,2561]{2,1,0:T(1,128)}), f32[32,1,2561]{2,1,0:T(1,128)}, u32[]{:S(2)}, u32[]{:S(2)}) async-start(f32[32,1,2561]{2,1,0:T(1,128)} %broadcast_in_dim.34), calls=%async_computation | async-start | bytes 688128 | tf_op jit(solution)/shard_map/all_to_all | solution.py:94
  558.6 20.6 %collective-permute-start.25 = (bf16[2,2,4,12,128,128]{5,4,3,2,1,0:T(8,128)(2,1)}, bf16[2,2,4,12,128,128]{5,4,3,2,1,0:T(8,128)(2,1)}, u32[]{:S(2)}, u32[]{:S(2)}) collective-permute-start(bf16[2,2,4,12,128,128]{5,4,3,2,1,0:T(8,128)(2,1)} %get-tuple-element.132), channel_id=1, source_target_pairs={{0,1},{1,0},{2,3},{3,2},{4,5},{5,4},{6,7},{7,6},{8,9},{9,8},{10,11... | collective-permute-start | bytes 18874376 | tf_op jit(solution)/shard_map/ppermute | solution.py:76
  577.0 49.6 %collective-permute-start.28 = (bf16[2,2,4,11,128,128]{5,4,3,2,1,0:T(8,128)(2,1)}, bf16[2,2,4,11,128,128]{5,4,3,2,1,0:T(8,128)(2,1)}, u32[]{:S(2)}, u32[]{:S(2)}) collective-permute-start(bf16[2,2,4,11,128,128]{5,4,3,2,1,0:T(8,128)(2,1)} %get-tuple-element.143), channel_id=1, source_target_pairs={{0,1},{1,0},{2,3},{3,2},{4,5},{5,4},{6,7},{7,6},{8,9},{9,8},{10,11... | collective-permute-start | bytes 17301512 | tf_op jit(solution)/shard_map/ppermute | solution.py:76
  583.7 35.6 %collective-permute-start.26 = (bf16[2,4,6,128,128]{4,3,2,1,0:T(8,128)(2,1)S(1)}, bf16[2,4,6,128,128]{4,3,2,1,0:T(8,128)(2,1)S(1)}, u32[]{:S(2)}, u32[]{:S(2)}) collective-permute-start(bf16[2,4,6,128,128]{4,3,2,1,0:T(8,128)(2,1)S(1)} %get-tuple-element.133.tie_ref), channel_id=1, source_target_pairs={{0,4},{4,0},{8,12},{12,8},{16,20},{20,16},{24,28},{28,24},{1,5},{5... | collective-permute-start | bytes 4718600 | tf_op jit(solution)/shard_map/ppermute | solution.py:76
  584.2 35.5 %collective-permute-start.27 = (bf16[2,4,6,128,128]{4,3,2,1,0:T(8,128)(2,1)}, bf16[2,4,6,128,128]{4,3,2,1,0:T(8,128)(2,1)S(1)}, u32[]{:S(2)}, u32[]{:S(2)}) collective-permute-start(bf16[2,4,6,128,128]{4,3,2,1,0:T(8,128)(2,1)} %get-tuple-element.141), channel_id=1, source_target_pairs={{0,2},{1,3},{2,0},{3,1},{4,6},{5,7},{6,4},{7,5},{8,10},{9,11},{10,... | collective-permute-start | bytes 4718600 | tf_op jit(solution)/shard_map/ppermute | solution.py:76
  603.4 44.7 %collective-permute-start.31 = (bf16[2,2,4,33,16,128]{5,4,3,2,1,0:T(8,128)(2,1)}, bf16[2,2,4,33,16,128]{5,4,3,2,1,0:T(8,128)(2,1)S(1)}, u32[]{:S(2)}, u32[]{:S(2)}) collective-permute-start(bf16[2,2,4,33,16,128]{5,4,3,2,1,0:T(8,128)(2,1)} %get-tuple-element.148), channel_id=1, source_target_pairs={{0,1},{1,0},{2,3},{3,2},{4,5},{5,4},{6,7},{7,6},{8,9},{9,8},{10,11... | collective-permute-start | bytes 6488072 | tf_op jit(solution)/shard_map/ppermute | solution.py:76
  613.6 69.9 %collective-permute-start.34 = (bf16[2,2,4,6,128,128]{5,4,3,2,1,0:T(8,128)(2,1)}, bf16[2,2,4,6,128,128]{5,4,3,2,1,0:T(8,128)(2,1)}, u32[]{:S(2)}, u32[]{:S(2)}) collective-permute-start(bf16[2,2,4,6,128,128]{5,4,3,2,1,0:T(8,128)(2,1)} %get-tuple-element.152), channel_id=1, source_target_pairs={{0,1},{1,0},{2,3},{3,2},{4,5},{5,4},{6,7},{7,6},{8,9},{9,8},{10,11... | collective-permute-start | bytes 9437192 | tf_op jit(solution)/shard_map/ppermute | solution.py:76
  624.9 17.5 %collective-permute-start.29 = (bf16[4,6,128,128]{3,2,1,0:T(8,128)(2,1)S(1)}, bf16[4,6,128,128]{3,2,1,0:T(8,128)(2,1)S(1)}, u32[]{:S(2)}, u32[]{:S(2)}) collective-permute-start(bf16[4,6,128,128]{3,2,1,0:T(8,128)(2,1)S(1)} %get-tuple-element.142.tie_ref), channel_id=1, source_target_pairs={{0,2},{1,3},{2,0},{3,1},{4,6},{5,7},{6,4},{7,5},{8,10},{9,11},{10,... | collective-permute-start | bytes 2359304 | tf_op jit(solution)/shard_map/ppermute | solution.py:76
  625.6 19.3 %collective-permute-start.30 = (bf16[4,6,128,128]{3,2,1,0:T(8,128)(2,1)S(1)}, bf16[4,6,128,128]{3,2,1,0:T(8,128)(2,1)S(1)}, u32[]{:S(2)}, u32[]{:S(2)}) collective-permute-start(bf16[4,6,128,128]{3,2,1,0:T(8,128)(2,1)S(1)} %get-tuple-element.146), channel_id=1, source_target_pairs={{0,4},{4,0},{8,12},{12,8},{16,20},{20,16},{24,28},{28,24},{1,5},{5... | collective-permute-start | bytes 2359304 | tf_op jit(solution)/shard_map/ppermute | solution.py:76
  630.7 46.5 %collective-permute-start.33 = (bf16[2,4,6,128,128]{4,3,2,1,0:T(8,128)(2,1)}, bf16[2,4,6,128,128]{4,3,2,1,0:T(8,128)(2,1)S(1)}, u32[]{:S(2)}, u32[]{:S(2)}) collective-permute-start(bf16[2,4,6,128,128]{4,3,2,1,0:T(8,128)(2,1)} %get-tuple-element.150), channel_id=1, source_target_pairs={{0,2},{1,3},{2,0},{3,1},{4,6},{5,7},{6,4},{7,5},{8,10},{9,11},{10,... | collective-permute-start | bytes 4718600 | tf_op jit(solution)/shard_map/ppermute | solution.py:76
  642.5 34.8 %collective-permute-start.32 = (bf16[2,4,5,128,128]{4,3,2,1,0:T(8,128)(2,1)S(1)}, bf16[2,4,5,128,128]{4,3,2,1,0:T(8,128)(2,1)S(1)}, u32[]{:S(2)}, u32[]{:S(2)}) collective-permute-start(bf16[2,4,5,128,128]{4,3,2,1,0:T(8,128)(2,1)S(1)} %get-tuple-element.144.tie_ref), channel_id=1, source_target_pairs={{0,4},{4,0},{8,12},{12,8},{16,20},{20,16},{24,28},{28,24},{1,5},{5... | collective-permute-start | bytes 3932168 | tf_op jit(solution)/shard_map/ppermute | solution.py:76
  649.5 42.1 %collective-permute-start.35 = (bf16[2,4,33,16,128]{4,3,2,1,0:T(8,128)(2,1)S(1)}, bf16[2,4,33,16,128]{4,3,2,1,0:T(8,128)(2,1)S(1)}, u32[]{:S(2)}, u32[]{:S(2)}) collective-permute-start(bf16[2,4,33,16,128]{4,3,2,1,0:T(8,128)(2,1)S(1)} %move.42.tie_ref), channel_id=1, source_target_pairs={{0,4},{4,0},{8,12},{12,8},{16,20},{20,16},{24,28},{28,24},{1,5},{5... | collective-permute-start | bytes 3244040 | tf_op jit(solution)/shard_map/ppermute | solution.py:76
  651.2 48.5 %collective-permute-start.36 = (bf16[2,12,128,128]{3,2,1,0:T(8,128)(2,1)}, bf16[2,12,128,128]{3,2,1,0:T(8,128)(2,1)}, u32[]{:S(2)}, u32[]{:S(2)}) collective-permute-start(bf16[2,12,128,128]{3,2,1,0:T(8,128)(2,1)} %get-tuple-element.147.tie_ref), channel_id=1, source_target_pairs={{0,16},{4,20},{8,24},{12,28},{16,0},{20,4},{24,8},{28,12},{1,17},{... | collective-permute-start | bytes 2359304 | tf_op jit(solution)/shard_map/ppermute | solution.py:76
  682.6 25.9 %collective-permute-start.38 = (bf16[4,6,128,128]{3,2,1,0:T(8,128)(2,1)}, bf16[4,6,128,128]{3,2,1,0:T(8,128)(2,1)}, u32[]{:S(2)}, u32[]{:S(2)}) collective-permute-start(bf16[4,6,128,128]{3,2,1,0:T(8,128)(2,1)} %get-tuple-element.158), channel_id=1, source_target_pairs={{0,4},{4,0},{8,12},{12,8},{16,20},{20,16},{24,28},{28,24},{1,5},{5... | collective-permute-start | bytes 2359304 | tf_op jit(solution)/shard_map/ppermute | solution.py:76
  683.6 17.8 %collective-permute-start.37 = (bf16[4,5,128,128]{3,2,1,0:T(8,128)(2,1)}, bf16[4,5,128,128]{3,2,1,0:T(8,128)(2,1)}, u32[]{:S(2)}, u32[]{:S(2)}) collective-permute-start(bf16[4,5,128,128]{3,2,1,0:T(8,128)(2,1)} %get-tuple-element.151.tie_ref), channel_id=1, source_target_pairs={{0,2},{1,3},{2,0},{3,1},{4,6},{5,7},{6,4},{7,5},{8,10},{9,11},{10,... | collective-permute-start | bytes 1966088 | tf_op jit(solution)/shard_map/ppermute | solution.py:76
  686.3 39.1 %collective-permute-start.39 = (bf16[2,4,3,128,128]{4,3,2,1,0:T(8,128)(2,1)}, bf16[2,4,3,128,128]{4,3,2,1,0:T(8,128)(2,1)}, u32[]{:S(2)}, u32[]{:S(2)}) collective-permute-start(bf16[2,4,3,128,128]{4,3,2,1,0:T(8,128)(2,1)} %get-tuple-element.153.tie_ref), channel_id=1, source_target_pairs={{0,4},{4,0},{8,12},{12,8},{16,20},{20,16},{24,28},{28,24},{1,5},{5... | collective-permute-start | bytes 2359304 | tf_op jit(solution)/shard_map/ppermute | solution.py:76
  692.6 32.8 %collective-permute-start.40 = (bf16[2,4,3,128,128]{4,3,2,1,0:T(8,128)(2,1)}, bf16[2,4,3,128,128]{4,3,2,1,0:T(8,128)(2,1)}, u32[]{:S(2)}, u32[]{:S(2)}) collective-permute-start(bf16[2,4,3,128,128]{4,3,2,1,0:T(8,128)(2,1)} %get-tuple-element.160), channel_id=1, source_target_pairs={{0,2},{1,3},{2,0},{3,1},{4,6},{5,7},{6,4},{7,5},{8,10},{9,11},{10,... | collective-permute-start | bytes 2359304 | tf_op jit(solution)/shard_map/ppermute | solution.py:76
  699.6 33.5 %collective-permute-start.41 = (bf16[4,33,16,128]{3,2,1,0:T(8,128)(2,1)S(1)}, bf16[4,33,16,128]{3,2,1,0:T(8,128)(2,1)S(1)}, u32[]{:S(2)}, u32[]{:S(2)}) collective-permute-start(bf16[4,33,16,128]{3,2,1,0:T(8,128)(2,1)S(1)} %get-tuple-element.154.tie_ref), channel_id=1, source_target_pairs={{0,2},{1,3},{2,0},{3,1},{4,6},{5,7},{6,4},{7,5},{8,10},{9,11},{10,... | collective-permute-start | bytes 1622024 | tf_op jit(solution)/shard_map/ppermute | solution.py:76
  711.7 39.6 %collective-permute-start.45 = (bf16[2,11,128,128]{3,2,1,0:T(8,128)(2,1)}, bf16[2,11,128,128]{3,2,1,0:T(8,128)(2,1)}, u32[]{:S(2)}, u32[]{:S(2)}) collective-permute-start(bf16[2,11,128,128]{3,2,1,0:T(8,128)(2,1)} %get-tuple-element.159.tie_ref), channel_id=1, source_target_pairs={{0,16},{4,20},{8,24},{12,28},{16,0},{20,4},{24,8},{28,12},{1,17},{... | collective-permute-start | bytes 2162696 | tf_op jit(solution)/shard_map/ppermute | solution.py:76
  713.6 22.0 %collective-permute-start.42 = (bf16[12,128,128]{2,1,0:T(8,128)(2,1)S(1)}, bf16[12,128,128]{2,1,0:T(8,128)(2,1)S(1)}, u32[]{:S(2)}, u32[]{:S(2)}) collective-permute-start(bf16[12,128,128]{2,1,0:T(8,128)(2,1)S(1)} %get-tuple-element.156.tie_ref), channel_id=1, source_target_pairs={{0,8},{4,12},{8,0},{12,4},{16,24},{20,28},{24,16},{28,20},{1,9},{5... | collective-permute-start | bytes 1179656 | tf_op jit(solution)/shard_map/ppermute | solution.py:76
  728.8 15.4 %collective-permute-start.43 = (bf16[4,3,128,128]{3,2,1,0:T(8,128)(2,1)}, bf16[4,3,128,128]{3,2,1,0:T(8,128)(2,1)S(1)}, u32[]{:S(2)}, u32[]{:S(2)}) collective-permute-start(bf16[4,3,128,128]{3,2,1,0:T(8,128)(2,1)} %get-tuple-element.161.tie_ref), channel_id=1, source_target_pairs={{0,2},{1,3},{2,0},{3,1},{4,6},{5,7},{6,4},{7,5},{8,10},{9,11},{10,... | collective-permute-start | bytes 1179656 | tf_op jit(solution)/shard_map/ppermute | solution.py:76
  729.8 15.1 %collective-permute-start.44 = (bf16[4,3,128,128]{3,2,1,0:T(8,128)(2,1)}, bf16[4,3,128,128]{3,2,1,0:T(8,128)(2,1)S(1)}, u32[]{:S(2)}, u32[]{:S(2)}) collective-permute-start(bf16[4,3,128,128]{3,2,1,0:T(8,128)(2,1)} %get-tuple-element.166), channel_id=1, source_target_pairs={{0,4},{4,0},{8,12},{12,8},{16,20},{20,16},{24,28},{28,24},{1,5},{5... | collective-permute-start | bytes 1179656 | tf_op jit(solution)/shard_map/ppermute | solution.py:76
  734.7 28.7 %collective-permute-start.46 = (bf16[2,33,16,128]{3,2,1,0:T(8,128)(2,1)}, bf16[2,33,16,128]{3,2,1,0:T(8,128)(2,1)}, u32[]{:S(2)}, u32[]{:S(2)}) collective-permute-start(bf16[2,33,16,128]{3,2,1,0:T(8,128)(2,1)} %get-tuple-element.163.tie_ref), channel_id=1, source_target_pairs={{0,16},{4,20},{8,24},{12,28},{16,0},{20,4},{24,8},{28,12},{1,17},{... | collective-permute-start | bytes 811016 | tf_op jit(solution)/shard_map/ppermute | solution.py:76
  738.7 26.4 %collective-permute-start.53 = (bf16[12,128,64]{1,2,0:T(8,128)(2,1)}, bf16[12,128,64]{1,2,0:T(8,128)(2,1)}, u32[]{:S(2)}, u32[]{:S(2)}) collective-permute-start(bf16[12,128,64]{1,2,0:T(8,128)(2,1)} %fusion.32), channel_id=1, source_target_pairs={{0,1},{1,0},{2,3},{3,2},{4,5},{5,4},{6,7},{7,6},{8,9},{9,8},{10,11... | collective-permute-start | bytes 589832 | tf_op jit(solution)/shard_map/ppermute | solution.py:76
  749.5 22.4 %collective-permute-start.47 = (bf16[2,6,128,128]{3,2,1,0:T(8,128)(2,1)}, bf16[2,6,128,128]{3,2,1,0:T(8,128)(2,1)}, u32[]{:S(2)}, u32[]{:S(2)}) collective-permute-start(bf16[2,6,128,128]{3,2,1,0:T(8,128)(2,1)} %get-tuple-element.167.tie_ref), channel_id=1, source_target_pairs={{0,16},{4,20},{8,24},{12,28},{16,0},{20,4},{24,8},{28,12},{1,17},{... | collective-permute-start | bytes 1179656 | tf_op jit(solution)/shard_map/ppermute | solution.py:76
  753.3 20.4 %collective-permute-start.48 = (bf16[11,128,128]{2,1,0:T(8,128)(2,1)}, bf16[11,128,128]{2,1,0:T(8,128)(2,1)}, u32[]{:S(2)}, u32[]{:S(2)}) collective-permute-start(bf16[11,128,128]{2,1,0:T(8,128)(2,1)} %get-tuple-element.169.tie_ref), channel_id=1, source_target_pairs={{0,8},{4,12},{8,0},{12,4},{16,24},{20,28},{24,16},{28,20},{1,9},{5... | collective-permute-start | bytes 1081352 | tf_op jit(solution)/shard_map/ppermute | solution.py:76
  773.7 13.1 %collective-permute-start.51 = (bf16[6,128,128]{2,1,0:T(8,128)(2,1)}, bf16[6,128,128]{2,1,0:T(8,128)(2,1)S(1)}, u32[]{:S(2)}, u32[]{:S(2)}) collective-permute-start(bf16[6,128,128]{2,1,0:T(8,128)(2,1)} %get-tuple-element.173.tie_ref), channel_id=1, source_target_pairs={{0,8},{4,12},{8,0},{12,4},{16,24},{20,28},{24,16},{28,20},{1,9},{5... | collective-permute-start | bytes 589832 | tf_op jit(solution)/shard_map/ppermute | solution.py:76
  (239 other events, 2856.0 us)

commit v5 on v4

--- a/solution.py
+++ b/solution.py
@@ -67,7 +67,7 @@
         return (flat[before : before + 2], atrous.reshape(shape))
 
 
-GATHER = Layout((5, 6, 9, 9), 0)
+GATHER = Layout((5, 6, 6, 3, 3, 6), 0)
 SCATTER = Layout((3, 3, 5, 6, 6, 6), 2)
 
 
@@ -144,18 +144,19 @@
     return jnp.where(mark == mark, values, jnp.zeros_like(values))
 
 
-def one_step(body, outs, args, specs=None, tie=None):
+def one_step(body, outs, args, specs=None, tie=None, vmem=32 * 1024 * 1024):
     def whole_spec(array):
         return pl.BlockSpec(array.shape, lambda step: (0,) * len(array.shape))
 
     specs = list(specs or [None] * len(args))
     run = body
     if tie is not None:
-        args = [tie] + list(args)
-        specs = [pl.BlockSpec(memory_space=pl.ANY)] + specs
-
-        def run(tie_ref, *refs):
-            body(*refs)
+        ties = tie if isinstance(tie, list) else [tie]
+        args = ties + list(args)
+        specs = [pl.BlockSpec(memory_space=pl.ANY)] * len(ties) + specs
+
+        def run(*refs):
+            body(*refs[len(ties) :])
 
     return pl.pallas_call(
         run,
@@ -163,7 +164,7 @@
         grid=(1,),
         in_specs=[spec or whole_spec(arg) for spec, arg in zip(specs, args)],
         out_specs=[whole_spec(out) for out in outs],
-        compiler_params=pltpu.CompilerParams(vmem_limit_bytes=VMEM_BYTES),
+        compiler_params=pltpu.CompilerParams(vmem_limit_bytes=vmem),
         cost_estimate=cost(0, args),
         name="move",
     )(*args)
@@ -212,6 +213,26 @@
             refs[2 * count + index][1] = refs[count + index][...]
 
     return one_step(body, outs, list(values) + list(others), tie=tie)
+
+
+def pair_cut(sizes, values, others, tie=None):
+    count = len(values)
+    outs = [
+        jax.ShapeDtypeStruct((2, ROUNDS, size) + values[0].shape[2:], values[0].dtype)
+        for part in sizes
+        for size in part
+    ]
+
+    def body(*refs):
+        for index in range(count):
+            taps = cut([part[index] for part in sizes])
+            for part in range(len(sizes)):
+                target = refs[2 * count + part * count + index]
+                for half in range(2):
+                    target[half] = refs[half * count + index][:, taps[part]]
+
+    results = one_step(body, outs, list(values) + list(others), tie=tie)
+    return [results[part * count : (part + 1) * count] for part in range(len(sizes))]
 
 
 def pair_all(values, others, tie=None):
@@ -304,7 +325,7 @@
     return [("wide", 1), ("narrow", 2)] if index % 2 == 0 else [("narrow", 2), ("wide", 1)]
 
 
-def gather_taps(weights, small, fillers, kernels):
+def gather_taps(weights, small, fillers, kernels, prepared):
     rounds = ROUNDS
     sizes = GATHER.sizes
     shapes = [item.shape for item in small]
@@ -343,25 +364,40 @@
     def across(values):
         return (values, exchange(values, "narrow", 1))
 
+    first, second = sizes[1], sizes[2]
+    weights = [
+        weights[0],
+        jnp.concatenate(
+            [
+                weights[1][: first[0]],
+                weights[2][: second[0]],
+                weights[1][first[0] :],
+                weights[2][second[0] :],
+            ]
+        ),
+    ]
+    joint = [first[0] + second[0], first[1] + second[1]]
     shared = [share_core(values) for values in weights]
     z0 = gather_depth(shared[0])
     small = small_block(small)
     xs = exchange(small, "wide", 1)
     small = pair_up([small], [xs], shared[1])[0]
     ys = exchange(small, "narrow", 2)
+    small = pair_up([small], [ys])[0]
     s0 = lay_out(sizes[0], shared[0], z0, small)
     f0 = along(0, s0, 0)
     z1 = gather_depth(shared[1])
-    s0 = pair_up(s0, f0, z1[0])
+    s0 = pair_up(s0, f0, [z1[1]] + prepared)
     g0 = along(0, s0, 1)
     ready = fillers[0]()
-    small = pair_up([small], [ys], s0[0])[0]
+    s1 = lay_out(joint, shared[1], z1, s0[0])
+    f1 = along(0, s1, 0)
+    small = pass_on(small, s1[0])
     zs = gather_depth(small)
-    s1 = lay_out(sizes[1], shared[1], z1, small)
-    f1 = along(1, s1, 0)
     p0 = across(pair_all(s0, g0, s1[0]))
-    s1 = pair_up(s1, f1, p0[0])
-    g1 = along(1, s1, 1)
+    s1, s2 = pair_cut([first, second], s1, f1, zs[0])
+    g1 = along(0, s1, 1)
+    g2 = along(0, s2, 1)
     result = kernels[0](ready, p0, None, s1[0])
     small = lay_out([2], small, zs, result[0][0])[0]
     cs = exchange(small, "narrow", 1)
@@ -369,7 +405,9 @@
     unpacked = unpack_block(small, cs, shapes=shapes)
     results = fillers[1](*unpacked)
     result = kernels[1](ready, p1, result)
-    return ([p0, p1], unpacked, ready, results, result)
+    p2 = across(pair_all(s2, g2, p1[0]))
+    result = kernels[2](ready, p2, result)
+    return ([p0, p1, p2], unpacked, ready, results, result)
 
 
 def scatter_taps(grads, shapes, kernels, pack, fillers):
@@ -1457,6 +1495,97 @@
     )(local, z, rows, sums, params, up, low, wide, low_vectors, table, masks, weights)
 
 
+def branch_back(
+    upstream, z, vectors, joined, weights, branch_z, pool_z, branch_vectors, mask, pool_mask, member,
+    devices
+):
+    positions, channels = z.shape
+    width = joined.shape[1]
+    count = len(branch_z)
+    outs = [
+        jax.ShapeDtypeStruct((width, channels), jnp.float32),
+        jax.ShapeDtypeStruct((positions, count * channels), jnp.float32),
+        jax.ShapeDtypeStruct(pool_z.shape, jnp.float32),
+        jax.ShapeDtypeStruct((devices, 2 * width), jnp.float32),
+    ]
+    args = [upstream, z, vectors, joined, weights, pool_z, branch_vectors, mask, pool_mask, member]
+    args += list(branch_z)
+
+    def body(*refs):
+        (up_ref, z_ref, vector_ref, joined_ref, w_ref, pool_ref, branch_ref, mask_ref) = refs[:8]
+        pool_mask_ref, member_ref = refs[8:10]
+        z_refs = refs[10 : 10 + count]
+        weight_ref, local_ref, pool_local_ref, rows_ref = refs[10 + count :]
+        valid = mask_ref[...]
+        centered, shaped = shaped_of(z_ref[...], vector_ref)
+        local = valid * up_ref[...] * slope_of(shaped, sigmoid(shaped))
+        grad = finish_grad(local, centered, valid, vector_ref).astype(jnp.bfloat16)
+        weight_ref[...] = lax.dot_general(
+            joined_ref[...], grad, (((0,), (0,)), ((), ())), preferred_element_type=jnp.float32
+        )
+        spread = lax.dot_general(
+            grad, w_ref[...], (((1,), (1,)), ((), ())), preferred_element_type=jnp.float32
+        )
+        gains = []
+        biases = []
+        for index in range(count + 1):
+            lanes = slice(index * channels, (index + 1) * channels)
+            values = spread[:, lanes]
+            if index < count:
+                source, allowed = z_refs[index], valid
+            else:
+                source, allowed = pool_ref, pool_mask_ref[...]
+                upper = values.astype(jnp.bfloat16)
+                lower = (values - upper.astype(jnp.float32)).astype(jnp.bfloat16)
+                values = jnp.dot(member_ref[...], upper, preferred_element_type=jnp.float32)
+                values += jnp.dot(member_ref[...], lower, preferred_element_type=jnp.float32)
+            centered, shaped = shaped_of(source[...], branch_ref.at[:, lanes])
+            term = allowed * values * slope_of(shaped, sigmoid(shaped))
+            if index < count:
+                local_ref[:, lanes] = term
+            else:
+                pool_local_ref[...] = term
+            gains.append(jnp.sum(term * centered, axis=0, keepdims=True))
+            biases.append(jnp.sum(term, axis=0, keepdims=True))
+        send_rows(rows_ref, gains + biases)
+
+    return one_step(body, outs, args, vmem=60 * 1024 * 1024)
+
+
+def branch_grads(rows, local, pool_local, branch_z, pool_z, branch_vectors, counts, mask, pool_mask):
+    positions, channels = branch_z[0].shape
+    count = len(branch_z)
+    width = (count + 1) * channels
+    outs = [jax.ShapeDtypeStruct((positions, channels), jnp.bfloat16)] * count
+    outs += [jax.ShapeDtypeStruct(pool_z.shape, jnp.bfloat16)]
+    outs += [jax.ShapeDtypeStruct((8, width), jnp.float32)]
+    args = [rows, local, pool_local, pool_z, branch_vectors, counts, mask, pool_mask]
+    args += list(branch_z)
+
+    def body(*refs):
+        rows_ref, local_ref, pool_local_ref, pool_ref, branch_ref, counts_ref = refs[:6]
+        mask_ref, pool_mask_ref = refs[6:8]
+        z_refs = refs[8 : 8 + count]
+        grad_refs, totals_ref = refs[8 + count : -1], refs[-1]
+        totals_ref[...] = jnp.zeros_like(totals_ref)
+        totals_ref[0:1, :] = jnp.sum(rows_ref[:, :width], axis=0, keepdims=True)
+        totals_ref[1:2, :] = jnp.sum(rows_ref[:, width:], axis=0, keepdims=True)
+        for index in range(count + 1):
+            lanes = slice(index * channels, (index + 1) * channels)
+            vectors = branch_ref.at[:, lanes]
+            source = z_refs[index] if index < count else pool_ref
+            allowed = mask_ref[...] if index < count else pool_mask_ref[...]
+            term = local_ref[:, lanes] if index < count else pool_local_ref[...]
+            centered, _ = shaped_of(source[...], vectors)
+            share = 1.0 / counts_ref[:, lanes]
+            inner = term - totals_ref[1:2, lanes] * share
+            inner = inner - centered * (totals_ref[0:1, lanes] * share)
+            grad = allowed * vector(vectors, 2) * vector(vectors, 1) * inner
+            grad_refs[index][...] = grad.astype(jnp.bfloat16)
+
+    return one_step(body, outs, args, vmem=60 * 1024 * 1024)
+
+
 def low_backward_kernel(
     vector_ref, local_ref, low_ref, wide_ref, masks_ref, out_ref, weight_ref
 ):
@@ -1614,13 +1743,6 @@
     local_term = valid_map * upstream * sigmoid_value * (1.0 + shaped * (1.0 - sigmoid_value))
     axes = tuple(range(local_term.ndim - 1))
     return (local_term, jnp.sum(local_term * centered, axis=axes), jnp.sum(local_term, axis=axes))
-
-
-def norm_grad_finish(
-    local_term, valid_map, centered, norm_scale, gain_row, gain_sum, bias_sum, count_all
-):
-    inner = local_term - bias_sum / count_all - centered * gain_sum / count_all
-    return (valid_map * gain_row * norm_scale * inner).astype(jnp.bfloat16)
 
 
 def moments(values, valid_map, local_count, count_all):
@@ -2024,6 +2146,29 @@
     sizes_inverse = jnp.pad(1.0 / image_sizes[0], (0, 8 - images)).reshape(8, 1)
     pool_inputs = (member_rows.T.astype(jnp.bfloat16), sizes_inverse)
 
+    cols_table = column_table(ids_coarse)[0].astype(jnp.bfloat16)
+    up_table = jnp.concatenate([cols_table, cols_table], axis=1)
+    down_table = jnp.concatenate([cols_table.T, cols_table.T], axis=1)
+    decode_params = jnp.stack([gains[6], biases[6]])
+    refine_params = jnp.stack([gains[7], biases[7]])
+    pool_mask = (jnp.arange(8) < images).astype(jnp.float32).reshape(8, 1)
+    grad_flat = logit_grad.reshape(-1, logit_grad.shape[-1])
+    spread_rows = member_rows * sizes_inverse.reshape(1, 8)
+    prepared = [
+        masks,
+        mask_column,
+        sizes_inverse,
+        pool_inputs[0],
+        up_table,
+        down_table,
+        decode_params,
+        refine_params,
+        pool_mask,
+        grad_flat,
+        w_cls,
+        spread_rows,
+    ]
+
     def all_sides():
         sides = [
             [
@@ -2032,7 +2177,7 @@
             ]
             for dilation in dilations
         ]
-        return (sides, logit_grad.reshape(-1, logit_grad.shape[-1]))
+        return (sides, grad_flat)
 
     def low_part(proj, wide, decode, refine):
         return low_moments(low_flat, wide, masks)
@@ -2056,11 +2201,13 @@
         small,
         [all_sides, low_part],
         [functools.partial(forward, part) for part in range(len(GATHER.parts))],
+        prepared,
     )
     proj_full, low_wide, decode_full, refine_full = unpacked
     sides, grad_flat = ready
     sums, stats, pool_results = coarse
     point_z, point_stats, pool_z, pooled = pool_results
+    pool_wide = pool_z
     pool_z = pool_z[None, :images]
     coarse_stats = [point_stats, stats[0], stats[1], stats[2]]
     coarse_z = [
@@ -2136,14 +2283,11 @@
         proj_z, valid_coarse, proj_mean, proj_var, gains[5], biases[5]
     )
     proj_act = proj_act.astype(jnp.bfloat16).astype(jnp.float32)
-    cols_table = column_table(ids_coarse)[0].astype(jnp.bfloat16)
     low_vectors = widen(norm_vectors(low_mean, low_var, low_gain, low_bias))
     devices = device_count()
-    decode_params = jnp.stack([gains[6], biases[6]])
-    refine_params = jnp.stack([gains[7], biases[7]])
     decode_z, rows, upsampled = decode_forward(
         proj_act[0],
-        jnp.concatenate([cols_table, cols_table], axis=1),
+        up_table,
         low_flat,
         low_wide,
         low_vectors,
@@ -2194,7 +2338,7 @@
         low_flat,
         low_wide,
         low_vectors,
-        jnp.concatenate([cols_table.T, cols_table.T], axis=1),
+        down_table,
         masks,
         decode_full,
         coarse_shape,
@@ -2209,49 +2353,62 @@
     summed_pairs = gradient_sums([(proj_gain, proj_bias), (reduce_gain, reduce_bias)])
     proj_gain, proj_bias = summed_pairs[0]
     reduce_gain, reduce_bias = summed_pairs[1]
-    proj_dz = norm_grad_finish(
-        proj_local,
-        valid_coarse,
-        proj_centered,
-        proj_scale,
-        gains[5],
-        proj_gain,
-        proj_bias,
-        pixel_count,
-    )
-    proj_kernel_grad = jnp.einsum(
-        "nhwc,nhwd->cd", joined_coarse, proj_dz, preferred_element_type=jnp.float32
-    )
-    concat_grad = jnp.einsum(
-        "nhwd,cd->nhwc", proj_dz, proj_full, preferred_element_type=jnp.float32
-    )
-    branch_terms = []
-    for index in range(4):
-        upstream = concat_grad[..., index * channels : (index + 1) * channels]
-        branch_terms.append(norm_grad_terms(upstream, valid_coarse, kept[index][0], kept[index][1]))
-    pool_up = jnp.einsum(
-        "nhwd,nwk->nkd", concat_grad[..., 4 * channels :], member, precision=highest
-    )
-    branch_terms.append(norm_grad_terms(pool_up, all_ones, kept[4][0], kept[4][1]))
-    local_pairs = [(term_item[1], term_item[2]) for term_item in branch_terms]
-    last_pairs = gradient_sums(local_pairs)
-    valid_list = [valid_coarse, valid_coarse, valid_coarse, valid_coarse, all_ones]
-    count_list = [pixel_count, pixel_count, pixel_count, pixel_count, images_total]
-    branch_dz = [
-        norm_grad_finish(
-            branch_terms[index][0],
-            valid_list[index],
-            kept[index][0],
-            kept[index][2],
-            gains[index],
-            last_pairs[index][0],
-            last_pairs[index][1],
-            count_list[index],
+    flat_z = [item.reshape(height * columns, channels) for item in coarse_z]
+    branch_vectors = jnp.concatenate(
+        [
+            norm_vectors(section_means[index], section_vars[index], gains[index], biases[index])
+            for index in range(5)
+        ],
+        axis=1,
+    )
+    branch_counts = jnp.concatenate(
+        [
+            jnp.full((1, 4 * channels), 1.0) * pixel_count,
+            jnp.full((1, channels), images_total, jnp.float32),
+        ],
+        axis=1,
+    )
+    proj_kernel_grad, branch_local, pool_local, rows = branch_back(
+        proj_up.reshape(height * columns, channels),
+        proj_z.reshape(height * columns, channels),
+        norm_vectors(
+            proj_mean,
+            proj_var,
+            gains[5],
+            biases[5],
+            proj_gain / pixel_count,
+            proj_bias / pixel_count,
+        ),
+        joined_coarse.reshape(height * columns, -1),
+        proj_full,
+        flat_z,
+        pool_wide,
+        branch_vectors,
+        mask_column,
+        pool_mask,
+        pool_inputs[0],
+        devices,
+    )
+    rows = hand_out(rows)
+    branch_dz = branch_grads(
+        rows,
+        branch_local,
+        pool_local,
+        flat_z,
+        pool_wide,
+        branch_vectors,
+        branch_counts,
+        mask_column,
+        pool_mask,
+    )
+    flat_dz, pool_dz, branch_totals = list(branch_dz[:4]), branch_dz[4], branch_dz[5]
+    last_pairs = [
+        (
+            branch_totals[0, index * channels : (index + 1) * channels],
+            branch_totals[1, index * channels : (index + 1) * channels],
         )
         for index in range(5)
     ]
-    flat_dz = [item.reshape(height * columns, channels) for item in branch_dz[:4]]
-    pool_dz = jnp.pad(branch_dz[4][0], ((0, 8 - images), (0, 0)))
     low_vectors = widen(
         norm_vectors(
             low_mean,
@@ -2268,15 +2425,17 @@
 
     def input_late(tie):
         side_dz = [
-            side_grads(branch_dz[branch + 1], ids_coarse, dilations[branch]).reshape(
-                height * columns, -1
-            )
+            side_grads(
+                flat_dz[branch + 1].reshape(1, height, columns, channels),
+                ids_coarse,
+                dilations[branch],
+            ).reshape(height * columns, -1)
             for branch in range(3)
         ]
         return coarse_input(
             flat_dz[0],
             pool_dz,
-            member_rows * sizes_inverse.reshape(1, 8),
+            spread_rows,
             side_dz,
             parts,
             coarse_shape,

time: 809 us -> 786 us (0.972)
  blocking collectives: 25.4 us -> 0 us
  other arithmetic: 53.4 us -> 30.2 us
  local copies, waits for them, and re-layouts: 80.2 us -> 103 us
  starting transfers between devices: 110 us -> 100 us
    all_to_all x2 -> x0, blocking collectives: 25.4 us -> none  [hand_out(): return lax.all_to_all(rows, ('wide', 'narrow'), 0, 0, tiled=True)]
    unnamed x485 -> x445, local copies, waits for them, and re-layouts: 54.3 us -> 69.3 us
    all_to_all x6 -> x8, waiting for transfers between devices: 27.7 us -> 41.5 us  [hand_out(): return lax.all_to_all(rows, ('wide', 'narrow'), 0, 0, tiled=True)]
    ppermute x55 -> x58, waiting for transfers between devices: 175 us -> 167 us  [exchange(): lax.ppermute(values, axis, [(place, place ^ bit) for place in range(size)])]
    ppermute x55 -> x58, starting transfers between devices: 79.7 us -> 73.3 us  [exchange(): lax.ppermute(values, axis, [(place, place ^ bit) for place in range(size)])]
    pallas_call x2 -> x3, Pallas kernels: 31.7 us -> 37.4 us  [coarse_forward(): pl.pallas_call(kernel, out_shape=outs, grid_spec=pltpu.PrefetchScalarGrid...]
    all_to_all x6 -> x8, starting transfers between devices: 30.3 us -> 26.8 us  [hand_out(): return lax.all_to_all(rows, ('wide', 'narrow'), 0, 0, tiled=True)]
    pallas_call x29 -> x33, Pallas kernels: 62.6 us -> 64.1 us  [one_step(): pl.pallas_call(run, out_shape=outs, grid=(1,), in_specs=[spec or whole_sp...]
  transfers between devices with their start and end apart: 61 -> 66, of which waited for: 25 -> 27; matrix products, arithmetic and copies ran while one was open for 7% -> 7% of each run, Pallas kernels for 19% -> 20%
where the time goes in v5:
time: 786 us; the launch traced here: 773 us
  Pallas kernels  323 us (41%)
  waiting for transfers between devices  209 us (27%)
  local copies, waits for them, and re-layouts  103 us (13%)
  starting transfers between devices  100 us (13%)
  other arithmetic  30.2 us (4%)
    ppermute x58, waiting for transfers between devices, exchange(): lax.ppermute(values, axis, [(place, place ^ bit) for place in range(size)])  167 us
    ppermute x58, starting transfers between devices, exchange(): lax.ppermute(values, axis, [(place, place ^ bit) for place in range(size)])  73.3 us
    unnamed x445, local copies, waits for them, and re-layouts  69.3 us
    pallas_call x33, Pallas kernels, one_step(): pl.pallas_call(run, out_shape=outs, grid=(1,), in_specs=[spec or whole_sp...  64.1 us
    pallas_call x1, Pallas kernels, decode_backward(): pl.pallas_call(functools.partial(decode_backward_kernel, steps, columns),...  45.9 us
    all_to_all x8, waiting for transfers between devices, hand_out(): return lax.all_to_all(rows, ('wide', 'narrow'), 0, 0, tiled=True)  41.5 us
    pallas_call x3, Pallas kernels, coarse_weight(): pl.pallas_call(kernel, out_shape=outs, grid_spec=pltpu.PrefetchScalarGrid...  38.8 us
    pallas_call x3, Pallas kernels, coarse_forward(): pl.pallas_call(kernel, out_shape=outs, grid_spec=pltpu.PrefetchScalarGrid...  37.4 us
  transfers between devices with their start and end apart: 66, of which 27 were waited for; matrix products, arithmetic and copies ran while one was open for 7% of the time, Pallas kernels for 20%

profile of v5, /device:TPU:1, one launch (start us, length us, event | category | flops | bytes accessed | tf_op | source)
XLA Modules:
  0.0 772.9 jit_solution(16838258902752062634)
XLA Ops:
  21.5 5.0 collective-permute-done.4.refs_1_
  26.5 3.7 collective-permute-done.6.refs_2_
  30.2 10.4 %collective-permute-done.8.refs_4_ = bf16[11,128,128]{2,1,0:T(8,128)(2,1)S(1)} collective-permute-done((bf16[11,128,128]{2,1,0:T(8,128)(2,1)S(1)}, bf16[11,128,128]{2,1,0:T(8,128)(2,1)S(1)}, u32[]{:S(2)}, u32[]{:S(2)}) %collective-permute-start.8) | collective-permute-done | bytes 360480 | tf_op jit(solution)/shard_map/ppermute | solution.py:76
  43.0 8.9 %collective-permute-start.1 = (bf16[18,128,128]{2,1,0:T(8,128)(2,1)}, bf16[18,128,128]{2,1,0:T(8,128)(2,1)}, u32[]{:S(2)}, u32[]{:S(2)}) collective-permute-start(bf16[18,128,128]{2,1,0:T(8,128)(2,1)} %pad_maximum_fusion.6.refs_0_.refs_1_), channel_id=1, source_target_pairs={{0,16},{4,20},{8,24},{12,28},{16,0},{20,4},{24,8},{28,12},{1,17},{... | collective-permute-start | bytes 1769480 | tf_op jit(solution)/shard_map/ppermute | solution.py:76
  54.8 22.7 %collective-permute-done.1.refs_0_.refs_3_ = bf16[18,128,128]{2,1,0:T(8,128)(2,1)} collective-permute-done((bf16[18,128,128]{2,1,0:T(8,128)(2,1)}, bf16[18,128,128]{2,1,0:T(8,128)(2,1)}, u32[]{:S(2)}, u32[]{:S(2)}) %collective-permute-start.1) | collective-permute-done | bytes 589856 | tf_op jit(solution)/shard_map/ppermute | solution.py:76
  80.6 13.8 %collective-permute-done.11.refs_2_ = bf16[18,128,128]{2,1,0:T(8,128)(2,1)S(1)} collective-permute-done((bf16[18,128,128]{2,1,0:T(8,128)(2,1)}, bf16[18,128,128]{2,1,0:T(8,128)(2,1)S(1)}, u32[]{:S(2)}, u32[]{:S(2)}) %collective-permute-start.11) | collective-permute-done | bytes 589856 | tf_op jit(solution)/shard_map/ppermute | solution.py:76
  94.3 9.9 %collective-permute-done.12.refs_4_ = bf16[18,128,128]{2,1,0:T(8,128)(2,1)S(1)} collective-permute-done((bf16[18,128,128]{2,1,0:T(8,128)(2,1)}, bf16[18,128,128]{2,1,0:T(8,128)(2,1)S(1)}, u32[]{:S(2)}, u32[]{:S(2)}) %collective-permute-start.12) | collective-permute-done | bytes 589856 | tf_op jit(solution)/shard_map/ppermute | solution.py:76
  108.2 5.6 collective-permute-done.17.refs_4_
  120.6 13.6 %collective-permute-done.13.refs_0_.refs_2_ = bf16[2,2,33,16,128]{4,3,2,1,0:T(8,128)(2,1)} collective-permute-done((bf16[2,2,33,16,128]{4,3,2,1,0:T(8,128)(2,1)}, bf16[2,2,33,16,128]{4,3,2,1,0:T(8,128)(2,1)}, u32[]{:S(2)}, u32[]{:S(2)}) %collective-permute-start.13) | collective-permute-done | bytes 540704 | tf_op jit(solution)/shard_map/ppermute | solution.py:76
  134.2 13.0 %collective-permute-done.14.refs_3_ = bf16[4,9,128,128]{3,2,1,0:T(8,128)(2,1)} collective-permute-done((bf16[4,9,128,128]{3,2,1,0:T(8,128)(2,1)}, bf16[4,9,128,128]{3,2,1,0:T(8,128)(2,1)}, u32[]{:S(2)}, u32[]{:S(2)}) %collective-permute-start.14) | collective-permute-done | bytes 1179680 | tf_op jit(solution)/shard_map/ppermute | solution.py:76
  151.9 24.3 %collective-permute-done.19.refs_3_ = bf16[2,2,33,16,128]{4,3,2,1,0:T(8,128)(2,1)S(1)} collective-permute-done((bf16[2,2,33,16,128]{4,3,2,1,0:T(8,128)(2,1)}, bf16[2,2,33,16,128]{4,3,2,1,0:T(8,128)(2,1)S(1)}, u32[]{:S(2)}, u32[]{:S(2)}) %collective-permute-start.19) | collective-permute-done | bytes 540704 | tf_op jit(solution)/shard_map/ppermute | solution.py:76
  179.3 6.1 fusion.5
  185.5 15.4 %coarse_forward.3 = (f32[480,256]{1,0:T(8,128)S(1)}, f32[8,256]{1,0:T(8,128)S(1)}, f32[480,256]{1,0:T(8,128)S(1)}, f32[8,256]{1,0:T(8,128)S(1)}, f32[8,256]{1,0:T(8,128)S(1)}, /*index=5*/bf16[8,2048]{1,0:T(8,128)(2,1)S(1)}) custom-call(s32[4]{0:T(128)S(1)} %pad_add_fusion.place_ref, bf16[2,4,6,128,128]{4,3,2,1,0:T(8,128)(2,1)S(1)} %get-tuple-element.114.tie_ref.refs_1_, ...), custom_call_target="tpu_custom_call" | custom-call | flops 1 | bytes 1 | tf_op jit(solution)/shard_map/coarse_forward/pallas_call | solution.py:685
  216.6 11.0 %coarse_forward.4 = (f32[480,256]{1,0:T(8,128)S(1)}, f32[8,256]{1,0:T(8,128)S(1)}) custom-call(s32[4]{0:T(128)S(1)} %pad_add_fusion.place_ref, f32[480,1]{1,0:T(8,128)S(1)} %broadcast_in_dim.46.refs_2_.refs_0_.refs_7_.refs_6_, bf16[480,2048]{1,0:T(8,128)(2,1)S(1)} %bitcast.243, bf16[480,2048]{1,0:T(8,128)(2,1)S(1)} %bitcast.265, ...), custom_call_target="tpu_custom_call" | custom-call | flops 1 | bytes 1 | tf_op jit(solution)/shard_map/coarse_forward/pallas_call | solution.py:685
  228.4 11.0 %coarse_forward.5 = (f32[480,256]{1,0:T(8,128)S(1)}, f32[8,256]{1,0:T(8,128)S(1)}) custom-call(s32[4]{0:T(128)S(1)} %pad_add_fusion.place_ref, f32[480,1]{1,0:T(8,128)S(1)} %broadcast_in_dim.46.refs_2_.refs_0_.refs_7_.refs_6_, bf16[480,2048]{1,0:T(8,128)(2,1)S(1)} %bitcast.244, bf16[480,2048]{1,0:T(8,128)(2,1)S(1)} %bitcast.271, ...), custom_call_target="tpu_custom_call" | custom-call | flops 1 | bytes 1 | tf_op jit(solution)/shard_map/coarse_forward/pallas_call | solution.py:685
  251.1 4.7 low_moments.1
  263.6 6.0 all-to-all-start.1
  272.1 4.9 all-to-all-done.1
  284.1 24.3 %decode_forward.1 = (f32[7680,256]{1,0:T(8,128)}, f32[32,640]{1,0:T(8,128)S(1)}, bf16[7680,256]{1,0:T(8,128)(2,1)}) custom-call(f32[20,24,256]{2,1,0:T(8,128)S(1)} %fusion.24.act_ref, bf16[96,48]{1,0:T(8,128)(2,1)S(1)} %copy-done.87, bf16[7680,256]{1,0:T(8,128)(2,1)} %bitcast.248, bf16[256,256]{1,0:T(8,128)(2,1)S(1)} %copy-done.53, ...), custom_call_target="tpu_custom_call" | custom-call | flops 1 | bytes 1 | tf_op jit(solution)/shard_map/decode_forward/pallas_call | solution.py:1072
  320.9 18.4 %refine_forward.1 = (f32[7680,256]{1,0:T(8,128)}, f32[32,640]{1,0:T(8,128)S(1)}) custom-call(f32[7680,256]{1,0:T(8,128)} %get-tuple-element.131.z_in_ref.z_ref, f32[32,640]{1,0:T(8,128)S(1)} %bitcast.282, f32[2,256]{1,0:T(2,128)S(1)} %copy-done.94, f32[768,3]{1,0:T(8,128)S(1)} %copy.326.refs_1_.masks_ref.refs_3_, bf16[9,256,256]{2,1,0:T(8,128)(2,1)S(1)} %copy-done.37), custom_call_target="tpu_custom_call" | custom-call | flops 1 | bytes 1 | tf_op jit(solution)/shard_map/refine_forward/pallas_call | solution.py:1143
  340.1 3.5 all-to-all-start.3
  346.9 4.1 all-to-all-done.3
  354.2 10.4 %classify.1 = (bf16[7680,21]{1,0:T(8,128)(2,1)S(1)}, f32[32,768]{1,0:T(8,128)S(1)}) custom-call(f32[7680,256]{1,0:T(8,128)} %get-tuple-element.134.z_ref, bf16[7680,21]{1,0:T(8,128)(2,1)S(1)} %bitcast.268, f32[32,640]{1,0:T(8,128)S(1)} %bitcast.285, f32[2,256]{1,0:T(2,128)S(1)} %copy-done.100, f32[768,3]{1,0:T(8,128)S(1)} %copy.326.refs_1_.masks_ref.refs_3_, ...), custom_call_target="tpu_custom_call" | custom-call | flops 1 | bytes 1 | tf_op jit(solution)/shard_map/classify/pallas_call | solution.py:1228
  370.5 6.7 all-to-all-done.4
  380.1 35.8 %refine_backward.1 = (f32[7680,256]{1,0:T(8,128)}, f32[32,768]{1,0:T(8,128)S(1)}, f32[8,256]{1,0:T(8,128)S(1)}, f32[3,256,768]{2,1,0:T(8,128)}) custom-call(f32[7680,256]{1,0:T(8,128)} %get-tuple-element.134.z_ref, bf16[7680,21]{1,0:T(8,128)(2,1)S(1)} %bitcast.269, f32[32,640]{1,0:T(8,128)S(1)} %bitcast.286, f32[32,768]{1,0:T(8,128)S(1)} %bitcast.290, ...), custom_call_target="tpu_custom_call" | custom-call | flops 1 | bytes 1 | tf_op jit(solution)/shard_map/refine_backward/pallas_call | solution.py:1338
  420.2 6.9 all-to-all-done.5
  428.5 45.9 %decode_backward.1 = (f32[20,24,256]{2,1,0:T(8,128)S(1)}, f32[7680,64]{1,0:T(8,128)}, f32[8,256]{1,0:T(8,128)S(1)}, f32[8,256]{1,0:T(8,128)S(1)}, f32[3,256,768]{2,1,0:T(8,128)S(1)}, /*index=5*/f32[3,64,768]{2,1,0:T(8,128)S(1)}) custom-call(f32[7680,256]{1,0:T(8,128)} %get-tuple-element.138.local_ref, f32[7680,256]{1,0:T(8,128)} %get-tuple-element.131.z_in_ref.z_ref, ...), custom_call_target="tpu_custom_call" | custom-call | flops 1 | bytes 1 | tf_op jit(solution)/shard_map/decode_backward/pallas_call | solution.py:1467
  482.8 6.2 all-to-all-done.6
  490.4 5.8 move.44
  502.3 10.1 %all-to-all-done.7 = f32[32,1,2560]{2,1,0:T(1,128)S(1)} async-done(((f32[32,1,2560]{2,1,0:T(1,128)}), f32[32,1,2560]{2,1,0:T(1,128)S(1)}, u32[]{:S(2)}, u32[]{:S(2)}) %all-to-all-start.7) | async-done | bytes 327712 | tf_op jit(solution)/shard_map/all_to_all | solution.py:94
  513.2 3.6 move.45
  520.3 14.4 %coarse_weight.3 = (bf16[2,2,4,12,128,128]{5,4,3,2,1,0:T(8,128)(2,1)}, bf16[2,2,4,12,128,128]{5,4,3,2,1,0:T(8,128)(2,1)}) custom-call(s32[4]{0:T(128)S(1)} %copy-done.96, bf16[480,2048]{1,0:T(8,128)(2,1)S(1)} %bitcast.245, bf16[480,2048]{1,0:T(8,128)(2,1)S(1)} %bitcast.266, bf16[480,2048]{1,0:T(8,128)(2,1)} %bitcast.297, bf16[480,2048]{1,0:T(8,128)(2,1)} %bitcast.270, ...), custom_call_target="tpu_custom_call" | custom-call | flops 1 | bytes 1 | tf_op jit(solution)/shard_map/coarse_weight/pallas_call | solution.py:789
  535.7 15.2 %coarse_weight.4 = (bf16[2,2,4,11,128,128]{5,4,3,2,1,0:T(8,128)(2,1)}, bf16[2,2,4,11,128,128]{5,4,3,2,1,0:T(8,128)(2,1)}) custom-call(s32[4]{0:T(128)S(1)} %copy-done.96, bf16[2,2,4,12,128,128]{5,4,3,2,1,0:T(8,128)(2,1)} %get-tuple-element.148.tie_ref.refs_1_, bf16[480,2048]{1,0:T(8,128)(2,1)S(1)} %bitcast.246, bf16[480,2048]{1,0:T(8,128)(2,1)S(1)} %bitcast.262, ...), custom_call_target="tpu_custom_call" | custom-call | flops 1 | bytes 1 | tf_op jit(solution)/shard_map/coarse_weight/pallas_call | solution.py:789
  553.6 3.9 move.46
  562.1 9.6 %low_backward.1 = (bf16[7680,256]{1,0:T(8,128)(2,1)}, f32[64,256]{1,0:T(8,128)S(1)}) custom-call(f32[8,256]{1,0:T(8,128)S(1)} %maximum_maximum_fusion.1.place_ref, bf16[2,4,6,128,128]{4,3,2,1,0:T(8,128)(2,1)} %get-tuple-element.155.tie_ref, f32[7680,64]{1,0:T(8,128)S(1)} %copy-done.42, bf16[7680,256]{1,0:T(8,128)(2,1)} %bitcast.250, ...), custom_call_target="tpu_custom_call" | custom-call | flops 1509949440 | bytes 9830400 | tf_op jit(solution)/shard_map/low_backward/pallas_call | solution.py:1618
  573.0 5.3 pack_gradients.1
  583.8 9.3 %coarse_weight.5 = (bf16[2,2,4,6,128,128]{5,4,3,2,1,0:T(8,128)(2,1)}, bf16[2,2,4,6,128,128]{5,4,3,2,1,0:T(8,128)(2,1)}) custom-call(s32[4]{0:T(128)S(1)} %copy-done.96, bf16[2,2,4,33,16,128]{5,4,3,2,1,0:T(8,128)(2,1)} %copy-done.14, bf16[480,2048]{1,0:T(8,128)(2,1)S(1)} %bitcast.247, bf16[480,2048]{1,0:T(8,128)(2,1)S(1)} %bitcast.263, ...), custom_call_target="tpu_custom_call" | custom-call | flops 1 | bytes 1 | tf_op jit(solution)/shard_map/coarse_weight/pallas_call | solution.py:789
  595.5 3.9 move.47
  611.3 8.1 %collective-permute-done.32.refs_2_ = bf16[4,6,128,128]{3,2,1,0:T(8,128)(2,1)S(1)} collective-permute-done((bf16[4,6,128,128]{3,2,1,0:T(8,128)(2,1)S(1)}, bf16[4,6,128,128]{3,2,1,0:T(8,128)(2,1)S(1)}, u32[]{:S(2)}, u32[]{:S(2)}) %collective-permute-start.32) | collective-permute-done | bytes 786464 | tf_op jit(solution)/shard_map/ppermute | solution.py:76
  627.5 25.3 %coarse_input.1.refs_0_ = bf16[480,2048]{1,0:T(8,128)(2,1)} custom-call(s32[4]{0:T(128)S(1)} %copy-done.96, bf16[2,4,33,16,128]{4,3,2,1,0:T(8,128)(2,1)S(1)} %move.50.tie_ref, bf16[480,256]{1,0:T(8,128)(2,1)S(1)} %copy-done.71, bf16[8,256]{1,0:T(8,128)(2,1)S(1)} %copy-done.101, f32[480,8]{1,0:T(8,128)S(1)} %copy-done.51, ...), custom_call_target="tpu_custom_call" | custom-call | flops 1 | bytes 1 | tf_op jit(solution)/shard_map/coarse_input/pallas_call | solution.py:867
  665.3 3.9 collective-permute-done.38.refs_3_
  678.6 7.4 collective-permute-done.41.refs_3_
  693.1 9.8 %collective-permute-done.42.refs_3_ = bf16[2,4,3,128,128]{4,3,2,1,0:T(8,128)(2,1)} collective-permute-done((bf16[2,4,3,128,128]{4,3,2,1,0:T(8,128)(2,1)}, bf16[2,4,3,128,128]{4,3,2,1,0:T(8,128)(2,1)}, u32[]{:S(2)}, u32[]{:S(2)}) %collective-permute-start.42) | collective-permute-done | bytes 786464 | tf_op jit(solution)/shard_map/ppermute | solution.py:76
  715.0 8.5 %collective-permute-start.56 = (bf16[12,128,64]{1,2,0:T(8,128)(2,1)}, bf16[12,128,64]{1,2,0:T(8,128)(2,1)}, u32[]{:S(2)}, u32[]{:S(2)}) collective-permute-start(bf16[12,128,64]{1,2,0:T(8,128)(2,1)} %fusion.25), channel_id=1, source_target_pairs={{0,1},{1,0},{2,3},{3,2},{4,5},{5,4},{6,7},{7,6},{8,9},{9,8},{10,11... | collective-permute-start | bytes 589832 | tf_op jit(solution)/shard_map/ppermute | solution.py:76
  735.2 6.2 collective-permute-start.53
  743.5 5.7 collective-permute-done.50.refs_2_
  750.8 4.9 collective-permute-done.53.refs_2_
  757.6 6.5 collective-permute-start.52
  (794 shorter events, 248.1 us)
Async XLA Ops:
  13.3 16.9 %collective-permute-start.6 = (bf16[11,128,128]{2,1,0:T(8,128)(2,1)S(1)}, bf16[11,128,128]{2,1,0:T(8,128)(2,1)S(1)}, u32[]{:S(2)}, u32[]{:S(2)}) collective-permute-start(bf16[11,128,128]{2,1,0:T(8,128)(2,1)S(1)} %pad_maximum_fusion.7.refs_1_), channel_id=1, source_target_pairs={{0,8},{4,12},{8,0},{12,4},{16,24},{20,28},{24,16},{28,20},{1,9},{5... | collective-permute-start | bytes 1081352 | tf_op jit(solution)/shard_map/ppermute | solution.py:76
  14.6 15.6 %collective-permute-start.7 = (bf16[11,128,128]{2,1,0:T(8,128)(2,1)S(1)}, bf16[11,128,128]{2,1,0:T(8,128)(2,1)S(1)}, u32[]{:S(2)}, u32[]{:S(2)}) collective-permute-start(bf16[11,128,128]{2,1,0:T(8,128)(2,1)S(1)} %pad_maximum_fusion.7.refs_1_), channel_id=1, source_target_pairs={{0,16},{4,20},{8,24},{12,28},{16,0},{20,4},{24,8},{28,12},{1,17},{... | collective-permute-start | bytes 1081352 | tf_op jit(solution)/shard_map/ppermute | solution.py:76
  17.0 23.6 %collective-permute-start.8 = (bf16[11,128,128]{2,1,0:T(8,128)(2,1)S(1)}, bf16[11,128,128]{2,1,0:T(8,128)(2,1)S(1)}, u32[]{:S(2)}, u32[]{:S(2)}) collective-permute-start(bf16[11,128,128]{2,1,0:T(8,128)(2,1)S(1)} %pad_maximum_fusion.7.refs_1_), channel_id=1, source_target_pairs={{0,24},{4,28},{8,16},{12,20},{16,8},{20,12},{24,0},{28,4},{1,25},{... | collective-permute-start | bytes 1081352 | tf_op jit(solution)/shard_map/ppermute | solution.py:76
  41.8 35.8 %collective-permute-start.10 = (bf16[4,6,128,128]{3,2,1,0:T(8,128)(2,1)}, bf16[4,6,128,128]{3,2,1,0:T(8,128)(2,1)}, u32[]{:S(2)}, u32[]{:S(2)}) collective-permute-start(bf16[4,6,128,128]{3,2,1,0:T(8,128)(2,1)} %get-tuple-element.110.refs_14_), channel_id=1, source_target_pairs={{0,2},{1,3},{2,0},{3,1},{4,6},{5,7},{6,4},{7,5},{8,10},{9,11},{10,... | collective-permute-start | bytes 2359304 | tf_op jit(solution)/shard_map/ppermute | solution.py:76
  43.0 34.5 %collective-permute-start.1 = (bf16[18,128,128]{2,1,0:T(8,128)(2,1)}, bf16[18,128,128]{2,1,0:T(8,128)(2,1)}, u32[]{:S(2)}, u32[]{:S(2)}) collective-permute-start(bf16[18,128,128]{2,1,0:T(8,128)(2,1)} %pad_maximum_fusion.6.refs_0_.refs_1_), channel_id=1, source_target_pairs={{0,16},{4,20},{8,24},{12,28},{16,0},{20,4},{24,8},{28,12},{1,17},{... | collective-permute-start | bytes 1769480 | tf_op jit(solution)/shard_map/ppermute | solution.py:76
  51.9 25.6 %collective-permute-start.9 = (bf16[4,5,128,128]{3,2,1,0:T(8,128)(2,1)}, bf16[4,5,128,128]{3,2,1,0:T(8,128)(2,1)}, u32[]{:S(2)}, u32[]{:S(2)}) collective-permute-start(bf16[4,5,128,128]{3,2,1,0:T(8,128)(2,1)} %get-tuple-element.109.refs_13_), channel_id=1, source_target_pairs={{0,4},{4,0},{8,12},{12,8},{16,20},{20,16},{24,28},{28,24},{1,5},{5... | collective-permute-start | bytes 1966088 | tf_op jit(solution)/shard_map/ppermute | solution.py:76
  79.6 34.3 %collective-permute-start.17 = (bf16[2,4,6,128,128]{4,3,2,1,0:T(8,128)(2,1)S(1)}, bf16[2,4,6,128,128]{4,3,2,1,0:T(8,128)(2,1)S(1)}, u32[]{:S(2)}, u32[]{:S(2)}) collective-permute-start(bf16[2,4,6,128,128]{4,3,2,1,0:T(8,128)(2,1)S(1)} %get-tuple-element.115.refs_2_), channel_id=1, source_target_pairs={{0,4},{4,0},{8,12},{12,8},{16,20},{20,16},{24,28},{28,24},{1,5},{5... | collective-permute-start | bytes 4718600 | tf_op jit(solution)/shard_map/ppermute | solution.py:76
  79.9 28.4 %collective-permute-start.16 = (bf16[2,4,5,128,128]{4,3,2,1,0:T(8,128)(2,1)S(1)}, bf16[2,4,5,128,128]{4,3,2,1,0:T(8,128)(2,1)S(1)}, u32[]{:S(2)}, u32[]{:S(2)}) collective-permute-start(bf16[2,4,5,128,128]{4,3,2,1,0:T(8,128)(2,1)S(1)} %get-tuple-element.111.refs_0_.refs_1_), channel_id=1, source_target_pairs={{0,2},{1,3},{2,0},{3,1},{4,6},{5,7},{6,4},{7,5},{8,10},{9,11},{10,... | collective-permute-start | bytes 3932168 | tf_op jit(solution)/shard_map/ppermute | solution.py:76
  80.1 24.1 %collective-permute-start.12 = (bf16[18,128,128]{2,1,0:T(8,128)(2,1)}, bf16[18,128,128]{2,1,0:T(8,128)(2,1)S(1)}, u32[]{:S(2)}, u32[]{:S(2)}) collective-permute-start(bf16[18,128,128]{2,1,0:T(8,128)(2,1)} %pad_maximum_fusion.6.refs_0_.refs_1_), channel_id=1, source_target_pairs={{0,24},{4,28},{8,16},{12,20},{16,8},{20,12},{24,0},{28,4},{1,25},{... | collective-permute-start | bytes 1769480 | tf_op jit(solution)/shard_map/ppermute | solution.py:76
  116.7 60.8 %collective-permute-start.18 = (bf16[2,2,4,11,128,128]{5,4,3,2,1,0:T(8,128)(2,1)}, bf16[2,2,4,11,128,128]{5,4,3,2,1,0:T(8,128)(2,1)}, u32[]{:S(2)}, u32[]{:S(2)}) collective-permute-start(bf16[2,2,4,11,128,128]{5,4,3,2,1,0:T(8,128)(2,1)} %move.40.refs_6_), channel_id=1, source_target_pairs={{0,1},{1,0},{2,3},{3,2},{4,5},{5,4},{6,7},{7,6},{8,9},{9,8},{10,11... | collective-permute-start | bytes 17301512 | tf_op jit(solution)/shard_map/ppermute | solution.py:76
  119.3 27.9 %collective-permute-start.14 = (bf16[4,9,128,128]{3,2,1,0:T(8,128)(2,1)}, bf16[4,9,128,128]{3,2,1,0:T(8,128)(2,1)}, u32[]{:S(2)}, u32[]{:S(2)}) collective-permute-start(bf16[4,9,128,128]{3,2,1,0:T(8,128)(2,1)} %get-tuple-element.112.refs_0_.refs_1_), channel_id=1, source_target_pairs={{0,4},{4,0},{8,12},{12,8},{16,20},{20,16},{24,28},{28,24},{1,5},{5... | collective-permute-start | bytes 3538952 | tf_op jit(solution)/shard_map/ppermute | solution.py:76
  119.5 27.7 %collective-permute-start.15 = (bf16[4,9,128,128]{3,2,1,0:T(8,128)(2,1)}, bf16[4,9,128,128]{3,2,1,0:T(8,128)(2,1)}, u32[]{:S(2)}, u32[]{:S(2)}) collective-permute-start(bf16[4,9,128,128]{3,2,1,0:T(8,128)(2,1)} %get-tuple-element.113.refs_2_), channel_id=1, source_target_pairs={{0,2},{1,3},{2,0},{3,1},{4,6},{5,7},{6,4},{7,5},{8,10},{9,11},{10,... | collective-permute-start | bytes 3538952 | tf_op jit(solution)/shard_map/ppermute | solution.py:76
  149.8 52.8 %collective-permute-start.21 = (bf16[2,4,6,128,128]{4,3,2,1,0:T(8,128)(2,1)S(1)}, bf16[2,4,6,128,128]{4,3,2,1,0:T(8,128)(2,1)S(1)}, u32[]{:S(2)}, u32[]{:S(2)}) collective-permute-start(bf16[2,4,6,128,128]{4,3,2,1,0:T(8,128)(2,1)S(1)} %get-tuple-element.114.tie_ref.refs_1_), channel_id=1, source_target_pairs={{0,2},{1,3},{2,0},{3,1},{4,6},{5,7},{6,4},{7,5},{8,10},{9,11},{10,... | collective-permute-start | bytes 4718600 | tf_op jit(solution)/shard_map/ppermute | solution.py:76
  150.1 57.0 %collective-permute-start.25 = (bf16[2,4,6,128,128]{4,3,2,1,0:T(8,128)(2,1)S(1)}, bf16[2,4,6,128,128]{4,3,2,1,0:T(8,128)(2,1)S(1)}, u32[]{:S(2)}, u32[]{:S(2)}) collective-permute-start(bf16[2,4,6,128,128]{4,3,2,1,0:T(8,128)(2,1)S(1)} %get-tuple-element.123.refs_2_), channel_id=1, source_target_pairs={{0,4},{4,0},{8,12},{12,8},{16,20},{20,16},{24,28},{28,24},{1,5},{5... | collective-permute-start | bytes 4718600 | tf_op jit(solution)/shard_map/ppermute | solution.py:76
  151.3 24.9 %collective-permute-start.19 = (bf16[2,2,33,16,128]{4,3,2,1,0:T(8,128)(2,1)}, bf16[2,2,33,16,128]{4,3,2,1,0:T(8,128)(2,1)S(1)}, u32[]{:S(2)}, u32[]{:S(2)}) collective-permute-start(bf16[2,2,33,16,128]{4,3,2,1,0:T(8,128)(2,1)} %move.38.refs_1_), channel_id=1, source_target_pairs={{0,16},{4,20},{8,24},{12,28},{16,0},{20,4},{24,8},{28,12},{1,17},{... | collective-permute-start | bytes 1622024 | tf_op jit(solution)/shard_map/ppermute | solution.py:76
  151.5 51.1 %collective-permute-start.22 = (bf16[2,4,3,128,128]{4,3,2,1,0:T(8,128)(2,1)S(1)}, bf16[2,4,3,128,128]{4,3,2,1,0:T(8,128)(2,1)S(1)}, u32[]{:S(2)}, u32[]{:S(2)}) collective-permute-start(bf16[2,4,3,128,128]{4,3,2,1,0:T(8,128)(2,1)S(1)} %get-tuple-element.120.refs_2_), channel_id=1, source_target_pairs={{0,4},{4,0},{8,12},{12,8},{16,20},{20,16},{24,28},{28,24},{1,5},{5... | collective-permute-start | bytes 2359304 | tf_op jit(solution)/shard_map/ppermute | solution.py:76
  176.2 31.0 %collective-permute-start.24 = (bf16[2,4,3,128,128]{4,3,2,1,0:T(8,128)(2,1)S(1)}, bf16[2,4,3,128,128]{4,3,2,1,0:T(8,128)(2,1)S(1)}, u32[]{:S(2)}, u32[]{:S(2)}) collective-permute-start(bf16[2,4,3,128,128]{4,3,2,1,0:T(8,128)(2,1)S(1)} %get-tuple-element.122.refs_1_), channel_id=1, source_target_pairs={{0,2},{1,3},{2,0},{3,1},{4,6},{5,7},{6,4},{7,5},{8,10},{9,11},{10,... | collective-permute-start | bytes 2359304 | tf_op jit(solution)/shard_map/ppermute | solution.py:76
  177.5 23.4 %collective-permute-start.20 = (bf16[2,2,33,16,128]{4,3,2,1,0:T(8,128)(2,1)}, bf16[2,2,33,16,128]{4,3,2,1,0:T(8,128)(2,1)S(1)}, u32[]{:S(2)}, u32[]{:S(2)}) collective-permute-start(bf16[2,2,33,16,128]{4,3,2,1,0:T(8,128)(2,1)} %move.38.refs_1_), channel_id=1, source_target_pairs={{0,24},{4,28},{8,16},{12,20},{16,8},{20,12},{24,0},{28,4},{1,25},{... | collective-permute-start | bytes 1622024 | tf_op jit(solution)/shard_map/ppermute | solution.py:76
  209.6 18.8 %collective-permute-start.26 = (bf16[2,2,4,9,128,128]{5,4,3,2,1,0:T(8,128)(2,1)}, bf16[2,2,4,9,128,128]{5,4,3,2,1,0:T(8,128)(2,1)}, u32[]{:S(2)}, u32[]{:S(2)}) collective-permute-start(bf16[2,2,4,9,128,128]{5,4,3,2,1,0:T(8,128)(2,1)} %move.43.refs_4_.refs_10_), channel_id=1, source_target_pairs={{0,1},{1,0},{2,3},{3,2},{4,5},{5,4},{6,7},{7,6},{8,9},{9,8},{10,11... | collective-permute-start | bytes 14155784 | tf_op jit(solution)/shard_map/ppermute | solution.py:76
  210.9 34.4 %collective-permute-start.27 = (bf16[4,2,2,33,16,128]{5,4,3,2,1,0:T(8,128)(2,1)}, bf16[4,2,2,33,16,128]{5,4,3,2,1,0:T(8,128)(2,1)}, u32[]{:S(2)}, u32[]{:S(2)}) collective-permute-start(bf16[4,2,2,33,16,128]{5,4,3,2,1,0:T(8,128)(2,1)} %copy-done.17), channel_id=1, source_target_pairs={{0,1},{1,0},{2,3},{3,2},{4,5},{5,4},{6,7},{7,6},{8,9},{9,8},{10,11... | collective-permute-start | bytes 6488072 | tf_op jit(solution)/shard_map/ppermute | solution.py:76
  241.3 15.1 %all-to-all-start = ((f32[32,1,2561]{2,1,0:T(1,128)}), f32[32,1,2561]{2,1,0:T(1,128)}, u32[]{:S(2)}, u32[]{:S(2)}) async-start(f32[32,1,2561]{2,1,0:T(1,128)} %broadcast_in_dim.38), calls=%async_computation | async-start | bytes 688128 | tf_op jit(solution)/shard_map/all_to_all | solution.py:94
  534.7 16.2 %collective-permute-start.28 = (bf16[2,2,4,12,128,128]{5,4,3,2,1,0:T(8,128)(2,1)}, bf16[2,2,4,12,128,128]{5,4,3,2,1,0:T(8,128)(2,1)}, u32[]{:S(2)}, u32[]{:S(2)}) collective-permute-start(bf16[2,2,4,12,128,128]{5,4,3,2,1,0:T(8,128)(2,1)} %get-tuple-element.154), channel_id=1, source_target_pairs={{0,1},{1,0},{2,3},{3,2},{4,5},{5,4},{6,7},{7,6},{8,9},{9,8},{10,11... | collective-permute-start | bytes 18874376 | tf_op jit(solution)/shard_map/ppermute | solution.py:76
  550.9 53.5 %collective-permute-start.31 = (bf16[2,2,4,11,128,128]{5,4,3,2,1,0:T(8,128)(2,1)}, bf16[2,2,4,11,128,128]{5,4,3,2,1,0:T(8,128)(2,1)}, u32[]{:S(2)}, u32[]{:S(2)}) collective-permute-start(bf16[2,2,4,11,128,128]{5,4,3,2,1,0:T(8,128)(2,1)} %get-tuple-element.166), channel_id=1, source_target_pairs={{0,1},{1,0},{2,3},{3,2},{4,5},{5,4},{6,7},{7,6},{8,9},{9,8},{10,11... | collective-permute-start | bytes 17301512 | tf_op jit(solution)/shard_map/ppermute | solution.py:76
  557.5 35.8 %collective-permute-start.29 = (bf16[2,4,6,128,128]{4,3,2,1,0:T(8,128)(2,1)}, bf16[2,4,6,128,128]{4,3,2,1,0:T(8,128)(2,1)}, u32[]{:S(2)}, u32[]{:S(2)}) collective-permute-start(bf16[2,4,6,128,128]{4,3,2,1,0:T(8,128)(2,1)} %get-tuple-element.155.tie_ref), channel_id=1, source_target_pairs={{0,4},{4,0},{8,12},{12,8},{16,20},{20,16},{24,28},{28,24},{1,5},{5... | collective-permute-start | bytes 4718600 | tf_op jit(solution)/shard_map/ppermute | solution.py:76
  558.1 35.5 %collective-permute-start.30 = (bf16[2,4,6,128,128]{4,3,2,1,0:T(8,128)(2,1)}, bf16[2,4,6,128,128]{4,3,2,1,0:T(8,128)(2,1)}, u32[]{:S(2)}, u32[]{:S(2)}) collective-permute-start(bf16[2,4,6,128,128]{4,3,2,1,0:T(8,128)(2,1)} %get-tuple-element.164), channel_id=1, source_target_pairs={{0,2},{1,3},{2,0},{3,1},{4,6},{5,7},{6,4},{7,5},{8,10},{9,11},{10,... | collective-permute-start | bytes 4718600 | tf_op jit(solution)/shard_map/ppermute | solution.py:76
  579.6 43.0 %collective-permute-start.34 = (bf16[2,2,4,33,16,128]{5,4,3,2,1,0:T(8,128)(2,1)}, bf16[2,2,4,33,16,128]{5,4,3,2,1,0:T(8,128)(2,1)}, u32[]{:S(2)}, u32[]{:S(2)}) collective-permute-start(bf16[2,2,4,33,16,128]{5,4,3,2,1,0:T(8,128)(2,1)} %get-tuple-element.171), channel_id=1, source_target_pairs={{0,1},{1,0},{2,3},{3,2},{4,5},{5,4},{6,7},{7,6},{8,9},{9,8},{10,11... | collective-permute-start | bytes 6488072 | tf_op jit(solution)/shard_map/ppermute | solution.py:76
  593.0 68.7 %collective-permute-start.37 = (bf16[2,2,4,6,128,128]{5,4,3,2,1,0:T(8,128)(2,1)}, bf16[2,2,4,6,128,128]{5,4,3,2,1,0:T(8,128)(2,1)}, u32[]{:S(2)}, u32[]{:S(2)}) collective-permute-start(bf16[2,2,4,6,128,128]{5,4,3,2,1,0:T(8,128)(2,1)} %get-tuple-element.175), channel_id=1, source_target_pairs={{0,1},{1,0},{2,3},{3,2},{4,5},{5,4},{6,7},{7,6},{8,9},{9,8},{10,11... | collective-permute-start | bytes 9437192 | tf_op jit(solution)/shard_map/ppermute | solution.py:76
  601.9 17.4 %collective-permute-start.32 = (bf16[4,6,128,128]{3,2,1,0:T(8,128)(2,1)S(1)}, bf16[4,6,128,128]{3,2,1,0:T(8,128)(2,1)S(1)}, u32[]{:S(2)}, u32[]{:S(2)}) collective-permute-start(bf16[4,6,128,128]{3,2,1,0:T(8,128)(2,1)S(1)} %get-tuple-element.165.refs_0_), channel_id=1, source_target_pairs={{0,2},{1,3},{2,0},{3,1},{4,6},{5,7},{6,4},{7,5},{8,10},{9,11},{10,... | collective-permute-start | bytes 2359304 | tf_op jit(solution)/shard_map/ppermute | solution.py:76
  603.1 18.3 %collective-permute-start.33 = (bf16[4,6,128,128]{3,2,1,0:T(8,128)(2,1)}, bf16[4,6,128,128]{3,2,1,0:T(8,128)(2,1)S(1)}, u32[]{:S(2)}, u32[]{:S(2)}) collective-permute-start(bf16[4,6,128,128]{3,2,1,0:T(8,128)(2,1)} %copy-done.103), channel_id=1, source_target_pairs={{0,4},{4,0},{8,12},{12,8},{16,20},{20,16},{24,28},{28,24},{1,5},{5... | collective-permute-start | bytes 2359304 | tf_op jit(solution)/shard_map/ppermute | solution.py:76
  610.6 43.3 %collective-permute-start.36 = (bf16[2,4,6,128,128]{4,3,2,1,0:T(8,128)(2,1)}, bf16[2,4,6,128,128]{4,3,2,1,0:T(8,128)(2,1)S(1)}, u32[]{:S(2)}, u32[]{:S(2)}) collective-permute-start(bf16[2,4,6,128,128]{4,3,2,1,0:T(8,128)(2,1)} %get-tuple-element.173), channel_id=1, source_target_pairs={{0,2},{1,3},{2,0},{3,1},{4,6},{5,7},{6,4},{7,5},{8,10},{9,11},{10,... | collective-permute-start | bytes 4718600 | tf_op jit(solution)/shard_map/ppermute | solution.py:76
  620.2 32.6 %collective-permute-start.35 = (bf16[2,4,5,128,128]{4,3,2,1,0:T(8,128)(2,1)S(1)}, bf16[2,4,5,128,128]{4,3,2,1,0:T(8,128)(2,1)S(1)}, u32[]{:S(2)}, u32[]{:S(2)}) collective-permute-start(bf16[2,4,5,128,128]{4,3,2,1,0:T(8,128)(2,1)S(1)} %get-tuple-element.167.refs_0_), channel_id=1, source_target_pairs={{0,4},{4,0},{8,12},{12,8},{16,20},{20,16},{24,28},{28,24},{1,5},{5... | collective-permute-start | bytes 3932168 | tf_op jit(solution)/shard_map/ppermute | solution.py:76
  624.9 44.3 %collective-permute-start.38 = (bf16[2,4,33,16,128]{4,3,2,1,0:T(8,128)(2,1)S(1)}, bf16[2,4,33,16,128]{4,3,2,1,0:T(8,128)(2,1)}, u32[]{:S(2)}, u32[]{:S(2)}) collective-permute-start(bf16[2,4,33,16,128]{4,3,2,1,0:T(8,128)(2,1)S(1)} %move.50.tie_ref), channel_id=1, source_target_pairs={{0,4},{4,0},{8,12},{12,8},{16,20},{20,16},{24,28},{28,24},{1,5},{5... | collective-permute-start | bytes 3244040 | tf_op jit(solution)/shard_map/ppermute | solution.py:76
  626.1 50.5 %collective-permute-start.39 = (bf16[2,12,128,128]{3,2,1,0:T(8,128)(2,1)}, bf16[2,12,128,128]{3,2,1,0:T(8,128)(2,1)}, u32[]{:S(2)}, u32[]{:S(2)}) collective-permute-start(bf16[2,12,128,128]{3,2,1,0:T(8,128)(2,1)} %get-tuple-element.170.refs_0_), channel_id=1, source_target_pairs={{0,16},{4,20},{8,24},{12,28},{16,0},{20,4},{24,8},{28,12},{1,17},{... | collective-permute-start | bytes 2359304 | tf_op jit(solution)/shard_map/ppermute | solution.py:76
  660.1 25.9 %collective-permute-start.41 = (bf16[4,6,128,128]{3,2,1,0:T(8,128)(2,1)}, bf16[4,6,128,128]{3,2,1,0:T(8,128)(2,1)}, u32[]{:S(2)}, u32[]{:S(2)}) collective-permute-start(bf16[4,6,128,128]{3,2,1,0:T(8,128)(2,1)} %get-tuple-element.181), channel_id=1, source_target_pairs={{0,4},{4,0},{8,12},{12,8},{16,20},{20,16},{24,28},{28,24},{1,5},{5... | collective-permute-start | bytes 2359304 | tf_op jit(solution)/shard_map/ppermute | solution.py:76
  660.8 17.8 %collective-permute-start.40 = (bf16[4,5,128,128]{3,2,1,0:T(8,128)(2,1)}, bf16[4,5,128,128]{3,2,1,0:T(8,128)(2,1)}, u32[]{:S(2)}, u32[]{:S(2)}) collective-permute-start(bf16[4,5,128,128]{3,2,1,0:T(8,128)(2,1)} %get-tuple-element.174.refs_0_), channel_id=1, source_target_pairs={{0,2},{1,3},{2,0},{3,1},{4,6},{5,7},{6,4},{7,5},{8,10},{9,11},{10,... | collective-permute-start | bytes 1966088 | tf_op jit(solution)/shard_map/ppermute | solution.py:76
  664.5 38.3 %collective-permute-start.42 = (bf16[2,4,3,128,128]{4,3,2,1,0:T(8,128)(2,1)}, bf16[2,4,3,128,128]{4,3,2,1,0:T(8,128)(2,1)}, u32[]{:S(2)}, u32[]{:S(2)}) collective-permute-start(bf16[2,4,3,128,128]{4,3,2,1,0:T(8,128)(2,1)} %get-tuple-element.176.refs_0_), channel_id=1, source_target_pairs={{0,4},{4,0},{8,12},{12,8},{16,20},{20,16},{24,28},{28,24},{1,5},{5... | collective-permute-start | bytes 2359304 | tf_op jit(solution)/shard_map/ppermute | solution.py:76
  669.2 33.7 %collective-permute-start.43 = (bf16[2,4,3,128,128]{4,3,2,1,0:T(8,128)(2,1)}, bf16[2,4,3,128,128]{4,3,2,1,0:T(8,128)(2,1)}, u32[]{:S(2)}, u32[]{:S(2)}) collective-permute-start(bf16[2,4,3,128,128]{4,3,2,1,0:T(8,128)(2,1)} %get-tuple-element.183), channel_id=1, source_target_pairs={{0,2},{1,3},{2,0},{3,1},{4,6},{5,7},{6,4},{7,5},{8,10},{9,11},{10,... | collective-permute-start | bytes 2359304 | tf_op jit(solution)/shard_map/ppermute | solution.py:76
  676.6 33.5 %collective-permute-start.44 = (bf16[4,33,16,128]{3,2,1,0:T(8,128)(2,1)S(1)}, bf16[4,33,16,128]{3,2,1,0:T(8,128)(2,1)S(1)}, u32[]{:S(2)}, u32[]{:S(2)}) collective-permute-start(bf16[4,33,16,128]{3,2,1,0:T(8,128)(2,1)S(1)} %get-tuple-element.177.refs_0_), channel_id=1, source_target_pairs={{0,2},{1,3},{2,0},{3,1},{4,6},{5,7},{6,4},{7,5},{8,10},{9,11},{10,... | collective-permute-start | bytes 1622024 | tf_op jit(solution)/shard_map/ppermute | solution.py:76
  689.5 37.7 %collective-permute-start.48 = (bf16[2,11,128,128]{3,2,1,0:T(8,128)(2,1)}, bf16[2,11,128,128]{3,2,1,0:T(8,128)(2,1)}, u32[]{:S(2)}, u32[]{:S(2)}) collective-permute-start(bf16[2,11,128,128]{3,2,1,0:T(8,128)(2,1)} %get-tuple-element.182.refs_0_), channel_id=1, source_target_pairs={{0,16},{4,20},{8,24},{12,28},{16,0},{20,4},{24,8},{28,12},{1,17},{... | collective-permute-start | bytes 2162696 | tf_op jit(solution)/shard_map/ppermute | solution.py:76
  693.1 18.9 %collective-permute-start.45 = (bf16[12,128,128]{2,1,0:T(8,128)(2,1)S(1)}, bf16[12,128,128]{2,1,0:T(8,128)(2,1)S(1)}, u32[]{:S(2)}, u32[]{:S(2)}) collective-permute-start(bf16[12,128,128]{2,1,0:T(8,128)(2,1)S(1)} %get-tuple-element.179.refs_0_), channel_id=1, source_target_pairs={{0,8},{4,12},{8,0},{12,4},{16,24},{20,28},{24,16},{28,20},{1,9},{5... | collective-permute-start | bytes 1179656 | tf_op jit(solution)/shard_map/ppermute | solution.py:76
  705.8 17.7 %collective-permute-start.46 = (bf16[4,3,128,128]{3,2,1,0:T(8,128)(2,1)}, bf16[4,3,128,128]{3,2,1,0:T(8,128)(2,1)S(1)}, u32[]{:S(2)}, u32[]{:S(2)}) collective-permute-start(bf16[4,3,128,128]{3,2,1,0:T(8,128)(2,1)} %get-tuple-element.184.refs_0_), channel_id=1, source_target_pairs={{0,2},{1,3},{2,0},{3,1},{4,6},{5,7},{6,4},{7,5},{8,10},{9,11},{10,... | collective-permute-start | bytes 1179656 | tf_op jit(solution)/shard_map/ppermute | solution.py:76
  706.8 17.4 %collective-permute-start.47 = (bf16[4,3,128,128]{3,2,1,0:T(8,128)(2,1)}, bf16[4,3,128,128]{3,2,1,0:T(8,128)(2,1)S(1)}, u32[]{:S(2)}, u32[]{:S(2)}) collective-permute-start(bf16[4,3,128,128]{3,2,1,0:T(8,128)(2,1)} %get-tuple-element.189), channel_id=1, source_target_pairs={{0,4},{4,0},{8,12},{12,8},{16,20},{20,16},{24,28},{28,24},{1,5},{5... | collective-permute-start | bytes 1179656 | tf_op jit(solution)/shard_map/ppermute | solution.py:76
  711.7 21.9 %collective-permute-start.49 = (bf16[2,33,16,128]{3,2,1,0:T(8,128)(2,1)}, bf16[2,33,16,128]{3,2,1,0:T(8,128)(2,1)}, u32[]{:S(2)}, u32[]{:S(2)}) collective-permute-start(bf16[2,33,16,128]{3,2,1,0:T(8,128)(2,1)} %get-tuple-element.186.refs_0_), channel_id=1, source_target_pairs={{0,16},{4,20},{8,24},{12,28},{16,0},{20,4},{24,8},{28,12},{1,17},{... | collective-permute-start | bytes 811016 | tf_op jit(solution)/shard_map/ppermute | solution.py:76
  715.0 26.4 %collective-permute-start.56 = (bf16[12,128,64]{1,2,0:T(8,128)(2,1)}, bf16[12,128,64]{1,2,0:T(8,128)(2,1)}, u32[]{:S(2)}, u32[]{:S(2)}) collective-permute-start(bf16[12,128,64]{1,2,0:T(8,128)(2,1)} %fusion.25), channel_id=1, source_target_pairs={{0,1},{1,0},{2,3},{3,2},{4,5},{5,4},{6,7},{7,6},{8,9},{9,8},{10,11... | collective-permute-start | bytes 589832 | tf_op jit(solution)/shard_map/ppermute | solution.py:76
  727.2 22.1 %collective-permute-start.50 = (bf16[2,6,128,128]{3,2,1,0:T(8,128)(2,1)S(1)}, bf16[2,6,128,128]{3,2,1,0:T(8,128)(2,1)S(1)}, u32[]{:S(2)}, u32[]{:S(2)}) collective-permute-start(bf16[2,6,128,128]{3,2,1,0:T(8,128)(2,1)S(1)} %get-tuple-element.190.refs_0_), channel_id=1, source_target_pairs={{0,16},{4,20},{8,24},{12,28},{16,0},{20,4},{24,8},{28,12},{1,17},{... | collective-permute-start | bytes 1179656 | tf_op jit(solution)/shard_map/ppermute | solution.py:76
  729.3 20.1 %collective-permute-start.51 = (bf16[11,128,128]{2,1,0:T(8,128)(2,1)}, bf16[11,128,128]{2,1,0:T(8,128)(2,1)}, u32[]{:S(2)}, u32[]{:S(2)}) collective-permute-start(bf16[11,128,128]{2,1,0:T(8,128)(2,1)} %get-tuple-element.192.refs_0_), channel_id=1, source_target_pairs={{0,8},{4,12},{8,0},{12,4},{16,24},{20,28},{24,16},{28,20},{1,9},{5... | collective-permute-start | bytes 1081352 | tf_op jit(solution)/shard_map/ppermute | solution.py:76
  735.2 20.4 %collective-permute-start.53 = (bf16[33,16,128]{2,1,0:T(8,128)(2,1)}, bf16[33,16,128]{2,1,0:T(8,128)(2,1)}, u32[]{:S(2)}, u32[]{:S(2)}) collective-permute-start(bf16[33,16,128]{2,1,0:T(8,128)(2,1)} %get-tuple-element.194.refs_0_), channel_id=1, source_target_pairs={{0,8},{4,12},{8,0},{12,4},{16,24},{20,28},{24,16},{28,20},{1,9},{5... | collective-permute-start | bytes 405512 | tf_op jit(solution)/shard_map/ppermute | solution.py:76
  749.3 14.8 %collective-permute-start.54 = (bf16[6,128,128]{2,1,0:T(8,128)(2,1)S(1)}, bf16[6,128,128]{2,1,0:T(8,128)(2,1)S(1)}, u32[]{:S(2)}, u32[]{:S(2)}) collective-permute-start(bf16[6,128,128]{2,1,0:T(8,128)(2,1)S(1)} %get-tuple-element.196.refs_0_), channel_id=1, source_target_pairs={{0,8},{4,12},{8,0},{12,4},{16,24},{20,28},{24,16},{28,20},{1,9},{5... | collective-permute-start | bytes 589832 | tf_op jit(solution)/shard_map/ppermute | solution.py:76
  (227 other events, 3059.9 us)

commit v6 on v5

--- a/solution.py
+++ b/solution.py
@@ -884,7 +884,7 @@
     )(kernel_place(), *args)
 
 
-STRIP = 8
+STRIP = 16
 
 
 def norm_vectors(mean, variance, gain, bias, *more):

time: 786 us -> 794 us (1.010)
  waiting for transfers between devices: 209 us -> 220 us
  starting transfers between devices: 100 us -> 90.3 us
    ppermute x58, starting transfers between devices: 73.3 us -> 63.7 us  [exchange(): lax.ppermute(values, axis, [(place, place ^ bit) for place in range(size)])]
    unnamed x445 -> x499, local copies, waits for them, and re-layouts: 69.3 us -> 70.1 us
  transfers between devices with their start and end apart: 66 -> 66, of which waited for: 27 -> 29; matrix products, arithmetic and copies ran while one was open for 7% -> 8% of each run, Pallas kernels for 20% -> 20%
where the time goes in v6:
time: 794 us; the launch traced here: 781 us
  Pallas kernels  317 us (40%)
  waiting for transfers between devices  220 us (28%)
  local copies, waits for them, and re-layouts  110 us (14%)
  starting transfers between devices  90.3 us (11%)
  other arithmetic  36.5 us (5%)
    ppermute x58, waiting for transfers between devices, exchange(): lax.ppermute(values, axis, [(place, place ^ bit) for place in range(size)])  174 us
    unnamed x499, local copies, waits for them, and re-layouts  70.1 us
    pallas_call x33, Pallas kernels, one_step(): pl.pallas_call(run, out_shape=outs, grid=(1,), in_specs=[spec or whole_sp...  63.9 us
    ppermute x58, starting transfers between devices, exchange(): lax.ppermute(values, axis, [(place, place ^ bit) for place in range(size)])  63.7 us
    pallas_call x1, Pallas kernels, decode_backward(): pl.pallas_call(functools.partial(decode_backward_kernel, steps, columns),...  46.4 us
    all_to_all x8, waiting for transfers between devices, hand_out(): return lax.all_to_all(rows, ('wide', 'narrow'), 0, 0, tiled=True)  45.6 us
    pallas_call x3, Pallas kernels, coarse_weight(): pl.pallas_call(kernel, out_shape=outs, grid_spec=pltpu.PrefetchScalarGrid...  38.7 us
    pallas_call x3, Pallas kernels, coarse_forward(): pl.pallas_call(kernel, out_shape=outs, grid_spec=pltpu.PrefetchScalarGrid...  37.5 us
  transfers between devices with their start and end apart: 66, of which 29 were waited for; matrix products, arithmetic and copies ran while one was open for 8% of the time, Pallas kernels for 20%

profile of v6, /device:TPU:1, one launch (start us, length us, event | category | flops | bytes accessed | tf_op | source)
XLA Modules:
  0.0 780.7 jit_solution(14693434979700530774)
XLA Ops:
  24.3 5.5 collective-permute-done.4.refs_1_
  31.8 10.4 %collective-permute-done.8.refs_4_ = bf16[11,128,128]{2,1,0:T(8,128)(2,1)S(1)} collective-permute-done((bf16[11,128,128]{2,1,0:T(8,128)(2,1)S(1)}, bf16[11,128,128]{2,1,0:T(8,128)(2,1)S(1)}, u32[]{:S(2)}, u32[]{:S(2)}) %collective-permute-start.8) | collective-permute-done | bytes 360480 | tf_op jit(solution)/shard_map/ppermute | solution.py:76
  44.6 8.9 %collective-permute-start.1 = (bf16[18,128,128]{2,1,0:T(8,128)(2,1)}, bf16[18,128,128]{2,1,0:T(8,128)(2,1)}, u32[]{:S(2)}, u32[]{:S(2)}) collective-permute-start(bf16[18,128,128]{2,1,0:T(8,128)(2,1)} %pad_maximum_fusion.6.refs_0_.refs_1_), channel_id=1, source_target_pairs={{0,16},{4,20},{8,24},{12,28},{16,0},{20,4},{24,8},{28,12},{1,17},{... | collective-permute-start | bytes 1769480 | tf_op jit(solution)/shard_map/ppermute | solution.py:76
  57.6 21.5 %collective-permute-done.1.refs_0_.refs_3_ = bf16[18,128,128]{2,1,0:T(8,128)(2,1)} collective-permute-done((bf16[18,128,128]{2,1,0:T(8,128)(2,1)}, bf16[18,128,128]{2,1,0:T(8,128)(2,1)}, u32[]{:S(2)}, u32[]{:S(2)}) %collective-permute-start.1) | collective-permute-done | bytes 589856 | tf_op jit(solution)/shard_map/ppermute | solution.py:76
  82.1 13.8 %collective-permute-done.11.refs_2_ = bf16[18,128,128]{2,1,0:T(8,128)(2,1)S(1)} collective-permute-done((bf16[18,128,128]{2,1,0:T(8,128)(2,1)}, bf16[18,128,128]{2,1,0:T(8,128)(2,1)S(1)}, u32[]{:S(2)}, u32[]{:S(2)}) %collective-permute-start.11) | collective-permute-done | bytes 589856 | tf_op jit(solution)/shard_map/ppermute | solution.py:76
  95.9 9.9 %collective-permute-done.12.refs_4_ = bf16[18,128,128]{2,1,0:T(8,128)(2,1)S(1)} collective-permute-done((bf16[18,128,128]{2,1,0:T(8,128)(2,1)}, bf16[18,128,128]{2,1,0:T(8,128)(2,1)S(1)}, u32[]{:S(2)}, u32[]{:S(2)}) %collective-permute-start.12) | collective-permute-done | bytes 589856 | tf_op jit(solution)/shard_map/ppermute | solution.py:76
  109.8 5.6 collective-permute-done.17.refs_4_
  122.2 13.6 %collective-permute-done.13.refs_0_.refs_2_ = bf16[2,2,33,16,128]{4,3,2,1,0:T(8,128)(2,1)} collective-permute-done((bf16[2,2,33,16,128]{4,3,2,1,0:T(8,128)(2,1)}, bf16[2,2,33,16,128]{4,3,2,1,0:T(8,128)(2,1)}, u32[]{:S(2)}, u32[]{:S(2)}) %collective-permute-start.13) | collective-permute-done | bytes 540704 | tf_op jit(solution)/shard_map/ppermute | solution.py:76
  135.7 13.0 %collective-permute-done.14.refs_3_ = bf16[4,9,128,128]{3,2,1,0:T(8,128)(2,1)} collective-permute-done((bf16[4,9,128,128]{3,2,1,0:T(8,128)(2,1)}, bf16[4,9,128,128]{3,2,1,0:T(8,128)(2,1)}, u32[]{:S(2)}, u32[]{:S(2)}) %collective-permute-start.14) | collective-permute-done | bytes 1179680 | tf_op jit(solution)/shard_map/ppermute | solution.py:76
  153.5 24.3 %collective-permute-done.19.refs_3_ = bf16[2,2,33,16,128]{4,3,2,1,0:T(8,128)(2,1)S(1)} collective-permute-done((bf16[2,2,33,16,128]{4,3,2,1,0:T(8,128)(2,1)}, bf16[2,2,33,16,128]{4,3,2,1,0:T(8,128)(2,1)S(1)}, u32[]{:S(2)}, u32[]{:S(2)}) %collective-permute-start.19) | collective-permute-done | bytes 540704 | tf_op jit(solution)/shard_map/ppermute | solution.py:76
  180.9 6.1 fusion.5
  187.0 15.4 %coarse_forward.3 = (f32[480,256]{1,0:T(8,128)S(1)}, f32[8,256]{1,0:T(8,128)S(1)}, f32[480,256]{1,0:T(8,128)S(1)}, f32[8,256]{1,0:T(8,128)S(1)}, f32[8,256]{1,0:T(8,128)S(1)}, /*index=5*/bf16[8,2048]{1,0:T(8,128)(2,1)S(1)}) custom-call(s32[4]{0:T(128)S(1)} %pad_add_fusion.place_ref, bf16[2,4,6,128,128]{4,3,2,1,0:T(8,128)(2,1)S(1)} %get-tuple-element.114.tie_ref.refs_1_, ...), custom_call_target="tpu_custom_call" | custom-call | flops 1 | bytes 1 | tf_op jit(solution)/shard_map/coarse_forward/pallas_call | solution.py:685
  220.8 11.1 %coarse_forward.4 = (f32[480,256]{1,0:T(8,128)S(1)}, f32[8,256]{1,0:T(8,128)S(1)}) custom-call(s32[4]{0:T(128)S(1)} %copy-done.91, f32[480,1]{1,0:T(8,128)S(1)} %broadcast_in_dim.46.refs_2_.refs_0_.refs_7_.refs_6_, bf16[480,2048]{1,0:T(8,128)(2,1)S(1)} %bitcast.243, bf16[480,2048]{1,0:T(8,128)(2,1)S(1)} %bitcast.265, bf16[480,2048]{1,0:T(8,128)(2,1)} %bitcast.296, ...), custom_call_target="tpu_custom_call" | custom-call | flops 1 | bytes 1 | tf_op jit(solution)/shard_map/coarse_forward/pallas_call | solution.py:685
  232.7 11.1 %coarse_forward.5 = (f32[480,256]{1,0:T(8,128)S(1)}, f32[8,256]{1,0:T(8,128)S(1)}) custom-call(s32[4]{0:T(128)S(1)} %copy-done.92, f32[480,1]{1,0:T(8,128)S(1)} %broadcast_in_dim.46.refs_2_.refs_0_.refs_7_.refs_6_, bf16[480,2048]{1,0:T(8,128)(2,1)S(1)} %bitcast.244, bf16[480,2048]{1,0:T(8,128)(2,1)S(1)} %bitcast.271, bf16[480,2048]{1,0:T(8,128)(2,1)} %bitcast.299, ...), custom_call_target="tpu_custom_call" | custom-call | flops 1 | bytes 1 | tf_op jit(solution)/shard_map/coarse_forward/pallas_call | solution.py:685
  256.7 3.7 low_moments.1
  267.2 5.8 all-to-all-start.1
  276.6 4.0 all-to-all-done.1
  287.9 23.2 %decode_forward.1 = (f32[7680,256]{1,0:T(8,128)}, f32[32,640]{1,0:T(8,128)S(1)}, bf16[7680,256]{1,0:T(8,128)(2,1)}) custom-call(f32[20,24,256]{2,1,0:T(8,128)S(1)} %fusion.24.act_ref, bf16[96,48]{1,0:T(8,128)(2,1)S(1)} %copy-done.79, bf16[7680,256]{1,0:T(8,128)(2,1)} %bitcast.248, bf16[256,256]{1,0:T(8,128)(2,1)S(1)} %get-tuple-element.129.wide_ref.refs_2_, ...), custom_call_target="tpu_custom_call" | custom-call | flops 1 | bytes 1 | tf_op jit(solution)/shard_map/decode_forward/pallas_call | solution.py:1072
  314.9 7.3 all-to-all-done.2
  323.6 18.3 %refine_forward.1 = (f32[7680,256]{1,0:T(8,128)}, f32[32,640]{1,0:T(8,128)S(1)}) custom-call(f32[7680,256]{1,0:T(8,128)} %get-tuple-element.131.z_in_ref.z_ref, f32[32,640]{1,0:T(8,128)S(1)} %bitcast.282, f32[2,256]{1,0:T(2,128)S(1)} %copy-done.96, f32[1536,3]{1,0:T(8,128)S(1)} %copy.326.refs_1_.masks_ref.refs_3_, bf16[9,256,256]{2,1,0:T(8,128)(2,1)S(1)} %copy-done.37), custom_call_target="tpu_custom_call" | custom-call | flops 1 | bytes 1 | tf_op jit(solution)/shard_map/refine_forward/pallas_call | solution.py:1143
  345.9 6.9 all-to-all-done.3
  354.4 8.5 %classify.1 = (bf16[7680,21]{1,0:T(8,128)(2,1)S(1)}, f32[32,768]{1,0:T(8,128)S(1)}) custom-call(f32[7680,256]{1,0:T(8,128)} %get-tuple-element.134.z_ref, bf16[7680,21]{1,0:T(8,128)(2,1)S(1)} %bitcast.268, f32[32,640]{1,0:T(8,128)S(1)} %bitcast.285, f32[2,256]{1,0:T(2,128)S(1)} %copy-done.104, f32[1536,3]{1,0:T(8,128)S(1)} %copy.326.refs_1_.masks_ref.refs_3_, ...), custom_call_target="tpu_custom_call" | custom-call | flops 1 | bytes 1 | tf_op jit(solution)/shard_map/classify/pallas_call | solution.py:1228
  369.9 6.2 all-to-all-done.4
  380.7 35.7 %refine_backward.1 = (f32[7680,256]{1,0:T(8,128)}, f32[32,768]{1,0:T(8,128)S(1)}, f32[8,256]{1,0:T(8,128)S(1)}, f32[3,256,768]{2,1,0:T(8,128)}) custom-call(f32[7680,256]{1,0:T(8,128)} %get-tuple-element.134.z_ref, bf16[7680,21]{1,0:T(8,128)(2,1)S(1)} %bitcast.269, f32[32,640]{1,0:T(8,128)S(1)} %bitcast.286, f32[32,768]{1,0:T(8,128)S(1)} %bitcast.290, ...), custom_call_target="tpu_custom_call" | custom-call | flops 1 | bytes 1 | tf_op jit(solution)/shard_map/refine_backward/pallas_call | solution.py:1338
  422.1 6.3 all-to-all-done.5
  432.8 46.4 %decode_backward.1 = (f32[20,24,256]{2,1,0:T(8,128)S(1)}, f32[7680,64]{1,0:T(8,128)}, f32[8,256]{1,0:T(8,128)S(1)}, f32[8,256]{1,0:T(8,128)S(1)}, f32[3,256,768]{2,1,0:T(8,128)S(1)}, /*index=5*/f32[3,64,768]{2,1,0:T(8,128)S(1)}) custom-call(f32[7680,256]{1,0:T(8,128)} %get-tuple-element.138.local_ref, f32[7680,256]{1,0:T(8,128)} %get-tuple-element.131.z_in_ref.z_ref, ...), custom_call_target="tpu_custom_call" | custom-call | flops 1 | bytes 1 | tf_op jit(solution)/shard_map/decode_backward/pallas_call | solution.py:1467
  488.6 4.8 all-to-all-done.6
  497.4 5.8 move.44
  509.7 10.0 %all-to-all-done.7 = f32[32,1,2560]{2,1,0:T(1,128)S(1)} async-done(((f32[32,1,2560]{2,1,0:T(1,128)}), f32[32,1,2560]{2,1,0:T(1,128)S(1)}, u32[]{:S(2)}, u32[]{:S(2)}) %all-to-all-start.7) | async-done | bytes 327712 | tf_op jit(solution)/shard_map/all_to_all | solution.py:94
  520.4 3.6 move.45
  527.5 14.3 %coarse_weight.3 = (bf16[2,2,4,12,128,128]{5,4,3,2,1,0:T(8,128)(2,1)}, bf16[2,2,4,12,128,128]{5,4,3,2,1,0:T(8,128)(2,1)}) custom-call(s32[4]{0:T(128)S(1)} %copy-done.94, bf16[480,2048]{1,0:T(8,128)(2,1)S(1)} %bitcast.245, bf16[480,2048]{1,0:T(8,128)(2,1)S(1)} %bitcast.266, bf16[480,2048]{1,0:T(8,128)(2,1)} %bitcast.297, bf16[480,2048]{1,0:T(8,128)(2,1)} %bitcast.270, ...), custom_call_target="tpu_custom_call" | custom-call | flops 1 | bytes 1 | tf_op jit(solution)/shard_map/coarse_weight/pallas_call | solution.py:789
  542.8 15.2 %coarse_weight.4 = (bf16[2,2,4,11,128,128]{5,4,3,2,1,0:T(8,128)(2,1)}, bf16[2,2,4,11,128,128]{5,4,3,2,1,0:T(8,128)(2,1)}) custom-call(s32[4]{0:T(128)S(1)} %copy-done.94, bf16[2,2,4,12,128,128]{5,4,3,2,1,0:T(8,128)(2,1)} %get-tuple-element.148.tie_ref.refs_1_, bf16[480,2048]{1,0:T(8,128)(2,1)S(1)} %bitcast.246, bf16[480,2048]{1,0:T(8,128)(2,1)S(1)} %bitcast.262, ...), custom_call_target="tpu_custom_call" | custom-call | flops 1 | bytes 1 | tf_op jit(solution)/shard_map/coarse_weight/pallas_call | solution.py:789
  560.7 3.9 move.46
  568.0 8.0 %low_backward.1 = (bf16[7680,256]{1,0:T(8,128)(2,1)}, f32[64,256]{1,0:T(8,128)S(1)}) custom-call(f32[8,256]{1,0:T(8,128)S(1)} %maximum_maximum_fusion.1.place_ref, bf16[2,4,6,128,128]{4,3,2,1,0:T(8,128)(2,1)} %get-tuple-element.155.tie_ref, f32[7680,64]{1,0:T(8,128)} %get-tuple-element.156.refs_0_, bf16[7680,256]{1,0:T(8,128)(2,1)} %bitcast.250, ...), custom_call_target="tpu_custom_call" | custom-call | flops 1509949440 | bytes 9830400 | tf_op jit(solution)/shard_map/low_backward/pallas_call | solution.py:1618
  575.9 5.2 pack_gradients.1
  586.6 9.2 %coarse_weight.5 = (bf16[2,2,4,6,128,128]{5,4,3,2,1,0:T(8,128)(2,1)}, bf16[2,2,4,6,128,128]{5,4,3,2,1,0:T(8,128)(2,1)}) custom-call(s32[4]{0:T(128)S(1)} %copy-done.94, bf16[2,2,4,33,16,128]{5,4,3,2,1,0:T(8,128)(2,1)} %copy-done.14, bf16[480,2048]{1,0:T(8,128)(2,1)S(1)} %bitcast.247, bf16[480,2048]{1,0:T(8,128)(2,1)S(1)} %bitcast.263, ...), custom_call_target="tpu_custom_call" | custom-call | flops 1 | bytes 1 | tf_op jit(solution)/shard_map/coarse_weight/pallas_call | solution.py:789
  595.9 4.5 collective-permute-done.29.refs_3_
  602.6 3.9 move.47
  614.2 3.5 move.48
  618.4 8.1 %collective-permute-done.32.refs_2_ = bf16[4,6,128,128]{3,2,1,0:T(8,128)(2,1)S(1)} collective-permute-done((bf16[4,6,128,128]{3,2,1,0:T(8,128)(2,1)S(1)}, bf16[4,6,128,128]{3,2,1,0:T(8,128)(2,1)S(1)}, u32[]{:S(2)}, u32[]{:S(2)}) %collective-permute-start.32) | collective-permute-done | bytes 786464 | tf_op jit(solution)/shard_map/ppermute | solution.py:76
  634.1 25.4 %coarse_input.1.refs_0_ = bf16[480,2048]{1,0:T(8,128)(2,1)} custom-call(s32[4]{0:T(128)S(1)} %copy-done.94, bf16[2,4,33,16,128]{4,3,2,1,0:T(8,128)(2,1)S(1)} %move.50.tie_ref, bf16[480,256]{1,0:T(8,128)(2,1)S(1)} %copy-done.63, bf16[8,256]{1,0:T(8,128)(2,1)S(1)} %copy-done.105, f32[480,8]{1,0:T(8,128)S(1)} %copy-done.50, ...), custom_call_target="tpu_custom_call" | custom-call | flops 1 | bytes 1 | tf_op jit(solution)/shard_map/coarse_input/pallas_call | solution.py:867
  671.7 5.5 collective-permute-done.38.refs_3_
  687.9 6.1 collective-permute-done.41.refs_3_
  700.5 10.3 %collective-permute-done.42.refs_3_ = bf16[2,4,3,128,128]{4,3,2,1,0:T(8,128)(2,1)} collective-permute-done((bf16[2,4,3,128,128]{4,3,2,1,0:T(8,128)(2,1)}, bf16[2,4,3,128,128]{4,3,2,1,0:T(8,128)(2,1)}, u32[]{:S(2)}, u32[]{:S(2)}) %collective-permute-start.42) | collective-permute-done | bytes 786464 | tf_op jit(solution)/shard_map/ppermute | solution.py:76
  723.3 6.7 collective-permute-start.56
  740.5 10.1 %collective-permute-done.49.refs_2_ = bf16[2,33,16,128]{3,2,1,0:T(8,128)(2,1)} collective-permute-done((bf16[2,33,16,128]{3,2,1,0:T(8,128)(2,1)}, bf16[2,33,16,128]{3,2,1,0:T(8,128)(2,1)}, u32[]{:S(2)}, u32[]{:S(2)}) %collective-permute-start.49) | collective-permute-done | bytes 270368 | tf_op jit(solution)/shard_map/ppermute | solution.py:76
  754.4 4.5 collective-permute-done.50.refs_2_
  765.8 6.3 collective-permute-start.52
  (848 shorter events, 257.7 us)
Async XLA Ops:
  14.9 16.9 %collective-permute-start.6 = (bf16[11,128,128]{2,1,0:T(8,128)(2,1)S(1)}, bf16[11,128,128]{2,1,0:T(8,128)(2,1)S(1)}, u32[]{:S(2)}, u32[]{:S(2)}) collective-permute-start(bf16[11,128,128]{2,1,0:T(8,128)(2,1)S(1)} %pad_maximum_fusion.7.refs_1_), channel_id=1, source_target_pairs={{0,8},{4,12},{8,0},{12,4},{16,24},{20,28},{24,16},{28,20},{1,9},{5... | collective-permute-start | bytes 1081352 | tf_op jit(solution)/shard_map/ppermute | solution.py:76
  16.2 15.6 %collective-permute-start.7 = (bf16[11,128,128]{2,1,0:T(8,128)(2,1)S(1)}, bf16[11,128,128]{2,1,0:T(8,128)(2,1)S(1)}, u32[]{:S(2)}, u32[]{:S(2)}) collective-permute-start(bf16[11,128,128]{2,1,0:T(8,128)(2,1)S(1)} %pad_maximum_fusion.7.refs_1_), channel_id=1, source_target_pairs={{0,16},{4,20},{8,24},{12,28},{16,0},{20,4},{24,8},{28,12},{1,17},{... | collective-permute-start | bytes 1081352 | tf_op jit(solution)/shard_map/ppermute | solution.py:76
  18.5 23.6 %collective-permute-start.8 = (bf16[11,128,128]{2,1,0:T(8,128)(2,1)S(1)}, bf16[11,128,128]{2,1,0:T(8,128)(2,1)S(1)}, u32[]{:S(2)}, u32[]{:S(2)}) collective-permute-start(bf16[11,128,128]{2,1,0:T(8,128)(2,1)S(1)} %pad_maximum_fusion.7.refs_1_), channel_id=1, source_target_pairs={{0,24},{4,28},{8,16},{12,20},{16,8},{20,12},{24,0},{28,4},{1,25},{... | collective-permute-start | bytes 1081352 | tf_op jit(solution)/shard_map/ppermute | solution.py:76
  43.3 35.8 %collective-permute-start.10 = (bf16[4,6,128,128]{3,2,1,0:T(8,128)(2,1)}, bf16[4,6,128,128]{3,2,1,0:T(8,128)(2,1)}, u32[]{:S(2)}, u32[]{:S(2)}) collective-permute-start(bf16[4,6,128,128]{3,2,1,0:T(8,128)(2,1)} %get-tuple-element.110.refs_14_), channel_id=1, source_target_pairs={{0,2},{1,3},{2,0},{3,1},{4,6},{5,7},{6,4},{7,5},{8,10},{9,11},{10,... | collective-permute-start | bytes 2359304 | tf_op jit(solution)/shard_map/ppermute | solution.py:76
  44.6 34.5 %collective-permute-start.1 = (bf16[18,128,128]{2,1,0:T(8,128)(2,1)}, bf16[18,128,128]{2,1,0:T(8,128)(2,1)}, u32[]{:S(2)}, u32[]{:S(2)}) collective-permute-start(bf16[18,128,128]{2,1,0:T(8,128)(2,1)} %pad_maximum_fusion.6.refs_0_.refs_1_), channel_id=1, source_target_pairs={{0,16},{4,20},{8,24},{12,28},{16,0},{20,4},{24,8},{28,12},{1,17},{... | collective-permute-start | bytes 1769480 | tf_op jit(solution)/shard_map/ppermute | solution.py:76
  53.5 25.6 %collective-permute-start.9 = (bf16[4,5,128,128]{3,2,1,0:T(8,128)(2,1)}, bf16[4,5,128,128]{3,2,1,0:T(8,128)(2,1)}, u32[]{:S(2)}, u32[]{:S(2)}) collective-permute-start(bf16[4,5,128,128]{3,2,1,0:T(8,128)(2,1)} %get-tuple-element.109.refs_13_), channel_id=1, source_target_pairs={{0,4},{4,0},{8,12},{12,8},{16,20},{20,16},{24,28},{28,24},{1,5},{5... | collective-permute-start | bytes 1966088 | tf_op jit(solution)/shard_map/ppermute | solution.py:76
  81.1 34.3 %collective-permute-start.17 = (bf16[2,4,6,128,128]{4,3,2,1,0:T(8,128)(2,1)S(1)}, bf16[2,4,6,128,128]{4,3,2,1,0:T(8,128)(2,1)S(1)}, u32[]{:S(2)}, u32[]{:S(2)}) collective-permute-start(bf16[2,4,6,128,128]{4,3,2,1,0:T(8,128)(2,1)S(1)} %get-tuple-element.115.refs_2_), channel_id=1, source_target_pairs={{0,4},{4,0},{8,12},{12,8},{16,20},{20,16},{24,28},{28,24},{1,5},{5... | collective-permute-start | bytes 4718600 | tf_op jit(solution)/shard_map/ppermute | solution.py:76
  81.5 28.4 %collective-permute-start.16 = (bf16[2,4,5,128,128]{4,3,2,1,0:T(8,128)(2,1)S(1)}, bf16[2,4,5,128,128]{4,3,2,1,0:T(8,128)(2,1)S(1)}, u32[]{:S(2)}, u32[]{:S(2)}) collective-permute-start(bf16[2,4,5,128,128]{4,3,2,1,0:T(8,128)(2,1)S(1)} %get-tuple-element.111.refs_0_.refs_1_), channel_id=1, source_target_pairs={{0,2},{1,3},{2,0},{3,1},{4,6},{5,7},{6,4},{7,5},{8,10},{9,11},{10,... | collective-permute-start | bytes 3932168 | tf_op jit(solution)/shard_map/ppermute | solution.py:76
  81.7 14.2 %collective-permute-start.11 = (bf16[18,128,128]{2,1,0:T(8,128)(2,1)}, bf16[18,128,128]{2,1,0:T(8,128)(2,1)S(1)}, u32[]{:S(2)}, u32[]{:S(2)}) collective-permute-start(bf16[18,128,128]{2,1,0:T(8,128)(2,1)} %pad_maximum_fusion.6.refs_0_.refs_1_), channel_id=1, source_target_pairs={{0,8},{4,12},{8,0},{12,4},{16,24},{20,28},{24,16},{28,20},{1,9},{5... | collective-permute-start | bytes 1769480 | tf_op jit(solution)/shard_map/ppermute | solution.py:76
  81.7 24.1 %collective-permute-start.12 = (bf16[18,128,128]{2,1,0:T(8,128)(2,1)}, bf16[18,128,128]{2,1,0:T(8,128)(2,1)S(1)}, u32[]{:S(2)}, u32[]{:S(2)}) collective-permute-start(bf16[18,128,128]{2,1,0:T(8,128)(2,1)} %pad_maximum_fusion.6.refs_0_.refs_1_), channel_id=1, source_target_pairs={{0,24},{4,28},{8,16},{12,20},{16,8},{20,12},{24,0},{28,4},{1,25},{... | collective-permute-start | bytes 1769480 | tf_op jit(solution)/shard_map/ppermute | solution.py:76
  118.3 60.8 %collective-permute-start.18 = (bf16[2,2,4,11,128,128]{5,4,3,2,1,0:T(8,128)(2,1)}, bf16[2,2,4,11,128,128]{5,4,3,2,1,0:T(8,128)(2,1)}, u32[]{:S(2)}, u32[]{:S(2)}) collective-permute-start(bf16[2,2,4,11,128,128]{5,4,3,2,1,0:T(8,128)(2,1)} %move.40.refs_6_), channel_id=1, source_target_pairs={{0,1},{1,0},{2,3},{3,2},{4,5},{5,4},{6,7},{7,6},{8,9},{9,8},{10,11... | collective-permute-start | bytes 17301512 | tf_op jit(solution)/shard_map/ppermute | solution.py:76
  120.8 27.9 %collective-permute-start.14 = (bf16[4,9,128,128]{3,2,1,0:T(8,128)(2,1)}, bf16[4,9,128,128]{3,2,1,0:T(8,128)(2,1)}, u32[]{:S(2)}, u32[]{:S(2)}) collective-permute-start(bf16[4,9,128,128]{3,2,1,0:T(8,128)(2,1)} %get-tuple-element.112.refs_0_.refs_1_), channel_id=1, source_target_pairs={{0,4},{4,0},{8,12},{12,8},{16,20},{20,16},{24,28},{28,24},{1,5},{5... | collective-permute-start | bytes 3538952 | tf_op jit(solution)/shard_map/ppermute | solution.py:76
  121.1 27.7 %collective-permute-start.15 = (bf16[4,9,128,128]{3,2,1,0:T(8,128)(2,1)}, bf16[4,9,128,128]{3,2,1,0:T(8,128)(2,1)}, u32[]{:S(2)}, u32[]{:S(2)}) collective-permute-start(bf16[4,9,128,128]{3,2,1,0:T(8,128)(2,1)} %get-tuple-element.113.refs_2_), channel_id=1, source_target_pairs={{0,2},{1,3},{2,0},{3,1},{4,6},{5,7},{6,4},{7,5},{8,10},{9,11},{10,... | collective-permute-start | bytes 3538952 | tf_op jit(solution)/shard_map/ppermute | solution.py:76
  151.4 52.8 %collective-permute-start.21 = (bf16[2,4,6,128,128]{4,3,2,1,0:T(8,128)(2,1)S(1)}, bf16[2,4,6,128,128]{4,3,2,1,0:T(8,128)(2,1)S(1)}, u32[]{:S(2)}, u32[]{:S(2)}) collective-permute-start(bf16[2,4,6,128,128]{4,3,2,1,0:T(8,128)(2,1)S(1)} %get-tuple-element.114.tie_ref.refs_1_), channel_id=1, source_target_pairs={{0,2},{1,3},{2,0},{3,1},{4,6},{5,7},{6,4},{7,5},{8,10},{9,11},{10,... | collective-permute-start | bytes 4718600 | tf_op jit(solution)/shard_map/ppermute | solution.py:76
  151.7 57.1 %collective-permute-start.25 = (bf16[2,4,6,128,128]{4,3,2,1,0:T(8,128)(2,1)S(1)}, bf16[2,4,6,128,128]{4,3,2,1,0:T(8,128)(2,1)S(1)}, u32[]{:S(2)}, u32[]{:S(2)}) collective-permute-start(bf16[2,4,6,128,128]{4,3,2,1,0:T(8,128)(2,1)S(1)} %get-tuple-element.123.refs_2_), channel_id=1, source_target_pairs={{0,4},{4,0},{8,12},{12,8},{16,20},{20,16},{24,28},{28,24},{1,5},{5... | collective-permute-start | bytes 4718600 | tf_op jit(solution)/shard_map/ppermute | solution.py:76
  152.8 24.9 %collective-permute-start.19 = (bf16[2,2,33,16,128]{4,3,2,1,0:T(8,128)(2,1)}, bf16[2,2,33,16,128]{4,3,2,1,0:T(8,128)(2,1)S(1)}, u32[]{:S(2)}, u32[]{:S(2)}) collective-permute-start(bf16[2,2,33,16,128]{4,3,2,1,0:T(8,128)(2,1)} %move.38.refs_1_), channel_id=1, source_target_pairs={{0,16},{4,20},{8,24},{12,28},{16,0},{20,4},{24,8},{28,12},{1,17},{... | collective-permute-start | bytes 1622024 | tf_op jit(solution)/shard_map/ppermute | solution.py:76
  153.1 51.2 %collective-permute-start.22 = (bf16[2,4,3,128,128]{4,3,2,1,0:T(8,128)(2,1)S(1)}, bf16[2,4,3,128,128]{4,3,2,1,0:T(8,128)(2,1)S(1)}, u32[]{:S(2)}, u32[]{:S(2)}) collective-permute-start(bf16[2,4,3,128,128]{4,3,2,1,0:T(8,128)(2,1)S(1)} %get-tuple-element.120.refs_2_), channel_id=1, source_target_pairs={{0,4},{4,0},{8,12},{12,8},{16,20},{20,16},{24,28},{28,24},{1,5},{5... | collective-permute-start | bytes 2359304 | tf_op jit(solution)/shard_map/ppermute | solution.py:76
  177.8 31.0 %collective-permute-start.24 = (bf16[2,4,3,128,128]{4,3,2,1,0:T(8,128)(2,1)S(1)}, bf16[2,4,3,128,128]{4,3,2,1,0:T(8,128)(2,1)S(1)}, u32[]{:S(2)}, u32[]{:S(2)}) collective-permute-start(bf16[2,4,3,128,128]{4,3,2,1,0:T(8,128)(2,1)S(1)} %get-tuple-element.122.refs_1_), channel_id=1, source_target_pairs={{0,2},{1,3},{2,0},{3,1},{4,6},{5,7},{6,4},{7,5},{8,10},{9,11},{10,... | collective-permute-start | bytes 2359304 | tf_op jit(solution)/shard_map/ppermute | solution.py:76
  179.1 23.4 %collective-permute-start.20 = (bf16[2,2,33,16,128]{4,3,2,1,0:T(8,128)(2,1)}, bf16[2,2,33,16,128]{4,3,2,1,0:T(8,128)(2,1)S(1)}, u32[]{:S(2)}, u32[]{:S(2)}) collective-permute-start(bf16[2,2,33,16,128]{4,3,2,1,0:T(8,128)(2,1)} %move.38.refs_1_), channel_id=1, source_target_pairs={{0,24},{4,28},{8,16},{12,20},{16,8},{20,12},{24,0},{28,4},{1,25},{... | collective-permute-start | bytes 1622024 | tf_op jit(solution)/shard_map/ppermute | solution.py:76
  211.2 21.4 %collective-permute-start.26 = (bf16[2,2,4,9,128,128]{5,4,3,2,1,0:T(8,128)(2,1)}, bf16[2,2,4,9,128,128]{5,4,3,2,1,0:T(8,128)(2,1)}, u32[]{:S(2)}, u32[]{:S(2)}) collective-permute-start(bf16[2,2,4,9,128,128]{5,4,3,2,1,0:T(8,128)(2,1)} %move.43.refs_4_.refs_10_), channel_id=1, source_target_pairs={{0,1},{1,0},{2,3},{3,2},{4,5},{5,4},{6,7},{7,6},{8,9},{9,8},{10,11... | collective-permute-start | bytes 14155784 | tf_op jit(solution)/shard_map/ppermute | solution.py:76
  213.1 37.1 %collective-permute-start.27 = (bf16[4,2,2,33,16,128]{5,4,3,2,1,0:T(8,128)(2,1)}, bf16[4,2,2,33,16,128]{5,4,3,2,1,0:T(8,128)(2,1)}, u32[]{:S(2)}, u32[]{:S(2)}) collective-permute-start(bf16[4,2,2,33,16,128]{5,4,3,2,1,0:T(8,128)(2,1)} %copy-done.17), channel_id=1, source_target_pairs={{0,1},{1,0},{2,3},{3,2},{4,5},{5,4},{6,7},{7,6},{8,9},{9,8},{10,11... | collective-permute-start | bytes 6488072 | tf_op jit(solution)/shard_map/ppermute | solution.py:76
  245.7 15.3 %all-to-all-start = ((f32[32,1,2561]{2,1,0:T(1,128)}), f32[32,1,2561]{2,1,0:T(1,128)}, u32[]{:S(2)}, u32[]{:S(2)}) async-start(f32[32,1,2561]{2,1,0:T(1,128)} %broadcast_in_dim.38), calls=%async_computation | async-start | bytes 688128 | tf_op jit(solution)/shard_map/all_to_all | solution.py:94
  505.3 14.4 %all-to-all-start.7 = ((f32[32,1,2560]{2,1,0:T(1,128)}), f32[32,1,2560]{2,1,0:T(1,128)S(1)}, u32[]{:S(2)}, u32[]{:S(2)}) async-start(f32[32,1,2560]{2,1,0:T(1,128)} %copy.351), calls=%async_computation.7 | async-start | bytes 655360 | tf_op jit(solution)/shard_map/all_to_all | solution.py:94
  541.8 16.2 %collective-permute-start.28 = (bf16[2,2,4,12,128,128]{5,4,3,2,1,0:T(8,128)(2,1)}, bf16[2,2,4,12,128,128]{5,4,3,2,1,0:T(8,128)(2,1)}, u32[]{:S(2)}, u32[]{:S(2)}) collective-permute-start(bf16[2,2,4,12,128,128]{5,4,3,2,1,0:T(8,128)(2,1)} %get-tuple-element.154), channel_id=1, source_target_pairs={{0,1},{1,0},{2,3},{3,2},{4,5},{5,4},{6,7},{7,6},{8,9},{9,8},{10,11... | collective-permute-start | bytes 18874376 | tf_op jit(solution)/shard_map/ppermute | solution.py:76
  558.0 53.6 %collective-permute-start.31 = (bf16[2,2,4,11,128,128]{5,4,3,2,1,0:T(8,128)(2,1)}, bf16[2,2,4,11,128,128]{5,4,3,2,1,0:T(8,128)(2,1)}, u32[]{:S(2)}, u32[]{:S(2)}) collective-permute-start(bf16[2,2,4,11,128,128]{5,4,3,2,1,0:T(8,128)(2,1)} %get-tuple-element.166), channel_id=1, source_target_pairs={{0,1},{1,0},{2,3},{3,2},{4,5},{5,4},{6,7},{7,6},{8,9},{9,8},{10,11... | collective-permute-start | bytes 17301512 | tf_op jit(solution)/shard_map/ppermute | solution.py:76
  564.6 35.8 %collective-permute-start.29 = (bf16[2,4,6,128,128]{4,3,2,1,0:T(8,128)(2,1)}, bf16[2,4,6,128,128]{4,3,2,1,0:T(8,128)(2,1)}, u32[]{:S(2)}, u32[]{:S(2)}) collective-permute-start(bf16[2,4,6,128,128]{4,3,2,1,0:T(8,128)(2,1)} %get-tuple-element.155.tie_ref), channel_id=1, source_target_pairs={{0,4},{4,0},{8,12},{12,8},{16,20},{20,16},{24,28},{28,24},{1,5},{5... | collective-permute-start | bytes 4718600 | tf_op jit(solution)/shard_map/ppermute | solution.py:76
  565.2 35.5 %collective-permute-start.30 = (bf16[2,4,6,128,128]{4,3,2,1,0:T(8,128)(2,1)}, bf16[2,4,6,128,128]{4,3,2,1,0:T(8,128)(2,1)}, u32[]{:S(2)}, u32[]{:S(2)}) collective-permute-start(bf16[2,4,6,128,128]{4,3,2,1,0:T(8,128)(2,1)} %get-tuple-element.164), channel_id=1, source_target_pairs={{0,2},{1,3},{2,0},{3,1},{4,6},{5,7},{6,4},{7,5},{8,10},{9,11},{10,... | collective-permute-start | bytes 4718600 | tf_op jit(solution)/shard_map/ppermute | solution.py:76
  582.5 46.4 %collective-permute-start.34 = (bf16[2,2,4,33,16,128]{5,4,3,2,1,0:T(8,128)(2,1)}, bf16[2,2,4,33,16,128]{5,4,3,2,1,0:T(8,128)(2,1)}, u32[]{:S(2)}, u32[]{:S(2)}) collective-permute-start(bf16[2,2,4,33,16,128]{5,4,3,2,1,0:T(8,128)(2,1)} %get-tuple-element.171), channel_id=1, source_target_pairs={{0,1},{1,0},{2,3},{3,2},{4,5},{5,4},{6,7},{7,6},{8,9},{9,8},{10,11... | collective-permute-start | bytes 6488072 | tf_op jit(solution)/shard_map/ppermute | solution.py:76
  595.9 73.0 %collective-permute-start.37 = (bf16[2,2,4,6,128,128]{5,4,3,2,1,0:T(8,128)(2,1)}, bf16[2,2,4,6,128,128]{5,4,3,2,1,0:T(8,128)(2,1)}, u32[]{:S(2)}, u32[]{:S(2)}) collective-permute-start(bf16[2,2,4,6,128,128]{5,4,3,2,1,0:T(8,128)(2,1)} %get-tuple-element.175), channel_id=1, source_target_pairs={{0,1},{1,0},{2,3},{3,2},{4,5},{5,4},{6,7},{7,6},{8,9},{9,8},{10,11... | collective-permute-start | bytes 9437192 | tf_op jit(solution)/shard_map/ppermute | solution.py:76
  609.0 17.4 %collective-permute-start.32 = (bf16[4,6,128,128]{3,2,1,0:T(8,128)(2,1)S(1)}, bf16[4,6,128,128]{3,2,1,0:T(8,128)(2,1)S(1)}, u32[]{:S(2)}, u32[]{:S(2)}) collective-permute-start(bf16[4,6,128,128]{3,2,1,0:T(8,128)(2,1)S(1)} %get-tuple-element.165.refs_0_), channel_id=1, source_target_pairs={{0,2},{1,3},{2,0},{3,1},{4,6},{5,7},{6,4},{7,5},{8,10},{9,11},{10,... | collective-permute-start | bytes 2359304 | tf_op jit(solution)/shard_map/ppermute | solution.py:76
  610.2 17.5 %collective-permute-start.33 = (bf16[4,6,128,128]{3,2,1,0:T(8,128)(2,1)}, bf16[4,6,128,128]{3,2,1,0:T(8,128)(2,1)S(1)}, u32[]{:S(2)}, u32[]{:S(2)}) collective-permute-start(bf16[4,6,128,128]{3,2,1,0:T(8,128)(2,1)} %copy-done.111), channel_id=1, source_target_pairs={{0,4},{4,0},{8,12},{12,8},{16,20},{20,16},{24,28},{28,24},{1,5},{5... | collective-permute-start | bytes 2359304 | tf_op jit(solution)/shard_map/ppermute | solution.py:76
  617.7 42.9 %collective-permute-start.36 = (bf16[2,4,6,128,128]{4,3,2,1,0:T(8,128)(2,1)}, bf16[2,4,6,128,128]{4,3,2,1,0:T(8,128)(2,1)S(1)}, u32[]{:S(2)}, u32[]{:S(2)}) collective-permute-start(bf16[2,4,6,128,128]{4,3,2,1,0:T(8,128)(2,1)} %get-tuple-element.173), channel_id=1, source_target_pairs={{0,2},{1,3},{2,0},{3,1},{4,6},{5,7},{6,4},{7,5},{8,10},{9,11},{10,... | collective-permute-start | bytes 4718600 | tf_op jit(solution)/shard_map/ppermute | solution.py:76
  626.4 33.0 %collective-permute-start.35 = (bf16[2,4,5,128,128]{4,3,2,1,0:T(8,128)(2,1)S(1)}, bf16[2,4,5,128,128]{4,3,2,1,0:T(8,128)(2,1)S(1)}, u32[]{:S(2)}, u32[]{:S(2)}) collective-permute-start(bf16[2,4,5,128,128]{4,3,2,1,0:T(8,128)(2,1)S(1)} %get-tuple-element.167.refs_0_), channel_id=1, source_target_pairs={{0,4},{4,0},{8,12},{12,8},{16,20},{20,16},{24,28},{28,24},{1,5},{5... | collective-permute-start | bytes 3932168 | tf_op jit(solution)/shard_map/ppermute | solution.py:76
  631.1 46.0 %collective-permute-start.38 = (bf16[2,4,33,16,128]{4,3,2,1,0:T(8,128)(2,1)S(1)}, bf16[2,4,33,16,128]{4,3,2,1,0:T(8,128)(2,1)}, u32[]{:S(2)}, u32[]{:S(2)}) collective-permute-start(bf16[2,4,33,16,128]{4,3,2,1,0:T(8,128)(2,1)S(1)} %move.50.tie_ref), channel_id=1, source_target_pairs={{0,4},{4,0},{8,12},{12,8},{16,20},{20,16},{24,28},{28,24},{1,5},{5... | collective-permute-start | bytes 3244040 | tf_op jit(solution)/shard_map/ppermute | solution.py:76
  633.2 52.6 %collective-permute-start.39 = (bf16[2,12,128,128]{3,2,1,0:T(8,128)(2,1)}, bf16[2,12,128,128]{3,2,1,0:T(8,128)(2,1)}, u32[]{:S(2)}, u32[]{:S(2)}) collective-permute-start(bf16[2,12,128,128]{3,2,1,0:T(8,128)(2,1)} %get-tuple-element.170.refs_0_), channel_id=1, source_target_pairs={{0,16},{4,20},{8,24},{12,28},{16,0},{20,4},{24,8},{28,12},{1,17},{... | collective-permute-start | bytes 2359304 | tf_op jit(solution)/shard_map/ppermute | solution.py:76
  666.8 27.2 %collective-permute-start.41 = (bf16[4,6,128,128]{3,2,1,0:T(8,128)(2,1)}, bf16[4,6,128,128]{3,2,1,0:T(8,128)(2,1)}, u32[]{:S(2)}, u32[]{:S(2)}) collective-permute-start(bf16[4,6,128,128]{3,2,1,0:T(8,128)(2,1)} %get-tuple-element.181), channel_id=1, source_target_pairs={{0,4},{4,0},{8,12},{12,8},{16,20},{20,16},{24,28},{28,24},{1,5},{5... | collective-permute-start | bytes 2359304 | tf_op jit(solution)/shard_map/ppermute | solution.py:76
  667.4 20.5 %collective-permute-start.40 = (bf16[4,5,128,128]{3,2,1,0:T(8,128)(2,1)}, bf16[4,5,128,128]{3,2,1,0:T(8,128)(2,1)}, u32[]{:S(2)}, u32[]{:S(2)}) collective-permute-start(bf16[4,5,128,128]{3,2,1,0:T(8,128)(2,1)} %get-tuple-element.174.refs_0_), channel_id=1, source_target_pairs={{0,2},{1,3},{2,0},{3,1},{4,6},{5,7},{6,4},{7,5},{8,10},{9,11},{10,... | collective-permute-start | bytes 1966088 | tf_op jit(solution)/shard_map/ppermute | solution.py:76
  671.6 39.3 %collective-permute-start.42 = (bf16[2,4,3,128,128]{4,3,2,1,0:T(8,128)(2,1)}, bf16[2,4,3,128,128]{4,3,2,1,0:T(8,128)(2,1)}, u32[]{:S(2)}, u32[]{:S(2)}) collective-permute-start(bf16[2,4,3,128,128]{4,3,2,1,0:T(8,128)(2,1)} %get-tuple-element.176.refs_0_), channel_id=1, source_target_pairs={{0,4},{4,0},{8,12},{12,8},{16,20},{20,16},{24,28},{28,24},{1,5},{5... | collective-permute-start | bytes 2359304 | tf_op jit(solution)/shard_map/ppermute | solution.py:76
  677.1 33.7 %collective-permute-start.43 = (bf16[2,4,3,128,128]{4,3,2,1,0:T(8,128)(2,1)}, bf16[2,4,3,128,128]{4,3,2,1,0:T(8,128)(2,1)}, u32[]{:S(2)}, u32[]{:S(2)}) collective-permute-start(bf16[2,4,3,128,128]{4,3,2,1,0:T(8,128)(2,1)} %get-tuple-element.183), channel_id=1, source_target_pairs={{0,2},{1,3},{2,0},{3,1},{4,6},{5,7},{6,4},{7,5},{8,10},{9,11},{10,... | collective-permute-start | bytes 2359304 | tf_op jit(solution)/shard_map/ppermute | solution.py:76
  685.7 31.0 %collective-permute-start.44 = (bf16[4,33,16,128]{3,2,1,0:T(8,128)(2,1)S(1)}, bf16[4,33,16,128]{3,2,1,0:T(8,128)(2,1)S(1)}, u32[]{:S(2)}, u32[]{:S(2)}) collective-permute-start(bf16[4,33,16,128]{3,2,1,0:T(8,128)(2,1)S(1)} %get-tuple-element.177.refs_0_), channel_id=1, source_target_pairs={{0,2},{1,3},{2,0},{3,1},{4,6},{5,7},{6,4},{7,5},{8,10},{9,11},{10,... | collective-permute-start | bytes 1622024 | tf_op jit(solution)/shard_map/ppermute | solution.py:76
  697.6 38.8 %collective-permute-start.48 = (bf16[2,11,128,128]{3,2,1,0:T(8,128)(2,1)}, bf16[2,11,128,128]{3,2,1,0:T(8,128)(2,1)}, u32[]{:S(2)}, u32[]{:S(2)}) collective-permute-start(bf16[2,11,128,128]{3,2,1,0:T(8,128)(2,1)} %get-tuple-element.182.refs_0_), channel_id=1, source_target_pairs={{0,16},{4,20},{8,24},{12,28},{16,0},{20,4},{24,8},{28,12},{1,17},{... | collective-permute-start | bytes 2162696 | tf_op jit(solution)/shard_map/ppermute | solution.py:76
  700.5 19.8 %collective-permute-start.45 = (bf16[12,128,128]{2,1,0:T(8,128)(2,1)S(1)}, bf16[12,128,128]{2,1,0:T(8,128)(2,1)S(1)}, u32[]{:S(2)}, u32[]{:S(2)}) collective-permute-start(bf16[12,128,128]{2,1,0:T(8,128)(2,1)S(1)} %get-tuple-element.179.refs_0_), channel_id=1, source_target_pairs={{0,8},{4,12},{8,0},{12,4},{16,24},{20,28},{24,16},{28,20},{1,9},{5... | collective-permute-start | bytes 1179656 | tf_op jit(solution)/shard_map/ppermute | solution.py:76
  713.7 16.3 %collective-permute-start.46 = (bf16[4,3,128,128]{3,2,1,0:T(8,128)(2,1)}, bf16[4,3,128,128]{3,2,1,0:T(8,128)(2,1)S(1)}, u32[]{:S(2)}, u32[]{:S(2)}) collective-permute-start(bf16[4,3,128,128]{3,2,1,0:T(8,128)(2,1)} %get-tuple-element.184.refs_0_), channel_id=1, source_target_pairs={{0,2},{1,3},{2,0},{3,1},{4,6},{5,7},{6,4},{7,5},{8,10},{9,11},{10,... | collective-permute-start | bytes 1179656 | tf_op jit(solution)/shard_map/ppermute | solution.py:76
  714.6 16.2 %collective-permute-start.47 = (bf16[4,3,128,128]{3,2,1,0:T(8,128)(2,1)}, bf16[4,3,128,128]{3,2,1,0:T(8,128)(2,1)S(1)}, u32[]{:S(2)}, u32[]{:S(2)}) collective-permute-start(bf16[4,3,128,128]{3,2,1,0:T(8,128)(2,1)} %get-tuple-element.189), channel_id=1, source_target_pairs={{0,4},{4,0},{8,12},{12,8},{16,20},{20,16},{24,28},{28,24},{1,5},{5... | collective-permute-start | bytes 1179656 | tf_op jit(solution)/shard_map/ppermute | solution.py:76
  718.3 32.3 %collective-permute-start.49 = (bf16[2,33,16,128]{3,2,1,0:T(8,128)(2,1)}, bf16[2,33,16,128]{3,2,1,0:T(8,128)(2,1)}, u32[]{:S(2)}, u32[]{:S(2)}) collective-permute-start(bf16[2,33,16,128]{3,2,1,0:T(8,128)(2,1)} %get-tuple-element.186.refs_0_), channel_id=1, source_target_pairs={{0,16},{4,20},{8,24},{12,28},{16,0},{20,4},{24,8},{28,12},{1,17},{... | collective-permute-start | bytes 811016 | tf_op jit(solution)/shard_map/ppermute | solution.py:76
  723.3 28.9 %collective-permute-start.56 = (bf16[12,128,64]{1,2,0:T(8,128)(2,1)}, bf16[12,128,64]{1,2,0:T(8,128)(2,1)}, u32[]{:S(2)}, u32[]{:S(2)}) collective-permute-start(bf16[12,128,64]{1,2,0:T(8,128)(2,1)} %fusion.25), channel_id=1, source_target_pairs={{0,1},{1,0},{2,3},{3,2},{4,5},{5,4},{6,7},{7,6},{8,9},{9,8},{10,11... | collective-permute-start | bytes 589832 | tf_op jit(solution)/shard_map/ppermute | solution.py:76
  733.8 25.2 %collective-permute-start.50 = (bf16[2,6,128,128]{3,2,1,0:T(8,128)(2,1)S(1)}, bf16[2,6,128,128]{3,2,1,0:T(8,128)(2,1)S(1)}, u32[]{:S(2)}, u32[]{:S(2)}) collective-permute-start(bf16[2,6,128,128]{3,2,1,0:T(8,128)(2,1)S(1)} %get-tuple-element.190.refs_0_), channel_id=1, source_target_pairs={{0,16},{4,20},{8,24},{12,28},{16,0},{20,4},{24,8},{28,12},{1,17},{... | collective-permute-start | bytes 1179656 | tf_op jit(solution)/shard_map/ppermute | solution.py:76
  738.3 20.8 %collective-permute-start.51 = (bf16[11,128,128]{2,1,0:T(8,128)(2,1)}, bf16[11,128,128]{2,1,0:T(8,128)(2,1)}, u32[]{:S(2)}, u32[]{:S(2)}) collective-permute-start(bf16[11,128,128]{2,1,0:T(8,128)(2,1)} %get-tuple-element.192.refs_0_), channel_id=1, source_target_pairs={{0,8},{4,12},{8,0},{12,4},{16,24},{20,28},{24,16},{28,20},{1,9},{5... | collective-permute-start | bytes 1081352 | tf_op jit(solution)/shard_map/ppermute | solution.py:76
  (254 other events, 2975.2 us)

commit v7 on v5

--- a/solution.py
+++ b/solution.py
@@ -2154,8 +2154,10 @@
     pool_mask = (jnp.arange(8) < images).astype(jnp.float32).reshape(8, 1)
     grad_flat = logit_grad.reshape(-1, logit_grad.shape[-1])
     spread_rows = member_rows * sizes_inverse.reshape(1, 8)
+    tall_masks = jnp.concatenate([masks, masks])
     prepared = [
         masks,
+        tall_masks,
         mask_column,
         sizes_inverse,
         pool_inputs[0],
@@ -2180,7 +2182,7 @@
         return (sides, grad_flat)
 
     def low_part(proj, wide, decode, refine):
-        return low_moments(low_flat, wide, masks)
+        return low_moments(low_flat, wide, tall_masks)
 
     def forward(part, ready, pair, before, tie=None):
         sums, stats, pooling = ({}, {}, ()) if before is None else before
@@ -2299,7 +2301,7 @@
     refine_z, rows = refine_forward(decode_z, decode_rows, decode_params, masks, refine_full)
     refine_rows = hand_out(rows)
     logits, rows = classify(
-        refine_z, grad_flat, refine_rows, refine_params, masks, w_cls, b_cls.reshape(1, -1)
+        refine_z, grad_flat, refine_rows, refine_params, tall_masks, w_cls, b_cls.reshape(1, -1)
     )
     logits = logits.reshape(logit_grad.shape)
     refine_sums = hand_out(rows)
@@ -2421,7 +2423,7 @@
     )
 
     def low_late(tie):
-        return low_backward(reduce_local, low_flat, low_wide, low_vectors, masks, tie)
+        return low_backward(reduce_local, low_flat, low_wide, low_vectors, tall_masks, tie)
 
     def input_late(tie):
         side_dz = [

time: 786 us -> 786 us (level)
  waiting for transfers between devices: 209 us -> 223 us
  starting transfers between devices: 100 us -> 89 us
    ppermute x58, starting transfers between devices: 73.3 us -> 63.3 us  [exchange(): lax.ppermute(values, axis, [(place, place ^ bit) for place in range(size)])]
    ppermute x58, waiting for transfers between devices: 167 us -> 175 us  [exchange(): lax.ppermute(values, axis, [(place, place ^ bit) for place in range(size)])]
    unnamed x445 -> x435, local copies, waits for them, and re-layouts: 69.3 us -> 71.9 us
  transfers between devices with their start and end apart: 66 -> 66, of which waited for: 27 -> 31; matrix products, arithmetic and copies ran while one was open for 7% -> 7% of each run, Pallas kernels for 20% -> 20%
where the time goes in v7:
time: 786 us; the launch traced here: 773 us
  Pallas kernels  318 us (40%)
  waiting for transfers between devices  223 us (28%)
  local copies, waits for them, and re-layouts  104 us (13%)
  starting transfers between devices  89 us (11%)
  other arithmetic  32.3 us (4%)
    ppermute x58, waiting for transfers between devices, exchange(): lax.ppermute(values, axis, [(place, place ^ bit) for place in range(size)])  175 us
    unnamed x435, local copies, waits for them, and re-layouts  71.9 us
    pallas_call x33, Pallas kernels, one_step(): pl.pallas_call(run, out_shape=outs, grid=(1,), in_specs=[spec or whole_sp...  64.8 us
    ppermute x58, starting transfers between devices, exchange(): lax.ppermute(values, axis, [(place, place ^ bit) for place in range(size)])  63.3 us
    all_to_all x8, waiting for transfers between devices, hand_out(): return lax.all_to_all(rows, ('wide', 'narrow'), 0, 0, tiled=True)  47.9 us
    pallas_call x1, Pallas kernels, decode_backward(): pl.pallas_call(functools.partial(decode_backward_kernel, steps, columns),...  46 us
    pallas_call x3, Pallas kernels, coarse_weight(): pl.pallas_call(kernel, out_shape=outs, grid_spec=pltpu.PrefetchScalarGrid...  38.8 us
    pallas_call x3, Pallas kernels, coarse_forward(): pl.pallas_call(kernel, out_shape=outs, grid_spec=pltpu.PrefetchScalarGrid...  37.4 us
  transfers between devices with their start and end apart: 66, of which 31 were waited for; matrix products, arithmetic and copies ran while one was open for 7% of the time, Pallas kernels for 20%

profile of v7, /device:TPU:1, one launch (start us, length us, event | category | flops | bytes accessed | tf_op | source)
XLA Modules:
  0.0 773.2 jit_solution(541176942126345645)
XLA Ops:
  21.1 5.6 collective-permute-done.4.refs_1_
  26.8 3.7 collective-permute-done.6.refs_2_
  30.5 10.4 %collective-permute-done.8.refs_4_ = bf16[11,128,128]{2,1,0:T(8,128)(2,1)S(1)} collective-permute-done((bf16[11,128,128]{2,1,0:T(8,128)(2,1)S(1)}, bf16[11,128,128]{2,1,0:T(8,128)(2,1)S(1)}, u32[]{:S(2)}, u32[]{:S(2)}) %collective-permute-start.8) | collective-permute-done | bytes 360480 | tf_op jit(solution)/shard_map/ppermute | solution.py:76
  43.3 8.9 %collective-permute-start.1 = (bf16[18,128,128]{2,1,0:T(8,128)(2,1)}, bf16[18,128,128]{2,1,0:T(8,128)(2,1)}, u32[]{:S(2)}, u32[]{:S(2)}) collective-permute-start(bf16[18,128,128]{2,1,0:T(8,128)(2,1)} %pad_maximum_fusion.6.refs_0_.refs_1_), channel_id=1, source_target_pairs={{0,16},{4,20},{8,24},{12,28},{16,0},{20,4},{24,8},{28,12},{1,17},{... | collective-permute-start | bytes 1769480 | tf_op jit(solution)/shard_map/ppermute | solution.py:76
  58.2 19.6 %collective-permute-done.1.refs_0_.refs_3_ = bf16[18,128,128]{2,1,0:T(8,128)(2,1)} collective-permute-done((bf16[18,128,128]{2,1,0:T(8,128)(2,1)}, bf16[18,128,128]{2,1,0:T(8,128)(2,1)}, u32[]{:S(2)}, u32[]{:S(2)}) %collective-permute-start.1) | collective-permute-done | bytes 589856 | tf_op jit(solution)/shard_map/ppermute | solution.py:76
  80.8 13.8 %collective-permute-done.11.refs_2_ = bf16[18,128,128]{2,1,0:T(8,128)(2,1)S(1)} collective-permute-done((bf16[18,128,128]{2,1,0:T(8,128)(2,1)}, bf16[18,128,128]{2,1,0:T(8,128)(2,1)S(1)}, u32[]{:S(2)}, u32[]{:S(2)}) %collective-permute-start.11) | collective-permute-done | bytes 589856 | tf_op jit(solution)/shard_map/ppermute | solution.py:76
  94.6 9.9 %collective-permute-done.12.refs_4_ = bf16[18,128,128]{2,1,0:T(8,128)(2,1)S(1)} collective-permute-done((bf16[18,128,128]{2,1,0:T(8,128)(2,1)}, bf16[18,128,128]{2,1,0:T(8,128)(2,1)S(1)}, u32[]{:S(2)}, u32[]{:S(2)}) %collective-permute-start.12) | collective-permute-done | bytes 589856 | tf_op jit(solution)/shard_map/ppermute | solution.py:76
  108.5 5.6 collective-permute-done.17.refs_4_
  120.9 13.6 %collective-permute-done.13.refs_0_.refs_2_ = bf16[2,2,33,16,128]{4,3,2,1,0:T(8,128)(2,1)} collective-permute-done((bf16[2,2,33,16,128]{4,3,2,1,0:T(8,128)(2,1)}, bf16[2,2,33,16,128]{4,3,2,1,0:T(8,128)(2,1)}, u32[]{:S(2)}, u32[]{:S(2)}) %collective-permute-start.13) | collective-permute-done | bytes 540704 | tf_op jit(solution)/shard_map/ppermute | solution.py:76
  134.5 13.0 %collective-permute-done.14.refs_3_ = bf16[4,9,128,128]{3,2,1,0:T(8,128)(2,1)} collective-permute-done((bf16[4,9,128,128]{3,2,1,0:T(8,128)(2,1)}, bf16[4,9,128,128]{3,2,1,0:T(8,128)(2,1)}, u32[]{:S(2)}, u32[]{:S(2)}) %collective-permute-start.14) | collective-permute-done | bytes 1179680 | tf_op jit(solution)/shard_map/ppermute | solution.py:76
  152.2 24.3 %collective-permute-done.19.refs_3_ = bf16[2,2,33,16,128]{4,3,2,1,0:T(8,128)(2,1)S(1)} collective-permute-done((bf16[2,2,33,16,128]{4,3,2,1,0:T(8,128)(2,1)}, bf16[2,2,33,16,128]{4,3,2,1,0:T(8,128)(2,1)S(1)}, u32[]{:S(2)}, u32[]{:S(2)}) %collective-permute-start.19) | collective-permute-done | bytes 540704 | tf_op jit(solution)/shard_map/ppermute | solution.py:76
  179.6 6.1 fusion.5
  185.8 15.4 %coarse_forward.3 = (f32[480,256]{1,0:T(8,128)S(1)}, f32[8,256]{1,0:T(8,128)S(1)}, f32[480,256]{1,0:T(8,128)S(1)}, f32[8,256]{1,0:T(8,128)S(1)}, f32[8,256]{1,0:T(8,128)S(1)}, /*index=5*/bf16[8,2048]{1,0:T(8,128)(2,1)S(1)}) custom-call(s32[4]{0:T(128)S(1)} %pad_add_fusion.place_ref, bf16[2,4,6,128,128]{4,3,2,1,0:T(8,128)(2,1)S(1)} %get-tuple-element.114.tie_ref.refs_1_, ...), custom_call_target="tpu_custom_call" | custom-call | flops 1 | bytes 1 | tf_op jit(solution)/shard_map/coarse_forward/pallas_call | solution.py:685
  220.5 11.0 %coarse_forward.4 = (f32[480,256]{1,0:T(8,128)S(1)}, f32[8,256]{1,0:T(8,128)S(1)}) custom-call(s32[4]{0:T(128)S(1)} %pad_add_fusion.place_ref, f32[480,1]{1,0:T(8,128)S(1)} %broadcast_in_dim.46.refs_3_.refs_0_.refs_7_.refs_6_, bf16[480,2048]{1,0:T(8,128)(2,1)S(1)} %bitcast.243, bf16[480,2048]{1,0:T(8,128)(2,1)S(1)} %bitcast.265, ...), custom_call_target="tpu_custom_call" | custom-call | flops 1 | bytes 1 | tf_op jit(solution)/shard_map/coarse_forward/pallas_call | solution.py:685
  231.6 11.0 %coarse_forward.5 = (f32[480,256]{1,0:T(8,128)S(1)}, f32[8,256]{1,0:T(8,128)S(1)}) custom-call(s32[4]{0:T(128)S(1)} %pad_add_fusion.place_ref, f32[480,1]{1,0:T(8,128)S(1)} %broadcast_in_dim.46.refs_3_.refs_0_.refs_7_.refs_6_, bf16[480,2048]{1,0:T(8,128)(2,1)S(1)} %bitcast.244, bf16[480,2048]{1,0:T(8,128)(2,1)S(1)} %bitcast.271, ...), custom_call_target="tpu_custom_call" | custom-call | flops 1 | bytes 1 | tf_op jit(solution)/shard_map/coarse_forward/pallas_call | solution.py:685
  253.2 3.7 low_moments.1
  265.0 3.8 all-to-all-start.1
  272.7 3.7 all-to-all-done.1
  283.5 24.1 %decode_forward.1 = (f32[7680,256]{1,0:T(8,128)}, f32[32,640]{1,0:T(8,128)S(1)}, bf16[7680,256]{1,0:T(8,128)(2,1)}) custom-call(f32[20,24,256]{2,1,0:T(8,128)S(1)} %fusion.24.act_ref, bf16[96,48]{1,0:T(8,128)(2,1)S(1)} %pad_maximum_fusion.11.refs_6_.table_ref, bf16[7680,256]{1,0:T(8,128)(2,1)} %bitcast.248, ...), custom_call_target="tpu_custom_call" | custom-call | flops 1 | bytes 1 | tf_op jit(solution)/shard_map/decode_forward/pallas_call | solution.py:1072
  311.6 7.6 all-to-all-done.2
  321.4 18.4 %refine_forward.1 = (f32[7680,256]{1,0:T(8,128)}, f32[32,640]{1,0:T(8,128)S(1)}) custom-call(f32[7680,256]{1,0:T(8,128)} %get-tuple-element.131.z_in_ref.z_ref, f32[32,640]{1,0:T(8,128)S(1)} %bitcast.282, f32[2,256]{1,0:T(2,128)S(1)} %get-tuple-element.441.refs_8_.params_ref.params_in_ref, f32[768,3]{1,0:T(8,128)S(1)} %copy.330.refs_1_.masks_ref, ...), custom_call_target="tpu_custom_call" | custom-call | flops 1 | bytes 1 | tf_op jit(solution)/shard_map/refine_forward/pallas_call | solution.py:1143
  340.5 3.6 all-to-all-start.3
  345.4 6.1 all-to-all-done.3
  354.0 8.4 %classify.1 = (bf16[7680,21]{1,0:T(8,128)(2,1)S(1)}, f32[32,768]{1,0:T(8,128)S(1)}) custom-call(f32[7680,256]{1,0:T(8,128)} %get-tuple-element.134.z_ref, bf16[7680,21]{1,0:T(8,128)(2,1)S(1)} %bitcast.268, f32[32,640]{1,0:T(8,128)S(1)} %bitcast.285, f32[2,256]{1,0:T(2,128)S(1)} %copy-done.91, f32[1536,3]{1,0:T(8,128)S(1)} %copy.331.refs_2_.masks_ref.refs_3_, ...), custom_call_target="tpu_custom_call" | custom-call | flops 1 | bytes 1 | tf_op jit(solution)/shard_map/classify/pallas_call | solution.py:1228
  369.7 5.9 all-to-all-done.4
  379.3 35.6 %refine_backward.1 = (f32[7680,256]{1,0:T(8,128)}, f32[32,768]{1,0:T(8,128)S(1)}, f32[8,256]{1,0:T(8,128)S(1)}, f32[3,256,768]{2,1,0:T(8,128)}) custom-call(f32[7680,256]{1,0:T(8,128)} %get-tuple-element.134.z_ref, bf16[7680,21]{1,0:T(8,128)(2,1)S(1)} %bitcast.269, f32[32,640]{1,0:T(8,128)S(1)} %bitcast.286, f32[32,768]{1,0:T(8,128)S(1)} %bitcast.290, ...), custom_call_target="tpu_custom_call" | custom-call | flops 1 | bytes 1 | tf_op jit(solution)/shard_map/refine_backward/pallas_call | solution.py:1338
  420.8 5.9 all-to-all-done.5
  429.0 46.0 %decode_backward.1 = (f32[20,24,256]{2,1,0:T(8,128)S(1)}, f32[7680,64]{1,0:T(8,128)}, f32[8,256]{1,0:T(8,128)S(1)}, f32[8,256]{1,0:T(8,128)S(1)}, f32[3,256,768]{2,1,0:T(8,128)S(1)}, /*index=5*/f32[3,64,768]{2,1,0:T(8,128)S(1)}) custom-call(f32[7680,256]{1,0:T(8,128)} %get-tuple-element.138.local_ref, f32[7680,256]{1,0:T(8,128)} %get-tuple-element.131.z_in_ref.z_ref, ...), custom_call_target="tpu_custom_call" | custom-call | flops 1 | bytes 1 | tf_op jit(solution)/shard_map/decode_backward/pallas_call | solution.py:1467
  482.3 6.2 all-to-all-done.6
  490.0 5.8 move.44
  502.0 10.0 %all-to-all-done.7 = f32[32,1,2560]{2,1,0:T(1,128)S(1)} async-done(((f32[32,1,2560]{2,1,0:T(1,128)}), f32[32,1,2560]{2,1,0:T(1,128)S(1)}, u32[]{:S(2)}, u32[]{:S(2)}) %all-to-all-start.7) | async-done | bytes 327712 | tf_op jit(solution)/shard_map/all_to_all | solution.py:94
  512.8 3.6 move.45
  519.9 14.2 %coarse_weight.3 = (bf16[2,2,4,12,128,128]{5,4,3,2,1,0:T(8,128)(2,1)}, bf16[2,2,4,12,128,128]{5,4,3,2,1,0:T(8,128)(2,1)}) custom-call(s32[4]{0:T(128)S(1)} %copy-done.85, bf16[480,2048]{1,0:T(8,128)(2,1)S(1)} %bitcast.245, bf16[480,2048]{1,0:T(8,128)(2,1)S(1)} %bitcast.266, bf16[480,2048]{1,0:T(8,128)(2,1)} %bitcast.297, bf16[480,2048]{1,0:T(8,128)(2,1)} %bitcast.270, ...), custom_call_target="tpu_custom_call" | custom-call | flops 1 | bytes 1 | tf_op jit(solution)/shard_map/coarse_weight/pallas_call | solution.py:789
  535.1 15.1 %coarse_weight.4 = (bf16[2,2,4,11,128,128]{5,4,3,2,1,0:T(8,128)(2,1)}, bf16[2,2,4,11,128,128]{5,4,3,2,1,0:T(8,128)(2,1)}) custom-call(s32[4]{0:T(128)S(1)} %copy-done.85, bf16[2,2,4,12,128,128]{5,4,3,2,1,0:T(8,128)(2,1)} %get-tuple-element.148.tie_ref.refs_1_, bf16[480,2048]{1,0:T(8,128)(2,1)S(1)} %bitcast.246, bf16[480,2048]{1,0:T(8,128)(2,1)S(1)} %bitcast.262, ...), custom_call_target="tpu_custom_call" | custom-call | flops 1 | bytes 1 | tf_op jit(solution)/shard_map/coarse_weight/pallas_call | solution.py:789
  553.0 3.9 move.46
  559.5 8.0 %low_backward.1 = (bf16[7680,256]{1,0:T(8,128)(2,1)}, f32[64,256]{1,0:T(8,128)S(1)}) custom-call(f32[8,256]{1,0:T(8,128)S(1)} %maximum_maximum_fusion.2.place_ref, bf16[2,4,6,128,128]{4,3,2,1,0:T(8,128)(2,1)} %get-tuple-element.155.tie_ref, f32[7680,64]{1,0:T(8,128)} %get-tuple-element.156.refs_0_, bf16[7680,256]{1,0:T(8,128)(2,1)} %bitcast.250, ...), custom_call_target="tpu_custom_call" | custom-call | flops 1509949440 | bytes 9830400 | tf_op jit(solution)/shard_map/low_backward/pallas_call | solution.py:1618
  567.4 5.3 pack_gradients.1
  578.2 9.4 %coarse_weight.5 = (bf16[2,2,4,6,128,128]{5,4,3,2,1,0:T(8,128)(2,1)}, bf16[2,2,4,6,128,128]{5,4,3,2,1,0:T(8,128)(2,1)}) custom-call(s32[4]{0:T(128)S(1)} %copy-done.85, bf16[2,2,4,33,16,128]{5,4,3,2,1,0:T(8,128)(2,1)} %copy-done.14, bf16[480,2048]{1,0:T(8,128)(2,1)S(1)} %bitcast.247, bf16[480,2048]{1,0:T(8,128)(2,1)S(1)} %bitcast.263, ...), custom_call_target="tpu_custom_call" | custom-call | flops 1 | bytes 1 | tf_op jit(solution)/shard_map/coarse_weight/pallas_call | solution.py:789
  587.6 5.1 collective-permute-done.29.refs_3_
  594.9 3.9 move.47
  610.7 8.1 %collective-permute-done.32.refs_2_ = bf16[4,6,128,128]{3,2,1,0:T(8,128)(2,1)S(1)} collective-permute-done((bf16[4,6,128,128]{3,2,1,0:T(8,128)(2,1)S(1)}, bf16[4,6,128,128]{3,2,1,0:T(8,128)(2,1)S(1)}, u32[]{:S(2)}, u32[]{:S(2)}) %collective-permute-start.32) | collective-permute-done | bytes 786464 | tf_op jit(solution)/shard_map/ppermute | solution.py:76
  627.3 25.0 %coarse_input.1.refs_0_ = bf16[480,2048]{1,0:T(8,128)(2,1)} custom-call(s32[4]{0:T(128)S(1)} %copy-done.85, bf16[2,4,33,16,128]{4,3,2,1,0:T(8,128)(2,1)} %move.50.tie_ref, bf16[480,256]{1,0:T(8,128)(2,1)S(1)} %copy-done.64, bf16[8,256]{1,0:T(8,128)(2,1)S(1)} %copy-done.92, f32[480,8]{1,0:T(8,128)S(1)} %copy-done.49, ...), custom_call_target="tpu_custom_call" | custom-call | flops 1 | bytes 1 | tf_op jit(solution)/shard_map/coarse_input/pallas_call | solution.py:867
  679.4 6.9 collective-permute-done.41.refs_3_
  691.5 11.7 %collective-permute-done.42.refs_3_ = bf16[2,4,3,128,128]{4,3,2,1,0:T(8,128)(2,1)} collective-permute-done((bf16[2,4,3,128,128]{4,3,2,1,0:T(8,128)(2,1)}, bf16[2,4,3,128,128]{4,3,2,1,0:T(8,128)(2,1)}, u32[]{:S(2)}, u32[]{:S(2)}) %collective-permute-start.42) | collective-permute-done | bytes 786464 | tf_op jit(solution)/shard_map/ppermute | solution.py:76
  715.8 6.3 collective-permute-start.56
  732.8 10.1 %collective-permute-done.49.refs_2_ = bf16[2,33,16,128]{3,2,1,0:T(8,128)(2,1)} collective-permute-done((bf16[2,33,16,128]{3,2,1,0:T(8,128)(2,1)}, bf16[2,33,16,128]{3,2,1,0:T(8,128)(2,1)}, u32[]{:S(2)}, u32[]{:S(2)}) %collective-permute-start.49) | collective-permute-done | bytes 270368 | tf_op jit(solution)/shard_map/ppermute | solution.py:76
  746.7 4.5 collective-permute-done.50.refs_2_
  758.1 6.3 collective-permute-start.52
  (786 shorter events, 253.7 us)
Async XLA Ops:
  13.6 16.9 %collective-permute-start.6 = (bf16[11,128,128]{2,1,0:T(8,128)(2,1)S(1)}, bf16[11,128,128]{2,1,0:T(8,128)(2,1)S(1)}, u32[]{:S(2)}, u32[]{:S(2)}) collective-permute-start(bf16[11,128,128]{2,1,0:T(8,128)(2,1)S(1)} %pad_maximum_fusion.7.refs_1_), channel_id=1, source_target_pairs={{0,8},{4,12},{8,0},{12,4},{16,24},{20,28},{24,16},{28,20},{1,9},{5... | collective-permute-start | bytes 1081352 | tf_op jit(solution)/shard_map/ppermute | solution.py:76
  14.9 15.6 %collective-permute-start.7 = (bf16[11,128,128]{2,1,0:T(8,128)(2,1)S(1)}, bf16[11,128,128]{2,1,0:T(8,128)(2,1)S(1)}, u32[]{:S(2)}, u32[]{:S(2)}) collective-permute-start(bf16[11,128,128]{2,1,0:T(8,128)(2,1)S(1)} %pad_maximum_fusion.7.refs_1_), channel_id=1, source_target_pairs={{0,16},{4,20},{8,24},{12,28},{16,0},{20,4},{24,8},{28,12},{1,17},{... | collective-permute-start | bytes 1081352 | tf_op jit(solution)/shard_map/ppermute | solution.py:76
  17.2 23.6 %collective-permute-start.8 = (bf16[11,128,128]{2,1,0:T(8,128)(2,1)S(1)}, bf16[11,128,128]{2,1,0:T(8,128)(2,1)S(1)}, u32[]{:S(2)}, u32[]{:S(2)}) collective-permute-start(bf16[11,128,128]{2,1,0:T(8,128)(2,1)S(1)} %pad_maximum_fusion.7.refs_1_), channel_id=1, source_target_pairs={{0,24},{4,28},{8,16},{12,20},{16,8},{20,12},{24,0},{28,4},{1,25},{... | collective-permute-start | bytes 1081352 | tf_op jit(solution)/shard_map/ppermute | solution.py:76
  42.0 35.8 %collective-permute-start.10 = (bf16[4,6,128,128]{3,2,1,0:T(8,128)(2,1)}, bf16[4,6,128,128]{3,2,1,0:T(8,128)(2,1)}, u32[]{:S(2)}, u32[]{:S(2)}) collective-permute-start(bf16[4,6,128,128]{3,2,1,0:T(8,128)(2,1)} %get-tuple-element.110.refs_15_), channel_id=1, source_target_pairs={{0,2},{1,3},{2,0},{3,1},{4,6},{5,7},{6,4},{7,5},{8,10},{9,11},{10,... | collective-permute-start | bytes 2359304 | tf_op jit(solution)/shard_map/ppermute | solution.py:76
  43.3 34.5 %collective-permute-start.1 = (bf16[18,128,128]{2,1,0:T(8,128)(2,1)}, bf16[18,128,128]{2,1,0:T(8,128)(2,1)}, u32[]{:S(2)}, u32[]{:S(2)}) collective-permute-start(bf16[18,128,128]{2,1,0:T(8,128)(2,1)} %pad_maximum_fusion.6.refs_0_.refs_1_), channel_id=1, source_target_pairs={{0,16},{4,20},{8,24},{12,28},{16,0},{20,4},{24,8},{28,12},{1,17},{... | collective-permute-start | bytes 1769480 | tf_op jit(solution)/shard_map/ppermute | solution.py:76
  52.2 25.6 %collective-permute-start.9 = (bf16[4,5,128,128]{3,2,1,0:T(8,128)(2,1)}, bf16[4,5,128,128]{3,2,1,0:T(8,128)(2,1)}, u32[]{:S(2)}, u32[]{:S(2)}) collective-permute-start(bf16[4,5,128,128]{3,2,1,0:T(8,128)(2,1)} %get-tuple-element.109.refs_14_), channel_id=1, source_target_pairs={{0,4},{4,0},{8,12},{12,8},{16,20},{20,16},{24,28},{28,24},{1,5},{5... | collective-permute-start | bytes 1966088 | tf_op jit(solution)/shard_map/ppermute | solution.py:76
  79.8 34.3 %collective-permute-start.17 = (bf16[2,4,6,128,128]{4,3,2,1,0:T(8,128)(2,1)S(1)}, bf16[2,4,6,128,128]{4,3,2,1,0:T(8,128)(2,1)S(1)}, u32[]{:S(2)}, u32[]{:S(2)}) collective-permute-start(bf16[2,4,6,128,128]{4,3,2,1,0:T(8,128)(2,1)S(1)} %get-tuple-element.115.refs_2_), channel_id=1, source_target_pairs={{0,4},{4,0},{8,12},{12,8},{16,20},{20,16},{24,28},{28,24},{1,5},{5... | collective-permute-start | bytes 4718600 | tf_op jit(solution)/shard_map/ppermute | solution.py:76
  80.1 28.4 %collective-permute-start.16 = (bf16[2,4,5,128,128]{4,3,2,1,0:T(8,128)(2,1)S(1)}, bf16[2,4,5,128,128]{4,3,2,1,0:T(8,128)(2,1)S(1)}, u32[]{:S(2)}, u32[]{:S(2)}) collective-permute-start(bf16[2,4,5,128,128]{4,3,2,1,0:T(8,128)(2,1)S(1)} %get-tuple-element.111.refs_0_.refs_1_), channel_id=1, source_target_pairs={{0,2},{1,3},{2,0},{3,1},{4,6},{5,7},{6,4},{7,5},{8,10},{9,11},{10,... | collective-permute-start | bytes 3932168 | tf_op jit(solution)/shard_map/ppermute | solution.py:76
  80.4 14.2 %collective-permute-start.11 = (bf16[18,128,128]{2,1,0:T(8,128)(2,1)}, bf16[18,128,128]{2,1,0:T(8,128)(2,1)S(1)}, u32[]{:S(2)}, u32[]{:S(2)}) collective-permute-start(bf16[18,128,128]{2,1,0:T(8,128)(2,1)} %pad_maximum_fusion.6.refs_0_.refs_1_), channel_id=1, source_target_pairs={{0,8},{4,12},{8,0},{12,4},{16,24},{20,28},{24,16},{28,20},{1,9},{5... | collective-permute-start | bytes 1769480 | tf_op jit(solution)/shard_map/ppermute | solution.py:76
  80.4 24.1 %collective-permute-start.12 = (bf16[18,128,128]{2,1,0:T(8,128)(2,1)}, bf16[18,128,128]{2,1,0:T(8,128)(2,1)S(1)}, u32[]{:S(2)}, u32[]{:S(2)}) collective-permute-start(bf16[18,128,128]{2,1,0:T(8,128)(2,1)} %pad_maximum_fusion.6.refs_0_.refs_1_), channel_id=1, source_target_pairs={{0,24},{4,28},{8,16},{12,20},{16,8},{20,12},{24,0},{28,4},{1,25},{... | collective-permute-start | bytes 1769480 | tf_op jit(solution)/shard_map/ppermute | solution.py:76
  117.0 60.8 %collective-permute-start.18 = (bf16[2,2,4,11,128,128]{5,4,3,2,1,0:T(8,128)(2,1)}, bf16[2,2,4,11,128,128]{5,4,3,2,1,0:T(8,128)(2,1)}, u32[]{:S(2)}, u32[]{:S(2)}) collective-permute-start(bf16[2,2,4,11,128,128]{5,4,3,2,1,0:T(8,128)(2,1)} %move.40.refs_6_), channel_id=1, source_target_pairs={{0,1},{1,0},{2,3},{3,2},{4,5},{5,4},{6,7},{7,6},{8,9},{9,8},{10,11... | collective-permute-start | bytes 17301512 | tf_op jit(solution)/shard_map/ppermute | solution.py:76
  119.6 27.9 %collective-permute-start.14 = (bf16[4,9,128,128]{3,2,1,0:T(8,128)(2,1)}, bf16[4,9,128,128]{3,2,1,0:T(8,128)(2,1)}, u32[]{:S(2)}, u32[]{:S(2)}) collective-permute-start(bf16[4,9,128,128]{3,2,1,0:T(8,128)(2,1)} %get-tuple-element.112.refs_0_.refs_1_), channel_id=1, source_target_pairs={{0,4},{4,0},{8,12},{12,8},{16,20},{20,16},{24,28},{28,24},{1,5},{5... | collective-permute-start | bytes 3538952 | tf_op jit(solution)/shard_map/ppermute | solution.py:76
  119.8 27.7 %collective-permute-start.15 = (bf16[4,9,128,128]{3,2,1,0:T(8,128)(2,1)}, bf16[4,9,128,128]{3,2,1,0:T(8,128)(2,1)}, u32[]{:S(2)}, u32[]{:S(2)}) collective-permute-start(bf16[4,9,128,128]{3,2,1,0:T(8,128)(2,1)} %get-tuple-element.113.refs_2_), channel_id=1, source_target_pairs={{0,2},{1,3},{2,0},{3,1},{4,6},{5,7},{6,4},{7,5},{8,10},{9,11},{10,... | collective-permute-start | bytes 3538952 | tf_op jit(solution)/shard_map/ppermute | solution.py:76
  150.1 56.4 %collective-permute-start.21 = (bf16[2,4,6,128,128]{4,3,2,1,0:T(8,128)(2,1)S(1)}, bf16[2,4,6,128,128]{4,3,2,1,0:T(8,128)(2,1)S(1)}, u32[]{:S(2)}, u32[]{:S(2)}) collective-permute-start(bf16[2,4,6,128,128]{4,3,2,1,0:T(8,128)(2,1)S(1)} %get-tuple-element.114.tie_ref.refs_1_), channel_id=1, source_target_pairs={{0,2},{1,3},{2,0},{3,1},{4,6},{5,7},{6,4},{7,5},{8,10},{9,11},{10,... | collective-permute-start | bytes 4718600 | tf_op jit(solution)/shard_map/ppermute | solution.py:76
  150.4 60.6 %collective-permute-start.25 = (bf16[2,4,6,128,128]{4,3,2,1,0:T(8,128)(2,1)S(1)}, bf16[2,4,6,128,128]{4,3,2,1,0:T(8,128)(2,1)S(1)}, u32[]{:S(2)}, u32[]{:S(2)}) collective-permute-start(bf16[2,4,6,128,128]{4,3,2,1,0:T(8,128)(2,1)S(1)} %get-tuple-element.123.refs_2_), channel_id=1, source_target_pairs={{0,4},{4,0},{8,12},{12,8},{16,20},{20,16},{24,28},{28,24},{1,5},{5... | collective-permute-start | bytes 4718600 | tf_op jit(solution)/shard_map/ppermute | solution.py:76
  151.6 24.9 %collective-permute-start.19 = (bf16[2,2,33,16,128]{4,3,2,1,0:T(8,128)(2,1)}, bf16[2,2,33,16,128]{4,3,2,1,0:T(8,128)(2,1)S(1)}, u32[]{:S(2)}, u32[]{:S(2)}) collective-permute-start(bf16[2,2,33,16,128]{4,3,2,1,0:T(8,128)(2,1)} %move.38.refs_1_), channel_id=1, source_target_pairs={{0,16},{4,20},{8,24},{12,28},{16,0},{20,4},{24,8},{28,12},{1,17},{... | collective-permute-start | bytes 1622024 | tf_op jit(solution)/shard_map/ppermute | solution.py:76
  151.8 54.7 %collective-permute-start.22 = (bf16[2,4,3,128,128]{4,3,2,1,0:T(8,128)(2,1)S(1)}, bf16[2,4,3,128,128]{4,3,2,1,0:T(8,128)(2,1)S(1)}, u32[]{:S(2)}, u32[]{:S(2)}) collective-permute-start(bf16[2,4,3,128,128]{4,3,2,1,0:T(8,128)(2,1)S(1)} %get-tuple-element.120.refs_2_), channel_id=1, source_target_pairs={{0,4},{4,0},{8,12},{12,8},{16,20},{20,16},{24,28},{28,24},{1,5},{5... | collective-permute-start | bytes 2359304 | tf_op jit(solution)/shard_map/ppermute | solution.py:76
  176.5 34.5 %collective-permute-start.24 = (bf16[2,4,3,128,128]{4,3,2,1,0:T(8,128)(2,1)S(1)}, bf16[2,4,3,128,128]{4,3,2,1,0:T(8,128)(2,1)S(1)}, u32[]{:S(2)}, u32[]{:S(2)}) collective-permute-start(bf16[2,4,3,128,128]{4,3,2,1,0:T(8,128)(2,1)S(1)} %get-tuple-element.122.refs_1_), channel_id=1, source_target_pairs={{0,2},{1,3},{2,0},{3,1},{4,6},{5,7},{6,4},{7,5},{8,10},{9,11},{10,... | collective-permute-start | bytes 2359304 | tf_op jit(solution)/shard_map/ppermute | solution.py:76
  177.8 25.3 %collective-permute-start.20 = (bf16[2,2,33,16,128]{4,3,2,1,0:T(8,128)(2,1)}, bf16[2,2,33,16,128]{4,3,2,1,0:T(8,128)(2,1)S(1)}, u32[]{:S(2)}, u32[]{:S(2)}) collective-permute-start(bf16[2,2,33,16,128]{4,3,2,1,0:T(8,128)(2,1)} %move.38.refs_1_), channel_id=1, source_target_pairs={{0,24},{4,28},{8,16},{12,20},{16,8},{20,12},{24,0},{28,4},{1,25},{... | collective-permute-start | bytes 1622024 | tf_op jit(solution)/shard_map/ppermute | solution.py:76
  213.6 17.9 %collective-permute-start.26 = (bf16[2,2,4,9,128,128]{5,4,3,2,1,0:T(8,128)(2,1)}, bf16[2,2,4,9,128,128]{5,4,3,2,1,0:T(8,128)(2,1)}, u32[]{:S(2)}, u32[]{:S(2)}) collective-permute-start(bf16[2,2,4,9,128,128]{5,4,3,2,1,0:T(8,128)(2,1)} %move.43.refs_4_.refs_10_), channel_id=1, source_target_pairs={{0,1},{1,0},{2,3},{3,2},{4,5},{5,4},{6,7},{7,6},{8,9},{9,8},{10,11... | collective-permute-start | bytes 14155784 | tf_op jit(solution)/shard_map/ppermute | solution.py:76
  214.9 33.5 %collective-permute-start.27 = (bf16[4,2,2,33,16,128]{5,4,3,2,1,0:T(8,128)(2,1)}, bf16[4,2,2,33,16,128]{5,4,3,2,1,0:T(8,128)(2,1)}, u32[]{:S(2)}, u32[]{:S(2)}) collective-permute-start(bf16[4,2,2,33,16,128]{5,4,3,2,1,0:T(8,128)(2,1)} %copy-done.17), channel_id=1, source_target_pairs={{0,1},{1,0},{2,3},{3,2},{4,5},{5,4},{6,7},{7,6},{8,9},{9,8},{10,11... | collective-permute-start | bytes 6488072 | tf_op jit(solution)/shard_map/ppermute | solution.py:76
  244.5 15.0 %all-to-all-start = ((f32[32,1,2561]{2,1,0:T(1,128)}), f32[32,1,2561]{2,1,0:T(1,128)}, u32[]{:S(2)}, u32[]{:S(2)}) async-start(f32[32,1,2561]{2,1,0:T(1,128)} %broadcast_in_dim.38), calls=%async_computation | async-start | bytes 688128 | tf_op jit(solution)/shard_map/all_to_all | solution.py:94
  497.8 14.2 %all-to-all-start.7 = ((f32[32,1,2560]{2,1,0:T(1,128)}), f32[32,1,2560]{2,1,0:T(1,128)S(1)}, u32[]{:S(2)}, u32[]{:S(2)}) async-start(f32[32,1,2560]{2,1,0:T(1,128)} %copy.356), calls=%async_computation.7 | async-start | bytes 655360 | tf_op jit(solution)/shard_map/all_to_all | solution.py:94
  534.1 16.2 %collective-permute-start.28 = (bf16[2,2,4,12,128,128]{5,4,3,2,1,0:T(8,128)(2,1)}, bf16[2,2,4,12,128,128]{5,4,3,2,1,0:T(8,128)(2,1)}, u32[]{:S(2)}, u32[]{:S(2)}) collective-permute-start(bf16[2,2,4,12,128,128]{5,4,3,2,1,0:T(8,128)(2,1)} %get-tuple-element.154), channel_id=1, source_target_pairs={{0,1},{1,0},{2,3},{3,2},{4,5},{5,4},{6,7},{7,6},{8,9},{9,8},{10,11... | collective-permute-start | bytes 18874376 | tf_op jit(solution)/shard_map/ppermute | solution.py:76
  550.2 53.6 %collective-permute-start.31 = (bf16[2,2,4,11,128,128]{5,4,3,2,1,0:T(8,128)(2,1)}, bf16[2,2,4,11,128,128]{5,4,3,2,1,0:T(8,128)(2,1)}, u32[]{:S(2)}, u32[]{:S(2)}) collective-permute-start(bf16[2,2,4,11,128,128]{5,4,3,2,1,0:T(8,128)(2,1)} %get-tuple-element.166), channel_id=1, source_target_pairs={{0,1},{1,0},{2,3},{3,2},{4,5},{5,4},{6,7},{7,6},{8,9},{9,8},{10,11... | collective-permute-start | bytes 17301512 | tf_op jit(solution)/shard_map/ppermute | solution.py:76
  556.9 35.8 %collective-permute-start.29 = (bf16[2,4,6,128,128]{4,3,2,1,0:T(8,128)(2,1)}, bf16[2,4,6,128,128]{4,3,2,1,0:T(8,128)(2,1)}, u32[]{:S(2)}, u32[]{:S(2)}) collective-permute-start(bf16[2,4,6,128,128]{4,3,2,1,0:T(8,128)(2,1)} %get-tuple-element.155.tie_ref), channel_id=1, source_target_pairs={{0,4},{4,0},{8,12},{12,8},{16,20},{20,16},{24,28},{28,24},{1,5},{5... | collective-permute-start | bytes 4718600 | tf_op jit(solution)/shard_map/ppermute | solution.py:76
  557.5 35.5 %collective-permute-start.30 = (bf16[2,4,6,128,128]{4,3,2,1,0:T(8,128)(2,1)}, bf16[2,4,6,128,128]{4,3,2,1,0:T(8,128)(2,1)}, u32[]{:S(2)}, u32[]{:S(2)}) collective-permute-start(bf16[2,4,6,128,128]{4,3,2,1,0:T(8,128)(2,1)} %get-tuple-element.164), channel_id=1, source_target_pairs={{0,2},{1,3},{2,0},{3,1},{4,6},{5,7},{6,4},{7,5},{8,10},{9,11},{10,... | collective-permute-start | bytes 4718600 | tf_op jit(solution)/shard_map/ppermute | solution.py:76
  574.1 47.1 %collective-permute-start.34 = (bf16[2,2,4,33,16,128]{5,4,3,2,1,0:T(8,128)(2,1)}, bf16[2,2,4,33,16,128]{5,4,3,2,1,0:T(8,128)(2,1)}, u32[]{:S(2)}, u32[]{:S(2)}) collective-permute-start(bf16[2,2,4,33,16,128]{5,4,3,2,1,0:T(8,128)(2,1)} %get-tuple-element.171), channel_id=1, source_target_pairs={{0,1},{1,0},{2,3},{3,2},{4,5},{5,4},{6,7},{7,6},{8,9},{9,8},{10,11... | collective-permute-start | bytes 6488072 | tf_op jit(solution)/shard_map/ppermute | solution.py:76
  587.6 77.7 %collective-permute-start.37 = (bf16[2,2,4,6,128,128]{5,4,3,2,1,0:T(8,128)(2,1)}, bf16[2,2,4,6,128,128]{5,4,3,2,1,0:T(8,128)(2,1)}, u32[]{:S(2)}, u32[]{:S(2)}) collective-permute-start(bf16[2,2,4,6,128,128]{5,4,3,2,1,0:T(8,128)(2,1)} %get-tuple-element.175), channel_id=1, source_target_pairs={{0,1},{1,0},{2,3},{3,2},{4,5},{5,4},{6,7},{7,6},{8,9},{9,8},{10,11... | collective-permute-start | bytes 9437192 | tf_op jit(solution)/shard_map/ppermute | solution.py:76
  601.3 17.4 %collective-permute-start.32 = (bf16[4,6,128,128]{3,2,1,0:T(8,128)(2,1)S(1)}, bf16[4,6,128,128]{3,2,1,0:T(8,128)(2,1)S(1)}, u32[]{:S(2)}, u32[]{:S(2)}) collective-permute-start(bf16[4,6,128,128]{3,2,1,0:T(8,128)(2,1)S(1)} %get-tuple-element.165.refs_0_), channel_id=1, source_target_pairs={{0,2},{1,3},{2,0},{3,1},{4,6},{5,7},{6,4},{7,5},{8,10},{9,11},{10,... | collective-permute-start | bytes 2359304 | tf_op jit(solution)/shard_map/ppermute | solution.py:76
  602.6 17.5 %collective-permute-start.33 = (bf16[4,6,128,128]{3,2,1,0:T(8,128)(2,1)}, bf16[4,6,128,128]{3,2,1,0:T(8,128)(2,1)S(1)}, u32[]{:S(2)}, u32[]{:S(2)}) collective-permute-start(bf16[4,6,128,128]{3,2,1,0:T(8,128)(2,1)} %copy-done.95), channel_id=1, source_target_pairs={{0,4},{4,0},{8,12},{12,8},{16,20},{20,16},{24,28},{28,24},{1,5},{5... | collective-permute-start | bytes 2359304 | tf_op jit(solution)/shard_map/ppermute | solution.py:76
  610.0 43.5 %collective-permute-start.36 = (bf16[2,4,6,128,128]{4,3,2,1,0:T(8,128)(2,1)}, bf16[2,4,6,128,128]{4,3,2,1,0:T(8,128)(2,1)S(1)}, u32[]{:S(2)}, u32[]{:S(2)}) collective-permute-start(bf16[2,4,6,128,128]{4,3,2,1,0:T(8,128)(2,1)} %get-tuple-element.173), channel_id=1, source_target_pairs={{0,2},{1,3},{2,0},{3,1},{4,6},{5,7},{6,4},{7,5},{8,10},{9,11},{10,... | collective-permute-start | bytes 4718600 | tf_op jit(solution)/shard_map/ppermute | solution.py:76
  618.7 33.6 %collective-permute-start.35 = (bf16[2,4,5,128,128]{4,3,2,1,0:T(8,128)(2,1)S(1)}, bf16[2,4,5,128,128]{4,3,2,1,0:T(8,128)(2,1)S(1)}, u32[]{:S(2)}, u32[]{:S(2)}) collective-permute-start(bf16[2,4,5,128,128]{4,3,2,1,0:T(8,128)(2,1)S(1)} %get-tuple-element.167.refs_0_), channel_id=1, source_target_pairs={{0,4},{4,0},{8,12},{12,8},{16,20},{20,16},{24,28},{28,24},{1,5},{5... | collective-permute-start | bytes 3932168 | tf_op jit(solution)/shard_map/ppermute | solution.py:76
  624.5 45.0 %collective-permute-start.38 = (bf16[2,4,33,16,128]{4,3,2,1,0:T(8,128)(2,1)}, bf16[2,4,33,16,128]{4,3,2,1,0:T(8,128)(2,1)}, u32[]{:S(2)}, u32[]{:S(2)}) collective-permute-start(bf16[2,4,33,16,128]{4,3,2,1,0:T(8,128)(2,1)} %move.50.tie_ref), channel_id=1, source_target_pairs={{0,4},{4,0},{8,12},{12,8},{16,20},{20,16},{24,28},{28,24},{1,5},{5... | collective-permute-start | bytes 3244040 | tf_op jit(solution)/shard_map/ppermute | solution.py:76
  626.4 50.9 %collective-permute-start.39 = (bf16[2,12,128,128]{3,2,1,0:T(8,128)(2,1)}, bf16[2,12,128,128]{3,2,1,0:T(8,128)(2,1)}, u32[]{:S(2)}, u32[]{:S(2)}) collective-permute-start(bf16[2,12,128,128]{3,2,1,0:T(8,128)(2,1)} %get-tuple-element.170.refs_0_), channel_id=1, source_target_pairs={{0,16},{4,20},{8,24},{12,28},{16,0},{20,4},{24,8},{28,12},{1,17},{... | collective-permute-start | bytes 2359304 | tf_op jit(solution)/shard_map/ppermute | solution.py:76
  663.8 22.6 %collective-permute-start.41 = (bf16[4,6,128,128]{3,2,1,0:T(8,128)(2,1)}, bf16[4,6,128,128]{3,2,1,0:T(8,128)(2,1)}, u32[]{:S(2)}, u32[]{:S(2)}) collective-permute-start(bf16[4,6,128,128]{3,2,1,0:T(8,128)(2,1)} %get-tuple-element.181), channel_id=1, source_target_pairs={{0,4},{4,0},{8,12},{12,8},{16,20},{20,16},{24,28},{28,24},{1,5},{5... | collective-permute-start | bytes 2359304 | tf_op jit(solution)/shard_map/ppermute | solution.py:76
  664.4 15.0 %collective-permute-start.40 = (bf16[4,5,128,128]{3,2,1,0:T(8,128)(2,1)}, bf16[4,5,128,128]{3,2,1,0:T(8,128)(2,1)}, u32[]{:S(2)}, u32[]{:S(2)}) collective-permute-start(bf16[4,5,128,128]{3,2,1,0:T(8,128)(2,1)} %get-tuple-element.174.refs_0_), channel_id=1, source_target_pairs={{0,2},{1,3},{2,0},{3,1},{4,6},{5,7},{6,4},{7,5},{8,10},{9,11},{10,... | collective-permute-start | bytes 1966088 | tf_op jit(solution)/shard_map/ppermute | solution.py:76
  668.0 35.2 %collective-permute-start.42 = (bf16[2,4,3,128,128]{4,3,2,1,0:T(8,128)(2,1)}, bf16[2,4,3,128,128]{4,3,2,1,0:T(8,128)(2,1)}, u32[]{:S(2)}, u32[]{:S(2)}) collective-permute-start(bf16[2,4,3,128,128]{4,3,2,1,0:T(8,128)(2,1)} %get-tuple-element.176.refs_0_), channel_id=1, source_target_pairs={{0,4},{4,0},{8,12},{12,8},{16,20},{20,16},{24,28},{28,24},{1,5},{5... | collective-permute-start | bytes 2359304 | tf_op jit(solution)/shard_map/ppermute | solution.py:76
  669.5 33.7 %collective-permute-start.43 = (bf16[2,4,3,128,128]{4,3,2,1,0:T(8,128)(2,1)}, bf16[2,4,3,128,128]{4,3,2,1,0:T(8,128)(2,1)}, u32[]{:S(2)}, u32[]{:S(2)}) collective-permute-start(bf16[2,4,3,128,128]{4,3,2,1,0:T(8,128)(2,1)} %get-tuple-element.183), channel_id=1, source_target_pairs={{0,2},{1,3},{2,0},{3,1},{4,6},{5,7},{6,4},{7,5},{8,10},{9,11},{10,... | collective-permute-start | bytes 2359304 | tf_op jit(solution)/shard_map/ppermute | solution.py:76
  677.3 31.8 %collective-permute-start.44 = (bf16[4,33,16,128]{3,2,1,0:T(8,128)(2,1)S(1)}, bf16[4,33,16,128]{3,2,1,0:T(8,128)(2,1)S(1)}, u32[]{:S(2)}, u32[]{:S(2)}) collective-permute-start(bf16[4,33,16,128]{3,2,1,0:T(8,128)(2,1)S(1)} %get-tuple-element.177.refs_0_), channel_id=1, source_target_pairs={{0,2},{1,3},{2,0},{3,1},{4,6},{5,7},{6,4},{7,5},{8,10},{9,11},{10,... | collective-permute-start | bytes 1622024 | tf_op jit(solution)/shard_map/ppermute | solution.py:76
  689.9 38.9 %collective-permute-start.48 = (bf16[2,11,128,128]{3,2,1,0:T(8,128)(2,1)}, bf16[2,11,128,128]{3,2,1,0:T(8,128)(2,1)}, u32[]{:S(2)}, u32[]{:S(2)}) collective-permute-start(bf16[2,11,128,128]{3,2,1,0:T(8,128)(2,1)} %get-tuple-element.182.refs_0_), channel_id=1, source_target_pairs={{0,16},{4,20},{8,24},{12,28},{16,0},{20,4},{24,8},{28,12},{1,17},{... | collective-permute-start | bytes 2162696 | tf_op jit(solution)/shard_map/ppermute | solution.py:76
  691.4 21.3 %collective-permute-start.45 = (bf16[12,128,128]{2,1,0:T(8,128)(2,1)S(1)}, bf16[12,128,128]{2,1,0:T(8,128)(2,1)S(1)}, u32[]{:S(2)}, u32[]{:S(2)}) collective-permute-start(bf16[12,128,128]{2,1,0:T(8,128)(2,1)S(1)} %get-tuple-element.179.refs_0_), channel_id=1, source_target_pairs={{0,8},{4,12},{8,0},{12,4},{16,24},{20,28},{24,16},{28,20},{1,9},{5... | collective-permute-start | bytes 1179656 | tf_op jit(solution)/shard_map/ppermute | solution.py:76
  706.1 16.0 %collective-permute-start.46 = (bf16[4,3,128,128]{3,2,1,0:T(8,128)(2,1)}, bf16[4,3,128,128]{3,2,1,0:T(8,128)(2,1)S(1)}, u32[]{:S(2)}, u32[]{:S(2)}) collective-permute-start(bf16[4,3,128,128]{3,2,1,0:T(8,128)(2,1)} %get-tuple-element.184.refs_0_), channel_id=1, source_target_pairs={{0,2},{1,3},{2,0},{3,1},{4,6},{5,7},{6,4},{7,5},{8,10},{9,11},{10,... | collective-permute-start | bytes 1179656 | tf_op jit(solution)/shard_map/ppermute | solution.py:76
  706.9 15.9 %collective-permute-start.47 = (bf16[4,3,128,128]{3,2,1,0:T(8,128)(2,1)}, bf16[4,3,128,128]{3,2,1,0:T(8,128)(2,1)S(1)}, u32[]{:S(2)}, u32[]{:S(2)}) collective-permute-start(bf16[4,3,128,128]{3,2,1,0:T(8,128)(2,1)} %get-tuple-element.189), channel_id=1, source_target_pairs={{0,4},{4,0},{8,12},{12,8},{16,20},{20,16},{24,28},{28,24},{1,5},{5... | collective-permute-start | bytes 1179656 | tf_op jit(solution)/shard_map/ppermute | solution.py:76
  710.7 32.2 %collective-permute-start.49 = (bf16[2,33,16,128]{3,2,1,0:T(8,128)(2,1)}, bf16[2,33,16,128]{3,2,1,0:T(8,128)(2,1)}, u32[]{:S(2)}, u32[]{:S(2)}) collective-permute-start(bf16[2,33,16,128]{3,2,1,0:T(8,128)(2,1)} %get-tuple-element.186.refs_0_), channel_id=1, source_target_pairs={{0,16},{4,20},{8,24},{12,28},{16,0},{20,4},{24,8},{28,12},{1,17},{... | collective-permute-start | bytes 811016 | tf_op jit(solution)/shard_map/ppermute | solution.py:76
  715.8 28.8 %collective-permute-start.56 = (bf16[12,128,64]{1,2,0:T(8,128)(2,1)}, bf16[12,128,64]{1,2,0:T(8,128)(2,1)}, u32[]{:S(2)}, u32[]{:S(2)}) collective-permute-start(bf16[12,128,64]{1,2,0:T(8,128)(2,1)} %fusion.25), channel_id=1, source_target_pairs={{0,1},{1,0},{2,3},{3,2},{4,5},{5,4},{6,7},{7,6},{8,9},{9,8},{10,11... | collective-permute-start | bytes 589832 | tf_op jit(solution)/shard_map/ppermute | solution.py:76
  725.8 25.5 %collective-permute-start.50 = (bf16[2,6,128,128]{3,2,1,0:T(8,128)(2,1)S(1)}, bf16[2,6,128,128]{3,2,1,0:T(8,128)(2,1)S(1)}, u32[]{:S(2)}, u32[]{:S(2)}) collective-permute-start(bf16[2,6,128,128]{3,2,1,0:T(8,128)(2,1)S(1)} %get-tuple-element.190.refs_0_), channel_id=1, source_target_pairs={{0,16},{4,20},{8,24},{12,28},{16,0},{20,4},{24,8},{28,12},{1,17},{... | collective-permute-start | bytes 1179656 | tf_op jit(solution)/shard_map/ppermute | solution.py:76
  730.7 20.8 %collective-permute-start.51 = (bf16[11,128,128]{2,1,0:T(8,128)(2,1)}, bf16[11,128,128]{2,1,0:T(8,128)(2,1)}, u32[]{:S(2)}, u32[]{:S(2)}) collective-permute-start(bf16[11,128,128]{2,1,0:T(8,128)(2,1)} %get-tuple-element.192.refs_0_), channel_id=1, source_target_pairs={{0,8},{4,12},{8,0},{12,4},{16,24},{20,28},{24,16},{28,20},{1,9},{5... | collective-permute-start | bytes 1081352 | tf_op jit(solution)/shard_map/ppermute | solution.py:76
  (222 other events, 3325.8 us)
